TPU v7x, 512 devices: a whole 4x4x16 slice. The times are simulated.
512 devices in a mesh: index: 128 (over y, z, core), reader: 4 (over x).
Axes of the slice: x: 4, y: 4, z: 16, core: 2. Of those that a mesh axis runs over, the one named last changes fastest.
Arguments:
- index_emb: float32 [65536, 768], P('index'), may hold values from -6 to 6
- query_feat: bfloat16 [512, 768], P(('index', 'reader')), may hold values from -24 to 24
- query_proj: bfloat16 [768, 768], replicated, may hold values from -0.21875 to 0.21875
- passage_id: int32 [512, 20], P(('index', 'reader')), may hold values from 0 to 65535, as said below
- passage_len: int32 [512, 20], P('index'), may hold values from 1 to 8
- enc_out: bfloat16 [512, 20, 8, 4096], P('index', None, None, 'reader'), may hold values from -6 to 6
- key_proj: bfloat16 [4096, 4096], P('index', 'reader'), may hold values from -0.09375 to 0.09375
- key_gain: bfloat16 [4096], P('reader'), may hold values from 0.5 to 1.5
- dec_query: bfloat16 [512, 16, 4096], P('index', None, 'reader'), may hold values from -6 to 6
Outputs:
- grad_proj: float32 [768, 768], P('index')
- slab_best: float32 [512], P(('index', 'reader'))
- retr_loss: float32 [512], P(('index', 'reader'))
- log_target: float32 [512, 20], P(('index', 'reader'))
Inputs may be any that keep to these rules, and one draw needn't show every extreme that they name: `passage_id`: passage p is row p % 512 of index shard p // 512.
All inputs are finite; a program needn't handle non-finite values.
Results may differ from a plain program's by a relative error of at most 0.0003.
Values may be sent and summed in bfloat16 or wider, within the bound.
No kernel may reach another device: no remote copies, remote signals or barrier semaphores. Data moves between devices by JAX's collectives and lax.ppermute only.
A program may use at most 128 MiB of HBM per device.

v0:
```python
import math

import jax
import jax.numpy as jnp
from jax import lax
from jax.sharding import Mesh, PartitionSpec as P

HEADS = 64
DH = 64
ANS = 16
EPSILON = 1e-06
SOFTMAX_TEMPER = 0.05
EXACT = lax.Precision.HIGHEST
INDEX = ("y", "z", "core")


def shift(x, axis, step):
    size = lax.axis_size(axis)
    return lax.ppermute(x, axis, [((i + step) % size, i) for i in range(size)])


def reduce_direct(x, axis, merge):
    total = x[0]
    for s in range(1, lax.axis_size(axis)):
        total = merge(total, shift(x[s], axis, -s))
    return total


def ring_halves(x, axis):
    half = x.shape[0] // 2
    after = shift(x, axis, 1)
    before = shift(x, axis, -1)
    far = jnp.concatenate([shift(after[:half], axis, 1), shift(before[half:], axis, -1)])
    return [x, after, far, before]


def body(
    index_emb,
    query_feat,
    query_proj,
    passage_id,
    passage_len,
    enc_out,
    key_proj,
    key_gain,
    dec_query,
):
    y, z, core, r = (lax.axis_index(a) for a in ("y", "z", "core", "reader"))
    ny, nz, ncore, nx = (lax.axis_size(a) for a in ("y", "z", "core", "reader"))
    n_index = ny * nz * ncore
    my_shard = (y * nz + z) * ncore + core
    shard_rows, width = index_emb.shape
    topk = passage_id.shape[1]

    chip_pair = ("y", "core")
    n_pair = ny * ncore
    my_pair = y * ncore + core

    with jax.named_scope("gather_key_proj"):
        own_core = ring_halves(lax.all_gather(key_proj, "z"), "y")
        blocks = []
        for block in own_core:
            other = shift(block, "core", 1)
            low = jnp.where(core == 0, block, other)
            high = jnp.where(core == 0, other, block)
            blocks.append(jnp.stack([low, high], axis=1).reshape(-1, key_proj.shape[1]))
        weight_blocks = jnp.stack(blocks)

    group, _, plen, feats_here = enc_out.shape
    token_rows = group * topk * plen
    with jax.named_scope("gather_enc_out"):
        token_blocks = lax.all_gather(enc_out.reshape(token_rows, feats_here), "reader")

    with jax.named_scope("gather_queries"):
        ids_high = (passage_id // 256).astype(jnp.bfloat16)
        ids_low = (passage_id % 256).astype(jnp.bfloat16)
        packed = jnp.concatenate([query_feat, ids_high, ids_low], axis=1)
        packed = jnp.pad(packed, ((0, 0), (0, -packed.shape[1] % 128)))
        packed = lax.all_gather(packed[0], "reader")
        packed = lax.all_gather(packed, "z")
        packed = lax.all_gather(packed, chip_pair)
        packed = packed.reshape(n_index * nx, -1)
    feats = packed[:, :width]
    ids = packed[:, width : width + 2 * topk].astype(jnp.int32)
    ids = ids[:, :topk] * 256 + ids[:, topk:]
    row_index = ids - my_shard * shard_rows
    row_iota = lax.broadcasted_iota(jnp.int32, (1, shard_rows), 1)

    with jax.named_scope("scores"):
        query_vec = jnp.dot(feats, query_proj, preferred_element_type=jnp.float32)
        query_scale = lax.rsqrt(jnp.sum(query_vec * query_vec, axis=1, keepdims=True) + EPSILON)
        query_unit = query_vec * query_scale
        row_unit = index_emb * lax.rsqrt(
            jnp.sum(index_emb * index_emb, axis=1, keepdims=True) + EPSILON
        )
        share = lax.dynamic_index_in_dim(query_unit.reshape(n_index, nx, width), r, 1, False)
        share_rows = lax.dynamic_index_in_dim(row_index.reshape(n_index, nx, topk), r, 1, False)
        scores = (
            lax.dot_general(share, row_unit, (((1,), (1,)), ((), ())), precision=EXACT)
            / SOFTMAX_TEMPER
        )
        picked = [
            jnp.sum(
                jnp.where(share_rows[:, k : k + 1] == row_iota, scores, 0.0), axis=1, keepdims=True
            )
            for k in range(topk)
        ]
        state = jnp.concatenate(picked + [jnp.max(scores, axis=1, keepdims=True)], axis=1)

    def merge(a, b):
        lane = lax.broadcasted_iota(jnp.int32, a.shape, a.ndim - 1)
        return jnp.where(lane < topk, a + b, jnp.maximum(a, b))

    def merge_all(x):
        total = x[0]
        for part in range(1, x.shape[0]):
            total = merge(total, x[part])
        return total

    with jax.named_scope("reduce_scores"):
        state = state.reshape(n_pair, nz, topk + 1)
        state = merge_all(lax.all_to_all(state, chip_pair, 0, 0, tiled=True))
        state = merge_all(lax.all_to_all(state, "z", 0, 0, tiled=True))
        slab_best = state[topk:]
        fetched = lax.all_gather(state[:topk], "reader")
    expo = jnp.exp(fetched)
    total = jnp.sum(expo, axis=1, keepdims=True)
    prob = expo / total
    log_prob = fetched - jnp.log(total)

    with jax.named_scope("attention"):
        answer = dec_query.shape[1]
        heads_here = feats_here // DH
        keys = 0.0
        for j in range(nx):
            rows = lax.dynamic_index_in_dim(weight_blocks, (j - y) % ny, 0, False)
            keys += jnp.dot(token_blocks[j], rows, preferred_element_type=jnp.float32)
        keys = keys.reshape(group, topk * plen, heads_here, DH)
        gain = key_gain.astype(jnp.float32).reshape(heads_here, DH)
        key_unit = (
            keys * lax.rsqrt(jnp.mean(keys * keys, axis=3, keepdims=True) + EPSILON) * gain
        ).astype(jnp.bfloat16)
        decoded = dec_query.astype(jnp.float32).reshape(group, answer, heads_here, DH)
        dec_unit = (
            decoded * lax.rsqrt(jnp.mean(decoded * decoded, axis=3, keepdims=True) + EPSILON)
        ).astype(jnp.bfloat16)
        similarity_scores = jnp.einsum(
            "gahd,gnhd->ghan", dec_unit, key_unit, preferred_element_type=jnp.float32
        ) / math.sqrt(DH)
        positions = lax.broadcasted_iota(jnp.int32, (group, topk, plen), 2)
        live = (positions < passage_len[:, :, None]).reshape(group, 1, 1, topk * plen)
        weight = jnp.where(live, jnp.exp(similarity_scores), 0.0)
        attention = weight / jnp.sum(weight, axis=3, keepdims=True)
        partial_mass = jnp.sum(
            attention.reshape(group, heads_here, answer, topk, plen), axis=(1, 2, 4)
        ) / (HEADS * ANS)

    with jax.named_scope("targets"):
        target = jnp.sum(lax.all_gather(partial_mass, "reader"), axis=0)
        coef = (prob - target) / SOFTMAX_TEMPER
        all_coef = lax.all_gather(coef, "z")
        all_coef = lax.all_gather(all_coef, chip_pair)
        all_coef = all_coef.reshape(n_index * nx, topk)

    with jax.named_scope("gradient"):
        cols = width // nx
        my_rows = lax.dynamic_slice_in_dim(row_unit, r * cols, cols, 1)
        unit_cols = lax.dynamic_slice_in_dim(query_unit, r * cols, cols, 1)
        coef_matrix = jnp.zeros((n_index * nx, shard_rows), jnp.float32)
        for k in range(topk):
            coef_matrix = coef_matrix + jnp.where(
                row_index[:, k : k + 1] == row_iota, all_coef[:, k : k + 1], 0.0
            )
        along = SOFTMAX_TEMPER * jnp.sum(coef * fetched, axis=1, keepdims=True)
        part = jnp.dot(coef_matrix, my_rows, precision=EXACT)
        along = lax.dynamic_update_slice_in_dim(
            jnp.zeros((n_index * nx, 1), jnp.float32), along, (my_pair * nz + z) * nx, 0
        )
        part = (part - unit_cols * along) * query_scale
        six = width // n_index
        place = lax.broadcasted_iota(jnp.int32, (1, width), 1)
        to_core, to_y = place // (ny * nz * six), place // (nz * six) % ny
        to_z, within = place // six % nz, place % six
        column = ((to_y * nz + to_z) * ncore + (to_core + core) % ncore) * six + within
        chosen = (lax.broadcasted_iota(jnp.int32, (width, 1), 0) == column).astype(jnp.bfloat16)
        ordered = jnp.dot(feats, chosen, preferred_element_type=jnp.float32)
        term = lax.dot_general(ordered, part, (((0,), (0,)), ((), ())), precision=EXACT)

    with jax.named_scope("reduce_gradient"):
        term = term.reshape(ncore, ny, nz * six, cols)
        term = reduce_direct(term, "core", jnp.add)
        term = jnp.sum(lax.all_to_all(term, "y", 0, 0, tiled=True), axis=0)
        term = term.reshape(nz, six, cols)
        term = jnp.sum(lax.all_to_all(term, "z", 0, 0, tiled=True), axis=0)
        grad_proj = lax.all_gather(term, "reader")
        grad_proj = grad_proj.transpose(1, 0, 2).reshape(six, width)

    my_target = lax.dynamic_slice_in_dim(target, r, 1, 0)
    my_log_prob = lax.dynamic_slice_in_dim(log_prob, r, 1, 0)
    log_target = jnp.log(my_target)
    retr_loss = jnp.sum(my_target * (log_target - my_log_prob), axis=1)
    return (grad_proj, slab_best, retr_loss, log_target)


def solution(mesh):
    split = Mesh(mesh.devices.reshape(4, 16, 2, 4), INDEX + ("reader",))
    return jax.shard_map(
        body,
        mesh=split,
        in_specs=(
            P(INDEX, None),
            P(INDEX + ("reader",), None),
            P(),
            P(INDEX + ("reader",), None),
            P(INDEX, None),
            P(INDEX, None, None, "reader"),
            P(INDEX, "reader"),
            P("reader"),
            P(INDEX, None, "reader"),
        ),
        out_specs=(
            P(INDEX, None),
            P(INDEX + ("reader",)),
            P(INDEX + ("reader",)),
            P(INDEX + ("reader",), None),
        ),
        check_vma=False,
    )
```

profile of v0, /device:TPU:6, one launch (start us, length us, event | category | flops | bytes accessed | tf_op | source)
XLA Modules:
  0.0 317.2 jit_solution(8286154440853225403)
XLA Ops:
  10.1 14.5 %all-gather.8 = bf16[4,1,896]{2,1,0:T(2,128)(2,1)S(1)} all-gather(bf16[1,1,896]{2,1,0:T(2,128)(2,1)S(1)} %fusion.139), channel_id=1, replica_groups=mesh['y'=4,'z'=16,'core'=2,'reader'=4] {'reader'}, dimensions={0}, use_global_device_ids=true | all-gather | bytes 8960 | tf_op jit(solution)/shard_map/gather_queries/all_gather | solution.py:79
  24.6 33.4 %all-gather.9 = bf16[16,4,896]{2,1,0:T(4,128)(2,1)S(1)} all-gather(bf16[1,4,896]{2,1,0:T(4,128)(2,1)S(1)} %bitcast.279), channel_id=2, replica_groups=mesh['y'=4,'z'=16,'core'=2,'reader'=4] {'z'}, dimensions={0}, use_global_device_ids=true | all-gather | bytes 121856 | tf_op jit(solution)/shard_map/gather_queries/all_gather | solution.py:80
  58.0 14.1 %all-gather.1 = bf16[128,4,896]{2,1,0:T(4,128)(2,1)S(1)} all-gather(bf16[16,4,896]{2,1,0:T(4,128)(2,1)S(1)} %all-gather.9), channel_id=3, replica_groups=mesh['y'=4,'z'=16,'core'=2,'reader'=4] {'y','core'}, dimensions={0}, use_global_device_ids=true | all-gather | bytes 1032192 | tf_op jit(solution)/shard_map/gather_queries/all_gather | solution.py:81
  73.7 1.3 broadcast_multiply_fusion.1
  75.1 2.8 reshape.620
  77.9 1.7 constant_dynamic-slice_fusion.2
  80.0 1.1 copy-done.5
  81.2 1.9 select_reduce_fusion.17
  86.7 3.7 %all-to-all-start = ((f32[8,1,336]{2,1,0:T(1,128)}), f32[8,1,336]{2,1,0:T(1,128)S(1)}, u32[]{:S(2)}, u32[]{:S(2)}) async-start(f32[8,1,336]{2,1,0:T(1,128)} %reshape.665), calls=%async_computation | async-start | bytes 24576 | tf_op jit(solution)/shard_map/reduce_scores/all_to_all | solution.py:122
  90.9 2.0 fusion.1
  92.9 5.1 %collective-permute-start.1 = (bf16[16,32,1024]{2,1,0:T(8,128)(2,1)}, bf16[16,32,1024]{2,1,0:T(8,128)(2,1)S(1)}, u32[]{:S(2)}, u32[]{:S(2)}) collective-permute-start(bf16[16,32,1024]{2,1,0:T(8,128)(2,1)} %bitcast.268), channel_id=1, source_target_pairs={{128,0},{256,128},{384,256},{0,384},{129,1},{257,129},{385,257},{1... | collective-permute-start | bytes 3145736 | tf_op jit(solution)/shard_map/gather_key_proj/ppermute | solution.py:19
  99.0 1.9 collective-permute-start.4
  101.5 1.9 collective-permute-start
  105.7 7.0 %all-to-all-start.1 = ((f32[16,1,21]{2,1,0:T(1,128)}), f32[16,1,21]{2,1,0:T(1,128)S(1)}, u32[]{:S(2)}, u32[]{:S(2)}) async-start(f32[16,1,21]{2,1,0:T(1,128)} %bitcast.32), calls=%async_computation.1 | async-start | bytes 16384 | tf_op jit(solution)/shard_map/reduce_scores/all_to_all | solution.py:123
  113.5 1.3 dynamic-slice
  115.4 9.7 %all-to-all-done.1 = f32[16,1,21]{2,1,0:T(1,128)S(1)} async-done(((f32[16,1,21]{2,1,0:T(1,128)}), f32[16,1,21]{2,1,0:T(1,128)S(1)}, u32[]{:S(2)}, u32[]{:S(2)}) %all-to-all-start.1) | async-done | bytes 1376 | tf_op jit(solution)/shard_map/reduce_scores/all_to_all | solution.py:123
  125.9 5.1 %collective-permute-start.3 = (bf16[8,32,1024]{2,1,0:T(8,128)(2,1)}, bf16[8,32,1024]{2,1,0:T(8,128)(2,1)}, u32[]{:S(2)}, u32[]{:S(2)}) collective-permute-start(bf16[8,32,1024]{2,1,0:T(8,128)(2,1)} %slice.459), channel_id=1, source_target_pairs={{128,0},{256,128},{384,256},{0,384},{129,1},{257,129},{385,257},{1... | collective-permute-start | bytes 1572872 | tf_op jit(solution)/shard_map/gather_key_proj/ppermute | solution.py:19
  131.1 1.9 collective-permute-start.2
  133.1 7.5 %all-reduce.1 = f32[80]{0:T(128)S(1)} all-reduce(f32[80]{0:T(128)S(1)} %slice_dynamic-update-slice_fusion), channel_id=4, replica_groups=mesh['y'=4,'z'=16,'core'=2,'reader'=4] {'reader'}, use_global_device_ids=true, to_apply=%add.1 | all-reduce | flops 80 | bytes 640
  140.7 1.9 collective-permute-start.5
  142.8 1.9 collective-permute-start.7
  144.7 1.7 select_bitcast_fusion.7
  146.4 1.1 constant_dynamic-update-slice_fusion.22
  147.5 9.3 %collective-permute-done.5 = bf16[8,32,1024]{2,1,0:T(8,128)(2,1)S(1)} collective-permute-done((bf16[8,32,1024]{2,1,0:T(8,128)(2,1)S(1)}, bf16[8,32,1024]{2,1,0:T(8,128)(2,1)S(1)}, u32[]{:S(2)}, u32[]{:S(2)}) %collective-permute-start.5) | collective-permute-done | bytes 524320 | tf_op jit(solution)/shard_map/gather_key_proj/ppermute | solution.py:19
  156.9 1.9 collective-permute-start.6
  159.0 1.4 select_bitcast_fusion.5
  162.2 4.0 %pad_maximum_fusion = bf16[4,1024,1024]{2,1,0:T(8,128)(2,1)} fusion(bf16[1,1024,1024]{2,1,0:T(8,128)(2,1)S(1)} %bitcast.265, bf16[1,1024,1024]{2,1,0:T(8,128)(2,1)S(1)} %bitcast.266, bf16[1,1024,1024]{2,1,0:T(8,128)(2,1)S(1)} %bitcast.264, bf16[1,1024,1024]{2,1,0:T(8,128)(2,1)S(1)} %bitcast.263), kind=kLoop, calls=%fused_computation.1 | loop fusion | flops 12582912 | bytes 16777216 | tf_op jit(solution)/shard_map/gather_key_proj/stack | solution.py:67
  166.2 3.9 %fusion.4 = f32[1024,640]{1,0:T(8,128)S(1)} fusion(bf16[4,1024,1024]{2,1,0:T(8,128)(2,1)} %pad_maximum_fusion, s32[]{:T(128)S(6)} %select_n.467, bf16[4,640,1024]{2,1,0:T(8,128)(2,1)} %all-gather.16.cloned.1.call-done), kind=kOutput, calls=%fused_computation.13 | convolution fusion | flops 1342177280 | bytes 6029316 | tf_op jit(solution)/shard_map/attention/dot_general | solution.py:137
  170.6 3.4 %fusion.6 = f32[1024,640]{1,0:T(8,128)S(1)} fusion(bf16[4,1024,1024]{2,1,0:T(8,128)(2,1)S(1)} %copy-done.3, s32[]{:T(128)S(6)} %select_n.465, bf16[4,640,1024]{2,1,0:T(8,128)(2,1)} %all-gather.16.cloned.1.call-done), kind=kOutput, calls=%fused_computation.15 | convolution fusion | flops 1342177280 | bytes 6029316 | tf_op jit(solution)/shard_map/attention/dot_general | solution.py:137
  174.0 1.8 fusion.2
  175.8 3.5 %add_bitcast_fusion = f32[640,1024]{0,1:T(8,128)} fusion(f32[1024,640]{1,0:T(8,128)S(1)} %fusion.2, f32[1024,640]{1,0:T(8,128)S(1)} %fusion.4, f32[1024,640]{1,0:T(8,128)S(1)} %fusion.6, bf16[4,640,1024]{2,1,0:T(8,128)(2,1)S(1)} %bitcast.274, bf16[4,1024,1024]{2,1,0:T(8,128)(2,1)S(1)} %copy-done.3, s32[]{:T(128)S(6)} %select_n.463), kind=kOutput, calls=%fused_computation.4 | convolution fusion | flops 1344143360 | bytes 13893636 | tf_op jit(solution)/shard_map/attention/dot_general | solution.py:137
  179.3 6.0 %reshape.628 = f32[4,160,16,64]{1,0,3,2:T(4,128)} reshape(f32[640,1024]{0,1:T(8,128)} %add_bitcast_fusion) | data formatting | bytes 5242880 | tf_op jit(solution)/shard_map/attention/reshape | solution.py:138
  185.3 3.3 %multiply_reduce_fusion = f32[4,160,16]{1,0,2:T(4,128)S(1)} fusion(f32[4,160,16,64]{1,0,3,2:T(4,128)} %reshape.628), kind=kLoop, calls=%fused_computation.3 | loop fusion | flops 1300480 | bytes 2662400 | tf_op jit(solution)/shard_map/attention/reduce_sum | solution.py:141
  188.7 1.2 multiply_convert_fusion
  190.8 10.5 %all-gather.10 = f32[4,4,20]{2,1,0:T(4,128)S(1)} all-gather(f32[1,4,20]{2,1,0:T(4,128)S(1)} %multiply_bitcast_fusion), channel_id=6, replica_groups=mesh['y'=4,'z'=16,'core'=2,'reader'=4] {'reader'}, dimensions={0}, use_global_device_ids=true | all-gather | bytes 1600 | tf_op jit(solution)/shard_map/targets/all_gather | solution.py:159
  201.5 26.7 %all-gather.11 = f32[16,4,20]{2,1,0:T(4,128)S(1)} all-gather(f32[1,4,20]{2,1,0:T(4,128)S(1)} %bitcast.280), channel_id=7, replica_groups=mesh['y'=4,'z'=16,'core'=2,'reader'=4] {'z'}, dimensions={0}, use_global_device_ids=true | all-gather | bytes 5440 | tf_op jit(solution)/shard_map/targets/all_gather | solution.py:161
  228.2 13.0 %all-gather.6 = f32[128,4,20]{2,1,0:T(4,128)S(1)} all-gather(f32[16,4,20]{2,1,0:T(4,128)S(1)} %all-gather.11), channel_id=8, replica_groups=mesh['y'=4,'z'=16,'core'=2,'reader'=4] {'y','core'}, dimensions={0}, use_global_device_ids=true | all-gather | bytes 46080 | tf_op jit(solution)/shard_map/targets/all_gather | solution.py:162
  241.3 2.5 fusion.157
  247.8 1.1 copy.166
  253.7 7.0 %fusion.28 = f32[512,192]{1,0:T(8,128)S(1)} fusion(f32[512,768]{1,0:T(8,128)} %broadcast_multiply_fusion.1, s32[]{:T(128)S(6)} %select_n.491, f32[512,768]{1,0:T(8,128)} %copy-done.5, f32[512]{0:T(512)S(1)} %bitcast.300, s32[512]{0:T(512)S(1)} %bitcast.302, f32[512]{0:T(512)S(1)} %bitcast.287, s32[512]{0:T(512)} %bitcast.303, f32[512]{0:T(512)S(1)} %bitcast.286, ...), kind=kOutput, calls=%fused_computation.36 | convolution fusion | flops 619741184 | bytes 1528832 | tf_op jit(solution)/shard_map/gradient/dot_general | solution.py:175
  260.8 1.3 fusion.164
  262.5 2.4 collective-permute-start.8
  265.2 1.1 collective-permute-done.8
  266.3 11.3 %all_to_all.21 = f32[4,96,192]{1,2,0:T(8,128)S(1)} all-to-all(f32[4,96,192]{1,2,0:T(8,128)S(1)} %copy_add_fusion), channel_id=1, replica_groups=mesh['y'=4,'z'=16,'core'=2,'reader'=4] {'y'}, dimensions={0} | all-to-all | bytes 589824 | tf_op jit(solution)/shard_map/reduce_gradient/all_to_all | solution.py:192
  278.4 4.7 %all-to-all-start.3 = ((f32[16,6,192]{2,1,0:T(8,128)}), f32[16,6,192]{2,1,0:T(8,128)S(1)}, u32[]{:S(2)}, u32[]{:S(2)}) async-start(f32[16,6,192]{2,1,0:T(8,128)} %reshape.630), calls=%async_computation.3 | async-start | bytes 262144 | tf_op jit(solution)/shard_map/reduce_gradient/all_to_all | solution.py:194
  283.6 1.1 fusion.149
  284.7 12.5 %all-to-all-done.3 = f32[16,6,192]{2,1,0:T(8,128)S(1)} async-done(((f32[16,6,192]{2,1,0:T(8,128)}), f32[16,6,192]{2,1,0:T(8,128)S(1)}, u32[]{:S(2)}, u32[]{:S(2)}) %all-to-all-start.3) | async-done | bytes 73760 | tf_op jit(solution)/shard_map/reduce_gradient/all_to_all | solution.py:194
  297.2 12.4 %all-gather.12 = f32[4,6,192]{2,1,0:T(8,128)S(1)} all-gather(f32[1,6,192]{2,1,0:T(8,128)S(1)} %bitcast.278), channel_id=9, replica_groups=mesh['y'=4,'z'=16,'core'=2,'reader'=4] {'reader'}, dimensions={0}, use_global_device_ids=true | all-gather | bytes 23040 | tf_op jit(solution)/shard_map/reduce_gradient/all_gather | solution.py:195
  (190 shorter events, 29.4 us)
Async XLA Ops:
  7.2 65.7 %copy-start = (bf16[768,768]{1,0:T(8,128)(2,1)S(1)}, bf16[768,768]{1,0:T(8,128)(2,1)}, u32[]{:S(2)}) copy-start(bf16[768,768]{1,0:T(8,128)(2,1)} %param.11) | copy-start | bytes 3538948
  7.2 85.7 %all-gather.18.cloned.1.call-start = ((), (), s32[]{:S(2)}) async-start(), calls=%async_computation.5 | async-start | bytes 1114112 | tf_op jit(solution)/shard_map/gather_key_proj/all_gather | solution.py:60
  7.9 158.3 %all-gather.16.cloned.1.call-start = ((), (), s32[]{:S(2)}) async-start(), calls=%async_computation.4 | async-start | bytes 6553600 | tf_op jit(solution)/shard_map/gather_enc_out/all_gather | solution.py:72
  72.3 1.4 copy-start.7
  75.1 4.6 %copy-start.4 = (f32[512,768]{1,0:T(8,128)S(1)}, f32[512,768]{1,0:T(8,128)}, u32[]{:S(2)}) copy-start(f32[512,768]{1,0:T(8,128)} %param.9) | copy-start | bytes 4718596
  80.0 1.2 copy-start.5
  80.0 10.4 %copy-start.11 = (bf16[4,16,1024]{2,1,0:T(8,128)(2,1)S(1)}, bf16[4,16,1024]{2,1,0:T(8,128)(2,1)}, u32[]{:S(2)}) copy-start(bf16[4,16,1024]{2,1,0:T(8,128)(2,1)} %param.17) | copy-start | bytes 393220
  81.2 9.7 %copy-start.8 = (bf16[512,896]{1,0:T(8,128)(2,1)S(1)}, bf16[512,896]{1,0:T(8,128)(2,1)}, u32[]{:S(2)}) copy-start(bf16[512,896]{1,0:T(8,128)(2,1)} %copy-done.7) | copy-start | bytes 2752516
  86.7 17.0 %all-to-all-start = ((f32[8,1,336]{2,1,0:T(1,128)}), f32[8,1,336]{2,1,0:T(1,128)S(1)}, u32[]{:S(2)}, u32[]{:S(2)}) async-start(f32[8,1,336]{2,1,0:T(1,128)} %reshape.665), calls=%async_computation | async-start | bytes 24576 | tf_op jit(solution)/shard_map/reduce_scores/all_to_all | solution.py:122
  90.9 12.6 %copy-start.12 = (s32[4,20]{1,0:T(4,128)S(1)}, s32[4,20]{1,0:T(4,128)}, u32[]{:S(2)}) copy-start(s32[4,20]{1,0:T(4,128)} %param.13) | copy-start | bytes 964
  90.9 22.5 %copy-start.13 = (bf16[1024]{0:T(1024)(128)(2,1)S(1)}, bf16[1024]{0:T(1024)(128)(2,1)}, u32[]{:S(2)}) copy-start(bf16[1024]{0:T(1024)(128)(2,1)} %param.16) | copy-start | bytes 6148
  92.9 32.2 %collective-permute-start.1 = (bf16[16,32,1024]{2,1,0:T(8,128)(2,1)}, bf16[16,32,1024]{2,1,0:T(8,128)(2,1)S(1)}, u32[]{:S(2)}, u32[]{:S(2)}) collective-permute-start(bf16[16,32,1024]{2,1,0:T(8,128)(2,1)} %bitcast.268), channel_id=1, source_target_pairs={{128,0},{256,128},{384,256},{0,384},{129,1},{257,129},{385,257},{1... | collective-permute-start | bytes 3145736 | tf_op jit(solution)/shard_map/gather_key_proj/ppermute | solution.py:19
  99.0 41.8 %collective-permute-start.4 = (bf16[16,32,1024]{2,1,0:T(8,128)(2,1)}, bf16[16,32,1024]{2,1,0:T(8,128)(2,1)S(1)}, u32[]{:S(2)}, u32[]{:S(2)}) collective-permute-start(bf16[16,32,1024]{2,1,0:T(8,128)(2,1)} %bitcast.269), channel_id=1, source_target_pairs={{384,0},{0,128},{128,256},{256,384},{385,1},{1,129},{129,257},{257... | collective-permute-start | bytes 3145736 | tf_op jit(solution)/shard_map/gather_key_proj/ppermute | solution.py:19
  101.5 43.2 %collective-permute-start = (bf16[16,32,1024]{2,1,0:T(8,128)(2,1)}, bf16[16,32,1024]{2,1,0:T(8,128)(2,1)}, u32[]{:S(2)}, u32[]{:S(2)}) collective-permute-start(bf16[16,32,1024]{2,1,0:T(8,128)(2,1)} %bitcast.270), channel_id=1, source_target_pairs={{4,0},{0,4},{5,1},{1,5},{6,2},{2,6},{7,3},{3,7},{12,8},{8,12},{13,... | collective-permute-start | bytes 3145736 | tf_op jit(solution)/shard_map/gather_key_proj/ppermute | solution.py:19
  105.7 19.4 %all-to-all-start.1 = ((f32[16,1,21]{2,1,0:T(1,128)}), f32[16,1,21]{2,1,0:T(1,128)S(1)}, u32[]{:S(2)}, u32[]{:S(2)}) async-start(f32[16,1,21]{2,1,0:T(1,128)} %bitcast.32), calls=%async_computation.1 | async-start | bytes 16384 | tf_op jit(solution)/shard_map/reduce_scores/all_to_all | solution.py:123
  125.1 21.3 %copy-start.14 = (f32[21]{0:T(128)}, f32[21]{0:T(128)S(1)}, u32[]{:S(2)}) copy-start(f32[21]{0:T(128)S(1)} %maximum_select_fusion.1) | copy-start | bytes 256
  125.9 20.5 %collective-permute-start.3 = (bf16[8,32,1024]{2,1,0:T(8,128)(2,1)}, bf16[8,32,1024]{2,1,0:T(8,128)(2,1)}, u32[]{:S(2)}, u32[]{:S(2)}) collective-permute-start(bf16[8,32,1024]{2,1,0:T(8,128)(2,1)} %slice.459), channel_id=1, source_target_pairs={{128,0},{256,128},{384,256},{0,384},{129,1},{257,129},{385,257},{1... | collective-permute-start | bytes 1572872 | tf_op jit(solution)/shard_map/gather_key_proj/ppermute | solution.py:19
  131.1 28.0 %collective-permute-start.2 = (bf16[16,32,1024]{2,1,0:T(8,128)(2,1)S(1)}, bf16[16,32,1024]{2,1,0:T(8,128)(2,1)}, u32[]{:S(2)}, u32[]{:S(2)}) collective-permute-start(bf16[16,32,1024]{2,1,0:T(8,128)(2,1)S(1)} %collective-permute-done.1), channel_id=1, source_target_pairs={{4,0},{0,4},{5,1},{1,5},{6,2},{2,6},{7,3},{3,7},{12,8},{8,12},{13,... | collective-permute-start | bytes 3145736 | tf_op jit(solution)/shard_map/gather_key_proj/ppermute | solution.py:19
  140.7 16.1 %collective-permute-start.5 = (bf16[8,32,1024]{2,1,0:T(8,128)(2,1)S(1)}, bf16[8,32,1024]{2,1,0:T(8,128)(2,1)S(1)}, u32[]{:S(2)}, u32[]{:S(2)}) collective-permute-start(bf16[8,32,1024]{2,1,0:T(8,128)(2,1)S(1)} %slice.460), channel_id=1, source_target_pairs={{384,0},{0,128},{128,256},{256,384},{385,1},{1,129},{129,257},{257... | collective-permute-start | bytes 1572872 | tf_op jit(solution)/shard_map/gather_key_proj/ppermute | solution.py:19
  142.8 18.1 %collective-permute-start.7 = (bf16[16,32,1024]{2,1,0:T(8,128)(2,1)S(1)}, bf16[16,32,1024]{2,1,0:T(8,128)(2,1)S(1)}, u32[]{:S(2)}, u32[]{:S(2)}) collective-permute-start(bf16[16,32,1024]{2,1,0:T(8,128)(2,1)S(1)} %collective-permute-done.4), channel_id=1, source_target_pairs={{4,0},{0,4},{5,1},{1,5},{6,2},{2,6},{7,3},{3,7},{12,8},{8,12},{13,... | collective-permute-start | bytes 3145736 | tf_op jit(solution)/shard_map/gather_key_proj/ppermute | solution.py:19
  156.9 4.6 %collective-permute-start.6 = (bf16[16,32,1024]{2,1,0:T(8,128)(2,1)S(1)}, bf16[16,32,1024]{2,1,0:T(8,128)(2,1)S(1)}, u32[]{:S(2)}, u32[]{:S(2)}) collective-permute-start(bf16[16,32,1024]{2,1,0:T(8,128)(2,1)S(1)} %constant_dynamic-update-slice_fusion.21), channel_id=1, source_target_pairs={{4,0},{0,4},{5,1},{1,5},{6,2},{2,6},{7,3},{3,7},{12,8},{8,12},{13,... | collective-permute-start | bytes 3145736 | tf_op jit(solution)/shard_map/gather_key_proj/ppermute | solution.py:19
  166.2 4.4 %copy-start.3 = (bf16[4,1024,1024]{2,1,0:T(8,128)(2,1)S(1)}, bf16[4,1024,1024]{2,1,0:T(8,128)(2,1)}, u32[]{:S(2)}) copy-start(bf16[4,1024,1024]{2,1,0:T(8,128)(2,1)} %pad_maximum_fusion) | copy-start | bytes 25165828
  166.2 7.8 %slice-start = ((s8[5242880]{0:T(1024)(128)(4,1)}), s8[4194304]{0:T(1024)(128)(4,1)S(1)}, s32[]{:S(2)}) async-start(s8[5242880]{0:T(1024)(128)(4,1)} %bitcast.273), calls=%async_computation.6 | async-start | bytes 8388608
  170.6 3.4 %slice-start.1 = ((s8[5242880]{0:T(1024)(128)(4,1)}), s8[1048576]{0:T(1024)(128)(4,1)S(1)}, s32[]{:S(2)}) async-start(s8[5242880]{0:T(1024)(128)(4,1)} %bitcast.273), calls=%async_computation.7 | async-start | bytes 2097152
  185.3 3.4 %copy-start.2 = (f32[4,160,16,64]{1,0,3,2:T(4,128)S(1)}, f32[4,160,16,64]{1,0,3,2:T(4,128)}, u32[]{:S(2)}) copy-start(f32[4,160,16,64]{1,0,3,2:T(4,128)} %reshape.628) | copy-start | bytes 7864324
  188.7 1.3 copy-start.10
  247.8 5.8 %copy-start.9 = (f32[512,1]{1,0:T(8,128)S(1)}, f32[512,1]{1,0:T(8,128)}, u32[]{:S(2)}) copy-start(f32[512,1]{1,0:T(8,128)} %slice.503) | copy-start | bytes 6148
  253.7 7.0 %copy-start.6 = (f32[512,768]{1,0:T(8,128)S(1)}, f32[512,768]{1,0:T(8,128)}, u32[]{:S(2)}) copy-start(f32[512,768]{1,0:T(8,128)} %fusion.1) | copy-start | bytes 4718596
  262.5 47.8 %copy-start.1 = (bf16[768,768]{1,0:T(8,128)(2,1)S(1)}, bf16[768,768]{1,0:T(8,128)(2,1)}, u32[]{:S(2)}) copy-start(bf16[768,768]{1,0:T(8,128)(2,1)} %param.11) | copy-start | bytes 3538948
  262.5 20.5 %copy-start.15 = (f32[21]{0:T(128)S(1)}, f32[21]{0:T(128)}, u32[]{:S(2)}) copy-start(f32[21]{0:T(128)} %copy-done.14) | copy-start | bytes 256
  262.5 3.7 %collective-permute-start.8 = (f32[4,96,192]{1,2,0:T(8,128)S(1)}, f32[4,96,192]{1,2,0:T(8,128)S(1)}, u32[]{:S(2)}, u32[]{:S(2)}) collective-permute-start(f32[4,96,192]{1,2,0:T(8,128)S(1)} %copy.141), channel_id=1, source_target_pairs={{4,0},{0,4},{5,1},{1,5},{6,2},{2,6},{7,3},{3,7},{12,8},{8,12},{13,... | collective-permute-start | bytes 884744 | tf_op jit(solution)/shard_map/reduce_gradient/ppermute | solution.py:19
  278.4 18.9 %all-to-all-start.3 = ((f32[16,6,192]{2,1,0:T(8,128)}), f32[16,6,192]{2,1,0:T(8,128)S(1)}, u32[]{:S(2)}, u32[]{:S(2)}) async-start(f32[16,6,192]{2,1,0:T(8,128)} %reshape.630), calls=%async_computation.3 | async-start | bytes 262144 | tf_op jit(solution)/shard_map/reduce_gradient/all_to_all | solution.py:194
Sparse Core Ops, SparseCore 0:
  10.1 75.5 all-gather.17
  87.8 59.9 all-gather.15
where the time goes:
time: 320 us; the launch traced here: 317 us
  blocking collectives  143 us (45%)
  starting transfers between devices  39.6 us (12%)
  local copies, waits for them, and re-layouts  37.2 us (12%)
  waiting for transfers between devices  34 us (11%)
  matrix products  26.4 us (8%)
  other arithmetic  21 us (7%)
  between operations  15.7 us (5%)
    all_gather x1, blocking collectives, body(): packed = lax.all_gather(packed, 'z')  33.4 us
    all_gather x1, blocking collectives, body(): all_coef = lax.all_gather(coef, 'z')  26.7 us
    ppermute x9, starting transfers between devices, shift(): return lax.ppermute(x, axis, [((i + step) % size, i) for i in range(size)])  24.1 us
    all_gather x1, blocking collectives, body(): packed = lax.all_gather(packed[0], 'reader')  14.5 us
    unnamed x84, local copies, waits for them, and re-layouts  14.3 us
    all_gather x1, blocking collectives, body(): packed = lax.all_gather(packed, chip_pair)  14.1 us
    all_gather x1, blocking collectives, body(): all_coef = lax.all_gather(all_coef, chip_pair)  13 us
    dot_general x4, matrix products, body(): keys += jnp.dot(token_blocks[j], rows, preferred_element_type=jnp.float32)  12.6 us
  transfers between devices with their start and end apart: 14, of which 4 were waited for; matrix products, arithmetic and copies ran while one was open for 11% of the time, Pallas kernels for 0%

commit v1 on v0

v1 whole, which is shorter than its diff:
```python
import functools
import math

import jax
import jax.numpy as jnp
from jax import lax
from jax.experimental import pallas as pl
from jax.experimental.pallas import tpu as pltpu
from jax.sharding import Mesh, PartitionSpec as P

HEADS = 64
DH = 64
ANS = 16
EPSILON = 1e-06
SOFTMAX_TEMPER = 0.05
EXACT = lax.Precision.HIGHEST
INDEX = ("y", "zq", "zr", "core")
Z = ("zq", "zr")
NEAR = ("reader", "y", "core")
LANES = 128
SLOT = 32
TILE = 256
N_OWNERS = 128


def shift(x, axis, step):
    size = lax.axis_size(axis)
    return lax.ppermute(x, axis, [((i + step) % size, i) for i in range(size)])


def send_all(x, axis):
    size = lax.axis_size(axis)
    return lax.all_to_all(jnp.broadcast_to(x[None], (size, *x.shape)), axis, 0, 0, tiled=True)


def halves(x):
    high = x.astype(jnp.bfloat16)
    return high, (x - high.astype(jnp.float32)).astype(jnp.bfloat16)


def dot32(a, b):
    return jnp.dot(a, b, preferred_element_type=jnp.float32)


def attention_kernel(place, tokens, *refs):
    weights, refs = refs[:8], refs[8:]
    dec, gain, live, scores, out, token_v, weight_v, keys_v, column_v, token_sem, weight_sem = refs
    y, zr, core = place[0], place[1], place[2]
    group = dec.shape[0]
    n = live.shape[1]
    for c in range(4):
        pltpu.make_async_copy(tokens.at[c], token_v.at[c], token_sem.at[c]).start()

    def spot(row, residue, which):
        return weight_v.at[row, :, (zr + residue) % 4, (core + which) % 2]

    def weight_copy(ahead, which, residue):
        return pltpu.make_async_copy(
            weights[2 * ahead + which].at[pl.ds(4 * residue, 4)],
            spot((y + ahead) % 4, residue, which),
            weight_sem.at[(y + ahead) % 4, which, residue],
        )

    for ahead in range(4):
        for which in range(2):
            for residue in range(4):
                weight_copy(ahead, which, residue).start()
    for c in range(4):
        pltpu.make_async_copy(tokens.at[c], token_v.at[c], token_sem.at[c]).wait()
        for which in range(2):
            for residue in range(4):
                here = spot(c, residue, which)
                pltpu.make_async_copy(here, here, weight_sem.at[c, which, residue]).wait()

        @pl.loop(0, keys_v.shape[1] // TILE)
        def _(t):
            cols = pl.ds(pl.multiple_of(t * TILE, TILE), TILE)
            rows = weight_v[c, :, :, :, :, cols].reshape(-1, TILE)
            term = dot32(token_v[c], rows)
            if c == 0:
                keys_v[:, cols] = term
            else:
                keys_v[:, cols] += term

    column_v[...] = jnp.zeros_like(column_v)

    @pl.loop(0, keys_v.shape[1] // TILE)
    def _(t):
        cols = pl.ds(pl.multiple_of(t * TILE, TILE), TILE)
        same = (
            lax.broadcasted_iota(jnp.int32, (TILE, TILE), 0) // DH
            == lax.broadcasted_iota(jnp.int32, (TILE, TILE), 1) // DH
        ).astype(jnp.bfloat16)
        mine = (
            lax.broadcasted_iota(jnp.int32, (TILE // DH * ANS, TILE), 0) // ANS
            == lax.broadcasted_iota(jnp.int32, (TILE // DH * ANS, TILE), 1) // DH
        )
        keys = keys_v[:, cols]
        high, low = halves(keys * keys)
        square = (dot32(high, same) + dot32(low, same)) / DH
        unit = (keys * lax.rsqrt(square + EPSILON) * gain[:, cols]).astype(jnp.bfloat16)
        for g in range(group):
            answer = dec[g, :, cols].astype(jnp.float32)
            answer = jnp.concatenate([answer] * (TILE // DH), axis=0)
            answer = jnp.where(mine, answer, 0.0).astype(jnp.bfloat16)
            similarity = lax.dot_general(
                answer,
                unit[g * n : (g + 1) * n],
                (((1,), (1,)), ((), ())),
                preferred_element_type=jnp.float32,
            ) / math.sqrt(DH)
            weight = jnp.where(live[g : g + 1, :] > 0, jnp.exp(similarity), 0.0)
            weight = weight / jnp.sum(weight, axis=1, keepdims=True)
            column_v[g : g + 1, :] += jnp.sum(weight, axis=0, keepdims=True)

    mass = jnp.zeros((8, LANES), jnp.float32)
    for g in range(group):
        column = jnp.broadcast_to(column_v[g : g + 1, :], (8, n))
        to = (
            lax.broadcasted_iota(jnp.int32, (n, LANES), 0) // 8 + g * SLOT
            == lax.broadcasted_iota(jnp.int32, (n, LANES), 1)
        ).astype(jnp.float32)
        mass += jnp.dot(column, to, precision=EXACT, preferred_element_type=jnp.float32)
    out[:, :LANES] = jnp.broadcast_to(mass[:1] / (HEADS * ANS), (out.shape[0], LANES))
    out[:, LANES:] = jnp.broadcast_to(scores[...], (out.shape[0], LANES))


def attention_packet(place, tokens, weights, dec, gain, live, scores):
    vmem = pl.BlockSpec(memory_space=pltpu.VMEM)
    anywhere = pl.BlockSpec(memory_space=pl.ANY)
    _, rows, width = tokens.shape
    return pl.pallas_call(
        attention_kernel,
        out_shape=jax.ShapeDtypeStruct((32, 2 * LANES), jnp.float32),
        in_specs=[pl.BlockSpec(memory_space=pltpu.SMEM)] + [anywhere] * 9 + [vmem] * 4,
        out_specs=vmem,
        scratch_shapes=[
            pltpu.VMEM((4, rows, width), jnp.bfloat16),
            pltpu.VMEM((4, 4, 4, 2, *weights[0].shape[1:]), jnp.bfloat16),
            pltpu.VMEM((rows, width), jnp.float32),
            pltpu.VMEM((8, live.shape[1]), jnp.float32),
            pltpu.SemaphoreType.DMA((4,)),
            pltpu.SemaphoreType.DMA((4, 2, 4)),
        ],
        compiler_params=pltpu.CompilerParams(vmem_limit_bytes=40 << 20),
        cost_estimate=pl.CostEstimate(
            flops=2 * rows * 4 * width * width, bytes_accessed=14 << 20, transcendentals=200000
        ),
        name="attention",
    )(place, tokens, *weights, dec, gain, live, scores)


def coef_kernel(packets, out):
    lane = lax.broadcasted_iota(jnp.int32, (8, LANES), 1)
    target = prob = fetched = jnp.zeros((8, LANES), jnp.float32)
    for x in range(4):
        target += packets[x, :, :LANES]
        scores = packets[x, :, LANES:]
        own = (lane // SLOT == x) & (lane % SLOT < 20)
        moved = scores if x == 0 else pltpu.roll(scores, SLOT * x, 1)
        prob += jnp.where(own, moved, 0.0)
        moved = pltpu.roll(scores, (SLOT * x + LANES // 2) % LANES, 1)
        fetched += jnp.where(own, moved, 0.0)
    gap = prob - target
    to = (
        lax.broadcasted_iota(jnp.int32, (LANES, LANES), 0) // SLOT * SLOT + 20
        == lax.broadcasted_iota(jnp.int32, (LANES, LANES), 1)
    ).astype(jnp.float32)
    along = jnp.dot(gap * fetched, to, precision=EXACT, preferred_element_type=jnp.float32)
    packed = gap / SOFTMAX_TEMPER + along / N_OWNERS
    out[...] = jnp.broadcast_to(packed[None], out.shape)


def gradient_kernel(coef, slot, rows, unit, scale, ordered, keep, send, matrix_v):
    n_rows = matrix_v.shape[1]
    blocks = coef.shape[0]

    @pl.loop(0, blocks // 8)
    def _(b):
        eight = pl.ds(pl.multiple_of(b * 8, 8), 8)
        row = lax.broadcasted_iota(jnp.int32, (8, n_rows), 1)
        values, places = coef[eight, :], slot[eight, :]
        for x in range(4):
            total = jnp.zeros((8, n_rows), jnp.float32)
            for k in range(SLOT * x, SLOT * x + 20):
                total += jnp.where(places[:, k : k + 1] == row, values[:, k : k + 1], 0.0)
            matrix_v[pl.ds(pl.multiple_of(x * blocks + b * 8, 8), 8), :] = total

    row_high, row_low = halves(rows[...])
    parts_high, parts_low = [], []
    for x in range(4):
        mine = slice(x * blocks, (x + 1) * blocks)
        high, low = halves(matrix_v[mine, :])
        part = dot32(high, row_high) + (dot32(high, row_low) + dot32(low, row_high))
        along = coef[:, SLOT * x + 20 : SLOT * x + 21]
        part = (part - unit[mine, :] * along) * scale[mine, :]
        high, low = halves(part)
        parts_high.append(high)
        parts_low.append(low)
    high, low = jnp.concatenate(parts_high, axis=0), jnp.concatenate(parts_low, axis=0)
    half = keep.shape[0]
    keep[...] = dot32(ordered[:half, :], high) + dot32(ordered[:half, :], low)
    send[...] = dot32(ordered[half:, :], high) + dot32(ordered[half:, :], low)


def body(
    index_emb,
    query_feat,
    query_proj,
    passage_id,
    passage_len,
    enc_out,
    key_proj,
    key_gain,
    dec_query,
):
    y, zq, zr, core, r = (lax.axis_index(a) for a in (*INDEX, "reader"))
    ny, nz, ncore, nx = 4, 16, 2, 4
    z = zq * 4 + zr
    n_index = ny * nz * ncore
    n_pair = ny * ncore
    my_shard = (y * nz + z) * ncore + core
    shard_rows, width = index_emb.shape
    topk = passage_id.shape[1]

    group, _, plen, feats_here = enc_out.shape
    token_rows = group * topk * plen
    with jax.named_scope("gather_enc_out"):
        token_blocks = lax.all_gather(enc_out.reshape(token_rows, feats_here), "reader")

    with jax.named_scope("gather_key_proj"):
        own = send_all(key_proj, "zq")
        after, before = shift(own, Z, 1), shift(own, Z, -1)
        far = [shift(own[:2], Z, 2), shift(own[2:], Z, -2)]
        own = jnp.concatenate([own, after, *far, before])
        after, before = shift(own, "y", 1), shift(own, "y", -1)
        far = jnp.concatenate([shift(after[:8], "y", 1), shift(before[8:], "y", -1)])
        weights = []
        for block in (own, after, far, before):
            weights += [block, shift(block, "core", 1)]

    with jax.named_scope("gather_queries"):
        ids_high = (passage_id // 256).astype(jnp.bfloat16)
        ids_low = (passage_id % 256).astype(jnp.bfloat16)
        packed = jnp.concatenate([query_feat, ids_high, ids_low], axis=1)
        packed = jnp.pad(packed, ((0, 0), (0, -packed.shape[1] % LANES)))
        packed = send_all(packed[0], Z)
        packed = send_all(packed, NEAR)
        packed = packed.reshape(nx, n_pair, nz, -1).transpose(0, 2, 1, 3).reshape(n_index * nx, -1)
    feats = packed[:, :width]
    ids = packed[:, width : width + 2 * topk].astype(jnp.int32)
    ids = ids[:, :topk] * 256 + ids[:, topk:]
    row_index = (ids - my_shard * shard_rows).reshape(nx, n_index, topk)
    row_iota = lax.broadcasted_iota(jnp.int32, (1, shard_rows), 1)

    with jax.named_scope("scores"):
        query_vec = jnp.dot(feats, query_proj, preferred_element_type=jnp.float32)
        query_scale = lax.rsqrt(jnp.sum(query_vec * query_vec, axis=1, keepdims=True) + EPSILON)
        query_unit = query_vec * query_scale
        row_unit = index_emb * lax.rsqrt(
            jnp.sum(index_emb * index_emb, axis=1, keepdims=True) + EPSILON
        )
        share = lax.dynamic_index_in_dim(query_unit.reshape(nx, n_index, width), r, 0, False)
        share_rows = lax.dynamic_index_in_dim(row_index, r, 0, False)
        scores = (
            lax.dot_general(share, row_unit, (((1,), (1,)), ((), ())), precision=EXACT)
            / SOFTMAX_TEMPER
        )
        picked = [
            jnp.sum(
                jnp.where(share_rows[:, k : k + 1] == row_iota, scores, 0.0), axis=1, keepdims=True
            )
            for k in range(topk)
        ]
        state = jnp.concatenate(picked + [jnp.max(scores, axis=1, keepdims=True)], axis=1)

    def merge_all(x):
        lane = lax.broadcasted_iota(jnp.int32, x.shape[1:], x.ndim - 2)
        return jnp.where(lane < topk, jnp.sum(x, axis=0), jnp.max(x, axis=0))

    with jax.named_scope("reduce_scores"):
        state = state.reshape(nz, n_pair, topk + 1)
        state = merge_all(lax.all_to_all(state, Z, 0, 0, tiled=True))
        state = merge_all(lax.all_to_all(state, ("y", "core"), 0, 0, tiled=True))
        slab_best = state[topk:]
        fetched = state[:topk]
    expo = jnp.exp(fetched)
    total = jnp.sum(expo)
    prob = expo / total
    log_prob = fetched - jnp.log(total)
    score_row = jnp.zeros((1, LANES), jnp.float32)
    score_row = score_row.at[0, :topk].set(prob).at[0, LANES // 2 : LANES // 2 + topk].set(fetched)

    with jax.named_scope("gradient_operands"):
        cols = width // nx
        my_rows = lax.dynamic_slice_in_dim(row_unit, r * cols, cols, 1)
        my_unit = lax.dynamic_slice_in_dim(query_unit, r * cols, cols, 1)
        slot_rows = jnp.pad(row_index, ((0, 0), (0, 0), (0, SLOT - topk)), constant_values=-1)
        slot_rows = slot_rows.transpose(1, 0, 2).reshape(n_index, LANES)
        six = width // n_index
        place = lax.broadcasted_iota(jnp.int32, (1, width), 1)
        to_core, to_y = place // (ny * nz * six), place // (nz * six) % ny
        to_z, within = place // six % nz, place % six
        column = ((to_y * nz + to_z) * ncore + (to_core + core) % ncore) * six + within
        chosen = (lax.broadcasted_iota(jnp.int32, (width, 1), 0) == column).astype(jnp.bfloat16)
        ordered = lax.dot_general(
            chosen, feats, (((0,), (1,)), ((), ())), preferred_element_type=jnp.bfloat16
        )

    with jax.named_scope("attention"):
        answer = dec_query.shape[1]
        heads_here = feats_here // DH
        decoded = dec_query.astype(jnp.float32).reshape(group, answer, heads_here, DH)
        dec_unit = (
            decoded * lax.rsqrt(jnp.mean(decoded * decoded, axis=3, keepdims=True) + EPSILON)
        ).astype(jnp.bfloat16)
        positions = lax.broadcasted_iota(jnp.int32, (group, topk, plen), 2)
        live = (positions < passage_len[:, :, None]).reshape(group, topk * plen)
        packet = attention_packet(
            jnp.stack([y, zr, core]).astype(jnp.int32),
            token_blocks,
            weights,
            dec_unit.reshape(group, answer, feats_here),
            key_gain.astype(jnp.float32).reshape(1, feats_here),
            live.astype(jnp.float32),
            score_row,
        )

    with jax.named_scope("targets"):
        packets = lax.all_to_all(packet, NEAR, 0, 0, tiled=True).reshape(nx, n_pair, 2 * LANES)
        vmem = pl.BlockSpec(memory_space=pltpu.VMEM)
        coef = pl.pallas_call(
            coef_kernel,
            out_shape=jax.ShapeDtypeStruct((nz, n_pair, LANES), jnp.float32),
            in_specs=[vmem],
            out_specs=vmem,
            name="coef",
        )(packets)
        coef = lax.all_to_all(coef, Z, 0, 0, tiled=True).reshape(n_index, LANES)

    with jax.named_scope("gradient"):
        part = jax.ShapeDtypeStruct((width // ncore, cols), jnp.float32)
        keep, send = pl.pallas_call(
            gradient_kernel,
            out_shape=(part, part),
            in_specs=[vmem] * 6,
            out_specs=(vmem, vmem),
            scratch_shapes=[pltpu.VMEM((n_index * nx, shard_rows), jnp.float32)],
            compiler_params=pltpu.CompilerParams(vmem_limit_bytes=40 << 20),
            name="gradient",
        )(coef, slot_rows, my_rows, my_unit, query_scale, ordered)

    with jax.named_scope("reduce_gradient"):
        term = (keep + shift(send, "core", 1)).reshape(ny, nz * six, cols)
        term = jnp.sum(lax.all_to_all(term, "y", 0, 0, tiled=True), axis=0)
        term = term.reshape(nz, six, cols)
        term = jnp.sum(lax.all_to_all(term, Z, 0, 0, tiled=True), axis=0)
        grad_proj = send_all(term, "reader")
        grad_proj = grad_proj.transpose(1, 0, 2).reshape(six, width)

    mass = jnp.sum(lax.dynamic_index_in_dim(packets, y * ncore + core, 1, False), axis=0)
    my_target = lax.dynamic_slice_in_dim(mass, r * SLOT, topk, 0)
    log_target = jnp.log(my_target)
    retr_loss = jnp.sum(my_target * (log_target - log_prob))
    return (grad_proj, slab_best, retr_loss[None], log_target[None])


def solution(mesh):
    split = Mesh(mesh.devices.reshape(4, 4, 4, 2, 4), INDEX + ("reader",))
    return jax.shard_map(
        body,
        mesh=split,
        in_specs=(
            P(INDEX, None),
            P(INDEX + ("reader",), None),
            P(),
            P(INDEX + ("reader",), None),
            P(INDEX, None),
            P(INDEX, None, None, "reader"),
            P(INDEX, "reader"),
            P("reader"),
            P(INDEX, None, "reader"),
        ),
        out_specs=(
            P(INDEX, None),
            P(INDEX + ("reader",)),
            P(INDEX + ("reader",)),
            P(INDEX + ("reader",), None),
        ),
        check_vma=False,
    )
```

time: 320 us -> 314 us (0.981)
  blocking collectives: 143 us -> 11 us
  starting transfers between devices: 39.6 us -> 98.2 us
  waiting for transfers between devices: 34 us -> 92.3 us
  Pallas kernels: 0 us -> 22.1 us
  matrix products: 26.4 us -> 6.35 us
  local copies, waits for them, and re-layouts: 37.2 us -> 50.6 us
  other arithmetic: 21 us -> 14.6 us
    all_gather x7 -> x0, blocking collectives: 125 us -> none  [the longest x1 33.4 us: body(): packed = lax.all_gather(packed, 'z')]
    all_to_all x3 -> x9, waiting for transfers between devices: 22.1 us -> 69.3 us  [the longest x4 27.3 us: send_all(): lax.all_to_all(jnp.broadcast_to(x[None], (size, *x.shape)), axis, 0, 0, t...]
    all_to_all x3 -> x9, starting transfers between devices: 15.4 us -> 59.2 us  [the longest x4 31.6 us: send_all(): lax.all_to_all(jnp.broadcast_to(x[None], (size, *x.shape)), axis, 0, 0, t...]
    dot_general x7 -> x0, matrix products: 23 us -> none  [the longest x4 12.6 us: body(): keys += jnp.dot(token_blocks[j], rows, preferred_element_type=jnp.float32)]
    pallas_call x0 -> x3, Pallas kernels: none -> 22.1 us  [the longest x1 14.1 us: attention_packet(): pl.pallas_call(attention_kernel, out_shape=jax.ShapeDtypeStruct((32, 2 *...]
    concatenate x23 -> x22, local copies, waits for them, and re-layouts: 1.79 us -> 20.3 us  [body(): jnp.concatenate(picked + [jnp.max(scores, axis=1, keepdims=True)], axis=1)]
    ppermute x9 -> x13, starting transfers between devices: 24.1 us -> 39 us  [shift(): return lax.ppermute(x, axis, [((i + step) % size, i) for i in range(size)])]
    ppermute x9 -> x13, waiting for transfers between devices: 10.4 us -> 22.3 us  [shift(): return lax.ppermute(x, axis, [((i + step) % size, i) for i in range(size)])]
  transfers between devices with their start and end apart: 14 -> 23, of which waited for: 4 -> 12; matrix products, arithmetic and copies ran while one was open for 11% -> 21% of each run, Pallas kernels for 0% -> 0%
where the time goes in v1:
time: 314 us; the launch traced here: 311 us
  starting transfers between devices  98.2 us (31%)
  waiting for transfers between devices  92.3 us (29%)
  local copies, waits for them, and re-layouts  50.6 us (16%)
  Pallas kernels  22.1 us (7%)
  between operations  15.4 us (5%)
  other arithmetic  14.6 us (5%)
  blocking collectives  11 us (4%)
  matrix products  6.35 us (2%)
    ppermute x13, starting transfers between devices, shift(): return lax.ppermute(x, axis, [((i + step) % size, i) for i in range(size)])  39 us
    all_to_all x4, starting transfers between devices, send_all(): lax.all_to_all(jnp.broadcast_to(x[None], (size, *x.shape)), axis, 0, 0, t...  31.6 us
    all_to_all x4, waiting for transfers between devices, send_all(): lax.all_to_all(jnp.broadcast_to(x[None], (size, *x.shape)), axis, 0, 0, t...  27.3 us
    ppermute x13, waiting for transfers between devices, shift(): return lax.ppermute(x, axis, [((i + step) % size, i) for i in range(size)])  22.3 us
    concatenate x22, local copies, waits for them, and re-layouts, body(): jnp.concatenate(picked + [jnp.max(scores, axis=1, keepdims=True)], axis=1)  20.3 us
    pallas_call x1, Pallas kernels, attention_packet(): pl.pallas_call(attention_kernel, out_shape=jax.ShapeDtypeStruct((32, 2 *...  14.1 us
    all_to_all x1, waiting for transfers between devices, body(): term = jnp.sum(lax.all_to_all(term, Z, 0, 0, tiled=True), axis=0)  12.1 us
    all_to_all x1, waiting for transfers between devices, body(): coef = lax.all_to_all(coef, Z, 0, 0, tiled=True).reshape(n_index, LANES)  11.3 us
  transfers between devices with their start and end apart: 23, of which 12 were waited for; matrix products, arithmetic and copies ran while one was open for 21% of the time, Pallas kernels for 0%

profile of v1, /device:TPU:6, one launch (start us, length us, event | category | flops | bytes accessed | tf_op | source)
XLA Modules:
  0.0 310.7 jit_solution(3850026051882097026)
XLA Ops:
  11.4 15.2 %all-to-all-start.1 = ((bf16[16,2,448]{2,1,0:T(2,128)(2,1)}), bf16[16,2,448]{2,1,0:T(2,128)(2,1)}, u32[]{:S(2)}, u32[]{:S(2)}) async-start(bf16[16,2,448]{2,1,0:T(2,128)(2,1)} %reshape.381), calls=%async_computation.1 | async-start | bytes 65536 | tf_op jit(solution)/shard_map/gather_queries/all_to_all | solution.py:33
  27.7 11.6 %all-to-all-done.1 = bf16[16,2,448]{2,1,0:T(2,128)(2,1)} async-done(((bf16[16,2,448]{2,1,0:T(2,128)(2,1)}), bf16[16,2,448]{2,1,0:T(2,128)(2,1)}, u32[]{:S(2)}, u32[]{:S(2)}) %all-to-all-start.1) | async-done | bytes 28704 | tf_op jit(solution)/shard_map/gather_queries/all_to_all | solution.py:33
  39.3 1.6 broadcast_in_dim.37
  40.9 3.4 %all-to-all-start = ((bf16[4,32,1024]{2,1,0:T(8,128)(2,1)}), bf16[4,32,1024]{2,1,0:T(8,128)(2,1)S(1)}, u32[]{:S(2)}, u32[]{:S(2)}) async-start(bf16[4,32,1024]{2,1,0:T(8,128)(2,1)} %broadcast_in_dim.37), calls=%async_computation | async-start | bytes 524288 | tf_op jit(solution)/shard_map/gather_key_proj/all_to_all | solution.py:33
  49.1 12.0 %all-to-all-done = bf16[4,32,1024]{2,1,0:T(8,128)(2,1)S(1)} async-done(((bf16[4,32,1024]{2,1,0:T(8,128)(2,1)}), bf16[4,32,1024]{2,1,0:T(8,128)(2,1)S(1)}, u32[]{:S(2)}, u32[]{:S(2)}) %all-to-all-start) | async-done | bytes 262176 | tf_op jit(solution)/shard_map/gather_key_proj/all_to_all | solution.py:33
  62.1 7.7 %all-to-all-start.2 = ((bf16[32,16,896]{2,1,0:T(8,128)(2,1)}), bf16[32,16,896]{2,1,0:T(8,128)(2,1)}, u32[]{:S(2)}, u32[]{:S(2)}) async-start(bf16[32,16,896]{2,1,0:T(8,128)(2,1)} %broadcast_in_dim.40), calls=%async_computation.2 | async-start | bytes 1835008 | tf_op jit(solution)/shard_map/gather_queries/all_to_all | solution.py:33
  71.9 5.8 %collective-permute-start.1 = (bf16[2,32,1024]{2,1,0:T(8,128)(2,1)}, bf16[2,32,1024]{2,1,0:T(8,128)(2,1)S(1)}, u32[]{:S(2)}, u32[]{:S(2)}) collective-permute-start(bf16[2,32,1024]{2,1,0:T(8,128)(2,1)} %get-tuple-element.58), channel_id=1, source_target_pairs={{16,0},{24,8},{32,16},{40,24},{48,32},{56,40},{64,48},{72,56},{80,... | collective-permute-start | bytes 393224 | tf_op jit(solution)/shard_map/gather_key_proj/ppermute | solution.py:28
  77.7 2.9 collective-permute-start.2
  80.5 3.7 %collective-permute-start = (bf16[4,32,1024]{2,1,0:T(8,128)(2,1)S(1)}, bf16[4,32,1024]{2,1,0:T(8,128)(2,1)S(1)}, u32[]{:S(2)}, u32[]{:S(2)}) collective-permute-start(bf16[4,32,1024]{2,1,0:T(8,128)(2,1)S(1)} %all-to-all-done), channel_id=1, source_target_pairs={{8,0},{16,8},{24,16},{32,24},{40,32},{48,40},{56,48},{64,56},{72,6... | collective-permute-start | bytes 786440 | tf_op jit(solution)/shard_map/gather_key_proj/ppermute | solution.py:28
  84.3 2.2 collective-permute-start.3
  87.2 1.5 all-to-all-done.2
  90.0 1.9 multiply_reduce_fusion.1
  95.9 4.6 %collective-permute-start.5 = (bf16[16,32,1024]{2,1,0:T(8,128)(2,1)}, bf16[16,32,1024]{2,1,0:T(8,128)(2,1)S(1)}, u32[]{:S(2)}, u32[]{:S(2)}) collective-permute-start(bf16[16,32,1024]{2,1,0:T(8,128)(2,1)} %constant_dynamic-update-slice_fusion.refs_0_), channel_id=1, source_target_pairs={{128,0},{256,128},{384,256},{0,384},{129,1},{257,129},{385,257},{1... | collective-permute-start | bytes 3145736 | tf_op jit(solution)/shard_map/gather_key_proj/ppermute | solution.py:28
  100.6 1.9 collective-permute-start.8
  102.8 19.6 %collective-permute-done.5.refs_2_ = bf16[16,32,1024]{2,1,0:T(8,128)(2,1)S(1)} collective-permute-done((bf16[16,32,1024]{2,1,0:T(8,128)(2,1)}, bf16[16,32,1024]{2,1,0:T(8,128)(2,1)S(1)}, u32[]{:S(2)}, u32[]{:S(2)}) %collective-permute-start.5) | collective-permute-done | bytes 1048608 | tf_op jit(solution)/shard_map/gather_key_proj/ppermute | solution.py:28
  122.4 5.5 %collective-permute-start.7 = (bf16[8,32,1024]{2,1,0:T(8,128)(2,1)S(1)}, bf16[8,32,1024]{2,1,0:T(8,128)(2,1)S(1)}, u32[]{:S(2)}, u32[]{:S(2)}) collective-permute-start(bf16[8,32,1024]{2,1,0:T(8,128)(2,1)S(1)} %slice.159), channel_id=1, source_target_pairs={{128,0},{256,128},{384,256},{0,384},{129,1},{257,129},{385,257},{1... | collective-permute-start | bytes 1572872 | tf_op jit(solution)/shard_map/gather_key_proj/ppermute | solution.py:28
  127.9 2.5 select_reduce_fusion.17
  130.3 1.9 slice.160
  132.2 1.9 collective-permute-start.9
  150.7 1.5 concatenate.85
  152.2 1.5 concatenate.86
  153.7 1.7 concatenate.83
  156.2 9.8 %all-to-all-start.3 = ((f32[16,1,168]{2,1,0:T(1,128)}), f32[16,1,168]{2,1,0:T(1,128)S(1)}, u32[]{:S(2)}, u32[]{:S(2)}) async-start(f32[16,1,168]{2,1,0:T(1,128)} %reshape.383), calls=%async_computation.3 | async-start | bytes 32768 | tf_op jit(solution)/shard_map/reduce_scores/all_to_all | solution.py:283
  168.7 9.8 %all-to-all-done.3 = f32[16,1,168]{2,1,0:T(1,128)S(1)} async-done(((f32[16,1,168]{2,1,0:T(1,128)}), f32[16,1,168]{2,1,0:T(1,128)S(1)}, u32[]{:S(2)}, u32[]{:S(2)}) %all-to-all-start.3) | async-done | bytes 10784 | tf_op jit(solution)/shard_map/reduce_scores/all_to_all | solution.py:283
  180.0 1.9 collective-permute-start.4
  181.9 2.4 collective-permute-start.11
  184.3 1.9 collective-permute-start.6
  187.1 1.9 constant_dynamic-update-slice_fusion.5.refs_4_
  189.0 2.4 collective-permute-start.10
  192.1 4.5 %all-to-all-start.4 = ((f32[8,1,21]{2,1,0:T(1,128)}), f32[8,1,21]{2,1,0:T(1,128)S(1)}, u32[]{:S(2)}, u32[]{:S(2)}) async-start(f32[8,1,21]{2,1,0:T(1,128)} %copy.138), calls=%async_computation.4 | async-start | bytes 8192 | tf_op jit(solution)/shard_map/reduce_scores/all_to_all | solution.py:284
  196.6 1.5 constant_dynamic-slice_fusion
  198.2 3.7 %all-to-all-done.4 = f32[8,1,21]{2,1,0:T(1,128)S(1)} async-done(((f32[8,1,21]{2,1,0:T(1,128)}), f32[8,1,21]{2,1,0:T(1,128)S(1)}, u32[]{:S(2)}, u32[]{:S(2)}) %all-to-all-start.4) | async-done | bytes 704 | tf_op jit(solution)/shard_map/reduce_scores/all_to_all | solution.py:284
  206.2 2.5 copy-done.1
  208.7 14.1 %attention.1 = f32[32,256]{1,0:T(8,128)S(1)} custom-call(s32[3]{0:T(128)S(1)} %pad_add_fusion.place, bf16[4,640,1024]{2,1,0:T(8,128)(2,1)S(1)} %copy-done.1, bf16[16,32,1024]{2,1,0:T(8,128)(2,1)} %constant_dynamic-update-slice_fusion.refs_0_, bf16[16,32,1024]{2,1,0:T(8,128)(2,1)} %collective-permute-done.4.refs_1_, ...), custom_call_target="tpu_custom_call" | custom-call | flops 5368709120 | bytes 14680064 | tf_op jit(solution)/shard_map/attention/attention/pallas_call | solution.py:132
  223.4 6.3 %all-to-all-start.5 = ((f32[32,1,256]{2,1,0:T(1,128)}), f32[32,1,256]{2,1,0:T(1,128)S(1)}, u32[]{:S(2)}, u32[]{:S(2)}) async-start(f32[32,1,256]{2,1,0:T(1,128)} %copy.139), calls=%async_computation.5 | async-start | bytes 65536 | tf_op jit(solution)/shard_map/targets/all_to_all | solution.py:330
  230.0 5.2 %all-to-all-done.5 = f32[32,1,256]{2,1,0:T(1,128)S(1)} async-done(((f32[32,1,256]{2,1,0:T(1,128)}), f32[32,1,256]{2,1,0:T(1,128)S(1)}, u32[]{:S(2)}, u32[]{:S(2)}) %all-to-all-start.5) | async-done | bytes 32800 | tf_op jit(solution)/shard_map/targets/all_to_all | solution.py:330
  235.9 1.6 coef.1
  237.5 3.5 %all-to-all-start.6 = ((f32[16,8,128]{2,1,0:T(8,128)}), f32[16,8,128]{2,1,0:T(8,128)S(1)}, u32[]{:S(2)}, u32[]{:S(2)}) async-start(f32[16,8,128]{2,1,0:T(8,128)} %coef.1), calls=%async_computation.6 | async-start | bytes 131072 | tf_op jit(solution)/shard_map/targets/all_to_all | solution.py:339
  241.0 2.0 convolution_convert_fusion.ordered
  243.0 11.3 %all-to-all-done.6 = f32[16,8,128]{2,1,0:T(8,128)S(1)} async-done(((f32[16,8,128]{2,1,0:T(8,128)}), f32[16,8,128]{2,1,0:T(8,128)S(1)}, u32[]{:S(2)}, u32[]{:S(2)}) %all-to-all-start.6) | async-done | bytes 65568 | tf_op jit(solution)/shard_map/targets/all_to_all | solution.py:339
  254.3 6.4 %gradient.1 = (f32[384,192]{1,0:T(8,128)S(1)}, f32[384,192]{1,0:T(8,128)S(1)}) custom-call(f32[128,128]{1,0:T(8,128)S(1)} %bitcast.90, s32[128,128]{1,0:T(8,128)S(1)} %copy.141.slot, f32[512,192]{1,0:T(8,128)S(1)} %get-tuple-element.88.rows, f32[512,192]{1,0:T(8,128)S(1)} %get-tuple-element.87.unit, f32[512,1]{1,0:T(8,128)S(1)} %copy.142.scale, ...), custom_call_target="tpu_custom_call" | custom-call | tf_op jit(solution)/shard_map/gradient/gradient/pallas_call | solution.py:343
  260.7 1.9 collective-permute-start.12
  262.6 1.7 collective-permute-done.12
  264.3 11.0 %all_to_all.56 = f32[4,96,192]{2,1,0:T(8,128)S(1)} all-to-all(f32[4,96,192]{2,1,0:T(8,128)S(1)} %bitcast.94), channel_id=1, replica_groups=mesh['y'=4,'zq'=4,'zr'=4,'core'=2,'reader'=4] {'y'}, dimensions={0} | all-to-all | bytes 589824 | tf_op jit(solution)/shard_map/reduce_gradient/all_to_all | solution.py:355
  276.1 3.5 %all-to-all-start.8 = ((f32[16,6,192]{2,1,0:T(8,128)}), f32[16,6,192]{2,1,0:T(8,128)S(1)}, u32[]{:S(2)}, u32[]{:S(2)}) async-start(f32[16,6,192]{2,1,0:T(8,128)} %reshape.376), calls=%async_computation.8 | async-start | bytes 262144 | tf_op jit(solution)/shard_map/reduce_gradient/all_to_all | solution.py:357
  281.7 12.1 %all-to-all-done.8 = f32[16,6,192]{2,1,0:T(8,128)S(1)} async-done(((f32[16,6,192]{2,1,0:T(8,128)}), f32[16,6,192]{2,1,0:T(8,128)S(1)}, u32[]{:S(2)}, u32[]{:S(2)}) %all-to-all-start.8) | async-done | bytes 73760 | tf_op jit(solution)/shard_map/reduce_gradient/all_to_all | solution.py:357
  294.4 5.3 %all-to-all-start.9 = ((f32[4,6,192]{2,1,0:T(8,128)}), f32[4,6,192]{2,1,0:T(8,128)S(1)}, u32[]{:S(2)}, u32[]{:S(2)}) async-start(f32[4,6,192]{2,1,0:T(8,128)} %broadcast_in_dim.42), calls=%async_computation.9 | async-start | bytes 65536 | tf_op jit(solution)/shard_map/reduce_gradient/all_to_all | solution.py:33
  300.9 2.2 all-to-all-done.9
  (142 shorter events, 52.8 us)
Async XLA Ops:
  7.2 82.8 %copy-start = (bf16[768,768]{1,0:T(8,128)(2,1)S(1)}, bf16[768,768]{1,0:T(8,128)(2,1)}, u32[]{:S(2)}) copy-start(bf16[768,768]{1,0:T(8,128)(2,1)} %param.15) | copy-start | bytes 3538948
  7.2 19.5 %copy-start.7 = (bf16[4,16,1024]{2,1,0:T(8,128)(2,1)S(1)}, bf16[4,16,1024]{2,1,0:T(8,128)(2,1)}, u32[]{:S(2)}) copy-start(bf16[4,16,1024]{2,1,0:T(8,128)(2,1)} %param.21) | copy-start | bytes 393220
  7.2 199.0 %all-gather.2.cloned.1.call-start = ((), (), s32[]{:S(2)}) async-start(), calls=%async_computation.10 | async-start | bytes 6553600 | tf_op jit(solution)/shard_map/gather_enc_out/all_gather | solution.py:229
  11.4 27.9 %all-to-all-start.1 = ((bf16[16,2,448]{2,1,0:T(2,128)(2,1)}), bf16[16,2,448]{2,1,0:T(2,128)(2,1)}, u32[]{:S(2)}, u32[]{:S(2)}) async-start(bf16[16,2,448]{2,1,0:T(2,128)(2,1)} %reshape.381), calls=%async_computation.1 | async-start | bytes 65536 | tf_op jit(solution)/shard_map/gather_queries/all_to_all | solution.py:33
  26.9 20.2 %copy-start.11 = (s32[4,20]{1,0:T(4,128)S(1)}, s32[4,20]{1,0:T(4,128)}, u32[]{:S(2)}) copy-start(s32[4,20]{1,0:T(4,128)} %param.17) | copy-start | bytes 964
  26.9 21.1 %copy-start.3 = (f32[512,768]{1,0:T(8,128)S(1)}, f32[512,768]{1,0:T(8,128)}, u32[]{:S(2)}) copy-start(f32[512,768]{1,0:T(8,128)} %param.13) | copy-start | bytes 4718596
  40.9 20.2 %all-to-all-start = ((bf16[4,32,1024]{2,1,0:T(8,128)(2,1)}), bf16[4,32,1024]{2,1,0:T(8,128)(2,1)S(1)}, u32[]{:S(2)}, u32[]{:S(2)}) async-start(bf16[4,32,1024]{2,1,0:T(8,128)(2,1)} %broadcast_in_dim.37), calls=%async_computation | async-start | bytes 524288 | tf_op jit(solution)/shard_map/gather_key_proj/all_to_all | solution.py:33
  62.1 26.5 %all-to-all-start.2 = ((bf16[32,16,896]{2,1,0:T(8,128)(2,1)}), bf16[32,16,896]{2,1,0:T(8,128)(2,1)}, u32[]{:S(2)}, u32[]{:S(2)}) async-start(bf16[32,16,896]{2,1,0:T(8,128)(2,1)} %broadcast_in_dim.40), calls=%async_computation.2 | async-start | bytes 1835008 | tf_op jit(solution)/shard_map/gather_queries/all_to_all | solution.py:33
  71.9 21.0 %collective-permute-start.1 = (bf16[2,32,1024]{2,1,0:T(8,128)(2,1)}, bf16[2,32,1024]{2,1,0:T(8,128)(2,1)S(1)}, u32[]{:S(2)}, u32[]{:S(2)}) collective-permute-start(bf16[2,32,1024]{2,1,0:T(8,128)(2,1)} %get-tuple-element.58), channel_id=1, source_target_pairs={{16,0},{24,8},{32,16},{40,24},{48,32},{56,40},{64,48},{72,56},{80,... | collective-permute-start | bytes 393224 | tf_op jit(solution)/shard_map/gather_key_proj/ppermute | solution.py:28
  77.7 15.9 %collective-permute-start.2 = (bf16[2,32,1024]{2,1,0:T(8,128)(2,1)}, bf16[2,32,1024]{2,1,0:T(8,128)(2,1)S(1)}, u32[]{:S(2)}, u32[]{:S(2)}) collective-permute-start(bf16[2,32,1024]{2,1,0:T(8,128)(2,1)} %get-tuple-element.57), channel_id=1, source_target_pairs={{112,0},{120,8},{0,16},{8,24},{16,32},{24,40},{32,48},{40,56},{48,... | collective-permute-start | bytes 393224 | tf_op jit(solution)/shard_map/gather_key_proj/ppermute | solution.py:28
  80.5 11.6 %collective-permute-start = (bf16[4,32,1024]{2,1,0:T(8,128)(2,1)S(1)}, bf16[4,32,1024]{2,1,0:T(8,128)(2,1)S(1)}, u32[]{:S(2)}, u32[]{:S(2)}) collective-permute-start(bf16[4,32,1024]{2,1,0:T(8,128)(2,1)S(1)} %all-to-all-done), channel_id=1, source_target_pairs={{8,0},{16,8},{24,16},{32,24},{40,32},{48,40},{56,48},{64,56},{72,6... | collective-permute-start | bytes 786440 | tf_op jit(solution)/shard_map/gather_key_proj/ppermute | solution.py:28
  84.3 10.9 %collective-permute-start.3 = (bf16[4,32,1024]{2,1,0:T(8,128)(2,1)S(1)}, bf16[4,32,1024]{2,1,0:T(8,128)(2,1)S(1)}, u32[]{:S(2)}, u32[]{:S(2)}) collective-permute-start(bf16[4,32,1024]{2,1,0:T(8,128)(2,1)S(1)} %all-to-all-done), channel_id=1, source_target_pairs={{120,0},{0,8},{8,16},{16,24},{24,32},{32,40},{40,48},{48,56},{56,6... | collective-permute-start | bytes 786440 | tf_op jit(solution)/shard_map/gather_key_proj/ppermute | solution.py:28
  90.0 2.0 copy-start.6
  92.1 10.6 %copy-start.8 = (s32[4,128,20]{1,0,2:T(4,128)}, s32[4,128,20]{1,0,2:T(4,128)S(1)}, u32[]{:S(2)}) copy-start(s32[4,128,20]{1,0,2:T(4,128)S(1)} %reshape.367) | copy-start | bytes 122884
  92.1 10.4 %copy-start.5 = (f32[512,768]{1,0:T(8,128)S(1)}, f32[512,768]{1,0:T(8,128)}, u32[]{:S(2)}) copy-start(f32[512,768]{1,0:T(8,128)} %get-tuple-element.83) | copy-start | bytes 4718596
  95.9 26.4 %collective-permute-start.5 = (bf16[16,32,1024]{2,1,0:T(8,128)(2,1)}, bf16[16,32,1024]{2,1,0:T(8,128)(2,1)S(1)}, u32[]{:S(2)}, u32[]{:S(2)}) collective-permute-start(bf16[16,32,1024]{2,1,0:T(8,128)(2,1)} %constant_dynamic-update-slice_fusion.refs_0_), channel_id=1, source_target_pairs={{128,0},{256,128},{384,256},{0,384},{129,1},{257,129},{385,257},{1... | collective-permute-start | bytes 3145736 | tf_op jit(solution)/shard_map/gather_key_proj/ppermute | solution.py:28
  100.6 29.8 %collective-permute-start.8 = (bf16[16,32,1024]{2,1,0:T(8,128)(2,1)}, bf16[16,32,1024]{2,1,0:T(8,128)(2,1)}, u32[]{:S(2)}, u32[]{:S(2)}) collective-permute-start(bf16[16,32,1024]{2,1,0:T(8,128)(2,1)} %constant_dynamic-update-slice_fusion.refs_0_), channel_id=1, source_target_pairs={{384,0},{0,128},{128,256},{256,384},{385,1},{1,129},{129,257},{257... | collective-permute-start | bytes 3145736 | tf_op jit(solution)/shard_map/gather_key_proj/ppermute | solution.py:28
  102.6 25.3 %copy-start.2 = (f32[512,768]{1,0:T(8,128)S(1)}, f32[512,768]{1,0:T(8,128)}, u32[]{:S(2)}) copy-start(f32[512,768]{1,0:T(8,128)} %broadcast_multiply_fusion) | copy-start | bytes 4718596
  102.8 27.6 %copy-start.4 = (f32[512,768]{1,0:T(8,128)}, f32[512,768]{1,0:T(8,128)S(1)}, u32[]{:S(2)}) copy-start(f32[512,768]{1,0:T(8,128)S(1)} %broadcast_multiply_fusion.1) | copy-start | bytes 4718596
  122.4 63.9 %collective-permute-start.7 = (bf16[8,32,1024]{2,1,0:T(8,128)(2,1)S(1)}, bf16[8,32,1024]{2,1,0:T(8,128)(2,1)S(1)}, u32[]{:S(2)}, u32[]{:S(2)}) collective-permute-start(bf16[8,32,1024]{2,1,0:T(8,128)(2,1)S(1)} %slice.159), channel_id=1, source_target_pairs={{128,0},{256,128},{384,256},{0,384},{129,1},{257,129},{385,257},{1... | collective-permute-start | bytes 1572872 | tf_op jit(solution)/shard_map/gather_key_proj/ppermute | solution.py:28
  132.2 54.8 %collective-permute-start.9 = (bf16[8,32,1024]{2,1,0:T(8,128)(2,1)}, bf16[8,32,1024]{2,1,0:T(8,128)(2,1)}, u32[]{:S(2)}, u32[]{:S(2)}) collective-permute-start(bf16[8,32,1024]{2,1,0:T(8,128)(2,1)} %slice.160), channel_id=1, source_target_pairs={{384,0},{0,128},{128,256},{256,384},{385,1},{1,129},{129,257},{257... | collective-permute-start | bytes 1572872 | tf_op jit(solution)/shard_map/gather_key_proj/ppermute | solution.py:28
  155.4 35.9 %copy-start.12 = (pred[21]{0:T(512)(128)(4,1)S(1)}, pred[21]{0:T(512)(128)(4,1)}, u32[]{:S(2)}) copy-start(pred[21]{0:T(512)(128)(4,1)} %iota_compare_fusion.21) | copy-start | bytes 67
  156.2 22.3 %all-to-all-start.3 = ((f32[16,1,168]{2,1,0:T(1,128)}), f32[16,1,168]{2,1,0:T(1,128)S(1)}, u32[]{:S(2)}, u32[]{:S(2)}) async-start(f32[16,1,168]{2,1,0:T(1,128)} %reshape.383), calls=%async_computation.3 | async-start | bytes 32768 | tf_op jit(solution)/shard_map/reduce_scores/all_to_all | solution.py:283
  180.0 26.2 %collective-permute-start.4 = (bf16[16,32,1024]{2,1,0:T(8,128)(2,1)}, bf16[16,32,1024]{2,1,0:T(8,128)(2,1)}, u32[]{:S(2)}, u32[]{:S(2)}) collective-permute-start(bf16[16,32,1024]{2,1,0:T(8,128)(2,1)} %constant_dynamic-update-slice_fusion.refs_0_), channel_id=1, source_target_pairs={{4,0},{0,4},{5,1},{1,5},{6,2},{2,6},{7,3},{3,7},{12,8},{8,12},{13,... | collective-permute-start | bytes 3145736 | tf_op jit(solution)/shard_map/gather_key_proj/ppermute | solution.py:28
  181.9 24.3 %collective-permute-start.11 = (bf16[16,32,1024]{2,1,0:T(8,128)(2,1)}, bf16[16,32,1024]{2,1,0:T(8,128)(2,1)}, u32[]{:S(2)}, u32[]{:S(2)}) collective-permute-start(bf16[16,32,1024]{2,1,0:T(8,128)(2,1)} %collective-permute-done.8.refs_6_), channel_id=1, source_target_pairs={{4,0},{0,4},{5,1},{1,5},{6,2},{2,6},{7,3},{3,7},{12,8},{8,12},{13,... | collective-permute-start | bytes 3145736 | tf_op jit(solution)/shard_map/gather_key_proj/ppermute | solution.py:28
  184.3 21.9 %collective-permute-start.6 = (bf16[16,32,1024]{2,1,0:T(8,128)(2,1)S(1)}, bf16[16,32,1024]{2,1,0:T(8,128)(2,1)}, u32[]{:S(2)}, u32[]{:S(2)}) collective-permute-start(bf16[16,32,1024]{2,1,0:T(8,128)(2,1)S(1)} %collective-permute-done.5.refs_2_), channel_id=1, source_target_pairs={{4,0},{0,4},{5,1},{1,5},{6,2},{2,6},{7,3},{3,7},{12,8},{8,12},{13,... | collective-permute-start | bytes 3145736 | tf_op jit(solution)/shard_map/gather_key_proj/ppermute | solution.py:28
  189.0 17.2 %collective-permute-start.10 = (bf16[16,32,1024]{2,1,0:T(8,128)(2,1)}, bf16[16,32,1024]{2,1,0:T(8,128)(2,1)}, u32[]{:S(2)}, u32[]{:S(2)}) collective-permute-start(bf16[16,32,1024]{2,1,0:T(8,128)(2,1)} %constant_dynamic-update-slice_fusion.5.refs_4_), channel_id=1, source_target_pairs={{4,0},{0,4},{5,1},{1,5},{6,2},{2,6},{7,3},{3,7},{12,8},{8,12},{13,... | collective-permute-start | bytes 3145736 | tf_op jit(solution)/shard_map/gather_key_proj/ppermute | solution.py:28
  192.1 9.7 %all-to-all-start.4 = ((f32[8,1,21]{2,1,0:T(1,128)}), f32[8,1,21]{2,1,0:T(1,128)S(1)}, u32[]{:S(2)}, u32[]{:S(2)}) async-start(f32[8,1,21]{2,1,0:T(1,128)} %copy.138), calls=%async_computation.4 | async-start | bytes 8192 | tf_op jit(solution)/shard_map/reduce_scores/all_to_all | solution.py:284
  206.2 2.5 copy-start.1
  208.7 21.1 %copy-start.9 = (s32[4,128,20]{1,0,2:T(4,128)S(1)}, s32[4,128,20]{1,0,2:T(4,128)}, u32[]{:S(2)}) copy-start(s32[4,128,20]{1,0,2:T(4,128)} %copy-done.8) | copy-start | bytes 122884
  208.7 32.3 %copy-start.10 = (s32[768]{0:T(1024)S(1)}, s32[768]{0:T(1024)}, u32[]{:S(2)}) copy-start(s32[768]{0:T(1024)} %fusion.23) | copy-start | bytes 9220
  223.4 11.8 %all-to-all-start.5 = ((f32[32,1,256]{2,1,0:T(1,128)}), f32[32,1,256]{2,1,0:T(1,128)S(1)}, u32[]{:S(2)}, u32[]{:S(2)}) async-start(f32[32,1,256]{2,1,0:T(1,128)} %copy.139), calls=%async_computation.5 | async-start | bytes 65536 | tf_op jit(solution)/shard_map/targets/all_to_all | solution.py:330
  237.5 16.8 %all-to-all-start.6 = ((f32[16,8,128]{2,1,0:T(8,128)}), f32[16,8,128]{2,1,0:T(8,128)S(1)}, u32[]{:S(2)}, u32[]{:S(2)}) async-start(f32[16,8,128]{2,1,0:T(8,128)} %coef.1), calls=%async_computation.6 | async-start | bytes 131072 | tf_op jit(solution)/shard_map/targets/all_to_all | solution.py:339
  260.7 3.6 %collective-permute-start.12 = (f32[384,192]{1,0:T(8,128)S(1)}, f32[384,192]{1,0:T(8,128)S(1)}, u32[]{:S(2)}, u32[]{:S(2)}) collective-permute-start(f32[384,192]{1,0:T(8,128)S(1)} %get-tuple-element.31), channel_id=1, source_target_pairs={{4,0},{0,4},{5,1},{1,5},{6,2},{2,6},{7,3},{3,7},{12,8},{8,12},{13,... | collective-permute-start | bytes 884744 | tf_op jit(solution)/shard_map/reduce_gradient/ppermute | solution.py:28
  276.1 17.7 %all-to-all-start.8 = ((f32[16,6,192]{2,1,0:T(8,128)}), f32[16,6,192]{2,1,0:T(8,128)S(1)}, u32[]{:S(2)}, u32[]{:S(2)}) async-start(f32[16,6,192]{2,1,0:T(8,128)} %reshape.376), calls=%async_computation.8 | async-start | bytes 262144 | tf_op jit(solution)/shard_map/reduce_gradient/all_to_all | solution.py:357
  294.4 8.7 %all-to-all-start.9 = ((f32[4,6,192]{2,1,0:T(8,128)}), f32[4,6,192]{2,1,0:T(8,128)S(1)}, u32[]{:S(2)}, u32[]{:S(2)}) async-start(f32[4,6,192]{2,1,0:T(8,128)} %broadcast_in_dim.42), calls=%async_computation.9 | async-start | bytes 65536 | tf_op jit(solution)/shard_map/reduce_gradient/all_to_all | solution.py:33
Sparse Core Ops, SparseCore 0:
  10.1 75.2 all-gather.1

commit v2 on v1

v2 whole, which is shorter than its diff:
```python
import functools
import math

import jax
import jax.numpy as jnp
from jax import lax
from jax.experimental import pallas as pl
from jax.experimental.pallas import tpu as pltpu
from jax.sharding import Mesh, PartitionSpec as P

HEADS = 64
DH = 64
ANS = 16
EPSILON = 1e-06
SOFTMAX_TEMPER = 0.05
EXACT = lax.Precision.HIGHEST
INDEX = ("y", "zq", "zr", "core")
Z = ("zq", "zr")
Z_BY_CLASS = ("zr", "zq")
NEAR = ("reader", "y", "core")
LANES = 128
SLOT = 32
TILE = 256
N_OWNERS = 128
EARLY = (0, 1, 3)
LATE = 2


def shift(x, axis, step):
    size = lax.axis_size(axis)
    return lax.ppermute(x, axis, [((i + step) % size, i) for i in range(size)])


def send_all(x, axis):
    size = lax.axis_size(axis)
    return lax.all_to_all(jnp.broadcast_to(x[None], (size, *x.shape)), axis, 0, 0, tiled=True)


def halves(x):
    high = x.astype(jnp.bfloat16)
    return high, (x - high.astype(jnp.float32)).astype(jnp.bfloat16)


def dot32(a, b):
    return jnp.dot(a, b, preferred_element_type=jnp.float32)


def start_blocks(place, ahead, slot, tokens, weights, token_v, weight_v, sems):
    y, zr, core = place[0], place[1], place[2]
    copies = [pltpu.make_async_copy(tokens.at[(y + ahead) % 4], token_v.at[slot], sems.at[slot, 8])]
    for which in range(2):
        for residue in range(4):
            copies.append(
                pltpu.make_async_copy(
                    weights[which].at[pl.ds(4 * residue, 4)],
                    weight_v.at[slot, :, (zr + residue) % 4, (core + which) % 2],
                    sems.at[slot, 4 * which + residue],
                )
            )
    for copy in copies:
        copy.start()
    return copies


def early_keys_kernel(place, tokens, *refs):
    weights, (keys, token_v, weight_v, sems) = refs[:6], refs[6:]
    copies = [
        start_blocks(
            place, ahead, slot, tokens, weights[2 * slot : 2 * slot + 2], token_v, weight_v, sems
        )
        for slot, ahead in enumerate(EARLY)
    ]
    for slot in range(len(EARLY)):
        for copy in copies[slot]:
            copy.wait()

        @pl.loop(0, keys.shape[1] // TILE)
        def _(t):
            cols = pl.ds(pl.multiple_of(t * TILE, TILE), TILE)
            term = dot32(token_v[slot], weight_v[slot, :, :, :, :, cols].reshape(-1, TILE))
            if slot == 0:
                keys[:, cols] = term
            else:
                keys[:, cols] += term


def attention_kernel(place, tokens, *refs):
    weights, refs = refs[:2], refs[2:]
    early, dec, gain, live, scores, out, token_v, weight_v, column_v, sems = refs
    copies = start_blocks(place, LATE, 0, tokens, weights, token_v, weight_v, sems)
    group = dec.shape[0]
    n = live.shape[1]
    column_v[...] = jnp.zeros_like(column_v)
    for copy in copies:
        copy.wait()

    @pl.loop(0, early.shape[1] // TILE)
    def _(t):
        cols = pl.ds(pl.multiple_of(t * TILE, TILE), TILE)
        same = (
            lax.broadcasted_iota(jnp.int32, (TILE, TILE), 0) // DH
            == lax.broadcasted_iota(jnp.int32, (TILE, TILE), 1) // DH
        ).astype(jnp.bfloat16)
        mine = (
            lax.broadcasted_iota(jnp.int32, (TILE // DH * ANS, TILE), 0) // ANS
            == lax.broadcasted_iota(jnp.int32, (TILE // DH * ANS, TILE), 1) // DH
        )
        keys = early[:, cols] + dot32(
            token_v[0], weight_v[0, :, :, :, :, cols].reshape(-1, TILE)
        )
        high, low = halves(keys * keys)
        square = (dot32(high, same) + dot32(low, same)) / DH
        unit = (keys * lax.rsqrt(square + EPSILON) * gain[:, cols]).astype(jnp.bfloat16)
        for g in range(group):
            answer = dec[g, :, cols].astype(jnp.float32)
            answer = jnp.concatenate([answer] * (TILE // DH), axis=0)
            answer = jnp.where(mine, answer, 0.0).astype(jnp.bfloat16)
            similarity = lax.dot_general(
                answer,
                unit[g * n : (g + 1) * n],
                (((1,), (1,)), ((), ())),
                preferred_element_type=jnp.float32,
            ) / math.sqrt(DH)
            weight = jnp.where(live[g : g + 1, :] > 0, jnp.exp(similarity), 0.0)
            weight = weight / jnp.sum(weight, axis=1, keepdims=True)
            column_v[g : g + 1, :] += jnp.sum(weight, axis=0, keepdims=True)

    mass = jnp.zeros((8, LANES), jnp.float32)
    for g in range(group):
        column = jnp.broadcast_to(column_v[g : g + 1, :], (8, n))
        to = (
            lax.broadcasted_iota(jnp.int32, (n, LANES), 0) // 8 + g * SLOT
            == lax.broadcasted_iota(jnp.int32, (n, LANES), 1)
        ).astype(jnp.float32)
        mass += jnp.dot(column, to, precision=EXACT, preferred_element_type=jnp.float32)
    out[:, :LANES] = jnp.broadcast_to(mass[:1] / (HEADS * ANS), (out.shape[0], LANES))
    out[:, LANES:] = jnp.broadcast_to(scores[...], (out.shape[0], LANES))


def attention_packet(place, tokens, weights, dec, gain, live, scores):
    vmem = pl.BlockSpec(memory_space=pltpu.VMEM)
    anywhere = pl.BlockSpec(memory_space=pl.ANY)
    smem = pl.BlockSpec(memory_space=pltpu.SMEM)
    _, rows, width = tokens.shape

    def blocks(count):
        return [
            pltpu.VMEM((count, rows, width), jnp.bfloat16),
            pltpu.VMEM((count, 4, 4, 2, *weights[0][0].shape[1:]), jnp.bfloat16),
        ]

    def cost(count, size):
        return pl.CostEstimate(
            flops=2 * rows * count * width * width, bytes_accessed=size << 20, transcendentals=0
        )

    early = pl.pallas_call(
        early_keys_kernel,
        out_shape=jax.ShapeDtypeStruct((rows, width), jnp.float32),
        in_specs=[smem] + [anywhere] * 7,
        out_specs=vmem,
        scratch_shapes=blocks(3) + [pltpu.SemaphoreType.DMA((3, 9))],
        compiler_params=pltpu.CompilerParams(vmem_limit_bytes=48 << 20),
        cost_estimate=cost(3, 13),
        name="early_keys",
    )(place, tokens, *[block for ahead in EARLY for block in weights[ahead]])
    return pl.pallas_call(
        attention_kernel,
        out_shape=jax.ShapeDtypeStruct((32, 2 * LANES), jnp.float32),
        in_specs=[smem] + [anywhere] * 3 + [vmem] * 5,
        out_specs=vmem,
        scratch_shapes=blocks(1)
        + [pltpu.VMEM((8, live.shape[1]), jnp.float32), pltpu.SemaphoreType.DMA((1, 9))],
        compiler_params=pltpu.CompilerParams(vmem_limit_bytes=48 << 20),
        cost_estimate=cost(1, 6),
        name="attention",
    )(place, tokens, *weights[LATE], early, dec, gain, live, scores)


def scores_kernel(place, packed, proj, emb, chosen, state, slots, rows, unit, scale, ordered, unit_v, ids_v):
    shard, r = place[0], place[1]
    n_rows, width = emb.shape
    per_x = state.shape[0]
    cols = rows.shape[1]
    feats = packed[:, :, :width].reshape(4 * per_x, width)
    ordered[...] = lax.dot_general(
        chosen[...], feats, (((1,), (1,)), ((), ())), preferred_element_type=jnp.float32
    ).astype(jnp.bfloat16)

    lane = lax.broadcasted_iota(jnp.int32, (per_x, LANES), 1)
    spread = jnp.full((per_x, LANES), -1, jnp.int32)
    for x in range(4):
        coded = packed[8 * x : 8 * x + 8, :, width : width + LANES].reshape(per_x, LANES)
        coded = coded.astype(jnp.float32)
        ids = coded * 256 + pltpu.roll(coded, LANES // 2, 1)
        ids = ids.astype(jnp.int32) - shard * n_rows
        ids_v[x] = ids
        moved = ids if x == 0 else pltpu.roll(ids, SLOT * x, 1)
        spread = jnp.where((lane // SLOT == x) & (lane % SLOT < 20), moved, spread)
    slots[...] = spread

    vec = dot32(feats, proj[...])
    scale_all = lax.rsqrt(jnp.sum(vec * vec, axis=1, keepdims=True) + EPSILON)
    scale[...] = scale_all
    unit_all = vec * scale_all
    unit_v[...] = unit_all
    emb_all = emb[...]
    row_unit = emb_all * lax.rsqrt(jnp.sum(emb_all * emb_all, axis=1, keepdims=True) + EPSILON)
    for x in range(4):

        @pl.when(r == x)
        def _():
            rows[...] = row_unit[:, x * cols : (x + 1) * cols]
            unit[...] = unit_all[:, x * cols : (x + 1) * cols]

    share = unit_v[pl.ds(pl.multiple_of(r * per_x, per_x), per_x), :]
    found = (
        lax.dot_general(
            share,
            row_unit,
            (((1,), (1,)), ((), ())),
            precision=EXACT,
            preferred_element_type=jnp.float32,
        )
        / SOFTMAX_TEMPER
    )
    places = ids_v[r]
    row = lax.broadcasted_iota(jnp.int32, (per_x, n_rows), 1)
    total = jnp.where(lane == 20, jnp.max(found, axis=1, keepdims=True), 0.0)
    for k in range(20):
        picked = jnp.where(places[:, k : k + 1] == row, found, 0.0)
        total = jnp.where(lane == k, jnp.sum(picked, axis=1, keepdims=True), total)
    state[...] = total


def coef_kernel(packets, out):
    lane = lax.broadcasted_iota(jnp.int32, (8, LANES), 1)
    target = prob = fetched = jnp.zeros((8, LANES), jnp.float32)
    for x in range(4):
        target += packets[x, :, :LANES]
        scores = packets[x, :, LANES:]
        own = (lane // SLOT == x) & (lane % SLOT < 20)
        moved = scores if x == 0 else pltpu.roll(scores, SLOT * x, 1)
        prob += jnp.where(own, moved, 0.0)
        moved = pltpu.roll(scores, (SLOT * x + LANES // 2) % LANES, 1)
        fetched += jnp.where(own, moved, 0.0)
    gap = prob - target
    to = (
        lax.broadcasted_iota(jnp.int32, (LANES, LANES), 0) // SLOT * SLOT + 20
        == lax.broadcasted_iota(jnp.int32, (LANES, LANES), 1)
    ).astype(jnp.float32)
    along = jnp.dot(gap * fetched, to, precision=EXACT, preferred_element_type=jnp.float32)
    packed = gap / SOFTMAX_TEMPER + along / N_OWNERS
    out[...] = jnp.broadcast_to(packed[None], out.shape)


def gradient_kernel(coef, slot, rows, unit, scale, ordered, keep, send, matrix_v):
    n_rows = matrix_v.shape[1]
    blocks = coef.shape[0]

    @pl.loop(0, blocks // 8)
    def _(b):
        eight = pl.ds(pl.multiple_of(b * 8, 8), 8)
        row = lax.broadcasted_iota(jnp.int32, (8, n_rows), 1)
        values = coef[pl.ds(b // 2 + b % 2 * 64, 8, stride=8), :]
        places = slot[eight, :]
        for x in range(4):
            total = jnp.zeros((8, n_rows), jnp.float32)
            for k in range(SLOT * x, SLOT * x + 20):
                total += jnp.where(places[:, k : k + 1] == row, values[:, k : k + 1], 0.0)
            matrix_v[pl.ds(pl.multiple_of(x * blocks + b * 8, 8), 8), :] = total

    along_all = jnp.concatenate([coef[pl.ds(p, 16, stride=8), :] for p in range(8)], axis=0)
    row_high, row_low = halves(rows[...])
    parts_high, parts_low = [], []
    for x in range(4):
        mine = slice(x * blocks, (x + 1) * blocks)
        high, low = halves(matrix_v[mine, :])
        part = dot32(high, row_high) + (dot32(high, row_low) + dot32(low, row_high))
        along = along_all[:, SLOT * x + 20 : SLOT * x + 21]
        part = (part - unit[mine, :] * along) * scale[mine, :]
        high, low = halves(part)
        parts_high.append(high)
        parts_low.append(low)
    high, low = jnp.concatenate(parts_high, axis=0), jnp.concatenate(parts_low, axis=0)
    half = keep.shape[0]
    keep[...] = dot32(ordered[:half, :], high) + dot32(ordered[:half, :], low)
    send[...] = dot32(ordered[half:, :], high) + dot32(ordered[half:, :], low)


def body(
    index_emb,
    query_feat,
    query_proj,
    passage_id,
    passage_len,
    enc_out,
    key_proj,
    key_gain,
    dec_query,
):
    y, zq, zr, core, r = (lax.axis_index(a) for a in (*INDEX, "reader"))
    ny, nz, ncore, nx = 4, 16, 2, 4
    z = zq * 4 + zr
    n_index = ny * nz * ncore
    n_pair = ny * ncore
    my_shard = (y * nz + z) * ncore + core
    shard_rows, width = index_emb.shape
    topk = passage_id.shape[1]

    group, _, plen, feats_here = enc_out.shape
    token_rows = group * topk * plen
    with jax.named_scope("gather_enc_out"):
        token_blocks = lax.all_gather(enc_out.reshape(token_rows, feats_here), "reader")

    width_here = key_proj.shape[1]
    ids_high = (passage_id // 256).astype(jnp.bfloat16)
    ids_low = (passage_id % 256).astype(jnp.bfloat16)
    gap = ((0, 0), (0, LANES // 2 - topk))
    coded = jnp.concatenate([query_feat, jnp.pad(ids_high, gap), jnp.pad(ids_low, gap)], axis=1)
    coded = jnp.pad(coded, ((0, 0), (0, width_here - coded.shape[1])))
    with jax.named_scope("gather_key_proj"):
        own = send_all(jnp.concatenate([key_proj, coded]), "zq")
        after, before = shift(own, Z, 1), shift(own, Z, -1)
        far = [shift(own[:2], Z, 2), shift(own[2:], Z, -2)]
        classes = (own, after, *far, before)
        own = jnp.concatenate([block[:, :-1] for block in classes])
        after, before = shift(own, "y", 1), shift(own, "y", -1)
        far = jnp.concatenate([shift(after[:8], "y", 1), shift(before[8:], "y", -1)])
        weights = [(block, shift(block, "core", 1)) for block in (own, after, far, before)]

    with jax.named_scope("gather_queries"):
        coded = jnp.concatenate([block[:, -1] for block in classes])
        coded = jnp.roll(coded.reshape(4, 4, width_here), zr, axis=0).reshape(nz, width_here)
        packed = send_all(coded[:, : width + LANES], NEAR)

    cols = width // nx
    six = width // n_index
    place = lax.broadcasted_iota(jnp.int32, (width, 1), 0)
    to_core, to_y = place // (ny * nz * six), place // (nz * six) % ny
    to_z, within = place // six % nz, place % six
    column = ((to_y * nz + to_z) * ncore + (to_core + core) % ncore) * six + within
    chosen = (lax.broadcasted_iota(jnp.int32, (1, width), 1) == column).astype(jnp.bfloat16)

    vmem = pl.BlockSpec(memory_space=pltpu.VMEM)
    with jax.named_scope("scores"):
        queries = n_index * nx
        state, slots, my_rows, my_unit, query_scale, ordered = pl.pallas_call(
            scores_kernel,
            out_shape=(
                jax.ShapeDtypeStruct((n_index, LANES), jnp.float32),
                jax.ShapeDtypeStruct((n_index, LANES), jnp.int32),
                jax.ShapeDtypeStruct((shard_rows, cols), jnp.float32),
                jax.ShapeDtypeStruct((queries, cols), jnp.float32),
                jax.ShapeDtypeStruct((queries, 1), jnp.float32),
                jax.ShapeDtypeStruct((width, queries), jnp.bfloat16),
            ),
            in_specs=[pl.BlockSpec(memory_space=pltpu.SMEM)] + [vmem] * 4,
            out_specs=(vmem,) * 6,
            scratch_shapes=[
                pltpu.VMEM((queries, width), jnp.float32),
                pltpu.VMEM((nx, n_index, LANES), jnp.int32),
            ],
            compiler_params=pltpu.CompilerParams(vmem_limit_bytes=48 << 20),
            cost_estimate=pl.CostEstimate(
                flops=4 << 30, bytes_accessed=8 << 20, transcendentals=0
            ),
            name="scores",
        )(jnp.stack([my_shard, r]).astype(jnp.int32), packed, query_proj, index_emb, chosen)

    def merge_all(x):
        lane = lax.broadcasted_iota(jnp.int32, x.shape[1:], x.ndim - 2)
        return jnp.where(lane < topk, jnp.sum(x, axis=0), jnp.max(x, axis=0))

    with jax.named_scope("reduce_scores"):
        state = state.reshape(n_pair, nz, LANES)
        state = merge_all(lax.all_to_all(state, ("y", "core"), 0, 0, tiled=True))
        state = merge_all(lax.all_to_all(state, Z_BY_CLASS, 0, 0, tiled=True))
        slab_best = state[topk : topk + 1]
        fetched = state[:topk]
    expo = jnp.exp(fetched)
    total = jnp.sum(expo)
    prob = expo / total
    log_prob = fetched - jnp.log(total)
    score_row = jnp.zeros((1, LANES), jnp.float32)
    score_row = score_row.at[0, :topk].set(prob).at[0, LANES // 2 : LANES // 2 + topk].set(fetched)

    with jax.named_scope("attention"):
        answer = dec_query.shape[1]
        heads_here = feats_here // DH
        decoded = dec_query.astype(jnp.float32).reshape(group, answer, heads_here, DH)
        dec_unit = (
            decoded * lax.rsqrt(jnp.mean(decoded * decoded, axis=3, keepdims=True) + EPSILON)
        ).astype(jnp.bfloat16)
        positions = lax.broadcasted_iota(jnp.int32, (group, topk, plen), 2)
        live = (positions < passage_len[:, :, None]).reshape(group, topk * plen)
        packet = attention_packet(
            jnp.stack([y, zr, core]).astype(jnp.int32),
            token_blocks,
            weights,
            dec_unit.reshape(group, answer, feats_here),
            key_gain.astype(jnp.float32).reshape(1, feats_here),
            live.astype(jnp.float32),
            score_row,
        )

    with jax.named_scope("targets"):
        packets = lax.all_to_all(packet, NEAR, 0, 0, tiled=True).reshape(nx, n_pair, 2 * LANES)
        coef = pl.pallas_call(
            coef_kernel,
            out_shape=jax.ShapeDtypeStruct((nz, n_pair, LANES), jnp.float32),
            in_specs=[vmem],
            out_specs=vmem,
            name="coef",
        )(packets)
        coef = lax.all_to_all(coef, Z_BY_CLASS, 0, 0, tiled=True).reshape(n_index, LANES)

    with jax.named_scope("gradient"):
        part = jax.ShapeDtypeStruct((width // ncore, cols), jnp.float32)
        keep, send = pl.pallas_call(
            gradient_kernel,
            out_shape=(part, part),
            in_specs=[vmem] * 6,
            out_specs=(vmem, vmem),
            scratch_shapes=[pltpu.VMEM((queries, shard_rows), jnp.float32)],
            compiler_params=pltpu.CompilerParams(vmem_limit_bytes=40 << 20),
            name="gradient",
        )(coef, slots, my_rows, my_unit, query_scale, ordered)

    with jax.named_scope("reduce_gradient"):
        term = (keep + shift(send, "core", 1)).reshape(ny, nz * six, cols)
        term = jnp.sum(lax.all_to_all(term, "y", 0, 0, tiled=True), axis=0)
        term = term.reshape(nz, six, cols)
        term = jnp.sum(lax.all_to_all(term, Z, 0, 0, tiled=True), axis=0)
        grad_proj = send_all(term, "reader")
        grad_proj = grad_proj.transpose(1, 0, 2).reshape(six, width)

    mass = jnp.sum(lax.dynamic_index_in_dim(packets, y * ncore + core, 1, False), axis=0)
    my_target = lax.dynamic_slice_in_dim(mass, r * SLOT, topk, 0)
    log_target = jnp.log(my_target)
    retr_loss = jnp.sum(my_target * (log_target - log_prob))
    return (grad_proj, slab_best, retr_loss[None], log_target[None])


def solution(mesh):
    split = Mesh(mesh.devices.reshape(4, 4, 4, 2, 4), INDEX + ("reader",))
    return jax.shard_map(
        body,
        mesh=split,
        in_specs=(
            P(INDEX, None),
            P(INDEX + ("reader",), None),
            P(),
            P(INDEX + ("reader",), None),
            P(INDEX, None),
            P(INDEX, None, None, "reader"),
            P(INDEX, "reader"),
            P("reader"),
            P(INDEX, None, "reader"),
        ),
        out_specs=(
            P(INDEX, None),
            P(INDEX + ("reader",)),
            P(INDEX + ("reader",)),
            P(INDEX + ("reader",), None),
        ),
        check_vma=False,
    )
```

time: 314 us -> 268 us (0.85)
  blocking collectives: 11 us -> 45.3 us
  waiting for transfers between devices: 92.3 us -> 58.5 us
  local copies, waits for them, and re-layouts: 50.6 us -> 24.2 us
  starting transfers between devices: 98.2 us -> 79.9 us
  Pallas kernels: 22.1 us -> 31.9 us
  matrix products: 6.35 us -> 0 us
  other arithmetic: 14.6 us -> 10.1 us
    all_to_all x0 -> x2, blocking collectives: none -> 34.2 us  [the longest x1 20.8 us: body(): lax.all_to_all(coef, Z_BY_CLASS, 0, 0, tiled=True).reshape(n_index, LANES)]
    all_to_all x3 -> x1, waiting for transfers between devices: 26.3 us -> 4.72 us  [body(): state = merge_all(lax.all_to_all(state, Z_BY_CLASS, 0, 0, tiled=True))]
    concatenate x23 -> x2, local copies, waits for them, and re-layouts: 21.1 us -> 0.78 us  [the longest x1 0.72 us: body(): own = jnp.concatenate([block[:, :-1] for block in classes])]
    pallas_call x0 -> x2, Pallas kernels: none -> 16.4 us  [the longest x1 10.4 us: attention_packet(): pl.pallas_call(early_keys_kernel, out_shape=jax.ShapeDtypeStruct((rows, w...]
    all_to_all x3 -> x1, starting transfers between devices: 19.6 us -> 5.36 us  [body(): state = merge_all(lax.all_to_all(state, Z_BY_CLASS, 0, 0, tiled=True))]
    pallas_call x1, Pallas kernels: 14.1 us -> 7.51 us  [attention_packet(): pl.pallas_call(attention_kernel, out_shape=jax.ShapeDtypeStruct((32, 2 *...]
    ppermute x13, waiting for transfers between devices: 22.3 us -> 16.5 us  [shift(): return lax.ppermute(x, axis, [((i + step) % size, i) for i in range(size)])]
    dot_general x2 -> x0, matrix products: 4.39 us -> none  [the longest x1 2.45 us: body(): lax.dot_general(share, row_unit, (((1,), (1,)), ((), ())), precision=EXACT)]
  transfers between devices with their start and end apart: 23 -> 20, of which waited for: 12 -> 9; matrix products, arithmetic and copies ran while one was open for 21% -> 9% of each run, Pallas kernels for 0% -> 6%
where the time goes in v2:
time: 268 us; the launch traced here: 265 us
  starting transfers between devices  79.9 us (30%)
  waiting for transfers between devices  58.5 us (22%)
  blocking collectives  45.3 us (17%)
  Pallas kernels  31.9 us (12%)
  local copies, waits for them, and re-layouts  24.2 us (9%)
  between operations  15.3 us (6%)
  other arithmetic  10.1 us (4%)
    ppermute x13, starting transfers between devices, shift(): return lax.ppermute(x, axis, [((i + step) % size, i) for i in range(size)])  39.5 us
    all_to_all x3, starting transfers between devices, send_all(): lax.all_to_all(jnp.broadcast_to(x[None], (size, *x.shape)), axis, 0, 0, t...  28 us
    all_to_all x3, waiting for transfers between devices, send_all(): lax.all_to_all(jnp.broadcast_to(x[None], (size, *x.shape)), axis, 0, 0, t...  24.4 us
    all_to_all x1, blocking collectives, body(): lax.all_to_all(coef, Z_BY_CLASS, 0, 0, tiled=True).reshape(n_index, LANES)  20.8 us
    ppermute x13, waiting for transfers between devices, shift(): return lax.ppermute(x, axis, [((i + step) % size, i) for i in range(size)])  16.5 us
    all_to_all x1, blocking collectives, body(): lax.all_to_all(packet, NEAR, 0, 0, tiled=True)  13.5 us
    all_to_all x1, waiting for transfers between devices, body(): term = jnp.sum(lax.all_to_all(term, Z, 0, 0, tiled=True), axis=0)  12.1 us
    unnamed x39, local copies, waits for them, and re-layouts  12 us
  transfers between devices with their start and end apart: 20, of which 9 were waited for; matrix products, arithmetic and copies ran while one was open for 9% of the time, Pallas kernels for 6%

profile of v2, /device:TPU:6, one launch (start us, length us, event | category | flops | bytes accessed | tf_op | source)
XLA Modules:
  0.0 265.2 jit_solution(649897782258843404)
XLA Ops:
  11.0 15.1 %all-to-all-start = ((bf16[4,33,1024]{2,1,0:T(8,128)(2,1)}), bf16[4,33,1024]{2,1,0:T(8,128)(2,1)S(1)}, u32[]{:S(2)}, u32[]{:S(2)}) async-start(bf16[4,33,1024]{2,1,0:T(8,128)(2,1)} %broadcast_in_dim.10), calls=%async_computation | async-start | bytes 655360 | tf_op jit(solution)/shard_map/gather_key_proj/all_to_all | solution.py:36
  27.2 18.0 %all-to-all-done = bf16[4,33,1024]{2,1,0:T(8,128)(2,1)S(1)} async-done(((bf16[4,33,1024]{2,1,0:T(8,128)(2,1)}), bf16[4,33,1024]{2,1,0:T(8,128)(2,1)S(1)}, u32[]{:S(2)}, u32[]{:S(2)}) %all-to-all-start) | async-done | bytes 270368 | tf_op jit(solution)/shard_map/gather_key_proj/all_to_all | solution.py:36
  45.1 7.2 %collective-permute-start.3 = (bf16[4,33,1024]{2,1,0:T(8,128)(2,1)S(1)}, bf16[4,33,1024]{2,1,0:T(8,128)(2,1)S(1)}, u32[]{:S(2)}, u32[]{:S(2)}) collective-permute-start(bf16[4,33,1024]{2,1,0:T(8,128)(2,1)S(1)} %all-to-all-done), channel_id=1, source_target_pairs={{120,0},{0,8},{8,16},{16,24},{24,32},{32,40},{40,48},{48,56},{56,6... | collective-permute-start | bytes 811016 | tf_op jit(solution)/shard_map/gather_key_proj/ppermute | solution.py:31
  52.4 1.9 collective-permute-start
  54.3 4.5 %collective-permute-start.2 = (bf16[2,33,1024]{2,1,0:T(8,128)(2,1)S(1)}, bf16[2,33,1024]{2,1,0:T(8,128)(2,1)S(1)}, u32[]{:S(2)}, u32[]{:S(2)}) collective-permute-start(bf16[2,33,1024]{2,1,0:T(8,128)(2,1)S(1)} %get-tuple-element.48), channel_id=1, source_target_pairs={{112,0},{120,8},{0,16},{8,24},{16,32},{24,40},{32,48},{40,56},{48,... | collective-permute-start | bytes 405512 | tf_op jit(solution)/shard_map/gather_key_proj/ppermute | solution.py:31
  58.8 3.5 %collective-permute-start.1 = (bf16[2,33,1024]{2,1,0:T(8,128)(2,1)S(1)}, bf16[2,33,1024]{2,1,0:T(8,128)(2,1)S(1)}, u32[]{:S(2)}, u32[]{:S(2)}) collective-permute-start(bf16[2,33,1024]{2,1,0:T(8,128)(2,1)S(1)} %get-tuple-element.49), channel_id=1, source_target_pairs={{16,0},{24,8},{32,16},{40,24},{48,32},{56,40},{64,48},{72,56},{80,... | collective-permute-start | bytes 405512 | tf_op jit(solution)/shard_map/gather_key_proj/ppermute | solution.py:31
  63.1 0.9 collective-permute-done.2
  64.0 6.0 %collective-permute-done.1 = bf16[2,33,1024]{2,1,0:T(8,128)(2,1)S(1)} collective-permute-done((bf16[2,33,1024]{2,1,0:T(8,128)(2,1)S(1)}, bf16[2,33,1024]{2,1,0:T(8,128)(2,1)S(1)}, u32[]{:S(2)}, u32[]{:S(2)}) %collective-permute-start.1) | collective-permute-done | bytes 135200 | tf_op jit(solution)/shard_map/gather_key_proj/ppermute | solution.py:31
  70.3 1.0 broadcast_in_dim.11
  71.3 7.6 %all-to-all-start.1 = ((bf16[32,16,896]{2,1,0:T(8,128)(2,1)}), bf16[32,16,896]{2,1,0:T(8,128)(2,1)S(1)}, u32[]{:S(2)}, u32[]{:S(2)}) async-start(bf16[32,16,896]{2,1,0:T(8,128)(2,1)} %broadcast_in_dim.11), calls=%async_computation.1 | async-start | bytes 1835008 | tf_op jit(solution)/shard_map/gather_queries/all_to_all | solution.py:36
  81.7 4.6 %collective-permute-start.4 = (bf16[16,32,1024]{2,1,0:T(8,128)(2,1)}, bf16[16,32,1024]{2,1,0:T(8,128)(2,1)}, u32[]{:S(2)}, u32[]{:S(2)}) collective-permute-start(bf16[16,32,1024]{2,1,0:T(8,128)(2,1)} %slice_dynamic-update-slice_fusion.refs_0_), channel_id=1, source_target_pairs={{128,0},{256,128},{384,256},{0,384},{129,1},{257,129},{385,257},{1... | collective-permute-start | bytes 3145736 | tf_op jit(solution)/shard_map/gather_key_proj/ppermute | solution.py:31
  86.3 1.9 collective-permute-start.6
  88.6 4.2 %all-to-all-done.1.packed = bf16[32,16,896]{2,1,0:T(8,128)(2,1)S(1)} async-done(((bf16[32,16,896]{2,1,0:T(8,128)(2,1)}), bf16[32,16,896]{2,1,0:T(8,128)(2,1)S(1)}, u32[]{:S(2)}, u32[]{:S(2)}) %all-to-all-start.1) | async-done | bytes 917536 | tf_op jit(solution)/shard_map/gather_queries/all_to_all | solution.py:36
  92.9 1.3 copy-done.8
  94.1 5.9 %scores.1 = (f32[128,128]{1,0:T(8,128)S(1)}, s32[128,128]{1,0:T(8,128)S(1)}, f32[512,192]{1,0:T(8,128)S(1)}, f32[512,192]{1,0:T(8,128)S(1)}, f32[512,1]{1,0:T(8,128)S(1)}, /*index=5*/bf16[768,512]{1,0:T(8,128)(2,1)S(1)}) custom-call(s32[2]{0:T(128)S(1)} %pad_add_fusion.1.place, bf16[32,16,896]{2,1,0:T(8,128)(2,1)S(1)} %all-to-all-done.1.packed, ...), custom_call_target="tpu_custom_call" | custom-call | flops 4294967296 | bytes 8388608 | tf_op jit(solution)/shard_map/scores/scores/pallas_call | solution.py:348
  102.8 3.5 %all-to-all-start.2 = ((f32[8,16,128]{2,1,0:T(8,128)}), f32[8,16,128]{2,1,0:T(8,128)S(1)}, u32[]{:S(2)}, u32[]{:S(2)}) async-start(f32[8,16,128]{2,1,0:T(8,128)} %bitcast.45), calls=%async_computation.2 | async-start | bytes 131072 | tf_op jit(solution)/shard_map/reduce_scores/all_to_all | solution.py:377
  106.3 7.9 %collective-permute-done.4.refs_2_ = bf16[16,32,1024]{2,1,0:T(8,128)(2,1)} collective-permute-done((bf16[16,32,1024]{2,1,0:T(8,128)(2,1)}, bf16[16,32,1024]{2,1,0:T(8,128)(2,1)}, u32[]{:S(2)}, u32[]{:S(2)}) %collective-permute-start.4) | collective-permute-done | bytes 1048608 | tf_op jit(solution)/shard_map/gather_key_proj/ppermute | solution.py:31
  114.3 1.1 slice.112
  115.3 3.3 %collective-permute-start.5 = (bf16[8,32,1024]{2,1,0:T(8,128)(2,1)S(1)}, bf16[8,32,1024]{2,1,0:T(8,128)(2,1)S(1)}, u32[]{:S(2)}, u32[]{:S(2)}) collective-permute-start(bf16[8,32,1024]{2,1,0:T(8,128)(2,1)S(1)} %slice.112), channel_id=1, source_target_pairs={{128,0},{256,128},{384,256},{0,384},{129,1},{257,129},{385,257},{1... | collective-permute-start | bytes 1572872 | tf_op jit(solution)/shard_map/gather_key_proj/ppermute | solution.py:31
  118.7 1.9 slice.113
  120.6 2.6 collective-permute-start.7
  123.8 5.4 %all-to-all-start.3 = ((f32[16,1,128]{2,1,0:T(1,128)}), f32[16,1,128]{2,1,0:T(1,128)S(1)}, u32[]{:S(2)}, u32[]{:S(2)}) async-start(f32[16,1,128]{2,1,0:T(1,128)} %broadcast_select_fusion), calls=%async_computation.3 | async-start | bytes 16384 | tf_op jit(solution)/shard_map/reduce_scores/all_to_all | solution.py:378
  130.5 1.9 collective-permute-start.9
  132.4 2.4 collective-permute-start.10
  134.8 1.9 collective-permute-start.11
  136.7 4.7 %all-to-all-done.3 = f32[16,1,128]{2,1,0:T(1,128)S(1)} async-done(((f32[16,1,128]{2,1,0:T(1,128)}), f32[16,1,128]{2,1,0:T(1,128)S(1)}, u32[]{:S(2)}, u32[]{:S(2)}) %all-to-all-start.3) | async-done | bytes 8224 | tf_op jit(solution)/shard_map/reduce_scores/all_to_all | solution.py:378
  141.5 1.1 constant_dynamic-update-slice_fusion.refs_0_
  142.6 1.9 collective-permute-start.8
  145.2 1.3 fusion.28
  146.5 1.8 broadcast_select_fusion.1
  148.3 1.4 scatter.9.refs_6_
  149.7 10.4 %early_keys.1.refs_2_ = f32[640,1024]{1,0:T(8,128)} custom-call(s32[3]{0:T(128)S(1)} %pad_add_fusion.place, bf16[4,640,1024]{2,1,0:T(8,128)(2,1)} %all-gather.2.cloned.1.call-done.tokens, bf16[16,32,1024]{2,1,0:T(8,128)(2,1)} %slice_dynamic-update-slice_fusion.refs_0_, bf16[16,32,1024]{2,1,0:T(8,128)(2,1)} %collective-permute-done.9.refs_1_, ...), custom_call_target="tpu_custom_call" | custom-call | flops 4026531840 | bytes 13631488 | tf_op jit(solution)/shard_map/attention/early_keys/pallas_call | solution.py:157
  160.2 1.7 copy-done
  161.9 7.5 %attention.1 = f32[32,256]{1,0:T(8,128)S(1)} custom-call(s32[3]{0:T(128)S(1)} %pad_add_fusion.place, bf16[4,640,1024]{2,1,0:T(8,128)(2,1)} %all-gather.2.cloned.1.call-done.tokens, bf16[16,32,1024]{2,1,0:T(8,128)(2,1)S(1)} %constant_dynamic-update-slice_fusion.refs_0_, bf16[16,32,1024]{2,1,0:T(8,128)(2,1)S(1)} %collective-permute-done.8.refs_1_, ...), custom_call_target="tpu_custom_call" | custom-call | flops 1342177280 | bytes 6291456 | tf_op jit(solution)/shard_map/attention/attention/pallas_call | solution.py:167
  169.5 13.5 %all_to_all.50 = f32[32,1,256]{2,1,0:T(1,128)S(1)} all-to-all(f32[32,1,256]{2,1,0:T(1,128)S(1)} %copy.31), channel_id=1, replica_groups=mesh['y'=4,'zq'=4,'zr'=4,'core'=2,'reader'=4] {'reader','y','core'}, dimensions={0} | all-to-all | bytes 65536 | tf_op jit(solution)/shard_map/targets/all_to_all | solution.py:408
  183.6 1.6 coef.1
  185.2 20.8 %all_to_all.51 = f32[16,8,128]{2,1,0:T(8,128)S(1)} all-to-all(f32[16,8,128]{2,1,0:T(8,128)} %coef.1), channel_id=1, replica_groups=mesh['y'=4,'zq'=4,'zr'=4,'core'=2,'reader'=4] {'zr','zq'}, dimensions={0} | all-to-all | bytes 131072 | tf_op jit(solution)/shard_map/targets/all_to_all | solution.py:416
  205.9 1.0 copy-done.2
  207.0 0.9 copy-done.4
  208.8 6.4 %gradient.1 = (f32[384,192]{1,0:T(8,128)S(1)}, f32[384,192]{1,0:T(8,128)S(1)}) custom-call(f32[128,128]{1,0:T(8,128)S(1)} %bitcast.43, s32[128,128]{1,0:T(8,128)S(1)} %copy-done.6, f32[512,192]{1,0:T(8,128)S(1)} %get-tuple-element.38.rows, f32[512,192]{1,0:T(8,128)S(1)} %copy-done.2, f32[512,1]{1,0:T(8,128)S(1)} %copy-done.4, ...), custom_call_target="tpu_custom_call" | custom-call | tf_op jit(solution)/shard_map/gradient/gradient/pallas_call | solution.py:420
  215.2 1.9 collective-permute-start.12
  217.2 1.7 collective-permute-done.12
  218.9 11.0 %all_to_all.52 = f32[4,96,192]{2,1,0:T(8,128)S(1)} all-to-all(f32[4,96,192]{2,1,0:T(8,128)S(1)} %bitcast.47), channel_id=1, replica_groups=mesh['y'=4,'zq'=4,'zr'=4,'core'=2,'reader'=4] {'y'}, dimensions={0} | all-to-all | bytes 589824 | tf_op jit(solution)/shard_map/reduce_gradient/all_to_all | solution.py:432
  230.7 3.5 %all-to-all-start.7 = ((f32[16,6,192]{2,1,0:T(8,128)}), f32[16,6,192]{2,1,0:T(8,128)S(1)}, u32[]{:S(2)}, u32[]{:S(2)}) async-start(f32[16,6,192]{2,1,0:T(8,128)} %reshape.297), calls=%async_computation.7 | async-start | bytes 262144 | tf_op jit(solution)/shard_map/reduce_gradient/all_to_all | solution.py:434
  236.2 12.1 %all-to-all-done.7 = f32[16,6,192]{2,1,0:T(8,128)S(1)} async-done(((f32[16,6,192]{2,1,0:T(8,128)}), f32[16,6,192]{2,1,0:T(8,128)S(1)}, u32[]{:S(2)}, u32[]{:S(2)}) %all-to-all-start.7) | async-done | bytes 73760 | tf_op jit(solution)/shard_map/reduce_gradient/all_to_all | solution.py:434
  249.0 5.3 %all-to-all-start.8 = ((f32[4,6,192]{2,1,0:T(8,128)}), f32[4,6,192]{2,1,0:T(8,128)S(1)}, u32[]{:S(2)}, u32[]{:S(2)}) async-start(f32[4,6,192]{2,1,0:T(8,128)} %broadcast_in_dim.12), calls=%async_computation.8 | async-start | bytes 65536 | tf_op jit(solution)/shard_map/reduce_gradient/all_to_all | solution.py:36
  254.3 1.2 log_bitcast_fusion
  255.5 2.2 all-to-all-done.8
  (101 shorter events, 19.3 us)
Async XLA Ops:
  7.2 18.9 %copy-start.9 = (bf16[4,16,1024]{2,1,0:T(8,128)(2,1)S(1)}, bf16[4,16,1024]{2,1,0:T(8,128)(2,1)}, u32[]{:S(2)}) copy-start(bf16[4,16,1024]{2,1,0:T(8,128)(2,1)} %param.21) | copy-start | bytes 393220
  7.2 142.5 %all-gather.2.cloned.1.call-start = ((), (), s32[]{:S(2)}) async-start(), calls=%async_computation.9 | async-start | bytes 6553600 | tf_op jit(solution)/shard_map/gather_enc_out/all_gather | solution.py:314
  11.0 34.2 %all-to-all-start = ((bf16[4,33,1024]{2,1,0:T(8,128)(2,1)}), bf16[4,33,1024]{2,1,0:T(8,128)(2,1)S(1)}, u32[]{:S(2)}, u32[]{:S(2)}) async-start(bf16[4,33,1024]{2,1,0:T(8,128)(2,1)} %broadcast_in_dim.10), calls=%async_computation | async-start | bytes 655360 | tf_op jit(solution)/shard_map/gather_key_proj/all_to_all | solution.py:36
  26.1 0.8 copy-start.12
  45.1 24.9 %collective-permute-start.3 = (bf16[4,33,1024]{2,1,0:T(8,128)(2,1)S(1)}, bf16[4,33,1024]{2,1,0:T(8,128)(2,1)S(1)}, u32[]{:S(2)}, u32[]{:S(2)}) collective-permute-start(bf16[4,33,1024]{2,1,0:T(8,128)(2,1)S(1)} %all-to-all-done), channel_id=1, source_target_pairs={{120,0},{0,8},{8,16},{16,24},{24,32},{32,40},{40,48},{48,56},{56,6... | collective-permute-start | bytes 811016 | tf_op jit(solution)/shard_map/gather_key_proj/ppermute | solution.py:31
  52.4 17.7 %collective-permute-start = (bf16[4,33,1024]{2,1,0:T(8,128)(2,1)S(1)}, bf16[4,33,1024]{2,1,0:T(8,128)(2,1)S(1)}, u32[]{:S(2)}, u32[]{:S(2)}) collective-permute-start(bf16[4,33,1024]{2,1,0:T(8,128)(2,1)S(1)} %all-to-all-done), channel_id=1, source_target_pairs={{8,0},{16,8},{24,16},{32,24},{40,32},{48,40},{56,48},{64,56},{72,6... | collective-permute-start | bytes 811016 | tf_op jit(solution)/shard_map/gather_key_proj/ppermute | solution.py:31
  54.3 9.6 %collective-permute-start.2 = (bf16[2,33,1024]{2,1,0:T(8,128)(2,1)S(1)}, bf16[2,33,1024]{2,1,0:T(8,128)(2,1)S(1)}, u32[]{:S(2)}, u32[]{:S(2)}) collective-permute-start(bf16[2,33,1024]{2,1,0:T(8,128)(2,1)S(1)} %get-tuple-element.48), channel_id=1, source_target_pairs={{112,0},{120,8},{0,16},{8,24},{16,32},{24,40},{32,48},{40,56},{48,... | collective-permute-start | bytes 405512 | tf_op jit(solution)/shard_map/gather_key_proj/ppermute | solution.py:31
  58.8 11.2 %collective-permute-start.1 = (bf16[2,33,1024]{2,1,0:T(8,128)(2,1)S(1)}, bf16[2,33,1024]{2,1,0:T(8,128)(2,1)S(1)}, u32[]{:S(2)}, u32[]{:S(2)}) collective-permute-start(bf16[2,33,1024]{2,1,0:T(8,128)(2,1)S(1)} %get-tuple-element.49), channel_id=1, source_target_pairs={{16,0},{24,8},{32,16},{40,24},{48,32},{56,40},{64,48},{72,56},{80,... | collective-permute-start | bytes 405512 | tf_op jit(solution)/shard_map/gather_key_proj/ppermute | solution.py:31
  71.3 21.5 %all-to-all-start.1 = ((bf16[32,16,896]{2,1,0:T(8,128)(2,1)}), bf16[32,16,896]{2,1,0:T(8,128)(2,1)S(1)}, u32[]{:S(2)}, u32[]{:S(2)}) async-start(bf16[32,16,896]{2,1,0:T(8,128)(2,1)} %broadcast_in_dim.11), calls=%async_computation.1 | async-start | bytes 1835008 | tf_op jit(solution)/shard_map/gather_queries/all_to_all | solution.py:36
  81.7 32.6 %collective-permute-start.4 = (bf16[16,32,1024]{2,1,0:T(8,128)(2,1)}, bf16[16,32,1024]{2,1,0:T(8,128)(2,1)}, u32[]{:S(2)}, u32[]{:S(2)}) collective-permute-start(bf16[16,32,1024]{2,1,0:T(8,128)(2,1)} %slice_dynamic-update-slice_fusion.refs_0_), channel_id=1, source_target_pairs={{128,0},{256,128},{384,256},{0,384},{129,1},{257,129},{385,257},{1... | collective-permute-start | bytes 3145736 | tf_op jit(solution)/shard_map/gather_key_proj/ppermute | solution.py:31
  86.3 32.3 %collective-permute-start.6 = (bf16[16,32,1024]{2,1,0:T(8,128)(2,1)}, bf16[16,32,1024]{2,1,0:T(8,128)(2,1)}, u32[]{:S(2)}, u32[]{:S(2)}) collective-permute-start(bf16[16,32,1024]{2,1,0:T(8,128)(2,1)} %slice_dynamic-update-slice_fusion.refs_0_), channel_id=1, source_target_pairs={{384,0},{0,128},{128,256},{256,384},{385,1},{1,129},{129,257},{257... | collective-permute-start | bytes 3145736 | tf_op jit(solution)/shard_map/gather_key_proj/ppermute | solution.py:31
  92.9 1.3 copy-start.8
  100.1 0.8 copy-start.1
  100.9 0.7 copy-start.3
  101.6 0.6 copy-start.5
  102.2 0.6 copy-start.7
  102.8 27.0 %copy-start.13 = (bf16[1024]{0:T(1024)(128)(2,1)S(1)}, bf16[1024]{0:T(1024)(128)(2,1)}, u32[]{:S(2)}) copy-start(bf16[1024]{0:T(1024)(128)(2,1)} %param.20) | copy-start | bytes 6148
  102.8 15.8 %all-to-all-start.2 = ((f32[8,16,128]{2,1,0:T(8,128)}), f32[8,16,128]{2,1,0:T(8,128)S(1)}, u32[]{:S(2)}, u32[]{:S(2)}) async-start(f32[8,16,128]{2,1,0:T(8,128)} %bitcast.45), calls=%async_computation.2 | async-start | bytes 131072 | tf_op jit(solution)/shard_map/reduce_scores/all_to_all | solution.py:377
  115.3 26.1 %collective-permute-start.5 = (bf16[8,32,1024]{2,1,0:T(8,128)(2,1)S(1)}, bf16[8,32,1024]{2,1,0:T(8,128)(2,1)S(1)}, u32[]{:S(2)}, u32[]{:S(2)}) collective-permute-start(bf16[8,32,1024]{2,1,0:T(8,128)(2,1)S(1)} %slice.112), channel_id=1, source_target_pairs={{128,0},{256,128},{384,256},{0,384},{129,1},{257,129},{385,257},{1... | collective-permute-start | bytes 1572872 | tf_op jit(solution)/shard_map/gather_key_proj/ppermute | solution.py:31
  120.6 20.9 %collective-permute-start.7 = (bf16[8,32,1024]{2,1,0:T(8,128)(2,1)}, bf16[8,32,1024]{2,1,0:T(8,128)(2,1)}, u32[]{:S(2)}, u32[]{:S(2)}) collective-permute-start(bf16[8,32,1024]{2,1,0:T(8,128)(2,1)} %slice.113), channel_id=1, source_target_pairs={{384,0},{0,128},{128,256},{256,384},{385,1},{1,129},{129,257},{257... | collective-permute-start | bytes 1572872 | tf_op jit(solution)/shard_map/gather_key_proj/ppermute | solution.py:31
  123.8 17.7 %all-to-all-start.3 = ((f32[16,1,128]{2,1,0:T(1,128)}), f32[16,1,128]{2,1,0:T(1,128)S(1)}, u32[]{:S(2)}, u32[]{:S(2)}) async-start(f32[16,1,128]{2,1,0:T(1,128)} %broadcast_select_fusion), calls=%async_computation.3 | async-start | bytes 16384 | tf_op jit(solution)/shard_map/reduce_scores/all_to_all | solution.py:378
  130.5 19.2 %collective-permute-start.9 = (bf16[16,32,1024]{2,1,0:T(8,128)(2,1)}, bf16[16,32,1024]{2,1,0:T(8,128)(2,1)}, u32[]{:S(2)}, u32[]{:S(2)}) collective-permute-start(bf16[16,32,1024]{2,1,0:T(8,128)(2,1)} %slice_dynamic-update-slice_fusion.refs_0_), channel_id=1, source_target_pairs={{4,0},{0,4},{5,1},{1,5},{6,2},{2,6},{7,3},{3,7},{12,8},{8,12},{13,... | collective-permute-start | bytes 3145736 | tf_op jit(solution)/shard_map/gather_key_proj/ppermute | solution.py:31
  132.4 17.3 %collective-permute-start.10 = (bf16[16,32,1024]{2,1,0:T(8,128)(2,1)}, bf16[16,32,1024]{2,1,0:T(8,128)(2,1)}, u32[]{:S(2)}, u32[]{:S(2)}) collective-permute-start(bf16[16,32,1024]{2,1,0:T(8,128)(2,1)} %collective-permute-done.4.refs_2_), channel_id=1, source_target_pairs={{4,0},{0,4},{5,1},{1,5},{6,2},{2,6},{7,3},{3,7},{12,8},{8,12},{13,... | collective-permute-start | bytes 3145736 | tf_op jit(solution)/shard_map/gather_key_proj/ppermute | solution.py:31
  134.8 14.9 %collective-permute-start.11 = (bf16[16,32,1024]{2,1,0:T(8,128)(2,1)}, bf16[16,32,1024]{2,1,0:T(8,128)(2,1)}, u32[]{:S(2)}, u32[]{:S(2)}) collective-permute-start(bf16[16,32,1024]{2,1,0:T(8,128)(2,1)} %collective-permute-done.6.refs_4_), channel_id=1, source_target_pairs={{4,0},{0,4},{5,1},{1,5},{6,2},{2,6},{7,3},{3,7},{12,8},{8,12},{13,... | collective-permute-start | bytes 3145736 | tf_op jit(solution)/shard_map/gather_key_proj/ppermute | solution.py:31
  142.6 17.6 %collective-permute-start.8 = (bf16[16,32,1024]{2,1,0:T(8,128)(2,1)S(1)}, bf16[16,32,1024]{2,1,0:T(8,128)(2,1)S(1)}, u32[]{:S(2)}, u32[]{:S(2)}) collective-permute-start(bf16[16,32,1024]{2,1,0:T(8,128)(2,1)S(1)} %constant_dynamic-update-slice_fusion.refs_0_), channel_id=1, source_target_pairs={{4,0},{0,4},{5,1},{1,5},{6,2},{2,6},{7,3},{3,7},{12,8},{8,12},{13,... | collective-permute-start | bytes 3145736 | tf_op jit(solution)/shard_map/gather_key_proj/ppermute | solution.py:31
  144.5 1.9 copy-start.10
  160.2 1.7 copy-start
  205.9 1.0 copy-start.2
  207.0 0.9 copy-start.4
  207.9 0.8 copy-start.6
  215.2 19.6 %copy-start.11 = (f32[128]{0:T(128)S(1)}, f32[128]{0:T(128)}, u32[]{:S(2)}) copy-start(f32[128]{0:T(128)} %copy-done.10) | copy-start | bytes 1540
  215.2 3.6 %collective-permute-start.12 = (f32[384,192]{1,0:T(8,128)S(1)}, f32[384,192]{1,0:T(8,128)S(1)}, u32[]{:S(2)}, u32[]{:S(2)}) collective-permute-start(f32[384,192]{1,0:T(8,128)S(1)} %get-tuple-element.43), channel_id=1, source_target_pairs={{4,0},{0,4},{5,1},{1,5},{6,2},{2,6},{7,3},{3,7},{12,8},{8,12},{13,... | collective-permute-start | bytes 884744 | tf_op jit(solution)/shard_map/reduce_gradient/ppermute | solution.py:31
  230.7 17.7 %all-to-all-start.7 = ((f32[16,6,192]{2,1,0:T(8,128)}), f32[16,6,192]{2,1,0:T(8,128)S(1)}, u32[]{:S(2)}, u32[]{:S(2)}) async-start(f32[16,6,192]{2,1,0:T(8,128)} %reshape.297), calls=%async_computation.7 | async-start | bytes 262144 | tf_op jit(solution)/shard_map/reduce_gradient/all_to_all | solution.py:434
  249.0 8.7 %all-to-all-start.8 = ((f32[4,6,192]{2,1,0:T(8,128)}), f32[4,6,192]{2,1,0:T(8,128)S(1)}, u32[]{:S(2)}, u32[]{:S(2)}) async-start(f32[4,6,192]{2,1,0:T(8,128)} %broadcast_in_dim.12), calls=%async_computation.8 | async-start | bytes 65536 | tf_op jit(solution)/shard_map/reduce_gradient/all_to_all | solution.py:36
Sparse Core Ops, SparseCore 0:
  10.1 67.4 all-gather.1

commit v3 on v2

--- a/solution.py
+++ b/solution.py
@@ -16,7 +16,6 @@
 EXACT = lax.Precision.HIGHEST
 INDEX = ("y", "zq", "zr", "core")
 Z = ("zq", "zr")
-Z_BY_CLASS = ("zr", "zq")
 NEAR = ("reader", "y", "core")
 LANES = 128
 SLOT = 32
@@ -46,15 +45,15 @@
 
 
 def start_blocks(place, ahead, slot, tokens, weights, token_v, weight_v, sems):
-    y, zr, core = place[0], place[1], place[2]
-    copies = [pltpu.make_async_copy(tokens.at[(y + ahead) % 4], token_v.at[slot], sems.at[slot, 8])]
+    y, core = place[0], place[1]
+    copies = [pltpu.make_async_copy(tokens.at[(y + ahead) % 4], token_v.at[slot], sems.at[slot, 4])]
     for which in range(2):
-        for residue in range(4):
+        for half in range(2):
             copies.append(
                 pltpu.make_async_copy(
-                    weights[which].at[pl.ds(4 * residue, 4)],
-                    weight_v.at[slot, :, (zr + residue) % 4, (core + which) % 2],
-                    sems.at[slot, 4 * which + residue],
+                    weights[which][half],
+                    weight_v.at[slot, :, (core + which) % 2, half],
+                    sems.at[slot, 2 * which + half],
                 )
             )
     for copy in copies:
@@ -63,13 +62,11 @@
 
 
 def early_keys_kernel(place, tokens, *refs):
-    weights, (keys, token_v, weight_v, sems) = refs[:6], refs[6:]
-    copies = [
-        start_blocks(
-            place, ahead, slot, tokens, weights[2 * slot : 2 * slot + 2], token_v, weight_v, sems
-        )
-        for slot, ahead in enumerate(EARLY)
-    ]
+    weights, (keys, token_v, weight_v, sems) = refs[:4], refs[4:]
+    copies = []
+    for slot, ahead in enumerate(EARLY):
+        blocks = [[weights[2 * which + half].at[slot] for half in range(2)] for which in range(2)]
+        copies.append(start_blocks(place, ahead, slot, tokens, blocks, token_v, weight_v, sems))
     for slot in range(len(EARLY)):
         for copy in copies[slot]:
             copy.wait()
@@ -87,7 +84,8 @@
 def attention_kernel(place, tokens, *refs):
     weights, refs = refs[:2], refs[2:]
     early, dec, gain, live, scores, out, token_v, weight_v, column_v, sems = refs
-    copies = start_blocks(place, LATE, 0, tokens, weights, token_v, weight_v, sems)
+    blocks = [[weights[which].at[half] for half in range(2)] for which in range(2)]
+    copies = start_blocks(place, LATE, 0, tokens, blocks, token_v, weight_v, sems)
     group = dec.shape[0]
     n = live.shape[1]
     column_v[...] = jnp.zeros_like(column_v)
@@ -137,7 +135,7 @@
     out[:, LANES:] = jnp.broadcast_to(scores[...], (out.shape[0], LANES))
 
 
-def attention_packet(place, tokens, weights, dec, gain, live, scores):
+def attention_packet(place, tokens, early_rows, late_rows, dec, gain, live, scores):
     vmem = pl.BlockSpec(memory_space=pltpu.VMEM)
     anywhere = pl.BlockSpec(memory_space=pl.ANY)
     smem = pl.BlockSpec(memory_space=pltpu.SMEM)
@@ -146,7 +144,7 @@
     def blocks(count):
         return [
             pltpu.VMEM((count, rows, width), jnp.bfloat16),
-            pltpu.VMEM((count, 4, 4, 2, *weights[0][0].shape[1:]), jnp.bfloat16),
+            pltpu.VMEM((count, 16, 2, 2, *late_rows[0].shape[2:]), jnp.bfloat16),
         ]
 
     def cost(count, size):
@@ -157,24 +155,24 @@
     early = pl.pallas_call(
         early_keys_kernel,
         out_shape=jax.ShapeDtypeStruct((rows, width), jnp.float32),
-        in_specs=[smem] + [anywhere] * 7,
+        in_specs=[smem] + [anywhere] * 5,
         out_specs=vmem,
-        scratch_shapes=blocks(3) + [pltpu.SemaphoreType.DMA((3, 9))],
+        scratch_shapes=blocks(3) + [pltpu.SemaphoreType.DMA((3, 5))],
         compiler_params=pltpu.CompilerParams(vmem_limit_bytes=48 << 20),
         cost_estimate=cost(3, 13),
         name="early_keys",
-    )(place, tokens, *[block for ahead in EARLY for block in weights[ahead]])
+    )(place, tokens, *early_rows)
     return pl.pallas_call(
         attention_kernel,
         out_shape=jax.ShapeDtypeStruct((32, 2 * LANES), jnp.float32),
         in_specs=[smem] + [anywhere] * 3 + [vmem] * 5,
         out_specs=vmem,
         scratch_shapes=blocks(1)
-        + [pltpu.VMEM((8, live.shape[1]), jnp.float32), pltpu.SemaphoreType.DMA((1, 9))],
+        + [pltpu.VMEM((8, live.shape[1]), jnp.float32), pltpu.SemaphoreType.DMA((1, 5))],
         compiler_params=pltpu.CompilerParams(vmem_limit_bytes=48 << 20),
         cost_estimate=cost(1, 6),
         name="attention",
-    )(place, tokens, *weights[LATE], early, dec, gain, live, scores)
+    )(place, tokens, *late_rows, early, dec, gain, live, scores)
 
 
 def scores_kernel(place, packed, proj, emb, chosen, state, slots, rows, unit, scale, ordered, unit_v, ids_v):
@@ -254,7 +252,12 @@
     out[...] = jnp.broadcast_to(packed[None], out.shape)
 
 
-def gradient_kernel(coef, slot, rows, unit, scale, ordered, keep, send, matrix_v):
+def gradient_kernel(coef, slot, *refs):
+    far, (keep, send, matrix_v), near, sems = refs[:4], refs[4:7], refs[7:11], refs[11]
+    copies = [pltpu.make_async_copy(a, b, sems.at[i]) for i, (a, b) in enumerate(zip(far, near))]
+    for copy in copies:
+        copy.start()
+    rows, unit, scale, ordered = near
     n_rows = matrix_v.shape[1]
     blocks = coef.shape[0]
 
@@ -270,6 +273,8 @@
                 total += jnp.where(places[:, k : k + 1] == row, values[:, k : k + 1], 0.0)
             matrix_v[pl.ds(pl.multiple_of(x * blocks + b * 8, 8), 8), :] = total
 
+    for copy in copies:
+        copy.wait()
     along_all = jnp.concatenate([coef[pl.ds(p, 16, stride=8), :] for p in range(8)], axis=0)
     row_high, row_low = halves(rows[...])
     parts_high, parts_low = [], []
@@ -313,25 +318,27 @@
     with jax.named_scope("gather_enc_out"):
         token_blocks = lax.all_gather(enc_out.reshape(token_rows, feats_here), "reader")
 
-    width_here = key_proj.shape[1]
+    half_rows, width_here = key_proj.shape[0] // 2, key_proj.shape[1]
     ids_high = (passage_id // 256).astype(jnp.bfloat16)
     ids_low = (passage_id % 256).astype(jnp.bfloat16)
     gap = ((0, 0), (0, LANES // 2 - topk))
     coded = jnp.concatenate([query_feat, jnp.pad(ids_high, gap), jnp.pad(ids_low, gap)], axis=1)
-    coded = jnp.pad(coded, ((0, 0), (0, width_here - coded.shape[1])))
+    coded = jnp.pad(coded, ((0, 0), (0, width_here - coded.shape[1]))).reshape(half_rows, -1)
+    beside = coded.shape[1]
+    coded = jnp.pad(coded, ((0, 0), (0, LANES - beside)))
     with jax.named_scope("gather_key_proj"):
-        own = send_all(jnp.concatenate([key_proj, coded]), "zq")
-        after, before = shift(own, Z, 1), shift(own, Z, -1)
-        far = [shift(own[:2], Z, 2), shift(own[2:], Z, -2)]
-        classes = (own, after, *far, before)
-        own = jnp.concatenate([block[:, :-1] for block in classes])
-        after, before = shift(own, "y", 1), shift(own, "y", -1)
-        far = jnp.concatenate([shift(after[:8], "y", 1), shift(before[8:], "y", -1)])
-        weights = [(block, shift(block, "core", 1)) for block in (own, after, far, before)]
+        first = send_all(jnp.concatenate([key_proj[:half_rows], coded], axis=1), Z)
+        coded = first[:, :, width_here : width_here + beside].reshape(nz, width_here)
+        early_rows, late_rows = [], []
+        for own in (first[:, :, :width_here], send_all(key_proj[half_rows:], Z)):
+            after, before = shift(own, "y", 1), shift(own, "y", -1)
+            early_rows.append(jnp.stack([own, after, before]))
+            late_rows += [shift(after[:8], "y", 1), shift(before[8:], "y", -1)]
+        late_rows = jnp.concatenate(late_rows).reshape(2, *first.shape[:2], width_here)
+        early_rows += [shift(rows, "core", 1) for rows in early_rows]
+        late_rows = [late_rows, shift(late_rows, "core", 1)]
 
     with jax.named_scope("gather_queries"):
-        coded = jnp.concatenate([block[:, -1] for block in classes])
-        coded = jnp.roll(coded.reshape(4, 4, width_here), zr, axis=0).reshape(nz, width_here)
         packed = send_all(coded[:, : width + LANES], NEAR)
 
     cols = width // nx
@@ -375,7 +382,7 @@
     with jax.named_scope("reduce_scores"):
         state = state.reshape(n_pair, nz, LANES)
         state = merge_all(lax.all_to_all(state, ("y", "core"), 0, 0, tiled=True))
-        state = merge_all(lax.all_to_all(state, Z_BY_CLASS, 0, 0, tiled=True))
+        state = merge_all(lax.all_to_all(state, Z, 0, 0, tiled=True))
         slab_best = state[topk : topk + 1]
         fetched = state[:topk]
     expo = jnp.exp(fetched)
@@ -395,9 +402,10 @@
         positions = lax.broadcasted_iota(jnp.int32, (group, topk, plen), 2)
         live = (positions < passage_len[:, :, None]).reshape(group, topk * plen)
         packet = attention_packet(
-            jnp.stack([y, zr, core]).astype(jnp.int32),
+            jnp.stack([y, core]).astype(jnp.int32),
             token_blocks,
-            weights,
+            early_rows,
+            late_rows,
             dec_unit.reshape(group, answer, feats_here),
             key_gain.astype(jnp.float32).reshape(1, feats_here),
             live.astype(jnp.float32),
@@ -413,16 +421,20 @@
             out_specs=vmem,
             name="coef",
         )(packets)
-        coef = lax.all_to_all(coef, Z_BY_CLASS, 0, 0, tiled=True).reshape(n_index, LANES)
+        coef = lax.all_to_all(coef, Z, 0, 0, tiled=True).reshape(n_index, LANES)
 
     with jax.named_scope("gradient"):
         part = jax.ShapeDtypeStruct((width // ncore, cols), jnp.float32)
         keep, send = pl.pallas_call(
             gradient_kernel,
             out_shape=(part, part),
-            in_specs=[vmem] * 6,
+            in_specs=[vmem] * 2 + [pl.BlockSpec(memory_space=pl.ANY)] * 4,
             out_specs=(vmem, vmem),
-            scratch_shapes=[pltpu.VMEM((queries, shard_rows), jnp.float32)],
+            scratch_shapes=[
+                pltpu.VMEM((queries, shard_rows), jnp.float32),
+                *[pltpu.VMEM(x.shape, x.dtype) for x in (my_rows, my_unit, query_scale, ordered)],
+                pltpu.SemaphoreType.DMA((4,)),
+            ],
             compiler_params=pltpu.CompilerParams(vmem_limit_bytes=40 << 20),
             name="gradient",
         )(coef, slots, my_rows, my_unit, query_scale, ordered)

time: 268 us -> 295 us (1.10)
  waiting for transfers between devices: 58.5 us -> 86.2 us
  blocking collectives: 45.3 us -> 37.9 us
  starting transfers between devices: 79.9 us -> 85.5 us
  other arithmetic: 10.1 us -> 13.8 us
  local copies, waits for them, and re-layouts: 24.2 us -> 21 us
    all_to_all x3 -> x4, waiting for transfers between devices: 24.4 us -> 53.6 us  [send_all(): lax.all_to_all(jnp.broadcast_to(x[None], (size, *x.shape)), axis, 0, 0, t...]
    all_to_all x3 -> x4, starting transfers between devices: 28 us -> 34.7 us  [send_all(): lax.all_to_all(jnp.broadcast_to(x[None], (size, *x.shape)), axis, 0, 0, t...]
    ppermute x13 -> x12, waiting for transfers between devices: 16.5 us -> 10.8 us  [shift(): return lax.ppermute(x, axis, [((i + step) % size, i) for i in range(size)])]
    all_to_all x1, waiting for transfers between devices: 4.72 us -> 8.96 us  [body(): state = merge_all(lax.all_to_all(state, Z, 0, 0, tiled=True))]
    unnamed x39 -> x47, local copies, waits for them, and re-layouts: 12 us -> 7.88 us
    all_to_all x1, blocking collectives: 20.8 us -> 16.8 us  [body(): coef = lax.all_to_all(coef, Z, 0, 0, tiled=True).reshape(n_index, LANES)]
    all_to_all x1, blocking collectives: 13.5 us -> 10 us  [body(): lax.all_to_all(packet, NEAR, 0, 0, tiled=True)]
    ppermute x13 -> x12, starting transfers between devices: 39.5 us -> 36.4 us  [shift(): return lax.ppermute(x, axis, [((i + step) % size, i) for i in range(size)])]
  transfers between devices with their start and end apart: 20 -> 20, of which waited for: 9 -> 7; matrix products, arithmetic and copies ran while one was open for 9% -> 8% of each run, Pallas kernels for 6% -> 6%
where the time goes in v3:
time: 295 us; the launch traced here: 292 us
  waiting for transfers between devices  86.2 us (29%)
  starting transfers between devices  85.5 us (29%)
  blocking collectives  37.9 us (13%)
  Pallas kernels  32.7 us (11%)
  local copies, waits for them, and re-layouts  21 us (7%)
  between operations  15.3 us (5%)
  other arithmetic  13.8 us (5%)
    all_to_all x4, waiting for transfers between devices, send_all(): lax.all_to_all(jnp.broadcast_to(x[None], (size, *x.shape)), axis, 0, 0, t...  53.6 us
    ppermute x12, starting transfers between devices, shift(): return lax.ppermute(x, axis, [((i + step) % size, i) for i in range(size)])  36.4 us
    all_to_all x4, starting transfers between devices, send_all(): lax.all_to_all(jnp.broadcast_to(x[None], (size, *x.shape)), axis, 0, 0, t...  34.7 us
    all_to_all x1, blocking collectives, body(): coef = lax.all_to_all(coef, Z, 0, 0, tiled=True).reshape(n_index, LANES)  16.8 us
    all_to_all x1, waiting for transfers between devices, body(): term = jnp.sum(lax.all_to_all(term, Z, 0, 0, tiled=True), axis=0)  12.1 us
    all_to_all x1, blocking collectives, body(): term = jnp.sum(lax.all_to_all(term, 'y', 0, 0, tiled=True), axis=0)  11 us
    ppermute x12, waiting for transfers between devices, shift(): return lax.ppermute(x, axis, [((i + step) % size, i) for i in range(size)])  10.8 us
    pallas_call x1, Pallas kernels, attention_packet(): pl.pallas_call(early_keys_kernel, out_shape=jax.ShapeDtypeStruct((rows, w...  10.2 us
  transfers between devices with their start and end apart: 20, of which 7 were waited for; matrix products, arithmetic and copies ran while one was open for 8% of the time, Pallas kernels for 6%

profile of v3, /device:TPU:6, one launch (start us, length us, event | category | flops | bytes accessed | tf_op | source)
XLA Modules:
  0.0 292.4 jit_solution(6799386452733646379)
XLA Ops:
  9.6 15.3 %all-to-all-start.1 = ((bf16[16,16,1024]{2,1,0:T(8,128)(2,1)}), bf16[16,16,1024]{2,1,0:T(8,128)(2,1)S(1)}, u32[]{:S(2)}, u32[]{:S(2)}) async-start(bf16[16,16,1024]{2,1,0:T(8,128)(2,1)} %broadcast_in_dim.13), calls=%async_computation.1 | async-start | bytes 1048576 | tf_op jit(solution)/shard_map/gather_key_proj/all_to_all | solution.py:35
  25.1 28.9 %all-to-all-done.1 = bf16[16,16,1024]{2,1,0:T(8,128)(2,1)S(1)} async-done(((bf16[16,16,1024]{2,1,0:T(8,128)(2,1)}), bf16[16,16,1024]{2,1,0:T(8,128)(2,1)S(1)}, u32[]{:S(2)}, u32[]{:S(2)}) %all-to-all-start.1) | async-done | bytes 524320 | tf_op jit(solution)/shard_map/gather_key_proj/all_to_all | solution.py:35
  55.0 6.3 %all-to-all-start = ((bf16[16,16,1152]{2,1,0:T(8,128)(2,1)}), bf16[16,16,1152]{2,1,0:T(8,128)(2,1)S(1)}, u32[]{:S(2)}, u32[]{:S(2)}) async-start(bf16[16,16,1152]{2,1,0:T(8,128)(2,1)} %broadcast_in_dim.12), calls=%async_computation | async-start | bytes 1179648 | tf_op jit(solution)/shard_map/gather_key_proj/all_to_all | solution.py:35
  62.4 3.5 %collective-permute-start.6 = (bf16[16,16,1024]{2,1,0:T(8,128)(2,1)S(1)}, bf16[16,16,1024]{2,1,0:T(8,128)(2,1)S(1)}, u32[]{:S(2)}, u32[]{:S(2)}) collective-permute-start(bf16[16,16,1024]{2,1,0:T(8,128)(2,1)S(1)} %all-to-all-done.1), channel_id=1, source_target_pairs={{384,0},{0,128},{128,256},{256,384},{385,1},{1,129},{129,257},{257... | collective-permute-start | bytes 1572872 | tf_op jit(solution)/shard_map/gather_key_proj/ppermute | solution.py:30
  65.9 3.6 %collective-permute-start.4 = (bf16[16,16,1024]{2,1,0:T(8,128)(2,1)S(1)}, bf16[16,16,1024]{2,1,0:T(8,128)(2,1)}, u32[]{:S(2)}, u32[]{:S(2)}) collective-permute-start(bf16[16,16,1024]{2,1,0:T(8,128)(2,1)S(1)} %all-to-all-done.1), channel_id=1, source_target_pairs={{128,0},{256,128},{384,256},{0,384},{129,1},{257,129},{385,257},{1... | collective-permute-start | bytes 1572872 | tf_op jit(solution)/shard_map/gather_key_proj/ppermute | solution.py:30
  69.5 22.6 %all-to-all-done = bf16[16,16,1152]{2,1,0:T(8,128)(2,1)S(1)} async-done(((bf16[16,16,1152]{2,1,0:T(8,128)(2,1)}), bf16[16,16,1152]{2,1,0:T(8,128)(2,1)S(1)}, u32[]{:S(2)}, u32[]{:S(2)}) %all-to-all-start) | async-done | bytes 589856 | tf_op jit(solution)/shard_map/gather_key_proj/all_to_all | solution.py:35
  92.2 1.0 broadcast_in_dim.14
  93.3 7.7 %all-to-all-start.2 = ((bf16[32,16,896]{2,1,0:T(8,128)(2,1)}), bf16[32,16,896]{2,1,0:T(8,128)(2,1)S(1)}, u32[]{:S(2)}, u32[]{:S(2)}) async-start(bf16[32,16,896]{2,1,0:T(8,128)(2,1)} %broadcast_in_dim.14), calls=%async_computation.2 | async-start | bytes 1835008 | tf_op jit(solution)/shard_map/gather_queries/all_to_all | solution.py:35
  101.1 3.5 %collective-permute-start.2 = (bf16[16,16,1024]{2,1,0:T(8,128)(2,1)S(1)}, bf16[16,16,1024]{2,1,0:T(8,128)(2,1)S(1)}, u32[]{:S(2)}, u32[]{:S(2)}) collective-permute-start(bf16[16,16,1024]{2,1,0:T(8,128)(2,1)S(1)} %get-tuple-element.49), channel_id=1, source_target_pairs={{384,0},{0,128},{128,256},{256,384},{385,1},{1,129},{129,257},{257... | collective-permute-start | bytes 1572872 | tf_op jit(solution)/shard_map/gather_key_proj/ppermute | solution.py:30
  104.6 3.7 %collective-permute-start = (bf16[16,16,1024]{2,1,0:T(8,128)(2,1)S(1)}, bf16[16,16,1024]{2,1,0:T(8,128)(2,1)S(1)}, u32[]{:S(2)}, u32[]{:S(2)}) collective-permute-start(bf16[16,16,1024]{2,1,0:T(8,128)(2,1)S(1)} %get-tuple-element.49), channel_id=1, source_target_pairs={{128,0},{256,128},{384,256},{0,384},{129,1},{257,129},{385,257},{1... | collective-permute-start | bytes 1572872 | tf_op jit(solution)/shard_map/gather_key_proj/ppermute | solution.py:30
  109.7 1.3 fusion.chosen
  111.8 2.2 collective-permute-start.7
  114.0 1.4 pad_maximum_fusion.1.refs_1_
  115.4 1.9 collective-permute-start.10
  117.3 9.0 %collective-permute-done.2 = bf16[16,16,1024]{2,1,0:T(8,128)(2,1)S(1)} collective-permute-done((bf16[16,16,1024]{2,1,0:T(8,128)(2,1)S(1)}, bf16[16,16,1024]{2,1,0:T(8,128)(2,1)S(1)}, u32[]{:S(2)}, u32[]{:S(2)}) %collective-permute-start.2) | collective-permute-done | bytes 524320 | tf_op jit(solution)/shard_map/gather_key_proj/ppermute | solution.py:30
  126.3 1.5 pad_maximum_fusion.refs_0_
  127.8 1.9 collective-permute-start.9
  129.8 1.3 copy-done.1
  131.0 1.3 copy-done.10
  132.3 6.6 %scores.1 = (f32[128,128]{1,0:T(8,128)}, s32[128,128]{1,0:T(8,128)S(1)}, f32[512,192]{1,0:T(8,128)S(1)}, f32[512,192]{1,0:T(8,128)S(1)}, f32[512,1]{1,0:T(8,128)S(1)}, /*index=5*/bf16[768,512]{1,0:T(8,128)(2,1)S(1)}) custom-call(s32[2]{0:T(128)S(1)} %pad_add_fusion.1.place, bf16[32,16,896]{2,1,0:T(8,128)(2,1)S(1)} %all-to-all-done.2.packed, ...), custom_call_target="tpu_custom_call" | custom-call | flops 4294967296 | bytes 8388608 | tf_op jit(solution)/shard_map/scores/scores/pallas_call | solution.py:355
  141.8 3.3 %all-to-all-start.3 = ((f32[8,16,128]{2,1,0:T(8,128)}), f32[8,16,128]{2,1,0:T(8,128)S(1)}, u32[]{:S(2)}, u32[]{:S(2)}) async-start(f32[8,16,128]{2,1,0:T(8,128)} %bitcast.13), calls=%async_computation.3 | async-start | bytes 131072 | tf_op jit(solution)/shard_map/reduce_scores/all_to_all | solution.py:384
  146.2 5.1 %collective-permute-start.5 = (bf16[8,16,1024]{2,1,0:T(8,128)(2,1)S(1)}, bf16[8,16,1024]{2,1,0:T(8,128)(2,1)}, u32[]{:S(2)}, u32[]{:S(2)}) collective-permute-start(bf16[8,16,1024]{2,1,0:T(8,128)(2,1)S(1)} %slice.84), channel_id=1, source_target_pairs={{128,0},{256,128},{384,256},{0,384},{129,1},{257,129},{385,257},{1... | collective-permute-start | bytes 786440 | tf_op jit(solution)/shard_map/gather_key_proj/ppermute | solution.py:30
  151.3 1.0 slice.83
  152.3 1.9 collective-permute-start.3
  154.2 1.0 slice.82
  155.2 5.1 %collective-permute-start.1 = (bf16[8,16,1024]{2,1,0:T(8,128)(2,1)S(1)}, bf16[8,16,1024]{2,1,0:T(8,128)(2,1)}, u32[]{:S(2)}, u32[]{:S(2)}) collective-permute-start(bf16[8,16,1024]{2,1,0:T(8,128)(2,1)S(1)} %slice.82), channel_id=1, source_target_pairs={{128,0},{256,128},{384,256},{0,384},{129,1},{257,129},{385,257},{1... | collective-permute-start | bytes 786440 | tf_op jit(solution)/shard_map/gather_key_proj/ppermute | solution.py:30
  161.0 7.5 %all-to-all-start.4 = ((f32[16,1,128]{2,1,0:T(1,128)}), f32[16,1,128]{2,1,0:T(1,128)}, u32[]{:S(2)}, u32[]{:S(2)}) async-start(f32[16,1,128]{2,1,0:T(1,128)} %broadcast_select_fusion), calls=%async_computation.4 | async-start | bytes 16384 | tf_op jit(solution)/shard_map/reduce_scores/all_to_all | solution.py:385
  168.6 1.3 pad_maximum_fusion.2
  169.9 2.1 collective-permute-start.8
  172.0 9.0 %all-to-all-done.4 = f32[16,1,128]{2,1,0:T(1,128)} async-done(((f32[16,1,128]{2,1,0:T(1,128)}), f32[16,1,128]{2,1,0:T(1,128)}, u32[]{:S(2)}, u32[]{:S(2)}) %all-to-all-start.4) | async-done | bytes 8224 | tf_op jit(solution)/shard_map/reduce_scores/all_to_all | solution.py:385
  182.3 1.2 fusion.27
  183.5 1.9 broadcast_select_fusion.1
  185.4 1.5 scatter.9.refs_6_
  187.0 10.2 %early_keys.1.refs_2_ = f32[640,1024]{1,0:T(8,128)} custom-call(s32[2]{0:T(128)S(1)} %pad_add_fusion.place, bf16[4,640,1024]{2,1,0:T(8,128)(2,1)} %all-gather.2.cloned.1.call-done.tokens, bf16[3,16,16,1024]{3,2,1,0:T(8,128)(2,1)} %pad_maximum_fusion.refs_0_, bf16[3,16,16,1024]{3,2,1,0:T(8,128)(2,1)S(1)} %pad_maximum_fusion.1.refs_1_, ...), custom_call_target="tpu_custom_call" | custom-call | flops 4026531840 | bytes 13631488 | tf_op jit(solution)/shard_map/attention/early_keys/pallas_call | solution.py:155
  197.2 1.7 copy-done
  198.9 7.7 %attention.1 = f32[32,256]{1,0:T(8,128)S(1)} custom-call(s32[2]{0:T(128)S(1)} %pad_add_fusion.place, bf16[4,640,1024]{2,1,0:T(8,128)(2,1)} %all-gather.2.cloned.1.call-done.tokens, bf16[2,16,16,1024]{3,2,1,0:T(8,128)(2,1)S(1)} %bitcast.36, bf16[2,16,16,1024]{3,2,1,0:T(8,128)(2,1)} %collective-permute-done.8.refs_1_, f32[640,1024]{1,0:T(8,128)S(1)} %copy-done, ...), custom_call_target="tpu_custom_call" | custom-call | flops 1342177280 | bytes 6291456 | tf_op jit(solution)/shard_map/attention/attention/pallas_call | solution.py:165
  206.7 10.0 %all_to_all.55 = f32[32,1,256]{2,1,0:T(1,128)S(1)} all-to-all(f32[32,1,256]{2,1,0:T(1,128)S(1)} %copy.20), channel_id=1, replica_groups=mesh['y'=4,'zq'=4,'zr'=4,'core'=2,'reader'=4] {'reader','y','core'}, dimensions={0} | all-to-all | bytes 65536 | tf_op jit(solution)/shard_map/targets/all_to_all | solution.py:416
  217.3 1.6 coef.1
  218.9 16.8 %all_to_all.56 = f32[16,8,128]{2,1,0:T(8,128)S(1)} all-to-all(f32[16,8,128]{2,1,0:T(8,128)} %coef.1), channel_id=1, replica_groups=mesh['y'=4,'zq'=4,'zr'=4,'core'=2,'reader'=4] {'zq','zr'}, dimensions={0} | all-to-all | bytes 131072 | tf_op jit(solution)/shard_map/targets/all_to_all | solution.py:424
  235.7 6.6 %gradient.1 = (f32[384,192]{1,0:T(8,128)S(1)}, f32[384,192]{1,0:T(8,128)S(1)}) custom-call(f32[128,128]{1,0:T(8,128)S(1)} %bitcast.37, s32[128,128]{1,0:T(8,128)S(1)} %copy-done.9, f32[512,192]{1,0:T(8,128)S(1)} %copy-done.3, f32[512,192]{1,0:T(8,128)S(1)} %copy-done.5, f32[512,1]{1,0:T(8,128)S(1)} %copy-done.7, bf16[768,512]{1,0:T(8,128)(2,1)S(1)} %get-tuple-element.41.refs_3_), custom_call_target="tpu_custom_call" | custom-call | tf_op jit(solution)/shard_map/gradient/gradient/pallas_call | solution.py:428
  242.4 1.9 collective-permute-start.11
  244.3 1.7 collective-permute-done.11
  246.1 11.0 %all_to_all.57 = f32[4,96,192]{2,1,0:T(8,128)S(1)} all-to-all(f32[4,96,192]{2,1,0:T(8,128)S(1)} %bitcast.41), channel_id=1, replica_groups=mesh['y'=4,'zq'=4,'zr'=4,'core'=2,'reader'=4] {'y'}, dimensions={0} | all-to-all | bytes 589824 | tf_op jit(solution)/shard_map/reduce_gradient/all_to_all | solution.py:444
  257.8 3.5 %all-to-all-start.8 = ((f32[16,6,192]{2,1,0:T(8,128)}), f32[16,6,192]{2,1,0:T(8,128)S(1)}, u32[]{:S(2)}, u32[]{:S(2)}) async-start(f32[16,6,192]{2,1,0:T(8,128)} %reshape.302), calls=%async_computation.8 | async-start | bytes 262144 | tf_op jit(solution)/shard_map/reduce_gradient/all_to_all | solution.py:446
  263.4 12.1 %all-to-all-done.8 = f32[16,6,192]{2,1,0:T(8,128)S(1)} async-done(((f32[16,6,192]{2,1,0:T(8,128)}), f32[16,6,192]{2,1,0:T(8,128)S(1)}, u32[]{:S(2)}, u32[]{:S(2)}) %all-to-all-start.8) | async-done | bytes 73760 | tf_op jit(solution)/shard_map/reduce_gradient/all_to_all | solution.py:446
  276.1 5.3 %all-to-all-start.9 = ((f32[4,6,192]{2,1,0:T(8,128)}), f32[4,6,192]{2,1,0:T(8,128)S(1)}, u32[]{:S(2)}, u32[]{:S(2)}) async-start(f32[4,6,192]{2,1,0:T(8,128)} %broadcast_in_dim.15), calls=%async_computation.9 | async-start | bytes 65536 | tf_op jit(solution)/shard_map/reduce_gradient/all_to_all | solution.py:35
  281.4 1.2 log_bitcast_fusion
  282.6 2.2 all-to-all-done.9
  (109 shorter events, 17.1 us)
Async XLA Ops:
  7.2 17.7 %copy-start.22 = (s32[1,20]{1,0:T(1,128)S(1)}, s32[1,20]{1,0:T(1,128)}, u32[]{:S(2)}) copy-start(s32[1,20]{1,0:T(1,128)} %param.16) | copy-start | bytes 244
  7.2 17.7 %copy-start.19 = (bf16[1,768]{1,0:T(2,128)(2,1)S(1)}, bf16[1,768]{1,0:T(2,128)(2,1)}, u32[]{:S(2)}) copy-start(bf16[1,768]{1,0:T(2,128)(2,1)} %param.14) | copy-start | bytes 4612
  7.2 179.8 %all-gather.2.cloned.1.call-start = ((), (), s32[]{:S(2)}) async-start(), calls=%async_computation.10 | async-start | bytes 6553600 | tf_op jit(solution)/shard_map/gather_enc_out/all_gather | solution.py:319
  9.6 51.7 %copy-start.16 = (bf16[4,16,1024]{2,1,0:T(8,128)(2,1)S(1)}, bf16[4,16,1024]{2,1,0:T(8,128)(2,1)}, u32[]{:S(2)}) copy-start(bf16[4,16,1024]{2,1,0:T(8,128)(2,1)} %param.21) | copy-start | bytes 393220
  9.6 44.4 %all-to-all-start.1 = ((bf16[16,16,1024]{2,1,0:T(8,128)(2,1)}), bf16[16,16,1024]{2,1,0:T(8,128)(2,1)S(1)}, u32[]{:S(2)}, u32[]{:S(2)}) async-start(bf16[16,16,1024]{2,1,0:T(8,128)(2,1)} %broadcast_in_dim.13), calls=%async_computation.1 | async-start | bytes 1048576 | tf_op jit(solution)/shard_map/gather_key_proj/all_to_all | solution.py:35
  54.0 11.9 %copy-start.11 = (bf16[16,16,1024]{2,1,0:T(8,128)(2,1)}, bf16[16,16,1024]{2,1,0:T(8,128)(2,1)S(1)}, u32[]{:S(2)}) copy-start(bf16[16,16,1024]{2,1,0:T(8,128)(2,1)S(1)} %all-to-all-done.1) | copy-start | bytes 1572868
  55.0 37.1 %all-to-all-start = ((bf16[16,16,1152]{2,1,0:T(8,128)(2,1)}), bf16[16,16,1152]{2,1,0:T(8,128)(2,1)S(1)}, u32[]{:S(2)}, u32[]{:S(2)}) async-start(bf16[16,16,1152]{2,1,0:T(8,128)(2,1)} %broadcast_in_dim.12), calls=%async_computation | async-start | bytes 1179648 | tf_op jit(solution)/shard_map/gather_key_proj/all_to_all | solution.py:35
  61.3 0.8 copy-start.20
  62.4 48.6 %collective-permute-start.6 = (bf16[16,16,1024]{2,1,0:T(8,128)(2,1)S(1)}, bf16[16,16,1024]{2,1,0:T(8,128)(2,1)S(1)}, u32[]{:S(2)}, u32[]{:S(2)}) collective-permute-start(bf16[16,16,1024]{2,1,0:T(8,128)(2,1)S(1)} %all-to-all-done.1), channel_id=1, source_target_pairs={{384,0},{0,128},{128,256},{256,384},{385,1},{1,129},{129,257},{257... | collective-permute-start | bytes 1572872 | tf_op jit(solution)/shard_map/gather_key_proj/ppermute | solution.py:30
  65.9 48.0 %collective-permute-start.4 = (bf16[16,16,1024]{2,1,0:T(8,128)(2,1)S(1)}, bf16[16,16,1024]{2,1,0:T(8,128)(2,1)}, u32[]{:S(2)}, u32[]{:S(2)}) collective-permute-start(bf16[16,16,1024]{2,1,0:T(8,128)(2,1)S(1)} %all-to-all-done.1), channel_id=1, source_target_pairs={{128,0},{256,128},{384,256},{0,384},{129,1},{257,129},{385,257},{1... | collective-permute-start | bytes 1572872 | tf_op jit(solution)/shard_map/gather_key_proj/ppermute | solution.py:30
  93.3 15.1 %copy-start.21 = (bf16[1024]{0:T(1024)(128)(2,1)S(1)}, bf16[1024]{0:T(1024)(128)(2,1)}, u32[]{:S(2)}) copy-start(bf16[1024]{0:T(1024)(128)(2,1)} %param.20) | copy-start | bytes 6148
  93.3 36.5 %all-to-all-start.2 = ((bf16[32,16,896]{2,1,0:T(8,128)(2,1)}), bf16[32,16,896]{2,1,0:T(8,128)(2,1)S(1)}, u32[]{:S(2)}, u32[]{:S(2)}) async-start(bf16[32,16,896]{2,1,0:T(8,128)(2,1)} %broadcast_in_dim.14), calls=%async_computation.2 | async-start | bytes 1835008 | tf_op jit(solution)/shard_map/gather_queries/all_to_all | solution.py:35
  101.0 13.0 %copy-start.12 = (bf16[16,16,1024]{2,1,0:T(8,128)(2,1)S(1)}, bf16[16,16,1024]{2,1,0:T(8,128)(2,1)}, u32[]{:S(2)}) copy-start(bf16[16,16,1024]{2,1,0:T(8,128)(2,1)} %copy-done.11) | copy-start | bytes 1572868
  101.1 25.2 %collective-permute-start.2 = (bf16[16,16,1024]{2,1,0:T(8,128)(2,1)S(1)}, bf16[16,16,1024]{2,1,0:T(8,128)(2,1)S(1)}, u32[]{:S(2)}, u32[]{:S(2)}) collective-permute-start(bf16[16,16,1024]{2,1,0:T(8,128)(2,1)S(1)} %get-tuple-element.49), channel_id=1, source_target_pairs={{384,0},{0,128},{128,256},{256,384},{385,1},{1,129},{129,257},{257... | collective-permute-start | bytes 1572872 | tf_op jit(solution)/shard_map/gather_key_proj/ppermute | solution.py:30
  104.6 21.7 %collective-permute-start = (bf16[16,16,1024]{2,1,0:T(8,128)(2,1)S(1)}, bf16[16,16,1024]{2,1,0:T(8,128)(2,1)S(1)}, u32[]{:S(2)}, u32[]{:S(2)}) collective-permute-start(bf16[16,16,1024]{2,1,0:T(8,128)(2,1)S(1)} %get-tuple-element.49), channel_id=1, source_target_pairs={{128,0},{256,128},{384,256},{0,384},{129,1},{257,129},{385,257},{1... | collective-permute-start | bytes 1572872 | tf_op jit(solution)/shard_map/gather_key_proj/ppermute | solution.py:30
  111.0 3.0 %copy-start.15 = (bf16[16,16,1024]{2,1,0:T(8,128)(2,1)}, bf16[16,16,1024]{2,1,0:T(8,128)(2,1)S(1)}, u32[]{:S(2)}) copy-start(bf16[16,16,1024]{2,1,0:T(8,128)(2,1)S(1)} %collective-permute-done.6) | copy-start | bytes 1572868
  111.8 43.4 %collective-permute-start.7 = (bf16[8,16,1024]{2,1,0:T(8,128)(2,1)}, bf16[8,16,1024]{2,1,0:T(8,128)(2,1)}, u32[]{:S(2)}, u32[]{:S(2)}) collective-permute-start(bf16[8,16,1024]{2,1,0:T(8,128)(2,1)} %slice.85), channel_id=1, source_target_pairs={{384,0},{0,128},{128,256},{256,384},{385,1},{1,129},{129,257},{257... | collective-permute-start | bytes 786440 | tf_op jit(solution)/shard_map/gather_key_proj/ppermute | solution.py:30
  115.4 71.6 %collective-permute-start.10 = (bf16[3,16,16,1024]{3,2,1,0:T(8,128)(2,1)S(1)}, bf16[3,16,16,1024]{3,2,1,0:T(8,128)(2,1)}, u32[]{:S(2)}, u32[]{:S(2)}) collective-permute-start(bf16[3,16,16,1024]{3,2,1,0:T(8,128)(2,1)S(1)} %pad_maximum_fusion.1.refs_1_), channel_id=1, source_target_pairs={{4,0},{0,4},{5,1},{1,5},{6,2},{2,6},{7,3},{3,7},{12,8},{8,12},{13,... | collective-permute-start | bytes 4718600 | tf_op jit(solution)/shard_map/gather_key_proj/ppermute | solution.py:30
  126.3 1.5 copy-start.14
  126.3 1.5 copy-start.13
  127.8 59.1 %collective-permute-start.9 = (bf16[3,16,16,1024]{3,2,1,0:T(8,128)(2,1)}, bf16[3,16,16,1024]{3,2,1,0:T(8,128)(2,1)}, u32[]{:S(2)}, u32[]{:S(2)}) collective-permute-start(bf16[3,16,16,1024]{3,2,1,0:T(8,128)(2,1)} %pad_maximum_fusion.refs_0_), channel_id=1, source_target_pairs={{4,0},{0,4},{5,1},{1,5},{6,2},{2,6},{7,3},{3,7},{12,8},{8,12},{13,... | collective-permute-start | bytes 4718600 | tf_op jit(solution)/shard_map/gather_key_proj/ppermute | solution.py:30
  129.8 1.3 copy-start.1
  131.0 1.3 copy-start.10
  138.9 0.8 copy-start.2
  139.7 0.8 copy-start.4
  140.5 0.7 copy-start.6
  141.2 0.6 copy-start.8
  141.8 18.5 %all-to-all-start.3 = ((f32[8,16,128]{2,1,0:T(8,128)}), f32[8,16,128]{2,1,0:T(8,128)S(1)}, u32[]{:S(2)}, u32[]{:S(2)}) async-start(f32[8,16,128]{2,1,0:T(8,128)} %bitcast.13), calls=%async_computation.3 | async-start | bytes 131072 | tf_op jit(solution)/shard_map/reduce_scores/all_to_all | solution.py:384
  146.2 22.3 %collective-permute-start.5 = (bf16[8,16,1024]{2,1,0:T(8,128)(2,1)S(1)}, bf16[8,16,1024]{2,1,0:T(8,128)(2,1)}, u32[]{:S(2)}, u32[]{:S(2)}) collective-permute-start(bf16[8,16,1024]{2,1,0:T(8,128)(2,1)S(1)} %slice.84), channel_id=1, source_target_pairs={{128,0},{256,128},{384,256},{0,384},{129,1},{257,129},{385,257},{1... | collective-permute-start | bytes 786440 | tf_op jit(solution)/shard_map/gather_key_proj/ppermute | solution.py:30
  152.3 16.2 %collective-permute-start.3 = (bf16[8,16,1024]{2,1,0:T(8,128)(2,1)S(1)}, bf16[8,16,1024]{2,1,0:T(8,128)(2,1)}, u32[]{:S(2)}, u32[]{:S(2)}) collective-permute-start(bf16[8,16,1024]{2,1,0:T(8,128)(2,1)S(1)} %slice.83), channel_id=1, source_target_pairs={{384,0},{0,128},{128,256},{256,384},{385,1},{1,129},{129,257},{257... | collective-permute-start | bytes 786440 | tf_op jit(solution)/shard_map/gather_key_proj/ppermute | solution.py:30
  155.2 13.3 %collective-permute-start.1 = (bf16[8,16,1024]{2,1,0:T(8,128)(2,1)S(1)}, bf16[8,16,1024]{2,1,0:T(8,128)(2,1)}, u32[]{:S(2)}, u32[]{:S(2)}) collective-permute-start(bf16[8,16,1024]{2,1,0:T(8,128)(2,1)S(1)} %slice.82), channel_id=1, source_target_pairs={{128,0},{256,128},{384,256},{0,384},{129,1},{257,129},{385,257},{1... | collective-permute-start | bytes 786440 | tf_op jit(solution)/shard_map/gather_key_proj/ppermute | solution.py:30
  161.0 20.0 %all-to-all-start.4 = ((f32[16,1,128]{2,1,0:T(1,128)}), f32[16,1,128]{2,1,0:T(1,128)}, u32[]{:S(2)}, u32[]{:S(2)}) async-start(f32[16,1,128]{2,1,0:T(1,128)} %broadcast_select_fusion), calls=%async_computation.4 | async-start | bytes 16384 | tf_op jit(solution)/shard_map/reduce_scores/all_to_all | solution.py:385
  169.9 27.3 %collective-permute-start.8 = (bf16[2,16,16,1024]{3,2,1,0:T(8,128)(2,1)S(1)}, bf16[2,16,16,1024]{3,2,1,0:T(8,128)(2,1)}, u32[]{:S(2)}, u32[]{:S(2)}) collective-permute-start(bf16[2,16,16,1024]{3,2,1,0:T(8,128)(2,1)S(1)} %bitcast.35), channel_id=1, source_target_pairs={{4,0},{0,4},{5,1},{1,5},{6,2},{2,6},{7,3},{3,7},{12,8},{8,12},{13,... | collective-permute-start | bytes 3145736 | tf_op jit(solution)/shard_map/gather_key_proj/ppermute | solution.py:30
  181.7 1.8 copy-start.17
  197.2 1.7 copy-start
  198.9 36.8 %copy-start.3 = (f32[512,192]{1,0:T(8,128)S(1)}, f32[512,192]{1,0:T(8,128)}, u32[]{:S(2)}) copy-start(f32[512,192]{1,0:T(8,128)} %copy-done.2) | copy-start | bytes 1179652
  198.9 36.8 %copy-start.5 = (f32[512,192]{1,0:T(8,128)S(1)}, f32[512,192]{1,0:T(8,128)}, u32[]{:S(2)}) copy-start(f32[512,192]{1,0:T(8,128)} %copy-done.4) | copy-start | bytes 1179652
  198.9 36.8 %copy-start.7 = (f32[512,1]{1,0:T(8,128)S(1)}, f32[512,1]{1,0:T(8,128)}, u32[]{:S(2)}) copy-start(f32[512,1]{1,0:T(8,128)} %copy-done.6) | copy-start | bytes 6148
  198.9 36.8 %copy-start.9 = (s32[128,128]{1,0:T(8,128)S(1)}, s32[128,128]{1,0:T(8,128)}, u32[]{:S(2)}) copy-start(s32[128,128]{1,0:T(8,128)} %copy-done.8) | copy-start | bytes 196612
  242.4 18.9 %copy-start.18 = (f32[128]{0:T(128)S(1)}, f32[128]{0:T(128)}, u32[]{:S(2)}) copy-start(f32[128]{0:T(128)} %copy-done.17) | copy-start | bytes 1540
  242.4 3.6 %collective-permute-start.11 = (f32[384,192]{1,0:T(8,128)S(1)}, f32[384,192]{1,0:T(8,128)S(1)}, u32[]{:S(2)}, u32[]{:S(2)}) collective-permute-start(f32[384,192]{1,0:T(8,128)S(1)} %get-tuple-element.43), channel_id=1, source_target_pairs={{4,0},{0,4},{5,1},{1,5},{6,2},{2,6},{7,3},{3,7},{12,8},{8,12},{13,... | collective-permute-start | bytes 884744 | tf_op jit(solution)/shard_map/reduce_gradient/ppermute | solution.py:30
  257.8 17.7 %all-to-all-start.8 = ((f32[16,6,192]{2,1,0:T(8,128)}), f32[16,6,192]{2,1,0:T(8,128)S(1)}, u32[]{:S(2)}, u32[]{:S(2)}) async-start(f32[16,6,192]{2,1,0:T(8,128)} %reshape.302), calls=%async_computation.8 | async-start | bytes 262144 | tf_op jit(solution)/shard_map/reduce_gradient/all_to_all | solution.py:446
  276.1 8.7 %all-to-all-start.9 = ((f32[4,6,192]{2,1,0:T(8,128)}), f32[4,6,192]{2,1,0:T(8,128)S(1)}, u32[]{:S(2)}, u32[]{:S(2)}) async-start(f32[4,6,192]{2,1,0:T(8,128)} %broadcast_in_dim.15), calls=%async_computation.9 | async-start | bytes 65536 | tf_op jit(solution)/shard_map/reduce_gradient/all_to_all | solution.py:35
Sparse Core Ops, SparseCore 0:
  10.1 67.4 all-gather.1

commit v4 on v3

--- a/solution.py
+++ b/solution.py
@@ -44,29 +44,44 @@
     return jnp.dot(a, b, preferred_element_type=jnp.float32)
 
 
-def start_blocks(place, ahead, slot, tokens, weights, token_v, weight_v, sems):
-    y, core = place[0], place[1]
-    copies = [pltpu.make_async_copy(tokens.at[(y + ahead) % 4], token_v.at[slot], sems.at[slot, 4])]
-    for which in range(2):
-        for half in range(2):
-            copies.append(
-                pltpu.make_async_copy(
-                    weights[which][half],
-                    weight_v.at[slot, :, (core + which) % 2, half],
-                    sems.at[slot, 2 * which + half],
-                )
-            )
+def token_copies(r, chunk, tokens, target, sems):
+    own, after, far_low, far_high, before = tokens
+    half = target.shape[0] // 2
+    low, high = target.at[pl.ds(0, half)], target.at[pl.ds(half, half)]
+    for j, block in enumerate((own, after, None, before)):
+
+        @pl.when((r + j) % 4 == chunk)
+        def _():
+            first = far_low if block is None else block.at[pl.ds(0, half)]
+            second = far_high if block is None else block.at[pl.ds(half, half)]
+            pltpu.make_async_copy(first, low, sems.at[0]).start()
+            pltpu.make_async_copy(second, high, sems.at[1]).start()
+
+    return [
+        pltpu.make_async_copy(low, low, sems.at[0]),
+        pltpu.make_async_copy(high, high, sems.at[1]),
+    ]
+
+
+def row_copies(core, own, other, target, sems):
+    copies = [
+        pltpu.make_async_copy(own, target.at[:, core], sems.at[0]),
+        pltpu.make_async_copy(other, target.at[:, 1 - core], sems.at[1]),
+    ]
     for copy in copies:
         copy.start()
     return copies
 
 
-def early_keys_kernel(place, tokens, *refs):
-    weights, (keys, token_v, weight_v, sems) = refs[:4], refs[4:]
+def early_keys_kernel(place, *refs):
+    tokens, (own, other), (keys, token_v, weight_v, sems) = refs[:5], refs[5:7], refs[7:]
+    y, core, r = place[0], place[1], place[2]
     copies = []
     for slot, ahead in enumerate(EARLY):
-        blocks = [[weights[2 * which + half].at[slot] for half in range(2)] for which in range(2)]
-        copies.append(start_blocks(place, ahead, slot, tokens, blocks, token_v, weight_v, sems))
+        waits = row_copies(core, own.at[slot], other.at[slot], weight_v.at[slot], sems.at[slot])
+        target = token_v.at[slot]
+        waits += token_copies(r, (y + ahead) % 4, tokens, target, sems.at[3 + slot])
+        copies.append(waits)
     for slot in range(len(EARLY)):
         for copy in copies[slot]:
             copy.wait()
@@ -74,57 +89,83 @@
         @pl.loop(0, keys.shape[1] // TILE)
         def _(t):
             cols = pl.ds(pl.multiple_of(t * TILE, TILE), TILE)
-            term = dot32(token_v[slot], weight_v[slot, :, :, :, :, cols].reshape(-1, TILE))
+            term = dot32(token_v[slot], weight_v[slot, :, :, :, cols].reshape(-1, TILE))
             if slot == 0:
                 keys[:, cols] = term
             else:
                 keys[:, cols] += term
 
 
-def attention_kernel(place, tokens, *refs):
-    weights, refs = refs[:2], refs[2:]
-    early, dec, gain, live, scores, out, token_v, weight_v, column_v, sems = refs
-    blocks = [[weights[which].at[half] for half in range(2)] for which in range(2)]
-    copies = start_blocks(place, LATE, 0, tokens, blocks, token_v, weight_v, sems)
-    group = dec.shape[0]
-    n = live.shape[1]
-    column_v[...] = jnp.zeros_like(column_v)
+def attend(keys, offset, dec, gain, live, column_v):
+    group, n = dec.shape[0], live.shape[1]
+    cols = pl.ds(pl.multiple_of(offset, TILE), TILE)
+    same = (
+        lax.broadcasted_iota(jnp.int32, (TILE, TILE), 0) // DH
+        == lax.broadcasted_iota(jnp.int32, (TILE, TILE), 1) // DH
+    ).astype(jnp.bfloat16)
+    mine = (
+        lax.broadcasted_iota(jnp.int32, (TILE // DH * ANS, TILE), 0) // ANS
+        == lax.broadcasted_iota(jnp.int32, (TILE // DH * ANS, TILE), 1) // DH
+    )
+    high, low = halves(keys * keys)
+    square = (dot32(high, same) + dot32(low, same)) / DH
+    unit = (keys * lax.rsqrt(square + EPSILON) * gain[:, cols]).astype(jnp.bfloat16)
+    for g in range(group):
+        answer = dec[g, :, cols].astype(jnp.float32)
+        answer = jnp.concatenate([answer] * (TILE // DH), axis=0)
+        answer = jnp.where(mine, answer, 0.0).astype(jnp.bfloat16)
+        similarity = lax.dot_general(
+            answer,
+            unit[g * n : (g + 1) * n],
+            (((1,), (1,)), ((), ())),
+            preferred_element_type=jnp.float32,
+        ) / math.sqrt(DH)
+        weight = jnp.where(live[g : g + 1, :] > 0, jnp.exp(similarity), 0.0)
+        weight = weight / jnp.sum(weight, axis=1, keepdims=True)
+        column_v[g : g + 1, :] += jnp.sum(weight, axis=0, keepdims=True)
+
+
+def whole_heads_kernel(place, *refs):
+    tokens, refs = refs[:5], refs[5:]
+    rows, dec, gain, live, columns, token_v, weight_v, sems = refs
+    r = place[2]
+    copies = []
+    for c in range(4):
+        copy = pltpu.make_async_copy(rows.at[c], weight_v.at[c], sems.at[c, 2])
+        copy.start()
+        copies += [copy] + token_copies(r, c, tokens, token_v.at[c], sems.at[c])
+    columns[...] = jnp.zeros_like(columns)
+    for copy in copies:
+        copy.wait()
+
+    @pl.loop(0, weight_v.shape[2] // TILE)
+    def _(t):
+        cols = pl.ds(pl.multiple_of(t * TILE, TILE), TILE)
+        keys = dot32(token_v[0], weight_v[0, :, cols])
+        for c in range(1, 4):
+            keys += dot32(token_v[c], weight_v[c, :, cols])
+        attend(keys, weight_v.shape[2] + t * TILE, dec, gain, live, columns)
+
+
+def late_heads_kernel(place, *refs):
+    tokens, (own, other), refs = refs[:5], refs[5:7], refs[7:]
+    early, columns, dec, gain, live, scores, out, token_v, weight_v, column_v, sems = refs
+    y, core, r = place[0], place[1], place[2]
+    copies = row_copies(core, own, other, weight_v, sems.at[0])
+    copies += token_copies(r, (y + LATE) % 4, tokens, token_v, sems.at[1])
+    column_v[...] = columns[...]
     for copy in copies:
         copy.wait()
 
     @pl.loop(0, early.shape[1] // TILE)
     def _(t):
         cols = pl.ds(pl.multiple_of(t * TILE, TILE), TILE)
-        same = (
-            lax.broadcasted_iota(jnp.int32, (TILE, TILE), 0) // DH
-            == lax.broadcasted_iota(jnp.int32, (TILE, TILE), 1) // DH
-        ).astype(jnp.bfloat16)
-        mine = (
-            lax.broadcasted_iota(jnp.int32, (TILE // DH * ANS, TILE), 0) // ANS
-            == lax.broadcasted_iota(jnp.int32, (TILE // DH * ANS, TILE), 1) // DH
-        )
-        keys = early[:, cols] + dot32(
-            token_v[0], weight_v[0, :, :, :, :, cols].reshape(-1, TILE)
-        )
-        high, low = halves(keys * keys)
-        square = (dot32(high, same) + dot32(low, same)) / DH
-        unit = (keys * lax.rsqrt(square + EPSILON) * gain[:, cols]).astype(jnp.bfloat16)
-        for g in range(group):
-            answer = dec[g, :, cols].astype(jnp.float32)
-            answer = jnp.concatenate([answer] * (TILE // DH), axis=0)
-            answer = jnp.where(mine, answer, 0.0).astype(jnp.bfloat16)
-            similarity = lax.dot_general(
-                answer,
-                unit[g * n : (g + 1) * n],
-                (((1,), (1,)), ((), ())),
-                preferred_element_type=jnp.float32,
-            ) / math.sqrt(DH)
-            weight = jnp.where(live[g : g + 1, :] > 0, jnp.exp(similarity), 0.0)
-            weight = weight / jnp.sum(weight, axis=1, keepdims=True)
-            column_v[g : g + 1, :] += jnp.sum(weight, axis=0, keepdims=True)
-
+        keys = early[:, cols] + dot32(token_v[...], weight_v[:, :, :, cols].reshape(-1, TILE))
+        attend(keys, t * TILE, dec, gain, live, column_v)
+
+    n = live.shape[1]
     mass = jnp.zeros((8, LANES), jnp.float32)
-    for g in range(group):
+    for g in range(dec.shape[0]):
         column = jnp.broadcast_to(column_v[g : g + 1, :], (8, n))
         to = (
             lax.broadcasted_iota(jnp.int32, (n, LANES), 0) // 8 + g * SLOT
@@ -135,44 +176,63 @@
     out[:, LANES:] = jnp.broadcast_to(scores[...], (out.shape[0], LANES))
 
 
-def attention_packet(place, tokens, early_rows, late_rows, dec, gain, live, scores):
+def attention_packet(place, tokens, early_rows, late_rows, whole_rows, dec, gain, live, scores):
     vmem = pl.BlockSpec(memory_space=pltpu.VMEM)
     anywhere = pl.BlockSpec(memory_space=pl.ANY)
     smem = pl.BlockSpec(memory_space=pltpu.SMEM)
-    _, rows, width = tokens.shape
-
-    def blocks(count):
-        return [
-            pltpu.VMEM((count, rows, width), jnp.bfloat16),
-            pltpu.VMEM((count, 16, 2, 2, *late_rows[0].shape[2:]), jnp.bfloat16),
-        ]
+    rows, width = tokens[0].shape
+    _, nz, chip_rows, half = early_rows[0].shape
+    block = (nz, 2, chip_rows, half)
+    params = pltpu.CompilerParams(vmem_limit_bytes=48 << 20)
 
     def cost(count, size):
         return pl.CostEstimate(
-            flops=2 * rows * count * width * width, bytes_accessed=size << 20, transcendentals=0
+            flops=2 * rows * count * width * half, bytes_accessed=size << 20, transcendentals=0
         )
 
     early = pl.pallas_call(
         early_keys_kernel,
-        out_shape=jax.ShapeDtypeStruct((rows, width), jnp.float32),
-        in_specs=[smem] + [anywhere] * 5,
+        out_shape=jax.ShapeDtypeStruct((rows, half), jnp.float32),
+        in_specs=[smem] + [anywhere] * 7,
         out_specs=vmem,
-        scratch_shapes=blocks(3) + [pltpu.SemaphoreType.DMA((3, 5))],
-        compiler_params=pltpu.CompilerParams(vmem_limit_bytes=48 << 20),
-        cost_estimate=cost(3, 13),
+        scratch_shapes=[
+            pltpu.VMEM((3, rows, width), jnp.bfloat16),
+            pltpu.VMEM((3, *block), jnp.bfloat16),
+            pltpu.SemaphoreType.DMA((6, 2)),
+        ],
+        compiler_params=params,
+        cost_estimate=cost(3, 8),
         name="early_keys",
-    )(place, tokens, *early_rows)
+    )(place, *tokens, *early_rows)
+    columns = pl.pallas_call(
+        whole_heads_kernel,
+        out_shape=jax.ShapeDtypeStruct((8, live.shape[1]), jnp.float32),
+        in_specs=[smem] + [anywhere] * 6 + [vmem] * 3,
+        out_specs=vmem,
+        scratch_shapes=[
+            pltpu.VMEM((4, rows, width), jnp.bfloat16),
+            pltpu.VMEM((4, width, half), jnp.bfloat16),
+            pltpu.SemaphoreType.DMA((4, 3)),
+        ],
+        compiler_params=params,
+        cost_estimate=cost(4, 9),
+        name="whole_heads",
+    )(place, *tokens, whole_rows, dec, gain, live)
     return pl.pallas_call(
-        attention_kernel,
+        late_heads_kernel,
         out_shape=jax.ShapeDtypeStruct((32, 2 * LANES), jnp.float32),
-        in_specs=[smem] + [anywhere] * 3 + [vmem] * 5,
+        in_specs=[smem] + [anywhere] * 7 + [vmem] * 6,
         out_specs=vmem,
-        scratch_shapes=blocks(1)
-        + [pltpu.VMEM((8, live.shape[1]), jnp.float32), pltpu.SemaphoreType.DMA((1, 5))],
-        compiler_params=pltpu.CompilerParams(vmem_limit_bytes=48 << 20),
-        cost_estimate=cost(1, 6),
-        name="attention",
-    )(place, tokens, *late_rows, early, dec, gain, live, scores)
+        scratch_shapes=[
+            pltpu.VMEM((rows, width), jnp.bfloat16),
+            pltpu.VMEM(block, jnp.bfloat16),
+            pltpu.VMEM((8, live.shape[1]), jnp.float32),
+            pltpu.SemaphoreType.DMA((2, 2)),
+        ],
+        compiler_params=params,
+        cost_estimate=cost(1, 4),
+        name="late_heads",
+    )(place, *tokens, *late_rows, early, columns, dec, gain, live, scores)
 
 
 def scores_kernel(place, packed, proj, emb, chosen, state, slots, rows, unit, scale, ordered, unit_v, ids_v):
@@ -316,26 +376,30 @@
     group, _, plen, feats_here = enc_out.shape
     token_rows = group * topk * plen
     with jax.named_scope("gather_enc_out"):
-        token_blocks = lax.all_gather(enc_out.reshape(token_rows, feats_here), "reader")
-
-    half_rows, width_here = key_proj.shape[0] // 2, key_proj.shape[1]
+        own = enc_out.reshape(token_rows, feats_here)
+        after, before = shift(own, "reader", 1), shift(own, "reader", -1)
+        mid = token_rows // 2
+        far_low, far_high = shift(after[:mid], "reader", 1), shift(before[mid:], "reader", -1)
+        tokens = (own, after, far_low, far_high, before)
+
+    rows_here, half = key_proj.shape[0], key_proj.shape[1] // 2
     ids_high = (passage_id // 256).astype(jnp.bfloat16)
     ids_low = (passage_id % 256).astype(jnp.bfloat16)
     gap = ((0, 0), (0, LANES // 2 - topk))
     coded = jnp.concatenate([query_feat, jnp.pad(ids_high, gap), jnp.pad(ids_low, gap)], axis=1)
-    coded = jnp.pad(coded, ((0, 0), (0, width_here - coded.shape[1]))).reshape(half_rows, -1)
+    coded = jnp.pad(coded, ((0, 0), (0, -coded.shape[1] % (rows_here * 4)))).reshape(rows_here, -1)
     beside = coded.shape[1]
     coded = jnp.pad(coded, ((0, 0), (0, LANES - beside)))
     with jax.named_scope("gather_key_proj"):
-        first = send_all(jnp.concatenate([key_proj[:half_rows], coded], axis=1), Z)
-        coded = first[:, :, width_here : width_here + beside].reshape(nz, width_here)
-        early_rows, late_rows = [], []
-        for own in (first[:, :, :width_here], send_all(key_proj[half_rows:], Z)):
-            after, before = shift(own, "y", 1), shift(own, "y", -1)
-            early_rows.append(jnp.stack([own, after, before]))
-            late_rows += [shift(after[:8], "y", 1), shift(before[8:], "y", -1)]
-        late_rows = jnp.concatenate(late_rows).reshape(2, *first.shape[:2], width_here)
-        early_rows += [shift(rows, "core", 1) for rows in early_rows]
+        whole_rows = lax.all_gather(key_proj[:, half:], INDEX)
+        whole_rows = whole_rows.reshape(ny, -1, half)
+        first = send_all(jnp.concatenate([key_proj[:, :half], coded], axis=1), Z)
+        coded = first[:, :, half : half + beside].reshape(nz, -1)
+        own = first[:, :, :half]
+        after, before = shift(own, "y", 1), shift(own, "y", -1)
+        early_rows = jnp.stack([own, after, before])
+        early_rows = [early_rows, shift(early_rows, "core", 1)]
+        late_rows = jnp.concatenate([shift(after[:8], "y", 1), shift(before[8:], "y", -1)])
         late_rows = [late_rows, shift(late_rows, "core", 1)]
 
     with jax.named_scope("gather_queries"):
@@ -402,10 +466,11 @@
         positions = lax.broadcasted_iota(jnp.int32, (group, topk, plen), 2)
         live = (positions < passage_len[:, :, None]).reshape(group, topk * plen)
         packet = attention_packet(
-            jnp.stack([y, core]).astype(jnp.int32),
-            token_blocks,
+            jnp.stack([y, core, r]).astype(jnp.int32),
+            tokens,
             early_rows,
             late_rows,
+            whole_rows,
             dec_unit.reshape(group, answer, feats_here),
             key_gain.astype(jnp.float32).reshape(1, feats_here),
             live.astype(jnp.float32),

time: 295 us -> 276 us (0.936)
  waiting for transfers between devices: 86.2 us -> 60.8 us
  starting transfers between devices: 85.5 us -> 75.5 us
  local copies, waits for them, and re-layouts: 21 us -> 28.6 us
  blocking collectives: 37.9 us -> 43.6 us
    all_to_all x4 -> x3, waiting for transfers between devices: 53.6 us -> 25.4 us  [send_all(): lax.all_to_all(jnp.broadcast_to(x[None], (size, *x.shape)), axis, 0, 0, t...]
    ppermute x12 -> x11, waiting for transfers between devices: 10.8 us -> 3.84 us  [shift(): return lax.ppermute(x, axis, [((i + step) % size, i) for i in range(size)])]
    all_to_all x4 -> x3, starting transfers between devices: 34.7 us -> 28 us  [send_all(): lax.all_to_all(jnp.broadcast_to(x[None], (size, *x.shape)), axis, 0, 0, t...]
    all_gather x1, waiting for transfers between devices: 0.02 us -> 6.53 us  [body(): whole_rows = lax.all_gather(key_proj[:, half:], INDEX)]
    all_to_all x1, blocking collectives: 16.8 us -> 21.2 us  [body(): coef = lax.all_to_all(coef, Z, 0, 0, tiled=True).reshape(n_index, LANES)]
    ppermute x12 -> x11, starting transfers between devices: 36.4 us -> 32.2 us  [shift(): return lax.ppermute(x, axis, [((i + step) % size, i) for i in range(size)])]
    all_to_all x1, waiting for transfers between devices: 0.01 us -> 3.93 us  [body(): state = merge_all(lax.all_to_all(state, ('y', 'core'), 0, 0, tiled=True))]
    slice x7 -> x6, local copies, waits for them, and re-layouts: 4.5 us -> 6.72 us  [the longest x1 1.69 us: body(): after[:8]]
  transfers between devices with their start and end apart: 20 -> 18, of which waited for: 7 -> 8; matrix products, arithmetic and copies ran while one was open for 8% -> 12% of each run, Pallas kernels for 6% -> 7%
where the time goes in v4:
time: 276 us; the launch traced here: 273 us
  starting transfers between devices  75.5 us (27%)
  waiting for transfers between devices  60.8 us (22%)
  blocking collectives  43.6 us (16%)
  Pallas kernels  34.4 us (12%)
  local copies, waits for them, and re-layouts  28.6 us (10%)
  other arithmetic  15.3 us (6%)
  between operations  15.2 us (6%)
    ppermute x11, starting transfers between devices, shift(): return lax.ppermute(x, axis, [((i + step) % size, i) for i in range(size)])  32.2 us
    all_to_all x3, starting transfers between devices, send_all(): lax.all_to_all(jnp.broadcast_to(x[None], (size, *x.shape)), axis, 0, 0, t...  28 us
    all_to_all x3, waiting for transfers between devices, send_all(): lax.all_to_all(jnp.broadcast_to(x[None], (size, *x.shape)), axis, 0, 0, t...  25.4 us
    all_to_all x1, blocking collectives, body(): coef = lax.all_to_all(coef, Z, 0, 0, tiled=True).reshape(n_index, LANES)  21.2 us
    all_to_all x1, waiting for transfers between devices, body(): term = jnp.sum(lax.all_to_all(term, Z, 0, 0, tiled=True), axis=0)  12.1 us
    all_to_all x1, blocking collectives, body(): lax.all_to_all(packet, NEAR, 0, 0, tiled=True)  11.3 us
    all_to_all x1, blocking collectives, body(): term = jnp.sum(lax.all_to_all(term, 'y', 0, 0, tiled=True), axis=0)  11 us
    unnamed x36, local copies, waits for them, and re-layouts  9.54 us
  transfers between devices with their start and end apart: 18, of which 8 were waited for; matrix products, arithmetic and copies ran while one was open for 12% of the time, Pallas kernels for 7%

profile of v4, /device:TPU:6, one launch (start us, length us, event | category | flops | bytes accessed | tf_op | source)
XLA Modules:
  0.0 273.2 jit_solution(4498039005110867226)
XLA Ops:
  7.2 1.4 fusion.34
  11.1 15.2 %all-to-all-start = ((bf16[16,32,640]{2,1,0:T(8,128)(2,1)}), bf16[16,32,640]{2,1,0:T(8,128)(2,1)S(1)}, u32[]{:S(2)}, u32[]{:S(2)}) async-start(bf16[16,32,640]{2,1,0:T(8,128)(2,1)} %broadcast_in_dim.12), calls=%async_computation | async-start | bytes 1310720 | tf_op jit(solution)/shard_map/gather_key_proj/all_to_all | solution.py:35
  26.3 2.7 %collective-permute-start = (bf16[640,1024]{1,0:T(8,128)(2,1)}, bf16[640,1024]{1,0:T(8,128)(2,1)S(1)}, u32[]{:S(2)}, u32[]{:S(2)}) collective-permute-start(bf16[640,1024]{1,0:T(8,128)(2,1)} %bitcast.3.refs_0_), channel_id=1, source_target_pairs={{1,0},{2,1},{3,2},{0,3},{5,4},{6,5},{7,6},{4,7},{9,8},{10,9},{11,1... | collective-permute-start | bytes 3932168 | tf_op jit(solution)/shard_map/gather_enc_out/ppermute | solution.py:30
  29.1 4.3 %collective-permute-start.2 = (bf16[640,1024]{1,0:T(8,128)(2,1)}, bf16[640,1024]{1,0:T(8,128)(2,1)S(1)}, u32[]{:S(2)}, u32[]{:S(2)}) collective-permute-start(bf16[640,1024]{1,0:T(8,128)(2,1)} %bitcast.3.refs_0_), channel_id=1, source_target_pairs={{3,0},{0,1},{1,2},{2,3},{7,4},{4,5},{5,6},{6,7},{11,8},{8,9},{9,10... | collective-permute-start | bytes 3932168 | tf_op jit(solution)/shard_map/gather_enc_out/ppermute | solution.py:30
  34.3 1.9 mul.67
  36.4 1.3 reduce_sum.74
  37.7 23.2 %all-to-all-done = bf16[16,32,640]{2,1,0:T(8,128)(2,1)S(1)} async-done(((bf16[16,32,640]{2,1,0:T(8,128)(2,1)}), bf16[16,32,640]{2,1,0:T(8,128)(2,1)S(1)}, u32[]{:S(2)}, u32[]{:S(2)}) %all-to-all-start) | async-done | bytes 655392 | tf_op jit(solution)/shard_map/gather_key_proj/all_to_all | solution.py:35
  62.2 7.5 %all-to-all-start.1 = ((bf16[32,16,896]{2,1,0:T(8,128)(2,1)}), bf16[32,16,896]{2,1,0:T(8,128)(2,1)}, u32[]{:S(2)}, u32[]{:S(2)}) async-start(bf16[32,16,896]{2,1,0:T(8,128)(2,1)} %broadcast_in_dim.14), calls=%async_computation.1 | async-start | bytes 1835008 | tf_op jit(solution)/shard_map/gather_queries/all_to_all | solution.py:35
  70.9 4.6 %collective-permute-start.4 = (bf16[16,32,512]{2,1,0:T(8,128)(2,1)}, bf16[16,32,512]{2,1,0:T(8,128)(2,1)}, u32[]{:S(2)}, u32[]{:S(2)}) collective-permute-start(bf16[16,32,512]{2,1,0:T(8,128)(2,1)} %get-tuple-element.49), channel_id=1, source_target_pairs={{128,0},{256,128},{384,256},{0,384},{129,1},{257,129},{385,257},{1... | collective-permute-start | bytes 1572872 | tf_op jit(solution)/shard_map/gather_key_proj/ppermute | solution.py:30
  75.5 1.9 collective-permute-start.6
  81.0 1.3 fusion.chosen
  83.2 2.7 collective-permute-start.1
  87.0 4.3 %collective-permute-start.3 = (bf16[320,1024]{1,0:T(8,128)(2,1)}, bf16[320,1024]{1,0:T(8,128)(2,1)}, u32[]{:S(2)}, u32[]{:S(2)}) collective-permute-start(bf16[320,1024]{1,0:T(8,128)(2,1)} %slice.78), channel_id=1, source_target_pairs={{3,0},{0,1},{1,2},{2,3},{7,4},{4,5},{5,6},{6,7},{11,8},{8,9},{9,10... | collective-permute-start | bytes 1966088 | tf_op jit(solution)/shard_map/gather_enc_out/ppermute | solution.py:30
  91.3 2.1 collective-permute-done.4
  93.4 1.7 slice.80
  95.1 3.4 %collective-permute-start.5 = (bf16[8,32,512]{2,1,0:T(8,128)(2,1)}, bf16[8,32,512]{2,1,0:T(8,128)(2,1)}, u32[]{:S(2)}, u32[]{:S(2)}) collective-permute-start(bf16[8,32,512]{2,1,0:T(8,128)(2,1)} %slice.80), channel_id=1, source_target_pairs={{128,0},{256,128},{384,256},{0,384},{129,1},{257,129},{385,257},{1... | collective-permute-start | bytes 786440 | tf_op jit(solution)/shard_map/gather_key_proj/ppermute | solution.py:30
  98.5 1.7 slice.81
  100.2 2.4 collective-permute-start.7
  102.6 2.6 pad_maximum_fusion.refs_5_
  105.2 1.9 collective-permute-start.9
  107.1 1.3 copy-done.3
  108.4 1.3 copy-done.12
  109.7 6.9 %scores.1 = (f32[128,128]{1,0:T(8,128)}, s32[128,128]{1,0:T(8,128)S(1)}, f32[512,192]{1,0:T(8,128)S(1)}, f32[512,192]{1,0:T(8,128)S(1)}, f32[512,1]{1,0:T(8,128)S(1)}, /*index=5*/bf16[768,512]{1,0:T(8,128)(2,1)S(1)}) custom-call(s32[2]{0:T(128)S(1)} %pad_add_fusion.1.place, bf16[32,16,896]{2,1,0:T(8,128)(2,1)} %all-to-all-done.1.packed, ...), custom_call_target="tpu_custom_call" | custom-call | flops 4294967296 | bytes 8388608 | tf_op jit(solution)/shard_map/scores/scores/pallas_call | solution.py:419
  118.1 4.1 %all-to-all-start.2 = ((f32[8,16,128]{2,1,0:T(8,128)}), f32[8,16,128]{2,1,0:T(8,128)S(1)}, u32[]{:S(2)}, u32[]{:S(2)}) async-start(f32[8,16,128]{2,1,0:T(8,128)} %bitcast.10), calls=%async_computation.2 | async-start | bytes 131072 | tf_op jit(solution)/shard_map/reduce_scores/all_to_all | solution.py:448
  122.2 1.7 constant_dynamic-update-slice_fusion.1
  123.9 3.9 %all-to-all-done.2 = f32[8,16,128]{2,1,0:T(8,128)S(1)} async-done(((f32[8,16,128]{2,1,0:T(8,128)}), f32[8,16,128]{2,1,0:T(8,128)S(1)}, u32[]{:S(2)}, u32[]{:S(2)}) %all-to-all-start.2) | async-done | bytes 65568 | tf_op jit(solution)/shard_map/reduce_scores/all_to_all | solution.py:448
  128.5 7.6 %all-to-all-start.3 = ((f32[16,1,128]{2,1,0:T(1,128)}), f32[16,1,128]{2,1,0:T(1,128)S(1)}, u32[]{:S(2)}, u32[]{:S(2)}) async-start(f32[16,1,128]{2,1,0:T(1,128)} %broadcast_select_fusion), calls=%async_computation.3 | async-start | bytes 16384 | tf_op jit(solution)/shard_map/reduce_scores/all_to_all | solution.py:449
  136.1 1.7 constant_dynamic-update-slice_fusion.refs_5_
  137.8 1.9 collective-permute-start.8
  139.7 8.9 %all-to-all-done.3 = f32[16,1,128]{2,1,0:T(1,128)S(1)} async-done(((f32[16,1,128]{2,1,0:T(1,128)}), f32[16,1,128]{2,1,0:T(1,128)S(1)}, u32[]{:S(2)}, u32[]{:S(2)}) %all-to-all-start.3) | async-done | bytes 8224 | tf_op jit(solution)/shard_map/reduce_scores/all_to_all | solution.py:449
  149.3 1.3 fusion.28
  150.5 1.4 broadcast_select_fusion.1
  152.9 4.9 %early_keys.1.refs_7_ = f32[640,512]{1,0:T(8,128)S(1)} custom-call(s32[3]{0:T(128)S(1)} %pad_add_fusion.place, bf16[640,1024]{1,0:T(8,128)(2,1)} %bitcast.3.refs_0_, bf16[640,1024]{1,0:T(8,128)(2,1)S(1)} %collective-permute-done.refs_1_, bf16[320,1024]{1,0:T(8,128)(2,1)S(1)} %collective-permute-done.1.refs_2_, ...), custom_call_target="tpu_custom_call" | custom-call | flops 2013265920 | bytes 8388608 | tf_op jit(solution)/shard_map/attention/early_keys/pallas_call | solution.py:193
  158.9 6.5 %all-gather.3.cloned.1.call-done = bf16[4096,512]{1,0:T(8,128)(2,1)} async-done(((bf16[32,512]{1,0:T(8,128)(2,1)}), bf16[4096,512]{1,0:T(8,128)(2,1)}) %all-gather.3.cloned.1.call-update) | async-done | bytes 4194320 | tf_op jit(solution)/shard_map/gather_key_proj/all_gather | solution.py:394
  165.4 8.3 %whole_heads.1.refs_8_ = f32[8,160]{1,0:T(8,128)S(1)} custom-call(s32[3]{0:T(128)S(1)} %pad_add_fusion.place, bf16[640,1024]{1,0:T(8,128)(2,1)} %bitcast.3.refs_0_, bf16[640,1024]{1,0:T(8,128)(2,1)S(1)} %collective-permute-done.refs_1_, bf16[320,1024]{1,0:T(8,128)(2,1)S(1)} %collective-permute-done.1.refs_2_, ...), custom_call_target="tpu_custom_call" | custom-call | flops 2684354560 | bytes 9437184 | tf_op jit(solution)/shard_map/attention/whole_heads/pallas_call | solution.py:207
  173.8 6.0 %late_heads.1 = f32[32,256]{1,0:T(8,128)S(1)} custom-call(s32[3]{0:T(128)S(1)} %pad_add_fusion.place, bf16[640,1024]{1,0:T(8,128)(2,1)} %bitcast.3.refs_0_, bf16[640,1024]{1,0:T(8,128)(2,1)S(1)} %collective-permute-done.refs_1_, bf16[320,1024]{1,0:T(8,128)(2,1)S(1)} %collective-permute-done.1.refs_2_, bf16[320,1024]{1,0:T(8,128)(2,1)} %collective-permute-done.3.refs_3_, ...), custom_call_target="tpu_custom_call" | custom-call | flops 671088640 | bytes 4194304 | tf_op jit(solution)/shard_map/attention/late_heads/pallas_call | solution.py:221
  179.9 11.3 %all_to_all.50 = f32[32,1,256]{2,1,0:T(1,128)S(1)} all-to-all(f32[32,1,256]{2,1,0:T(1,128)S(1)} %copy.20), channel_id=1, replica_groups=mesh['y'=4,'zq'=4,'zr'=4,'core'=2,'reader'=4] {'reader','y','core'}, dimensions={0} | all-to-all | bytes 65536 | tf_op jit(solution)/shard_map/targets/all_to_all | solution.py:481
  191.8 1.6 coef.1
  193.4 21.2 %all_to_all.51 = f32[16,8,128]{2,1,0:T(8,128)S(1)} all-to-all(f32[16,8,128]{2,1,0:T(8,128)} %coef.1), channel_id=1, replica_groups=mesh['y'=4,'zq'=4,'zr'=4,'core'=2,'reader'=4] {'zq','zr'}, dimensions={0} | all-to-all | bytes 131072 | tf_op jit(solution)/shard_map/targets/all_to_all | solution.py:489
  216.6 6.6 %gradient.1 = (f32[384,192]{1,0:T(8,128)S(1)}, f32[384,192]{1,0:T(8,128)S(1)}) custom-call(f32[128,128]{1,0:T(8,128)S(1)} %bitcast.32, s32[128,128]{1,0:T(8,128)S(1)} %get-tuple-element.37.slot, f32[512,192]{1,0:T(8,128)S(1)} %copy-done.7, f32[512,192]{1,0:T(8,128)S(1)} %copy-done.9, f32[512,1]{1,0:T(8,128)S(1)} %copy-done.11, bf16[768,512]{1,0:T(8,128)(2,1)S(1)} %copy-done.5), custom_call_target="tpu_custom_call" | custom-call | tf_op jit(solution)/shard_map/gradient/gradient/pallas_call | solution.py:493
  223.2 1.9 collective-permute-start.10
  225.2 1.7 collective-permute-done.10
  226.9 11.0 %all_to_all.52 = f32[4,96,192]{2,1,0:T(8,128)S(1)} all-to-all(f32[4,96,192]{2,1,0:T(8,128)S(1)} %bitcast.36), channel_id=1, replica_groups=mesh['y'=4,'zq'=4,'zr'=4,'core'=2,'reader'=4] {'y'}, dimensions={0} | all-to-all | bytes 589824 | tf_op jit(solution)/shard_map/reduce_gradient/all_to_all | solution.py:509
  238.6 3.5 %all-to-all-start.7 = ((f32[16,6,192]{2,1,0:T(8,128)}), f32[16,6,192]{2,1,0:T(8,128)S(1)}, u32[]{:S(2)}, u32[]{:S(2)}) async-start(f32[16,6,192]{2,1,0:T(8,128)} %reshape.298), calls=%async_computation.7 | async-start | bytes 262144 | tf_op jit(solution)/shard_map/reduce_gradient/all_to_all | solution.py:511
  244.2 12.1 %all-to-all-done.7 = f32[16,6,192]{2,1,0:T(8,128)S(1)} async-done(((f32[16,6,192]{2,1,0:T(8,128)}), f32[16,6,192]{2,1,0:T(8,128)S(1)}, u32[]{:S(2)}, u32[]{:S(2)}) %all-to-all-start.7) | async-done | bytes 73760 | tf_op jit(solution)/shard_map/reduce_gradient/all_to_all | solution.py:511
  257.0 5.3 %all-to-all-start.8 = ((f32[4,6,192]{2,1,0:T(8,128)}), f32[4,6,192]{2,1,0:T(8,128)S(1)}, u32[]{:S(2)}, u32[]{:S(2)}) async-start(f32[4,6,192]{2,1,0:T(8,128)} %broadcast_in_dim.15), calls=%async_computation.8 | async-start | bytes 65536 | tf_op jit(solution)/shard_map/reduce_gradient/all_to_all | solution.py:35
  262.3 1.2 log_bitcast_fusion
  263.5 2.2 all-to-all-done.8
  (91 shorter events, 22.4 us)
Async XLA Ops:
  7.2 26.3 %copy-start.14 = (bf16[4,16,1024]{2,1,0:T(8,128)(2,1)S(1)}, bf16[4,16,1024]{2,1,0:T(8,128)(2,1)}, u32[]{:S(2)}) copy-start(bf16[4,16,1024]{2,1,0:T(8,128)(2,1)} %param.21) | copy-start | bytes 393220
  7.2 158.2 %all-gather.3.cloned.1.call-start = ((), (), s32[]{:S(2)}) async-start(), calls=%async_computation.9 | async-start | bytes 4227072 | tf_op jit(solution)/shard_map/gather_key_proj/all_gather | solution.py:394
  10.2 25.9 %copy-start.15 = (s32[4,20]{1,0:T(4,128)S(1)}, s32[4,20]{1,0:T(4,128)}, u32[]{:S(2)}) copy-start(s32[4,20]{1,0:T(4,128)} %param.17) | copy-start | bytes 964
  11.1 49.8 %all-to-all-start = ((bf16[16,32,640]{2,1,0:T(8,128)(2,1)}), bf16[16,32,640]{2,1,0:T(8,128)(2,1)S(1)}, u32[]{:S(2)}, u32[]{:S(2)}) async-start(bf16[16,32,640]{2,1,0:T(8,128)(2,1)} %broadcast_in_dim.12), calls=%async_computation | async-start | bytes 1310720 | tf_op jit(solution)/shard_map/gather_key_proj/all_to_all | solution.py:35
  26.3 56.0 %collective-permute-start = (bf16[640,1024]{1,0:T(8,128)(2,1)}, bf16[640,1024]{1,0:T(8,128)(2,1)S(1)}, u32[]{:S(2)}, u32[]{:S(2)}) collective-permute-start(bf16[640,1024]{1,0:T(8,128)(2,1)} %bitcast.3.refs_0_), channel_id=1, source_target_pairs={{1,0},{2,1},{3,2},{0,3},{5,4},{6,5},{7,6},{4,7},{9,8},{10,9},{11,1... | collective-permute-start | bytes 3932168 | tf_op jit(solution)/shard_map/gather_enc_out/ppermute | solution.py:30
  29.1 56.8 %collective-permute-start.2 = (bf16[640,1024]{1,0:T(8,128)(2,1)}, bf16[640,1024]{1,0:T(8,128)(2,1)S(1)}, u32[]{:S(2)}, u32[]{:S(2)}) collective-permute-start(bf16[640,1024]{1,0:T(8,128)(2,1)} %bitcast.3.refs_0_), channel_id=1, source_target_pairs={{3,0},{0,1},{1,2},{2,3},{7,4},{4,5},{5,6},{6,7},{11,8},{8,9},{9,10... | collective-permute-start | bytes 3932168 | tf_op jit(solution)/shard_map/gather_enc_out/ppermute | solution.py:30
  62.2 44.9 %all-to-all-start.1 = ((bf16[32,16,896]{2,1,0:T(8,128)(2,1)}), bf16[32,16,896]{2,1,0:T(8,128)(2,1)}, u32[]{:S(2)}, u32[]{:S(2)}) async-start(bf16[32,16,896]{2,1,0:T(8,128)(2,1)} %broadcast_in_dim.14), calls=%async_computation.1 | async-start | bytes 1835008 | tf_op jit(solution)/shard_map/gather_queries/all_to_all | solution.py:35
  69.7 8.9 %copy-start.16 = (bf16[1024]{0:T(1024)(128)(2,1)S(1)}, bf16[1024]{0:T(1024)(128)(2,1)}, u32[]{:S(2)}) copy-start(bf16[1024]{0:T(1024)(128)(2,1)} %param.20) | copy-start | bytes 6148
  70.9 22.6 %collective-permute-start.4 = (bf16[16,32,512]{2,1,0:T(8,128)(2,1)}, bf16[16,32,512]{2,1,0:T(8,128)(2,1)}, u32[]{:S(2)}, u32[]{:S(2)}) collective-permute-start(bf16[16,32,512]{2,1,0:T(8,128)(2,1)} %get-tuple-element.49), channel_id=1, source_target_pairs={{128,0},{256,128},{384,256},{0,384},{129,1},{257,129},{385,257},{1... | collective-permute-start | bytes 1572872 | tf_op jit(solution)/shard_map/gather_key_proj/ppermute | solution.py:30
  75.5 23.0 %collective-permute-start.6 = (bf16[16,32,512]{2,1,0:T(8,128)(2,1)}, bf16[16,32,512]{2,1,0:T(8,128)(2,1)}, u32[]{:S(2)}, u32[]{:S(2)}) collective-permute-start(bf16[16,32,512]{2,1,0:T(8,128)(2,1)} %get-tuple-element.49), channel_id=1, source_target_pairs={{384,0},{0,128},{128,256},{256,384},{385,1},{1,129},{129,257},{257... | collective-permute-start | bytes 1572872 | tf_op jit(solution)/shard_map/gather_key_proj/ppermute | solution.py:30
  82.3 20.3 %copy-start.13 = (bf16[1,16,32,512]{3,2,1,0:T(8,128)(2,1)S(1)}, bf16[1,16,32,512]{3,2,1,0:T(8,128)(2,1)}, u32[]{:S(2)}) copy-start(bf16[1,16,32,512]{3,2,1,0:T(8,128)(2,1)} %get-tuple-element.48) | copy-start | bytes 1572868
  83.2 69.6 %collective-permute-start.1 = (bf16[320,1024]{1,0:T(8,128)(2,1)}, bf16[320,1024]{1,0:T(8,128)(2,1)S(1)}, u32[]{:S(2)}, u32[]{:S(2)}) collective-permute-start(bf16[320,1024]{1,0:T(8,128)(2,1)} %slice.77), channel_id=1, source_target_pairs={{1,0},{2,1},{3,2},{0,3},{5,4},{6,5},{7,6},{4,7},{9,8},{10,9},{11,1... | collective-permute-start | bytes 1966088 | tf_op jit(solution)/shard_map/gather_enc_out/ppermute | solution.py:30
  85.9 19.3 %copy-start = (bf16[640,1024]{1,0:T(8,128)(2,1)}, bf16[640,1024]{1,0:T(8,128)(2,1)S(1)}, u32[]{:S(2)}) copy-start(bf16[640,1024]{1,0:T(8,128)(2,1)S(1)} %collective-permute-done.2.refs_4_) | copy-start | bytes 3932164
  87.0 65.9 %collective-permute-start.3 = (bf16[320,1024]{1,0:T(8,128)(2,1)}, bf16[320,1024]{1,0:T(8,128)(2,1)}, u32[]{:S(2)}, u32[]{:S(2)}) collective-permute-start(bf16[320,1024]{1,0:T(8,128)(2,1)} %slice.78), channel_id=1, source_target_pairs={{3,0},{0,1},{1,2},{2,3},{7,4},{4,5},{5,6},{6,7},{11,8},{8,9},{9,10... | collective-permute-start | bytes 1966088 | tf_op jit(solution)/shard_map/gather_enc_out/ppermute | solution.py:30
  95.1 27.1 %collective-permute-start.5 = (bf16[8,32,512]{2,1,0:T(8,128)(2,1)}, bf16[8,32,512]{2,1,0:T(8,128)(2,1)}, u32[]{:S(2)}, u32[]{:S(2)}) collective-permute-start(bf16[8,32,512]{2,1,0:T(8,128)(2,1)} %slice.80), channel_id=1, source_target_pairs={{128,0},{256,128},{384,256},{0,384},{129,1},{257,129},{385,257},{1... | collective-permute-start | bytes 786440 | tf_op jit(solution)/shard_map/gather_key_proj/ppermute | solution.py:30
  100.2 35.9 %collective-permute-start.7 = (bf16[8,32,512]{2,1,0:T(8,128)(2,1)}, bf16[8,32,512]{2,1,0:T(8,128)(2,1)}, u32[]{:S(2)}, u32[]{:S(2)}) collective-permute-start(bf16[8,32,512]{2,1,0:T(8,128)(2,1)} %slice.81), channel_id=1, source_target_pairs={{384,0},{0,128},{128,256},{256,384},{385,1},{1,129},{129,257},{257... | collective-permute-start | bytes 786440 | tf_op jit(solution)/shard_map/gather_key_proj/ppermute | solution.py:30
  105.2 47.7 %collective-permute-start.9 = (bf16[3,16,32,512]{3,2,1,0:T(8,128)(2,1)}, bf16[3,16,32,512]{3,2,1,0:T(8,128)(2,1)}, u32[]{:S(2)}, u32[]{:S(2)}) collective-permute-start(bf16[3,16,32,512]{3,2,1,0:T(8,128)(2,1)} %pad_maximum_fusion.refs_5_), channel_id=1, source_target_pairs={{4,0},{0,4},{5,1},{1,5},{6,2},{2,6},{7,3},{3,7},{12,8},{8,12},{13,... | collective-permute-start | bytes 4718600 | tf_op jit(solution)/shard_map/gather_key_proj/ppermute | solution.py:30
  107.1 1.3 copy-start.3
  108.4 1.3 copy-start.12
  116.5 0.8 copy-start.6
  117.3 0.8 copy-start.8
  118.1 33.8 %copy-start.4 = (bf16[768,512]{1,0:T(8,128)(2,1)}, bf16[768,512]{1,0:T(8,128)(2,1)S(1)}, u32[]{:S(2)}) copy-start(bf16[768,512]{1,0:T(8,128)(2,1)S(1)} %get-tuple-element.41.refs_3_) | copy-start | bytes 2359300
  118.1 33.8 %copy-start.10 = (f32[512,1]{1,0:T(8,128)}, f32[512,1]{1,0:T(8,128)S(1)}, u32[]{:S(2)}) copy-start(f32[512,1]{1,0:T(8,128)S(1)} %get-tuple-element.40.refs_2_) | copy-start | bytes 6148
  118.1 9.7 %all-to-all-start.2 = ((f32[8,16,128]{2,1,0:T(8,128)}), f32[8,16,128]{2,1,0:T(8,128)S(1)}, u32[]{:S(2)}, u32[]{:S(2)}) async-start(f32[8,16,128]{2,1,0:T(8,128)} %bitcast.10), calls=%async_computation.2 | async-start | bytes 131072 | tf_op jit(solution)/shard_map/reduce_scores/all_to_all | solution.py:448
  128.5 20.2 %all-to-all-start.3 = ((f32[16,1,128]{2,1,0:T(1,128)}), f32[16,1,128]{2,1,0:T(1,128)S(1)}, u32[]{:S(2)}, u32[]{:S(2)}) async-start(f32[16,1,128]{2,1,0:T(1,128)} %broadcast_select_fusion), calls=%async_computation.3 | async-start | bytes 16384 | tf_op jit(solution)/shard_map/reduce_scores/all_to_all | solution.py:449
  137.8 36.0 %collective-permute-start.8 = (bf16[16,32,512]{2,1,0:T(8,128)(2,1)}, bf16[16,32,512]{2,1,0:T(8,128)(2,1)}, u32[]{:S(2)}, u32[]{:S(2)}) collective-permute-start(bf16[16,32,512]{2,1,0:T(8,128)(2,1)} %constant_dynamic-update-slice_fusion.refs_5_), channel_id=1, source_target_pairs={{4,0},{0,4},{5,1},{1,5},{6,2},{2,6},{7,3},{3,7},{12,8},{8,12},{13,... | collective-permute-start | bytes 1572872 | tf_op jit(solution)/shard_map/gather_key_proj/ppermute | solution.py:30
  152.8 12.6 %copy-start.1 = (bf16[640,1024]{1,0:T(8,128)(2,1)S(1)}, bf16[640,1024]{1,0:T(8,128)(2,1)}, u32[]{:S(2)}) copy-start(bf16[640,1024]{1,0:T(8,128)(2,1)} %copy-done) | copy-start | bytes 3932164
  157.8 1.1 copy-start.2
  173.7 40.8 %copy-start.5 = (bf16[768,512]{1,0:T(8,128)(2,1)S(1)}, bf16[768,512]{1,0:T(8,128)(2,1)}, u32[]{:S(2)}) copy-start(bf16[768,512]{1,0:T(8,128)(2,1)} %copy-done.4) | copy-start | bytes 2359300
  173.8 40.8 %copy-start.7 = (f32[512,192]{1,0:T(8,128)S(1)}, f32[512,192]{1,0:T(8,128)}, u32[]{:S(2)}) copy-start(f32[512,192]{1,0:T(8,128)} %copy-done.6) | copy-start | bytes 1179652
  214.6 1.0 copy-start.9
  215.6 0.9 copy-start.11
  223.2 3.6 %collective-permute-start.10 = (f32[384,192]{1,0:T(8,128)S(1)}, f32[384,192]{1,0:T(8,128)S(1)}, u32[]{:S(2)}, u32[]{:S(2)}) collective-permute-start(f32[384,192]{1,0:T(8,128)S(1)} %get-tuple-element.43), channel_id=1, source_target_pairs={{4,0},{0,4},{5,1},{1,5},{6,2},{2,6},{7,3},{3,7},{12,8},{8,12},{13,... | collective-permute-start | bytes 884744 | tf_op jit(solution)/shard_map/reduce_gradient/ppermute | solution.py:30
  238.6 17.7 %all-to-all-start.7 = ((f32[16,6,192]{2,1,0:T(8,128)}), f32[16,6,192]{2,1,0:T(8,128)S(1)}, u32[]{:S(2)}, u32[]{:S(2)}) async-start(f32[16,6,192]{2,1,0:T(8,128)} %reshape.298), calls=%async_computation.7 | async-start | bytes 262144 | tf_op jit(solution)/shard_map/reduce_gradient/all_to_all | solution.py:511
  257.0 8.7 %all-to-all-start.8 = ((f32[4,6,192]{2,1,0:T(8,128)}), f32[4,6,192]{2,1,0:T(8,128)S(1)}, u32[]{:S(2)}, u32[]{:S(2)}) async-start(f32[4,6,192]{2,1,0:T(8,128)} %broadcast_in_dim.15), calls=%async_computation.8 | async-start | bytes 65536 | tf_op jit(solution)/shard_map/reduce_gradient/all_to_all | solution.py:35
Sparse Core Ops, SparseCore 0:
  11.1 154.2 all-gather.2

commit v5 on v4

--- a/solution.py
+++ b/solution.py
@@ -21,8 +21,6 @@
 SLOT = 32
 TILE = 256
 N_OWNERS = 128
-EARLY = (0, 1, 3)
-LATE = 2
 
 
 def shift(x, axis, step):
@@ -63,37 +61,12 @@
     ]
 
 
-def row_copies(core, own, other, target, sems):
-    copies = [
-        pltpu.make_async_copy(own, target.at[:, core], sems.at[0]),
-        pltpu.make_async_copy(other, target.at[:, 1 - core], sems.at[1]),
-    ]
-    for copy in copies:
-        copy.start()
-    return copies
-
-
-def early_keys_kernel(place, *refs):
-    tokens, (own, other), (keys, token_v, weight_v, sems) = refs[:5], refs[5:7], refs[7:]
-    y, core, r = place[0], place[1], place[2]
-    copies = []
-    for slot, ahead in enumerate(EARLY):
-        waits = row_copies(core, own.at[slot], other.at[slot], weight_v.at[slot], sems.at[slot])
-        target = token_v.at[slot]
-        waits += token_copies(r, (y + ahead) % 4, tokens, target, sems.at[3 + slot])
-        copies.append(waits)
-    for slot in range(len(EARLY)):
-        for copy in copies[slot]:
-            copy.wait()
-
-        @pl.loop(0, keys.shape[1] // TILE)
-        def _(t):
-            cols = pl.ds(pl.multiple_of(t * TILE, TILE), TILE)
-            term = dot32(token_v[slot], weight_v[slot, :, :, :, cols].reshape(-1, TILE))
-            if slot == 0:
-                keys[:, cols] = term
-            else:
-                keys[:, cols] += term
+def row_copies(core, own, other, target, sem):
+    for residue in range(4):
+        to = target.at[:, residue]
+        pltpu.make_async_copy(own.at[residue], to.at[:, core], sem).start()
+        pltpu.make_async_copy(other.at[residue], to.at[:, 1 - core], sem).start()
+    return [pltpu.make_async_copy(target, target, sem)]
 
 
 def attend(keys, offset, dec, gain, live, column_v):
@@ -125,44 +98,51 @@
         column_v[g : g + 1, :] += jnp.sum(weight, axis=0, keepdims=True)
 
 
-def whole_heads_kernel(place, *refs):
-    tokens, refs = refs[:5], refs[5:]
-    rows, dec, gain, live, columns, token_v, weight_v, sems = refs
-    r = place[2]
+def load_and_attend(place, offset, tokens, own, other, dec, gain, live, column_v, token_v, weight_v, sems):
+    core, r = place[0], place[1]
     copies = []
     for c in range(4):
-        copy = pltpu.make_async_copy(rows.at[c], weight_v.at[c], sems.at[c, 2])
-        copy.start()
-        copies += [copy] + token_copies(r, c, tokens, token_v.at[c], sems.at[c])
-    columns[...] = jnp.zeros_like(columns)
-    for copy in copies:
-        copy.wait()
-
-    @pl.loop(0, weight_v.shape[2] // TILE)
+        copies.append(row_copies(core, own.at[c], other.at[c], weight_v.at[c], sems.at[2 * c, 0]))
+        copies[c] += token_copies(r, c, tokens, token_v.at[c], sems.at[2 * c + 1])
+    for c in range(4):
+        for copy in copies[c]:
+            copy.wait()
+
+    @pl.loop(0, weight_v.shape[-1] // TILE)
     def _(t):
         cols = pl.ds(pl.multiple_of(t * TILE, TILE), TILE)
-        keys = dot32(token_v[0], weight_v[0, :, cols])
+        keys = dot32(token_v[0], weight_v[0, :, :, :, :, cols].reshape(-1, TILE))
         for c in range(1, 4):
-            keys += dot32(token_v[c], weight_v[c, :, cols])
-        attend(keys, weight_v.shape[2] + t * TILE, dec, gain, live, columns)
-
-
-def late_heads_kernel(place, *refs):
-    tokens, (own, other), refs = refs[:5], refs[5:7], refs[7:]
-    early, columns, dec, gain, live, scores, out, token_v, weight_v, column_v, sems = refs
-    y, core, r = place[0], place[1], place[2]
-    copies = row_copies(core, own, other, weight_v, sems.at[0])
-    copies += token_copies(r, (y + LATE) % 4, tokens, token_v, sems.at[1])
+            keys += dot32(token_v[c], weight_v[c, :, :, :, :, cols].reshape(-1, TILE))
+        attend(keys, offset + t * TILE, dec, gain, live, column_v)
+
+
+def first_heads_kernel(place, *refs):
+    tokens, (own, other, dec, gain, live, columns, token_v, weight_v, sems) = refs[:5], refs[5:]
+    columns[...] = jnp.zeros_like(columns)
+    load_and_attend(
+        place, 0, tokens, own, other, dec, gain, live, columns, token_v, weight_v, sems
+    )
+
+
+def last_heads_kernel(place, *refs):
+    tokens, refs = refs[:5], refs[5:]
+    own, other, dec, gain, live, columns, scores, out, column_v, token_v, weight_v, sems = refs
     column_v[...] = columns[...]
-    for copy in copies:
-        copy.wait()
-
-    @pl.loop(0, early.shape[1] // TILE)
-    def _(t):
-        cols = pl.ds(pl.multiple_of(t * TILE, TILE), TILE)
-        keys = early[:, cols] + dot32(token_v[...], weight_v[:, :, :, cols].reshape(-1, TILE))
-        attend(keys, t * TILE, dec, gain, live, column_v)
-
+    load_and_attend(
+        place,
+        weight_v.shape[-1],
+        tokens,
+        own,
+        other,
+        dec,
+        gain,
+        live,
+        column_v,
+        token_v,
+        weight_v,
+        sems,
+    )
     n = live.shape[1]
     mass = jnp.zeros((8, LANES), jnp.float32)
     for g in range(dec.shape[0]):
@@ -176,63 +156,41 @@
     out[:, LANES:] = jnp.broadcast_to(scores[...], (out.shape[0], LANES))
 
 
-def attention_packet(place, tokens, early_rows, late_rows, whole_rows, dec, gain, live, scores):
+def attention_packet(place, tokens, first_rows, last_rows, dec, gain, live, scores):
     vmem = pl.BlockSpec(memory_space=pltpu.VMEM)
     anywhere = pl.BlockSpec(memory_space=pl.ANY)
     smem = pl.BlockSpec(memory_space=pltpu.SMEM)
     rows, width = tokens[0].shape
-    _, nz, chip_rows, half = early_rows[0].shape
-    block = (nz, 2, chip_rows, half)
-    params = pltpu.CompilerParams(vmem_limit_bytes=48 << 20)
-
-    def cost(count, size):
-        return pl.CostEstimate(
-            flops=2 * rows * count * width * half, bytes_accessed=size << 20, transcendentals=0
-        )
-
-    early = pl.pallas_call(
-        early_keys_kernel,
-        out_shape=jax.ShapeDtypeStruct((rows, half), jnp.float32),
-        in_specs=[smem] + [anywhere] * 7,
+    ny, nzr, nzq, chip_rows, half = first_rows[0].shape
+    common = dict(
         out_specs=vmem,
-        scratch_shapes=[
-            pltpu.VMEM((3, rows, width), jnp.bfloat16),
-            pltpu.VMEM((3, *block), jnp.bfloat16),
-            pltpu.SemaphoreType.DMA((6, 2)),
-        ],
-        compiler_params=params,
-        cost_estimate=cost(3, 8),
-        name="early_keys",
-    )(place, *tokens, *early_rows)
-    columns = pl.pallas_call(
-        whole_heads_kernel,
-        out_shape=jax.ShapeDtypeStruct((8, live.shape[1]), jnp.float32),
-        in_specs=[smem] + [anywhere] * 6 + [vmem] * 3,
-        out_specs=vmem,
-        scratch_shapes=[
-            pltpu.VMEM((4, rows, width), jnp.bfloat16),
-            pltpu.VMEM((4, width, half), jnp.bfloat16),
-            pltpu.SemaphoreType.DMA((4, 3)),
-        ],
-        compiler_params=params,
-        cost_estimate=cost(4, 9),
-        name="whole_heads",
-    )(place, *tokens, whole_rows, dec, gain, live)
+        compiler_params=pltpu.CompilerParams(vmem_limit_bytes=48 << 20),
+        cost_estimate=pl.CostEstimate(
+            flops=2 * rows * ny * width * half, bytes_accessed=9 << 20, transcendentals=0
+        ),
+    )
+    columns = pltpu.VMEM((8, live.shape[1]), jnp.float32)
+    scratch = [
+        pltpu.VMEM((ny, rows, width), jnp.bfloat16),
+        pltpu.VMEM((ny, nzq, nzr, 2, chip_rows, half), jnp.bfloat16),
+        pltpu.SemaphoreType.DMA((8, 2)),
+    ]
+    first = pl.pallas_call(
+        first_heads_kernel,
+        out_shape=jax.ShapeDtypeStruct(columns.shape, jnp.float32),
+        in_specs=[smem] + [anywhere] * 7 + [vmem] * 3,
+        scratch_shapes=scratch,
+        name="first_heads",
+        **common,
+    )(place, *tokens, *first_rows, dec, gain, live)
     return pl.pallas_call(
-        late_heads_kernel,
+        last_heads_kernel,
         out_shape=jax.ShapeDtypeStruct((32, 2 * LANES), jnp.float32),
-        in_specs=[smem] + [anywhere] * 7 + [vmem] * 6,
-        out_specs=vmem,
-        scratch_shapes=[
-            pltpu.VMEM((rows, width), jnp.bfloat16),
-            pltpu.VMEM(block, jnp.bfloat16),
-            pltpu.VMEM((8, live.shape[1]), jnp.float32),
-            pltpu.SemaphoreType.DMA((2, 2)),
-        ],
-        compiler_params=params,
-        cost_estimate=cost(1, 4),
-        name="late_heads",
-    )(place, *tokens, *late_rows, early, columns, dec, gain, live, scores)
+        in_specs=[smem] + [anywhere] * 7 + [vmem] * 5,
+        scratch_shapes=[columns] + scratch,
+        name="last_heads",
+        **common,
+    )(place, *tokens, *last_rows, dec, gain, live, first, scores)
 
 
 def scores_kernel(place, packed, proj, emb, chosen, state, slots, rows, unit, scale, ordered, unit_v, ids_v):
@@ -382,28 +340,22 @@
         far_low, far_high = shift(after[:mid], "reader", 1), shift(before[mid:], "reader", -1)
         tokens = (own, after, far_low, far_high, before)
 
-    rows_here, half = key_proj.shape[0], key_proj.shape[1] // 2
-    ids_high = (passage_id // 256).astype(jnp.bfloat16)
-    ids_low = (passage_id % 256).astype(jnp.bfloat16)
-    gap = ((0, 0), (0, LANES // 2 - topk))
-    coded = jnp.concatenate([query_feat, jnp.pad(ids_high, gap), jnp.pad(ids_low, gap)], axis=1)
-    coded = jnp.pad(coded, ((0, 0), (0, -coded.shape[1] % (rows_here * 4)))).reshape(rows_here, -1)
-    beside = coded.shape[1]
-    coded = jnp.pad(coded, ((0, 0), (0, LANES - beside)))
+    half = key_proj.shape[1] // 2
     with jax.named_scope("gather_key_proj"):
-        whole_rows = lax.all_gather(key_proj[:, half:], INDEX)
-        whole_rows = whole_rows.reshape(ny, -1, half)
-        first = send_all(jnp.concatenate([key_proj[:, :half], coded], axis=1), Z)
-        coded = first[:, :, half : half + beside].reshape(nz, -1)
-        own = first[:, :, :half]
-        after, before = shift(own, "y", 1), shift(own, "y", -1)
-        early_rows = jnp.stack([own, after, before])
-        early_rows = [early_rows, shift(early_rows, "core", 1)]
-        late_rows = jnp.concatenate([shift(after[:8], "y", 1), shift(before[8:], "y", -1)])
-        late_rows = [late_rows, shift(late_rows, "core", 1)]
+        rows = lax.all_gather(key_proj, "zq")
+        rows, query_feat, passage_id = lax.optimization_barrier((rows, query_feat, passage_id))
+        rows = lax.all_gather(rows, "zr")
+        heads = []
+        for columns in (rows[..., :half], rows[..., half:]):
+            own = lax.all_gather(columns, "y")
+            heads.append((own, shift(own, "core", 1)))
 
     with jax.named_scope("gather_queries"):
-        packed = send_all(coded[:, : width + LANES], NEAR)
+        ids_high = (passage_id // 256).astype(jnp.bfloat16)
+        ids_low = (passage_id % 256).astype(jnp.bfloat16)
+        gap = ((0, 0), (0, LANES // 2 - topk))
+        coded = [query_feat, jnp.pad(ids_high, gap), jnp.pad(ids_low, gap)]
+        packed = send_all(send_all(jnp.concatenate(coded, axis=1)[0], Z), NEAR)
 
     cols = width // nx
     six = width // n_index
@@ -466,11 +418,9 @@
         positions = lax.broadcasted_iota(jnp.int32, (group, topk, plen), 2)
         live = (positions < passage_len[:, :, None]).reshape(group, topk * plen)
         packet = attention_packet(
-            jnp.stack([y, core, r]).astype(jnp.int32),
+            jnp.stack([core, r]).astype(jnp.int32),
             tokens,
-            early_rows,
-            late_rows,
-            whole_rows,
+            *heads,
             dec_unit.reshape(group, answer, feats_here),
             key_gain.astype(jnp.float32).reshape(1, feats_here),
             live.astype(jnp.float32),

time: 276 us -> 340 us (1.23)
  waiting for transfers between devices: 60.8 us -> 133 us
  blocking collectives: 43.6 us -> 67.5 us
  starting transfers between devices: 75.5 us -> 61.8 us
  local copies, waits for them, and re-layouts: 28.6 us -> 20.2 us
  other arithmetic: 15.3 us -> 8.35 us
    all_gather x1 -> x3, waiting for transfers between devices: 6.53 us -> 79.7 us  [the longest x2 44.9 us: body(): own = lax.all_gather(columns, 'y')]
    all_gather x0 -> x1, blocking collectives: none -> 27.8 us  [body(): rows = lax.all_gather(key_proj, 'zq')]
    ppermute x11 -> x7, starting transfers between devices: 32.2 us -> 20 us  [shift(): return lax.ppermute(x, axis, [((i + step) % size, i) for i in range(size)])]
    all_to_all x3, waiting for transfers between devices: 25.4 us -> 13.7 us  [send_all(): lax.all_to_all(jnp.broadcast_to(x[None], (size, *x.shape)), axis, 0, 0, t...]
    ppermute x11 -> x7, waiting for transfers between devices: 3.84 us -> 10 us  [shift(): return lax.ppermute(x, axis, [((i + step) % size, i) for i in range(size)])]
    all_to_all x3, starting transfers between devices: 28 us -> 22.5 us  [send_all(): lax.all_to_all(jnp.broadcast_to(x[None], (size, *x.shape)), axis, 0, 0, t...]
    all_to_all x1, starting transfers between devices: 7.62 us -> 12.3 us  [body(): state = merge_all(lax.all_to_all(state, Z, 0, 0, tiled=True))]
    all_to_all x1, blocking collectives: 21.2 us -> 16.7 us  [body(): coef = lax.all_to_all(coef, Z, 0, 0, tiled=True).reshape(n_index, LANES)]
  transfers between devices with their start and end apart: 18 -> 16, of which waited for: 8 -> 10; matrix products, arithmetic and copies ran while one was open for 12% -> 5% of each run, Pallas kernels for 7% -> 4%
where the time goes in v5:
time: 340 us; the launch traced here: 338 us
  waiting for transfers between devices  133 us (39%)
  blocking collectives  67.5 us (20%)
  starting transfers between devices  61.8 us (18%)
  Pallas kernels  32.3 us (9%)
  local copies, waits for them, and re-layouts  20.2 us (6%)
  between operations  14.9 us (4%)
  other arithmetic  8.35 us (2%)
    all_gather x2, waiting for transfers between devices, body(): own = lax.all_gather(columns, 'y')  44.9 us
    all_gather x1, waiting for transfers between devices, body(): rows = lax.all_gather(rows, 'zr')  34.7 us
    all_gather x1, blocking collectives, body(): rows = lax.all_gather(key_proj, 'zq')  27.8 us
    all_to_all x3, starting transfers between devices, send_all(): lax.all_to_all(jnp.broadcast_to(x[None], (size, *x.shape)), axis, 0, 0, t...  22.5 us
    ppermute x7, starting transfers between devices, shift(): return lax.ppermute(x, axis, [((i + step) % size, i) for i in range(size)])  20 us
    all_to_all x1, blocking collectives, body(): coef = lax.all_to_all(coef, Z, 0, 0, tiled=True).reshape(n_index, LANES)  16.7 us
    all_to_all x3, waiting for transfers between devices, send_all(): lax.all_to_all(jnp.broadcast_to(x[None], (size, *x.shape)), axis, 0, 0, t...  13.7 us
    all_to_all x1, starting transfers between devices, body(): state = merge_all(lax.all_to_all(state, Z, 0, 0, tiled=True))  12.3 us
  transfers between devices with their start and end apart: 16, of which 10 were waited for; matrix products, arithmetic and copies ran while one was open for 5% of the time, Pallas kernels for 4%

profile of v5, /device:TPU:6, one launch (start us, length us, event | category | flops | bytes accessed | tf_op | source)
XLA Modules:
  0.0 337.7 jit_solution(3740497673933292397)
XLA Ops:
  7.2 27.8 %all-gather = bf16[128,1024]{1,0:T(8,128)(2,1)} all-gather(bf16[32,1024]{1,0:T(8,128)(2,1)} %param.19), channel_id=2, replica_groups=mesh['y'=4,'zq'=4,'zr'=4,'core'=2,'reader'=4] {'zq'}, dimensions={0}, use_global_device_ids=true | all-gather | bytes 327680 | tf_op jit(solution)/shard_map/gather_key_proj/all_gather | solution.py:345
  35.1 34.7 %all-gather.8.cloned.1.call-done = bf16[16,32,1024]{2,1,0:T(8,128)(2,1)} async-done(((bf16[4,32,1024]{2,1,0:T(8,128)(2,1)}), bf16[16,32,1024]{2,1,0:T(8,128)(2,1)}) %all-gather.8.cloned.1.call-update) | async-done | bytes 1048592 | tf_op jit(solution)/shard_map/gather_key_proj/all_gather | solution.py:347
  69.8 2.3 fusion.32
  72.9 2.8 collective-permute-start
  75.7 4.3 %collective-permute-start.2 = (bf16[640,1024]{1,0:T(8,128)(2,1)}, bf16[640,1024]{1,0:T(8,128)(2,1)}, u32[]{:S(2)}, u32[]{:S(2)}) collective-permute-start(bf16[640,1024]{1,0:T(8,128)(2,1)} %bitcast.2.refs_0_), channel_id=1, source_target_pairs={{3,0},{0,1},{1,2},{2,3},{7,4},{4,5},{5,6},{6,7},{11,8},{8,9},{9,10... | collective-permute-start | bytes 3932168 | tf_op jit(solution)/shard_map/gather_enc_out/ppermute | solution.py:28
  80.7 0.8 reduce.21
  82.2 10.0 %all-to-all-start = ((bf16[16,2,448]{2,1,0:T(2,128)(2,1)}), bf16[16,2,448]{2,1,0:T(2,128)(2,1)S(1)}, u32[]{:S(2)}, u32[]{:S(2)}) async-start(bf16[16,2,448]{2,1,0:T(2,128)(2,1)} %reshape.304), calls=%async_computation | async-start | bytes 65536 | tf_op jit(solution)/shard_map/gather_queries/all_to_all | solution.py:33
  93.3 11.5 %all-to-all-done = bf16[16,2,448]{2,1,0:T(2,128)(2,1)S(1)} async-done(((bf16[16,2,448]{2,1,0:T(2,128)(2,1)}), bf16[16,2,448]{2,1,0:T(2,128)(2,1)S(1)}, u32[]{:S(2)}, u32[]{:S(2)}) %all-to-all-start) | async-done | bytes 28704 | tf_op jit(solution)/shard_map/gather_queries/all_to_all | solution.py:33
  105.0 1.0 broadcast_in_dim.14
  105.9 7.2 %all-to-all-start.1 = ((bf16[32,16,896]{2,1,0:T(8,128)(2,1)}), bf16[32,16,896]{2,1,0:T(8,128)(2,1)S(1)}, u32[]{:S(2)}, u32[]{:S(2)}) async-start(bf16[32,16,896]{2,1,0:T(8,128)(2,1)} %broadcast_in_dim.14), calls=%async_computation.1 | async-start | bytes 1835008 | tf_op jit(solution)/shard_map/gather_queries/all_to_all | solution.py:33
  113.5 2.1 collective-permute-start.5
  115.6 44.9 %all-gather.10.cloned.1.call-done = bf16[16,4,32,512]{3,2,1,0:T(8,128)(2,1)} async-done(((bf16[4,4,32,512]{3,2,1,0:T(8,128)(2,1)}), bf16[16,4,32,512]{3,2,1,0:T(8,128)(2,1)}) %all-gather.10.cloned.1.call-update) | async-done | bytes 2097168 | tf_op jit(solution)/shard_map/gather_key_proj/all_gather | solution.py:350
  160.5 1.9 collective-permute-start.4
  162.5 1.3 copy-done.7
  163.7 6.0 %scores.1 = (f32[128,128]{1,0:T(8,128)S(1)}, s32[128,128]{1,0:T(8,128)S(1)}, f32[512,192]{1,0:T(8,128)S(1)}, f32[512,192]{1,0:T(8,128)S(1)}, f32[512,1]{1,0:T(8,128)S(1)}, /*index=5*/bf16[768,512]{1,0:T(8,128)(2,1)S(1)}) custom-call(s32[2]{0:T(128)S(1)} %pad_add_fusion.1.place, bf16[32,16,896]{2,1,0:T(8,128)(2,1)S(1)} %all-to-all-done.1.packed, ...), custom_call_target="tpu_custom_call" | custom-call | flops 4294967296 | bytes 8388608 | tf_op jit(solution)/shard_map/scores/scores/pallas_call | solution.py:371
  169.7 0.8 copy-done
  170.5 0.7 copy-done.2
  172.5 3.3 all-to-all-start.2
  175.9 5.5 %all-to-all-done.2 = f32[8,16,128]{2,1,0:T(8,128)S(1)} async-done(((f32[8,16,128]{2,1,0:T(8,128)}), f32[8,16,128]{2,1,0:T(8,128)S(1)}, u32[]{:S(2)}, u32[]{:S(2)}) %all-to-all-start.2) | async-done | bytes 65568 | tf_op jit(solution)/shard_map/reduce_scores/all_to_all | solution.py:400
  182.0 12.3 %all-to-all-start.3 = ((f32[16,1,128]{2,1,0:T(1,128)}), f32[16,1,128]{2,1,0:T(1,128)S(1)}, u32[]{:S(2)}, u32[]{:S(2)}) async-start(f32[16,1,128]{2,1,0:T(1,128)} %broadcast_select_fusion), calls=%async_computation.3 | async-start | bytes 16384 | tf_op jit(solution)/shard_map/reduce_scores/all_to_all | solution.py:401
  195.0 0.7 and_reduce_fusion
  195.8 10.9 %all-to-all-done.3 = f32[16,1,128]{2,1,0:T(1,128)S(1)} async-done(((f32[16,1,128]{2,1,0:T(1,128)}), f32[16,1,128]{2,1,0:T(1,128)S(1)}, u32[]{:S(2)}, u32[]{:S(2)}) %all-to-all-start.3) | async-done | bytes 8224 | tf_op jit(solution)/shard_map/reduce_scores/all_to_all | solution.py:401
  206.7 2.0 slice.61
  208.7 2.5 collective-permute-start.1
  211.2 2.0 slice.62
  213.1 4.5 %collective-permute-start.3 = (bf16[320,1024]{1,0:T(8,128)(2,1)}, bf16[320,1024]{1,0:T(8,128)(2,1)S(1)}, u32[]{:S(2)}, u32[]{:S(2)}) collective-permute-start(bf16[320,1024]{1,0:T(8,128)(2,1)} %slice.62), channel_id=1, source_target_pairs={{3,0},{0,1},{1,2},{2,3},{7,4},{4,5},{5,6},{6,7},{11,8},{8,9},{9,10... | collective-permute-start | bytes 1966088 | tf_op jit(solution)/shard_map/gather_enc_out/ppermute | solution.py:28
  218.3 1.3 fusion.26
  219.7 1.3 broadcast_select_fusion.1
  221.0 0.9 scatter.9.refs_11_
  221.9 5.0 %collective-permute-done.1.refs_2_ = bf16[320,1024]{1,0:T(8,128)(2,1)S(1)} collective-permute-done((bf16[320,1024]{1,0:T(8,128)(2,1)}, bf16[320,1024]{1,0:T(8,128)(2,1)S(1)}, u32[]{:S(2)}, u32[]{:S(2)}) %collective-permute-start.1) | collective-permute-done | bytes 655392 | tf_op jit(solution)/shard_map/gather_enc_out/ppermute | solution.py:28
  226.9 3.3 collective-permute-done.3.refs_3_
  230.2 8.9 %first_heads.1.refs_10_ = f32[8,160]{1,0:T(8,128)S(1)} custom-call(s32[2]{0:T(128)S(1)} %pad_add_fusion.place, bf16[640,1024]{1,0:T(8,128)(2,1)} %bitcast.2.refs_0_, bf16[640,1024]{1,0:T(8,128)(2,1)} %collective-permute-done.refs_1_, bf16[320,1024]{1,0:T(8,128)(2,1)S(1)} %collective-permute-done.1.refs_2_, ...), custom_call_target="tpu_custom_call" | custom-call | flops 2684354560 | bytes 9437184 | tf_op jit(solution)/shard_map/attention/first_heads/pallas_call | solution.py:178
  239.1 0.8 copy-done.8
  240.0 1.2 copy-done.9
  241.1 9.3 %last_heads.1 = f32[32,256]{1,0:T(8,128)S(1)} custom-call(s32[2]{0:T(128)S(1)} %pad_add_fusion.place, bf16[640,1024]{1,0:T(8,128)(2,1)} %bitcast.2.refs_0_, bf16[640,1024]{1,0:T(8,128)(2,1)} %collective-permute-done.refs_1_, bf16[320,1024]{1,0:T(8,128)(2,1)S(1)} %collective-permute-done.1.refs_2_, bf16[320,1024]{1,0:T(8,128)(2,1)S(1)} %copy-done.9, ...), custom_call_target="tpu_custom_call" | custom-call | flops 2684354560 | bytes 9437184 | tf_op jit(solution)/shard_map/attention/last_heads/pallas_call | solution.py:186
  250.4 11.9 %all_to_all.51 = f32[32,1,256]{2,1,0:T(1,128)S(1)} all-to-all(f32[32,1,256]{2,1,0:T(1,128)S(1)} %copy.20), channel_id=1, replica_groups=mesh['y'=4,'zq'=4,'zr'=4,'core'=2,'reader'=4] {'reader','y','core'}, dimensions={0} | all-to-all | bytes 65536 | tf_op jit(solution)/shard_map/targets/all_to_all | solution.py:431
  262.9 1.6 coef.1
  264.5 16.7 %all_to_all.52 = f32[16,8,128]{2,1,0:T(8,128)S(1)} all-to-all(f32[16,8,128]{2,1,0:T(8,128)} %coef.1), channel_id=1, replica_groups=mesh['y'=4,'zq'=4,'zr'=4,'core'=2,'reader'=4] {'zq','zr'}, dimensions={0} | all-to-all | bytes 131072 | tf_op jit(solution)/shard_map/targets/all_to_all | solution.py:439
  281.3 6.6 %gradient.1 = (f32[384,192]{1,0:T(8,128)S(1)}, f32[384,192]{1,0:T(8,128)S(1)}) custom-call(f32[128,128]{1,0:T(8,128)S(1)} %bitcast.33, s32[128,128]{1,0:T(8,128)S(1)} %copy-done.5, f32[512,192]{1,0:T(8,128)S(1)} %get-tuple-element.44.refs_0_, f32[512,192]{1,0:T(8,128)S(1)} %copy-done.1, f32[512,1]{1,0:T(8,128)S(1)} %copy-done.3, ...), custom_call_target="tpu_custom_call" | custom-call | tf_op jit(solution)/shard_map/gradient/gradient/pallas_call | solution.py:443
  287.9 1.9 collective-permute-start.6
  289.9 1.7 collective-permute-done.6
  291.6 11.0 %all_to_all.53 = f32[4,96,192]{2,1,0:T(8,128)S(1)} all-to-all(f32[4,96,192]{2,1,0:T(8,128)S(1)} %bitcast.38), channel_id=1, replica_groups=mesh['y'=4,'zq'=4,'zr'=4,'core'=2,'reader'=4] {'y'}, dimensions={0} | all-to-all | bytes 589824 | tf_op jit(solution)/shard_map/reduce_gradient/all_to_all | solution.py:459
  303.4 3.5 %all-to-all-start.7 = ((f32[16,6,192]{2,1,0:T(8,128)}), f32[16,6,192]{2,1,0:T(8,128)S(1)}, u32[]{:S(2)}, u32[]{:S(2)}) async-start(f32[16,6,192]{2,1,0:T(8,128)} %reshape.295), calls=%async_computation.7 | async-start | bytes 262144 | tf_op jit(solution)/shard_map/reduce_gradient/all_to_all | solution.py:461
  308.1 0.8 dynamic-slice_reduce_fusion
  308.9 12.1 %all-to-all-done.7 = f32[16,6,192]{2,1,0:T(8,128)S(1)} async-done(((f32[16,6,192]{2,1,0:T(8,128)}), f32[16,6,192]{2,1,0:T(8,128)S(1)}, u32[]{:S(2)}, u32[]{:S(2)}) %all-to-all-start.7) | async-done | bytes 73760 | tf_op jit(solution)/shard_map/reduce_gradient/all_to_all | solution.py:461
  321.7 5.4 %all-to-all-start.8 = ((f32[4,6,192]{2,1,0:T(8,128)}), f32[4,6,192]{2,1,0:T(8,128)S(1)}, u32[]{:S(2)}, u32[]{:S(2)}) async-start(f32[4,6,192]{2,1,0:T(8,128)} %broadcast_in_dim.15), calls=%async_computation.8 | async-start | bytes 65536 | tf_op jit(solution)/shard_map/reduce_gradient/all_to_all | solution.py:33
  327.1 1.2 log_bitcast_fusion
  328.2 2.2 all-to-all-done.8
  (80 shorter events, 10.3 us)
Async XLA Ops:
  7.2 62.7 %all-gather.8.cloned.1.call-start = ((), (), s32[]{:S(2)}) async-start(), calls=%async_computation.9 | async-start | bytes 1310720 | tf_op jit(solution)/shard_map/gather_key_proj/all_gather | solution.py:347
  35.1 78.4 %all-gather.12.cloned.1.call-start = ((), (), s32[]{:S(2)}) async-start(), calls=%async_computation.11 | async-start | bytes 2621440 | tf_op jit(solution)/shard_map/gather_key_proj/all_gather | solution.py:350
  69.8 10.2 %copy-start.14 = (s32[1,20]{1,0:T(1,128)S(1)}, s32[1,20]{1,0:T(1,128)}, u32[]{:S(2)}) copy-start(s32[1,20]{1,0:T(1,128)} %param.16) | copy-start | bytes 244
  69.8 10.2 %copy-start.11 = (bf16[1,768]{1,0:T(2,128)(2,1)S(1)}, bf16[1,768]{1,0:T(2,128)(2,1)}, u32[]{:S(2)}) copy-start(bf16[1,768]{1,0:T(2,128)(2,1)} %param.14) | copy-start | bytes 4612
  69.8 22.4 %copy-start.10 = (bf16[4,16,1024]{2,1,0:T(8,128)(2,1)S(1)}, bf16[4,16,1024]{2,1,0:T(8,128)(2,1)}, u32[]{:S(2)}) copy-start(bf16[4,16,1024]{2,1,0:T(8,128)(2,1)} %param.21) | copy-start | bytes 393220
  72.2 88.3 %all-gather.10.cloned.1.call-start = ((), (), s32[]{:S(2)}) async-start(), calls=%async_computation.10 | async-start | bytes 2621440 | tf_op jit(solution)/shard_map/gather_key_proj/all_gather | solution.py:350
  72.9 133.8 %collective-permute-start = (bf16[640,1024]{1,0:T(8,128)(2,1)}, bf16[640,1024]{1,0:T(8,128)(2,1)}, u32[]{:S(2)}, u32[]{:S(2)}) collective-permute-start(bf16[640,1024]{1,0:T(8,128)(2,1)} %bitcast.2.refs_0_), channel_id=1, source_target_pairs={{1,0},{2,1},{3,2},{0,3},{5,4},{6,5},{7,6},{4,7},{9,8},{10,9},{11,1... | collective-permute-start | bytes 3932168 | tf_op jit(solution)/shard_map/gather_enc_out/ppermute | solution.py:28
  75.7 135.5 %collective-permute-start.2 = (bf16[640,1024]{1,0:T(8,128)(2,1)}, bf16[640,1024]{1,0:T(8,128)(2,1)}, u32[]{:S(2)}, u32[]{:S(2)}) collective-permute-start(bf16[640,1024]{1,0:T(8,128)(2,1)} %bitcast.2.refs_0_), channel_id=1, source_target_pairs={{3,0},{0,1},{1,2},{2,3},{7,4},{4,5},{5,6},{6,7},{11,8},{8,9},{9,10... | collective-permute-start | bytes 3932168 | tf_op jit(solution)/shard_map/gather_enc_out/ppermute | solution.py:28
  82.2 22.6 %all-to-all-start = ((bf16[16,2,448]{2,1,0:T(2,128)(2,1)}), bf16[16,2,448]{2,1,0:T(2,128)(2,1)S(1)}, u32[]{:S(2)}, u32[]{:S(2)}) async-start(bf16[16,2,448]{2,1,0:T(2,128)(2,1)} %reshape.304), calls=%async_computation | async-start | bytes 65536 | tf_op jit(solution)/shard_map/gather_queries/all_to_all | solution.py:33
  92.2 0.8 copy-start.12
  105.9 56.5 %all-to-all-start.1 = ((bf16[32,16,896]{2,1,0:T(8,128)(2,1)}), bf16[32,16,896]{2,1,0:T(8,128)(2,1)S(1)}, u32[]{:S(2)}, u32[]{:S(2)}) async-start(bf16[32,16,896]{2,1,0:T(8,128)(2,1)} %broadcast_in_dim.14), calls=%async_computation.1 | async-start | bytes 1835008 | tf_op jit(solution)/shard_map/gather_queries/all_to_all | solution.py:33
  113.5 116.7 %collective-permute-start.5 = (bf16[4,4,4,32,512]{4,3,2,1,0:T(8,128)(2,1)}, bf16[4,4,4,32,512]{4,3,2,1,0:T(8,128)(2,1)}, u32[]{:S(2)}, u32[]{:S(2)}) collective-permute-start(bf16[4,4,4,32,512]{4,3,2,1,0:T(8,128)(2,1)} %bitcast.48), channel_id=1, source_target_pairs={{4,0},{0,4},{5,1},{1,5},{6,2},{2,6},{7,3},{3,7},{12,8},{8,12},{13,... | collective-permute-start | bytes 6291464 | tf_op jit(solution)/shard_map/gather_key_proj/ppermute | solution.py:28
  160.5 79.4 %collective-permute-start.4 = (bf16[4,4,4,32,512]{4,3,2,1,0:T(8,128)(2,1)}, bf16[4,4,4,32,512]{4,3,2,1,0:T(8,128)(2,1)}, u32[]{:S(2)}, u32[]{:S(2)}) collective-permute-start(bf16[4,4,4,32,512]{4,3,2,1,0:T(8,128)(2,1)} %bitcast.50), channel_id=1, source_target_pairs={{4,0},{0,4},{5,1},{1,5},{6,2},{2,6},{7,3},{3,7},{12,8},{8,12},{13,... | collective-permute-start | bytes 6291464 | tf_op jit(solution)/shard_map/gather_key_proj/ppermute | solution.py:28
  162.5 1.3 copy-start.7
  163.7 31.3 %copy-start.13 = (bf16[1024]{0:T(1024)(128)(2,1)S(1)}, bf16[1024]{0:T(1024)(128)(2,1)}, u32[]{:S(2)}) copy-start(bf16[1024]{0:T(1024)(128)(2,1)} %param.20) | copy-start | bytes 6148
  169.7 0.8 copy-start
  170.5 0.7 copy-start.2
  171.3 0.6 copy-start.4
  171.9 0.6 copy-start.6
  172.5 8.9 %all-to-all-start.2 = ((f32[8,16,128]{2,1,0:T(8,128)}), f32[8,16,128]{2,1,0:T(8,128)S(1)}, u32[]{:S(2)}, u32[]{:S(2)}) async-start(f32[8,16,128]{2,1,0:T(8,128)} %bitcast.34), calls=%async_computation.2 | async-start | bytes 131072 | tf_op jit(solution)/shard_map/reduce_scores/all_to_all | solution.py:400
  182.0 24.7 %all-to-all-start.3 = ((f32[16,1,128]{2,1,0:T(1,128)}), f32[16,1,128]{2,1,0:T(1,128)S(1)}, u32[]{:S(2)}, u32[]{:S(2)}) async-start(f32[16,1,128]{2,1,0:T(1,128)} %broadcast_select_fusion), calls=%async_computation.3 | async-start | bytes 16384 | tf_op jit(solution)/shard_map/reduce_scores/all_to_all | solution.py:401
  208.7 18.3 %collective-permute-start.1 = (bf16[320,1024]{1,0:T(8,128)(2,1)}, bf16[320,1024]{1,0:T(8,128)(2,1)S(1)}, u32[]{:S(2)}, u32[]{:S(2)}) collective-permute-start(bf16[320,1024]{1,0:T(8,128)(2,1)} %slice.61), channel_id=1, source_target_pairs={{1,0},{2,1},{3,2},{0,3},{5,4},{6,5},{7,6},{4,7},{9,8},{10,9},{11,1... | collective-permute-start | bytes 1966088 | tf_op jit(solution)/shard_map/gather_enc_out/ppermute | solution.py:28
  213.1 17.0 %collective-permute-start.3 = (bf16[320,1024]{1,0:T(8,128)(2,1)}, bf16[320,1024]{1,0:T(8,128)(2,1)S(1)}, u32[]{:S(2)}, u32[]{:S(2)}) collective-permute-start(bf16[320,1024]{1,0:T(8,128)(2,1)} %slice.62), channel_id=1, source_target_pairs={{3,0},{0,1},{1,2},{2,3},{7,4},{4,5},{5,6},{6,7},{11,8},{8,9},{9,10... | collective-permute-start | bytes 1966088 | tf_op jit(solution)/shard_map/gather_enc_out/ppermute | solution.py:28
  239.1 0.9 copy-start.8
  239.9 41.4 %copy-start.1 = (f32[512,192]{1,0:T(8,128)S(1)}, f32[512,192]{1,0:T(8,128)}, u32[]{:S(2)}) copy-start(f32[512,192]{1,0:T(8,128)} %copy-done) | copy-start | bytes 1179652
  239.9 41.4 %copy-start.3 = (f32[512,1]{1,0:T(8,128)S(1)}, f32[512,1]{1,0:T(8,128)}, u32[]{:S(2)}) copy-start(f32[512,1]{1,0:T(8,128)} %copy-done.2) | copy-start | bytes 6148
  239.9 41.4 %copy-start.5 = (s32[128,128]{1,0:T(8,128)S(1)}, s32[128,128]{1,0:T(8,128)}, u32[]{:S(2)}) copy-start(s32[128,128]{1,0:T(8,128)} %copy-done.4) | copy-start | bytes 196612
  239.9 1.2 copy-start.9
  287.9 3.6 %collective-permute-start.6 = (f32[384,192]{1,0:T(8,128)S(1)}, f32[384,192]{1,0:T(8,128)S(1)}, u32[]{:S(2)}, u32[]{:S(2)}) collective-permute-start(f32[384,192]{1,0:T(8,128)S(1)} %get-tuple-element.49), channel_id=1, source_target_pairs={{4,0},{0,4},{5,1},{1,5},{6,2},{2,6},{7,3},{3,7},{12,8},{8,12},{13,... | collective-permute-start | bytes 884744 | tf_op jit(solution)/shard_map/reduce_gradient/ppermute | solution.py:28
  303.4 17.7 %all-to-all-start.7 = ((f32[16,6,192]{2,1,0:T(8,128)}), f32[16,6,192]{2,1,0:T(8,128)S(1)}, u32[]{:S(2)}, u32[]{:S(2)}) async-start(f32[16,6,192]{2,1,0:T(8,128)} %reshape.295), calls=%async_computation.7 | async-start | bytes 262144 | tf_op jit(solution)/shard_map/reduce_gradient/all_to_all | solution.py:461
  321.7 8.7 %all-to-all-start.8 = ((f32[4,6,192]{2,1,0:T(8,128)}), f32[4,6,192]{2,1,0:T(8,128)S(1)}, u32[]{:S(2)}, u32[]{:S(2)}) async-start(f32[4,6,192]{2,1,0:T(8,128)} %broadcast_in_dim.15), calls=%async_computation.8 | async-start | bytes 65536 | tf_op jit(solution)/shard_map/reduce_gradient/all_to_all | solution.py:33
Sparse Core Ops, SparseCore 0:
  35.2 34.5 all-gather.7
  72.3 37.5 all-gather.11
  112.1 48.4 all-gather.9

commit v6 on v4

--- a/solution.py
+++ b/solution.py
@@ -63,22 +63,23 @@
     ]
 
 
-def row_copies(core, own, other, target, sems):
-    copies = [
-        pltpu.make_async_copy(own, target.at[:, core], sems.at[0]),
-        pltpu.make_async_copy(other, target.at[:, 1 - core], sems.at[1]),
-    ]
-    for copy in copies:
-        copy.start()
-    return copies
+def row_copies(place, own, other, target, sem):
+    zr, core = place[1], place[2]
+    for residue in range(4):
+        to = target.at[:, (zr + residue) % 4]
+        four = pl.ds(4 * residue, 4)
+        pltpu.make_async_copy(own.at[four], to.at[:, core], sem).start()
+        pltpu.make_async_copy(other.at[four], to.at[:, 1 - core], sem).start()
+    return [pltpu.make_async_copy(target, target, sem)]
 
 
 def early_keys_kernel(place, *refs):
-    tokens, (own, other), (keys, token_v, weight_v, sems) = refs[:5], refs[5:7], refs[7:]
-    y, core, r = place[0], place[1], place[2]
+    tokens, rows, (keys, token_v, weight_v, sems) = refs[:5], refs[5:11], refs[11:]
+    y, r = place[0], place[3]
     copies = []
     for slot, ahead in enumerate(EARLY):
-        waits = row_copies(core, own.at[slot], other.at[slot], weight_v.at[slot], sems.at[slot])
+        own, other = rows[2 * slot], rows[2 * slot + 1]
+        waits = row_copies(place, own, other, weight_v.at[slot], sems.at[slot, 0])
         target = token_v.at[slot]
         waits += token_copies(r, (y + ahead) % 4, tokens, target, sems.at[3 + slot])
         copies.append(waits)
@@ -89,7 +90,7 @@
         @pl.loop(0, keys.shape[1] // TILE)
         def _(t):
             cols = pl.ds(pl.multiple_of(t * TILE, TILE), TILE)
-            term = dot32(token_v[slot], weight_v[slot, :, :, :, cols].reshape(-1, TILE))
+            term = dot32(token_v[slot], weight_v[slot, :, :, :, :, cols].reshape(-1, TILE))
             if slot == 0:
                 keys[:, cols] = term
             else:
@@ -125,42 +126,32 @@
         column_v[g : g + 1, :] += jnp.sum(weight, axis=0, keepdims=True)
 
 
-def whole_heads_kernel(place, *refs):
-    tokens, refs = refs[:5], refs[5:]
-    rows, dec, gain, live, columns, token_v, weight_v, sems = refs
-    r = place[2]
-    copies = []
-    for c in range(4):
-        copy = pltpu.make_async_copy(rows.at[c], weight_v.at[c], sems.at[c, 2])
-        copy.start()
-        copies += [copy] + token_copies(r, c, tokens, token_v.at[c], sems.at[c])
-    columns[...] = jnp.zeros_like(columns)
-    for copy in copies:
-        copy.wait()
-
-    @pl.loop(0, weight_v.shape[2] // TILE)
-    def _(t):
-        cols = pl.ds(pl.multiple_of(t * TILE, TILE), TILE)
-        keys = dot32(token_v[0], weight_v[0, :, cols])
-        for c in range(1, 4):
-            keys += dot32(token_v[c], weight_v[c, :, cols])
-        attend(keys, weight_v.shape[2] + t * TILE, dec, gain, live, columns)
-
-
 def late_heads_kernel(place, *refs):
     tokens, (own, other), refs = refs[:5], refs[5:7], refs[7:]
-    early, columns, dec, gain, live, scores, out, token_v, weight_v, column_v, sems = refs
-    y, core, r = place[0], place[1], place[2]
-    copies = row_copies(core, own, other, weight_v, sems.at[0])
+    early, dec, gain, live, states, out, own_scores, token_v, weight_v, column_v, sems = refs
+    y, r = place[0], place[3]
+    copies = row_copies(place, own, other, weight_v, sems.at[0, 0])
     copies += token_copies(r, (y + LATE) % 4, tokens, token_v, sems.at[1])
-    column_v[...] = columns[...]
+    column_v[...] = jnp.zeros_like(column_v)
+
+    lane = lax.broadcasted_iota(jnp.int32, (1, LANES), 1)
+    found = states[...]
+    fetched = jnp.where(lane < 20, jnp.sum(found, axis=0, keepdims=True), 0.0)
+    expo = jnp.where(lane < 20, jnp.exp(fetched), 0.0)
+    total = jnp.sum(expo, axis=1, keepdims=True)
+    log_prob = fetched - jnp.log(total)
+    best = jnp.max(found, axis=0, keepdims=True)
+    own_scores[...] = jnp.broadcast_to(jnp.where(lane == 20, best, log_prob), own_scores.shape)
+    scores = expo / total + pltpu.roll(fetched, LANES // 2, 1)
+    out[:, LANES:] = jnp.broadcast_to(scores, (out.shape[0], LANES))
+
     for copy in copies:
         copy.wait()
 
     @pl.loop(0, early.shape[1] // TILE)
     def _(t):
         cols = pl.ds(pl.multiple_of(t * TILE, TILE), TILE)
-        keys = early[:, cols] + dot32(token_v[...], weight_v[:, :, :, cols].reshape(-1, TILE))
+        keys = early[:, cols] + dot32(token_v[...], weight_v[:, :, :, :, cols].reshape(-1, TILE))
         attend(keys, t * TILE, dec, gain, live, column_v)
 
     n = live.shape[1]
@@ -173,66 +164,54 @@
         ).astype(jnp.float32)
         mass += jnp.dot(column, to, precision=EXACT, preferred_element_type=jnp.float32)
     out[:, :LANES] = jnp.broadcast_to(mass[:1] / (HEADS * ANS), (out.shape[0], LANES))
-    out[:, LANES:] = jnp.broadcast_to(scores[...], (out.shape[0], LANES))
-
-
-def attention_packet(place, tokens, early_rows, late_rows, whole_rows, dec, gain, live, scores):
+
+
+def attention_packet(place, tokens, rows, dec, gain, live, states):
     vmem = pl.BlockSpec(memory_space=pltpu.VMEM)
     anywhere = pl.BlockSpec(memory_space=pl.ANY)
     smem = pl.BlockSpec(memory_space=pltpu.SMEM)
-    rows, width = tokens[0].shape
-    _, nz, chip_rows, half = early_rows[0].shape
-    block = (nz, 2, chip_rows, half)
-    params = pltpu.CompilerParams(vmem_limit_bytes=48 << 20)
+    token_rows, width = tokens[0].shape
+    block = (4, 4, 2, *rows[0][0].shape[1:])
 
     def cost(count, size):
         return pl.CostEstimate(
-            flops=2 * rows * count * width * half, bytes_accessed=size << 20, transcendentals=0
+            flops=2 * token_rows * count * width * width,
+            bytes_accessed=size << 20,
+            transcendentals=0,
         )
 
     early = pl.pallas_call(
         early_keys_kernel,
-        out_shape=jax.ShapeDtypeStruct((rows, half), jnp.float32),
-        in_specs=[smem] + [anywhere] * 7,
+        out_shape=jax.ShapeDtypeStruct((token_rows, width), jnp.float32),
+        in_specs=[smem] + [anywhere] * 11,
         out_specs=vmem,
         scratch_shapes=[
-            pltpu.VMEM((3, rows, width), jnp.bfloat16),
+            pltpu.VMEM((3, token_rows, width), jnp.bfloat16),
             pltpu.VMEM((3, *block), jnp.bfloat16),
             pltpu.SemaphoreType.DMA((6, 2)),
         ],
-        compiler_params=params,
-        cost_estimate=cost(3, 8),
+        compiler_params=pltpu.CompilerParams(vmem_limit_bytes=24 << 20),
+        cost_estimate=cost(3, 13),
         name="early_keys",
-    )(place, *tokens, *early_rows)
-    columns = pl.pallas_call(
-        whole_heads_kernel,
-        out_shape=jax.ShapeDtypeStruct((8, live.shape[1]), jnp.float32),
-        in_specs=[smem] + [anywhere] * 6 + [vmem] * 3,
-        out_specs=vmem,
-        scratch_shapes=[
-            pltpu.VMEM((4, rows, width), jnp.bfloat16),
-            pltpu.VMEM((4, width, half), jnp.bfloat16),
-            pltpu.SemaphoreType.DMA((4, 3)),
-        ],
-        compiler_params=params,
-        cost_estimate=cost(4, 9),
-        name="whole_heads",
-    )(place, *tokens, whole_rows, dec, gain, live)
+    )(place, *tokens, *[part for ahead in EARLY for part in rows[ahead]])
     return pl.pallas_call(
         late_heads_kernel,
-        out_shape=jax.ShapeDtypeStruct((32, 2 * LANES), jnp.float32),
-        in_specs=[smem] + [anywhere] * 7 + [vmem] * 6,
-        out_specs=vmem,
+        out_shape=(
+            jax.ShapeDtypeStruct((32, 2 * LANES), jnp.float32),
+            jax.ShapeDtypeStruct((8, LANES), jnp.float32),
+        ),
+        in_specs=[smem] + [anywhere] * 7 + [vmem] * 5,
+        out_specs=(vmem, vmem),
         scratch_shapes=[
-            pltpu.VMEM((rows, width), jnp.bfloat16),
+            pltpu.VMEM((token_rows, width), jnp.bfloat16),
             pltpu.VMEM(block, jnp.bfloat16),
             pltpu.VMEM((8, live.shape[1]), jnp.float32),
             pltpu.SemaphoreType.DMA((2, 2)),
         ],
-        compiler_params=params,
-        cost_estimate=cost(1, 4),
+        compiler_params=pltpu.CompilerParams(vmem_limit_bytes=24 << 20),
+        cost_estimate=cost(1, 6),
         name="late_heads",
-    )(place, *tokens, *late_rows, early, columns, dec, gain, live, scores)
+    )(place, *tokens, *rows[LATE], early, dec, gain, live, states)
 
 
 def scores_kernel(place, packed, proj, emb, chosen, state, slots, rows, unit, scale, ordered, unit_v, ids_v):
@@ -382,28 +361,22 @@
         far_low, far_high = shift(after[:mid], "reader", 1), shift(before[mid:], "reader", -1)
         tokens = (own, after, far_low, far_high, before)
 
-    rows_here, half = key_proj.shape[0], key_proj.shape[1] // 2
-    ids_high = (passage_id // 256).astype(jnp.bfloat16)
-    ids_low = (passage_id % 256).astype(jnp.bfloat16)
-    gap = ((0, 0), (0, LANES // 2 - topk))
-    coded = jnp.concatenate([query_feat, jnp.pad(ids_high, gap), jnp.pad(ids_low, gap)], axis=1)
-    coded = jnp.pad(coded, ((0, 0), (0, -coded.shape[1] % (rows_here * 4)))).reshape(rows_here, -1)
-    beside = coded.shape[1]
-    coded = jnp.pad(coded, ((0, 0), (0, LANES - beside)))
     with jax.named_scope("gather_key_proj"):
-        whole_rows = lax.all_gather(key_proj[:, half:], INDEX)
-        whole_rows = whole_rows.reshape(ny, -1, half)
-        first = send_all(jnp.concatenate([key_proj[:, :half], coded], axis=1), Z)
-        coded = first[:, :, half : half + beside].reshape(nz, -1)
-        own = first[:, :, :half]
+        own = send_all(key_proj, "zq")
+        own, query_feat, passage_id = lax.optimization_barrier((own, query_feat, passage_id))
+        after, before = shift(own, Z, 1), shift(own, Z, -1)
+        far = [shift(own[:2], Z, 2), shift(own[2:], Z, -2)]
+        own = jnp.concatenate([own, after, *far, before])
         after, before = shift(own, "y", 1), shift(own, "y", -1)
-        early_rows = jnp.stack([own, after, before])
-        early_rows = [early_rows, shift(early_rows, "core", 1)]
-        late_rows = jnp.concatenate([shift(after[:8], "y", 1), shift(before[8:], "y", -1)])
-        late_rows = [late_rows, shift(late_rows, "core", 1)]
+        far = jnp.concatenate([shift(after[:8], "y", 1), shift(before[8:], "y", -1)])
+        key_rows = [(block, shift(block, "core", 1)) for block in (own, after, far, before)]
 
     with jax.named_scope("gather_queries"):
-        packed = send_all(coded[:, : width + LANES], NEAR)
+        ids_high = (passage_id // 256).astype(jnp.bfloat16)
+        ids_low = (passage_id % 256).astype(jnp.bfloat16)
+        gap = ((0, 0), (0, LANES // 2 - topk))
+        coded = [query_feat, jnp.pad(ids_high, gap), jnp.pad(ids_low, gap)]
+        packed = send_all(send_all(jnp.concatenate(coded, axis=1)[0], Z), NEAR)
 
     cols = width // nx
     six = width // n_index
@@ -432,29 +405,15 @@
                 pltpu.VMEM((queries, width), jnp.float32),
                 pltpu.VMEM((nx, n_index, LANES), jnp.int32),
             ],
-            compiler_params=pltpu.CompilerParams(vmem_limit_bytes=48 << 20),
+            compiler_params=pltpu.CompilerParams(vmem_limit_bytes=28 << 20),
             cost_estimate=pl.CostEstimate(
                 flops=4 << 30, bytes_accessed=8 << 20, transcendentals=0
             ),
             name="scores",
         )(jnp.stack([my_shard, r]).astype(jnp.int32), packed, query_proj, index_emb, chosen)
 
-    def merge_all(x):
-        lane = lax.broadcasted_iota(jnp.int32, x.shape[1:], x.ndim - 2)
-        return jnp.where(lane < topk, jnp.sum(x, axis=0), jnp.max(x, axis=0))
-
     with jax.named_scope("reduce_scores"):
-        state = state.reshape(n_pair, nz, LANES)
-        state = merge_all(lax.all_to_all(state, ("y", "core"), 0, 0, tiled=True))
-        state = merge_all(lax.all_to_all(state, Z, 0, 0, tiled=True))
-        slab_best = state[topk : topk + 1]
-        fetched = state[:topk]
-    expo = jnp.exp(fetched)
-    total = jnp.sum(expo)
-    prob = expo / total
-    log_prob = fetched - jnp.log(total)
-    score_row = jnp.zeros((1, LANES), jnp.float32)
-    score_row = score_row.at[0, :topk].set(prob).at[0, LANES // 2 : LANES // 2 + topk].set(fetched)
+        states = lax.all_to_all(state, ("y", "core", *Z), 0, 0, tiled=True)
 
     with jax.named_scope("attention"):
         answer = dec_query.shape[1]
@@ -465,16 +424,14 @@
         ).astype(jnp.bfloat16)
         positions = lax.broadcasted_iota(jnp.int32, (group, topk, plen), 2)
         live = (positions < passage_len[:, :, None]).reshape(group, topk * plen)
-        packet = attention_packet(
-            jnp.stack([y, core, r]).astype(jnp.int32),
+        packet, own_scores = attention_packet(
+            jnp.stack([y, zr, core, r]).astype(jnp.int32),
             tokens,
-            early_rows,
-            late_rows,
-            whole_rows,
+            key_rows,
             dec_unit.reshape(group, answer, feats_here),
             key_gain.astype(jnp.float32).reshape(1, feats_here),
             live.astype(jnp.float32),
-            score_row,
+            states,
         )
 
     with jax.named_scope("targets"):
@@ -500,7 +457,7 @@
                 *[pltpu.VMEM(x.shape, x.dtype) for x in (my_rows, my_unit, query_scale, ordered)],
                 pltpu.SemaphoreType.DMA((4,)),
             ],
-            compiler_params=pltpu.CompilerParams(vmem_limit_bytes=40 << 20),
+            compiler_params=pltpu.CompilerParams(vmem_limit_bytes=16 << 20),
             name="gradient",
         )(coef, slots, my_rows, my_unit, query_scale, ordered)
 
@@ -515,7 +472,8 @@
     mass = jnp.sum(lax.dynamic_index_in_dim(packets, y * ncore + core, 1, False), axis=0)
     my_target = lax.dynamic_slice_in_dim(mass, r * SLOT, topk, 0)
     log_target = jnp.log(my_target)
-    retr_loss = jnp.sum(my_target * (log_target - log_prob))
+    retr_loss = jnp.sum(my_target * (log_target - own_scores[0, :topk]))
+    slab_best = own_scores[0, topk : topk + 1]
     return (grad_proj, slab_best, retr_loss[None], log_target[None])
 
 

time: 276 us -> 283 us (1.025)
  starting transfers between devices: 75.5 us -> 105 us
  between operations: 15.2 us -> 1.15 us
  local copies, waits for them, and re-layouts: 28.6 us -> 40.2 us
  other arithmetic: 15.3 us -> 6.05 us
  waiting for transfers between devices: 60.8 us -> 53.1 us
  Pallas kernels: 34.4 us -> 29.4 us
    ppermute x11 -> x17, starting transfers between devices: 32.2 us -> 50.3 us  [shift(): return lax.ppermute(x, axis, [((i + step) % size, i) for i in range(size)])]
    unnamed x36 -> x59, local copies, waits for them, and re-layouts: 9.54 us -> 25.7 us
    ppermute x11 -> x17, waiting for transfers between devices: 3.84 us -> 18.9 us  [shift(): return lax.ppermute(x, axis, [((i + step) % size, i) for i in range(size)])]
    all_to_all x2 -> x1, waiting for transfers between devices: 12.9 us -> 3.55 us  [body(): states = lax.all_to_all(state, ('y', 'core', *Z), 0, 0, tiled=True)]
    all_to_all x3 -> x4, starting transfers between devices: 28 us -> 36.5 us  [send_all(): lax.all_to_all(jnp.broadcast_to(x[None], (size, *x.shape)), axis, 0, 0, t...]
    all_to_all x3 -> x4, waiting for transfers between devices: 25.4 us -> 17.9 us  [send_all(): lax.all_to_all(jnp.broadcast_to(x[None], (size, *x.shape)), axis, 0, 0, t...]
    all_gather x1 -> x0, waiting for transfers between devices: 6.53 us -> none  [body(): whole_rows = lax.all_gather(key_proj[:, half:], INDEX)]
    another operation x6 -> x1, other arithmetic: 6.01 us -> 0.08 us  [body(): jnp.stack([y, zr, core, r]).astype(jnp.int32)]
  transfers between devices with their start and end apart: 18 -> 23, of which waited for: 8 -> 9; matrix products, arithmetic and copies ran while one was open for 12% -> 8% of each run, Pallas kernels for 7% -> 5%
where the time goes in v6:
time: 283 us; the launch traced here: 280 us
  starting transfers between devices  105 us (37%)
  waiting for transfers between devices  53.1 us (19%)
  blocking collectives  45 us (16%)
  local copies, waits for them, and re-layouts  40.2 us (14%)
  Pallas kernels  29.4 us (10%)
  other arithmetic  6.05 us (2%)
    ppermute x17, starting transfers between devices, shift(): return lax.ppermute(x, axis, [((i + step) % size, i) for i in range(size)])  50.3 us
    all_to_all x4, starting transfers between devices, send_all(): lax.all_to_all(jnp.broadcast_to(x[None], (size, *x.shape)), axis, 0, 0, t...  36.5 us
    unnamed x59, local copies, waits for them, and re-layouts  25.7 us
    all_to_all x1, blocking collectives, body(): coef = lax.all_to_all(coef, Z, 0, 0, tiled=True).reshape(n_index, LANES)  22.8 us
    ppermute x17, waiting for transfers between devices, shift(): return lax.ppermute(x, axis, [((i + step) % size, i) for i in range(size)])  18.9 us
    all_to_all x4, waiting for transfers between devices, send_all(): lax.all_to_all(jnp.broadcast_to(x[None], (size, *x.shape)), axis, 0, 0, t...  17.9 us
    all_to_all x1, starting transfers between devices, body(): states = lax.all_to_all(state, ('y', 'core', *Z), 0, 0, tiled=True)  14.7 us
    all_to_all x1, waiting for transfers between devices, body(): term = jnp.sum(lax.all_to_all(term, Z, 0, 0, tiled=True), axis=0)  12.8 us
  transfers between devices with their start and end apart: 23, of which 9 were waited for; matrix products, arithmetic and copies ran while one was open for 8% of the time, Pallas kernels for 5%

profile of v6, /device:TPU:6, one launch (start us, length us, event | category | flops | bytes accessed | tf_op | source)
XLA Modules:
  0.0 280.0 jit_solution(7317178906122827046)
XLA Ops:
  0.6 1.6 broadcast_in_dim.14
  2.2 15.1 %all-to-all-start = ((bf16[4,32,1024]{2,1,0:T(8,128)(2,1)}), bf16[4,32,1024]{2,1,0:T(8,128)(2,1)S(1)}, u32[]{:S(2)}, u32[]{:S(2)}) async-start(bf16[4,32,1024]{2,1,0:T(8,128)(2,1)} %broadcast_in_dim.14), calls=%async_computation | async-start | bytes 524288 | tf_op jit(solution)/shard_map/gather_key_proj/all_to_all | solution.py:35
  17.3 2.9 %collective-permute-start = (bf16[640,1024]{1,0:T(8,128)(2,1)}, bf16[640,1024]{1,0:T(8,128)(2,1)S(1)}, u32[]{:S(2)}, u32[]{:S(2)}) collective-permute-start(bf16[640,1024]{1,0:T(8,128)(2,1)} %bitcast.33), channel_id=1, source_target_pairs={{1,0},{2,1},{3,2},{0,3},{5,4},{6,5},{7,6},{4,7},{9,8},{10,9},{11,1... | collective-permute-start | bytes 3932168 | tf_op jit(solution)/shard_map/gather_enc_out/ppermute | solution.py:30
  20.1 15.7 %all-to-all-done = bf16[4,32,1024]{2,1,0:T(8,128)(2,1)S(1)} async-done(((bf16[4,32,1024]{2,1,0:T(8,128)(2,1)}), bf16[4,32,1024]{2,1,0:T(8,128)(2,1)S(1)}, u32[]{:S(2)}, u32[]{:S(2)}) %all-to-all-start) | async-done | bytes 262176 | tf_op jit(solution)/shard_map/gather_key_proj/all_to_all | solution.py:35
  35.8 4.9 %collective-permute-start.4 = (bf16[4,32,1024]{2,1,0:T(8,128)(2,1)S(1)}, bf16[4,32,1024]{2,1,0:T(8,128)(2,1)S(1)}, u32[]{:S(2)}, u32[]{:S(2)}) collective-permute-start(bf16[4,32,1024]{2,1,0:T(8,128)(2,1)S(1)} %all-to-all-done), channel_id=1, source_target_pairs={{8,0},{16,8},{24,16},{32,24},{40,32},{48,40},{56,48},{64,56},{72,6... | collective-permute-start | bytes 786440 | tf_op jit(solution)/shard_map/gather_key_proj/ppermute | solution.py:30
  40.7 1.9 collective-permute-start.5
  43.4 3.9 %collective-permute-start.7 = (bf16[4,32,1024]{2,1,0:T(8,128)(2,1)S(1)}, bf16[4,32,1024]{2,1,0:T(8,128)(2,1)S(1)}, u32[]{:S(2)}, u32[]{:S(2)}) collective-permute-start(bf16[4,32,1024]{2,1,0:T(8,128)(2,1)S(1)} %all-to-all-done), channel_id=1, source_target_pairs={{120,0},{0,8},{8,16},{16,24},{24,32},{32,40},{40,48},{48,56},{56,6... | collective-permute-start | bytes 786440 | tf_op jit(solution)/shard_map/gather_key_proj/ppermute | solution.py:30
  47.3 3.2 %collective-permute-start.6 = (bf16[2,32,1024]{2,1,0:T(8,128)(2,1)S(1)}, bf16[2,32,1024]{2,1,0:T(8,128)(2,1)S(1)}, u32[]{:S(2)}, u32[]{:S(2)}) collective-permute-start(bf16[2,32,1024]{2,1,0:T(8,128)(2,1)S(1)} %get-tuple-element.30), channel_id=1, source_target_pairs={{112,0},{120,8},{0,16},{8,24},{16,32},{24,40},{32,48},{40,56},{48,... | collective-permute-start | bytes 393224 | tf_op jit(solution)/shard_map/gather_key_proj/ppermute | solution.py:30
  52.4 6.1 %collective-permute-done.6 = bf16[2,32,1024]{2,1,0:T(8,128)(2,1)S(1)} collective-permute-done((bf16[2,32,1024]{2,1,0:T(8,128)(2,1)S(1)}, bf16[2,32,1024]{2,1,0:T(8,128)(2,1)S(1)}, u32[]{:S(2)}, u32[]{:S(2)}) %collective-permute-start.6) | collective-permute-done | bytes 131104 | tf_op jit(solution)/shard_map/gather_key_proj/ppermute | solution.py:30
  59.9 4.9 %collective-permute-start.8 = (bf16[16,32,1024]{2,1,0:T(8,128)(2,1)}, bf16[16,32,1024]{2,1,0:T(8,128)(2,1)}, u32[]{:S(2)}, u32[]{:S(2)}) collective-permute-start(bf16[16,32,1024]{2,1,0:T(8,128)(2,1)} %constant_dynamic-update-slice_fusion.refs_5_), channel_id=1, source_target_pairs={{128,0},{256,128},{384,256},{0,384},{129,1},{257,129},{385,257},{1... | collective-permute-start | bytes 3145736 | tf_op jit(solution)/shard_map/gather_key_proj/ppermute | solution.py:30
  64.8 1.9 collective-permute-start.10
  66.7 2.4 collective-permute-start.2
  72.1 8.4 %all-to-all-start.1 = ((bf16[16,2,448]{2,1,0:T(2,128)(2,1)}), bf16[16,2,448]{2,1,0:T(2,128)(2,1)S(1)}, u32[]{:S(2)}, u32[]{:S(2)}) async-start(bf16[16,2,448]{2,1,0:T(2,128)(2,1)} %reshape.206), calls=%async_computation.1 | async-start | bytes 65536 | tf_op jit(solution)/shard_map/gather_queries/all_to_all | solution.py:35
  80.6 3.1 %collective-permute-done.8.refs_7_ = bf16[16,32,1024]{2,1,0:T(8,128)(2,1)} collective-permute-done((bf16[16,32,1024]{2,1,0:T(8,128)(2,1)}, bf16[16,32,1024]{2,1,0:T(8,128)(2,1)}, u32[]{:S(2)}, u32[]{:S(2)}) %collective-permute-start.8) | collective-permute-done | bytes 1048608 | tf_op jit(solution)/shard_map/gather_key_proj/ppermute | solution.py:30
  83.6 1.9 slice.34
  85.5 5.6 %collective-permute-start.9 = (bf16[8,32,1024]{2,1,0:T(8,128)(2,1)}, bf16[8,32,1024]{2,1,0:T(8,128)(2,1)}, u32[]{:S(2)}, u32[]{:S(2)}) collective-permute-start(bf16[8,32,1024]{2,1,0:T(8,128)(2,1)} %slice.34), channel_id=1, source_target_pairs={{128,0},{256,128},{384,256},{0,384},{129,1},{257,129},{385,257},{1... | collective-permute-start | bytes 1572872 | tf_op jit(solution)/shard_map/gather_key_proj/ppermute | solution.py:30
  91.1 1.9 slice.35
  93.0 1.9 collective-permute-start.11
  97.0 7.6 %all-to-all-start.2 = ((bf16[32,16,896]{2,1,0:T(8,128)(2,1)}), bf16[32,16,896]{2,1,0:T(8,128)(2,1)S(1)}, u32[]{:S(2)}, u32[]{:S(2)}) async-start(bf16[32,16,896]{2,1,0:T(8,128)(2,1)} %broadcast_in_dim.17), calls=%async_computation.2 | async-start | bytes 1835008 | tf_op jit(solution)/shard_map/gather_queries/all_to_all | solution.py:35
  105.5 2.7 collective-permute-start.1
  108.3 1.9 collective-permute-start.13
  110.3 2.4 collective-permute-start.14
  112.7 1.9 collective-permute-start.15
  114.7 1.9 constant_dynamic-update-slice_fusion.6
  116.6 1.9 constant_dynamic-update-slice_fusion.5.refs_5_
  118.4 2.4 collective-permute-start.12
  122.5 7.5 %collective-permute-done.1.refs_2_ = bf16[320,1024]{1,0:T(8,128)(2,1)} collective-permute-done((bf16[320,1024]{1,0:T(8,128)(2,1)}, bf16[320,1024]{1,0:T(8,128)(2,1)}, u32[]{:S(2)}, u32[]{:S(2)}) %collective-permute-start.1) | collective-permute-done | bytes 655392 | tf_op jit(solution)/shard_map/gather_enc_out/ppermute | solution.py:30
  130.0 3.6 %collective-permute-start.3 = (bf16[320,1024]{1,0:T(8,128)(2,1)}, bf16[320,1024]{1,0:T(8,128)(2,1)}, u32[]{:S(2)}, u32[]{:S(2)}) collective-permute-start(bf16[320,1024]{1,0:T(8,128)(2,1)} %slice.33), channel_id=1, source_target_pairs={{3,0},{0,1},{1,2},{2,3},{7,4},{4,5},{5,6},{6,7},{11,8},{8,9},{9,10... | collective-permute-start | bytes 1966088 | tf_op jit(solution)/shard_map/gather_enc_out/ppermute | solution.py:30
  136.2 1.4 copy-done.19
  138.8 5.1 %scores.1 = (f32[128,128]{1,0:T(8,128)S(1)}, s32[128,128]{1,0:T(8,128)S(1)}, f32[512,192]{1,0:T(8,128)S(1)}, f32[512,192]{1,0:T(8,128)S(1)}, f32[512,1]{1,0:T(8,128)S(1)}, /*index=5*/bf16[768,512]{1,0:T(8,128)(2,1)S(1)}) custom-call(s32[2]{0:T(128)S(1)} %pad_add_fusion.1.place, bf16[32,16,896]{2,1,0:T(8,128)(2,1)S(1)} %all-to-all-done.2.packed, ...), custom_call_target="tpu_custom_call" | custom-call | flops 4294967296 | bytes 8388608 | tf_op jit(solution)/shard_map/scores/scores/pallas_call | solution.py:392
  148.3 14.7 %all-to-all-start.3 = ((f32[128,1,128]{2,1,0:T(1,128)}), f32[128,1,128]{2,1,0:T(1,128)S(1)}, u32[]{:S(2)}, u32[]{:S(2)}) async-start(f32[128,1,128]{2,1,0:T(1,128)} %bitcast.39), calls=%async_computation.3 | async-start | bytes 131072 | tf_op jit(solution)/shard_map/reduce_scores/all_to_all | solution.py:416
  164.5 8.4 %early_keys.1.refs_7_ = f32[640,1024]{1,0:T(8,128)S(1)} custom-call(s32[4]{0:T(128)S(1)} %pad_add_fusion.place, bf16[640,1024]{1,0:T(8,128)(2,1)S(1)} %bitcast.35, bf16[640,1024]{1,0:T(8,128)(2,1)S(1)} %collective-permute-done.refs_1_, bf16[320,1024]{1,0:T(8,128)(2,1)} %collective-permute-done.1.refs_2_, bf16[320,1024]{1,0:T(8,128)(2,1)} %collective-permute-done.3.refs_3_, ...), custom_call_target="tpu_custom_call" | custom-call | flops 4026531840 | bytes 13631488 | tf_op jit(solution)/shard_map/attention/early_keys/pallas_call | solution.py:183
  172.9 1.5 copy-done
  174.4 3.6 %all-to-all-done.3 = f32[128,1,128]{2,1,0:T(1,128)S(1)} async-done(((f32[128,1,128]{2,1,0:T(1,128)}), f32[128,1,128]{2,1,0:T(1,128)S(1)}, u32[]{:S(2)}, u32[]{:S(2)}) %all-to-all-start.3) | async-done | bytes 65568 | tf_op jit(solution)/shard_map/reduce_scores/all_to_all | solution.py:416
  178.6 1.7 copy-done.1
  180.3 1.3 copy-done.3
  182.5 7.6 %late_heads.1 = (f32[32,256]{1,0:T(8,128)S(1)}, f32[8,128]{1,0:T(8,128)S(1)}) custom-call(s32[4]{0:T(128)S(1)} %pad_add_fusion.place, bf16[640,1024]{1,0:T(8,128)(2,1)S(1)} %bitcast.36, bf16[640,1024]{1,0:T(8,128)(2,1)S(1)} %collective-permute-done.refs_1_, bf16[320,1024]{1,0:T(8,128)(2,1)} %collective-permute-done.1.refs_2_, ...), custom_call_target="tpu_custom_call" | custom-call | flops 1342177280 | bytes 6291456 | tf_op jit(solution)/shard_map/attention/late_heads/pallas_call | solution.py:197
  190.2 11.1 %all_to_all.56 = f32[32,1,256]{2,1,0:T(1,128)S(1)} all-to-all(f32[32,1,256]{2,1,0:T(1,128)S(1)} %copy.16), channel_id=1, replica_groups=mesh['y'=4,'zq'=4,'zr'=4,'core'=2,'reader'=4] {'reader','y','core'}, dimensions={0} | all-to-all | bytes 65536 | tf_op jit(solution)/shard_map/targets/all_to_all | solution.py:438
  201.9 1.6 coef.1
  203.5 22.8 %all_to_all.57 = f32[16,8,128]{2,1,0:T(8,128)S(1)} all-to-all(f32[16,8,128]{2,1,0:T(8,128)} %coef.1), channel_id=1, replica_groups=mesh['y'=4,'zq'=4,'zr'=4,'core'=2,'reader'=4] {'zq','zr'}, dimensions={0} | all-to-all | bytes 131072 | tf_op jit(solution)/shard_map/targets/all_to_all | solution.py:446
  230.3 6.6 %gradient.1 = (f32[384,192]{1,0:T(8,128)S(1)}, f32[384,192]{1,0:T(8,128)S(1)}) custom-call(f32[128,128]{1,0:T(8,128)S(1)} %bitcast.38, s32[128,128]{1,0:T(8,128)S(1)} %copy-done.17, f32[512,192]{1,0:T(8,128)S(1)} %copy-done.9, f32[512,192]{1,0:T(8,128)S(1)} %copy-done.11, f32[512,1]{1,0:T(8,128)S(1)} %copy-done.15, bf16[768,512]{1,0:T(8,128)(2,1)S(1)} %copy-done.6), custom_call_target="tpu_custom_call" | custom-call | tf_op jit(solution)/shard_map/gradient/gradient/pallas_call | solution.py:450
  236.9 1.9 collective-permute-start.16
  238.8 1.7 collective-permute-done.16
  240.6 11.0 %all_to_all.58 = f32[4,96,192]{2,1,0:T(8,128)S(1)} all-to-all(f32[4,96,192]{2,1,0:T(8,128)S(1)} %bitcast.42), channel_id=1, replica_groups=mesh['y'=4,'zq'=4,'zr'=4,'core'=2,'reader'=4] {'y'}, dimensions={0} | all-to-all | bytes 589824 | tf_op jit(solution)/shard_map/reduce_gradient/all_to_all | solution.py:466
  252.3 3.5 %all-to-all-start.7 = ((f32[16,6,192]{2,1,0:T(8,128)}), f32[16,6,192]{2,1,0:T(8,128)S(1)}, u32[]{:S(2)}, u32[]{:S(2)}) async-start(f32[16,6,192]{2,1,0:T(8,128)} %reshape.201), calls=%async_computation.7 | async-start | bytes 262144 | tf_op jit(solution)/shard_map/reduce_gradient/all_to_all | solution.py:468
  257.2 12.8 %all-to-all-done.7 = f32[16,6,192]{2,1,0:T(8,128)S(1)} async-done(((f32[16,6,192]{2,1,0:T(8,128)}), f32[16,6,192]{2,1,0:T(8,128)S(1)}, u32[]{:S(2)}, u32[]{:S(2)}) %all-to-all-start.7) | async-done | bytes 73760 | tf_op jit(solution)/shard_map/reduce_gradient/all_to_all | solution.py:468
  270.6 5.3 %all-to-all-start.8 = ((f32[4,6,192]{2,1,0:T(8,128)}), f32[4,6,192]{2,1,0:T(8,128)S(1)}, u32[]{:S(2)}, u32[]{:S(2)}) async-start(f32[4,6,192]{2,1,0:T(8,128)} %broadcast_in_dim.18), calls=%async_computation.8 | async-start | bytes 65536 | tf_op jit(solution)/shard_map/reduce_gradient/all_to_all | solution.py:35
  277.2 2.2 all-to-all-done.8
  (107 shorter events, 31.7 us)
Async XLA Ops:
  2.2 33.6 %all-to-all-start = ((bf16[4,32,1024]{2,1,0:T(8,128)(2,1)}), bf16[4,32,1024]{2,1,0:T(8,128)(2,1)S(1)}, u32[]{:S(2)}, u32[]{:S(2)}) async-start(bf16[4,32,1024]{2,1,0:T(8,128)(2,1)} %broadcast_in_dim.14), calls=%async_computation | async-start | bytes 524288 | tf_op jit(solution)/shard_map/gather_key_proj/all_to_all | solution.py:35
  17.3 51.9 %copy-start.21 = (bf16[4,16,1024]{2,1,0:T(8,128)(2,1)S(1)}, bf16[4,16,1024]{2,1,0:T(8,128)(2,1)}, u32[]{:S(2)}) copy-start(bf16[4,16,1024]{2,1,0:T(8,128)(2,1)} %param.17) | copy-start | bytes 393220
  17.3 87.4 %collective-permute-start = (bf16[640,1024]{1,0:T(8,128)(2,1)}, bf16[640,1024]{1,0:T(8,128)(2,1)S(1)}, u32[]{:S(2)}, u32[]{:S(2)}) collective-permute-start(bf16[640,1024]{1,0:T(8,128)(2,1)} %bitcast.33), channel_id=1, source_target_pairs={{1,0},{2,1},{3,2},{0,3},{5,4},{6,5},{7,6},{4,7},{9,8},{10,9},{11,1... | collective-permute-start | bytes 3932168 | tf_op jit(solution)/shard_map/gather_enc_out/ppermute | solution.py:30
  35.8 14.7 %collective-permute-start.4 = (bf16[4,32,1024]{2,1,0:T(8,128)(2,1)S(1)}, bf16[4,32,1024]{2,1,0:T(8,128)(2,1)S(1)}, u32[]{:S(2)}, u32[]{:S(2)}) collective-permute-start(bf16[4,32,1024]{2,1,0:T(8,128)(2,1)S(1)} %all-to-all-done), channel_id=1, source_target_pairs={{8,0},{16,8},{24,16},{32,24},{40,32},{48,40},{56,48},{64,56},{72,6... | collective-permute-start | bytes 786440 | tf_op jit(solution)/shard_map/gather_key_proj/ppermute | solution.py:30
  40.7 11.0 %collective-permute-start.5 = (bf16[2,32,1024]{2,1,0:T(8,128)(2,1)S(1)}, bf16[2,32,1024]{2,1,0:T(8,128)(2,1)S(1)}, u32[]{:S(2)}, u32[]{:S(2)}) collective-permute-start(bf16[2,32,1024]{2,1,0:T(8,128)(2,1)S(1)} %get-tuple-element.31), channel_id=1, source_target_pairs={{16,0},{24,8},{32,16},{40,24},{48,32},{56,40},{64,48},{72,56},{80,... | collective-permute-start | bytes 393224 | tf_op jit(solution)/shard_map/gather_key_proj/ppermute | solution.py:30
  43.4 15.8 %collective-permute-start.7 = (bf16[4,32,1024]{2,1,0:T(8,128)(2,1)S(1)}, bf16[4,32,1024]{2,1,0:T(8,128)(2,1)S(1)}, u32[]{:S(2)}, u32[]{:S(2)}) collective-permute-start(bf16[4,32,1024]{2,1,0:T(8,128)(2,1)S(1)} %all-to-all-done), channel_id=1, source_target_pairs={{120,0},{0,8},{8,16},{16,24},{24,32},{32,40},{40,48},{48,56},{56,6... | collective-permute-start | bytes 786440 | tf_op jit(solution)/shard_map/gather_key_proj/ppermute | solution.py:30
  47.3 11.2 %collective-permute-start.6 = (bf16[2,32,1024]{2,1,0:T(8,128)(2,1)S(1)}, bf16[2,32,1024]{2,1,0:T(8,128)(2,1)S(1)}, u32[]{:S(2)}, u32[]{:S(2)}) collective-permute-start(bf16[2,32,1024]{2,1,0:T(8,128)(2,1)S(1)} %get-tuple-element.30), channel_id=1, source_target_pairs={{112,0},{120,8},{0,16},{8,24},{16,32},{24,40},{32,48},{40,56},{48,... | collective-permute-start | bytes 393224 | tf_op jit(solution)/shard_map/gather_key_proj/ppermute | solution.py:30
  59.9 23.8 %collective-permute-start.8 = (bf16[16,32,1024]{2,1,0:T(8,128)(2,1)}, bf16[16,32,1024]{2,1,0:T(8,128)(2,1)}, u32[]{:S(2)}, u32[]{:S(2)}) collective-permute-start(bf16[16,32,1024]{2,1,0:T(8,128)(2,1)} %constant_dynamic-update-slice_fusion.refs_5_), channel_id=1, source_target_pairs={{128,0},{256,128},{384,256},{0,384},{129,1},{257,129},{385,257},{1... | collective-permute-start | bytes 3145736 | tf_op jit(solution)/shard_map/gather_key_proj/ppermute | solution.py:30
  64.8 26.3 %collective-permute-start.10 = (bf16[16,32,1024]{2,1,0:T(8,128)(2,1)}, bf16[16,32,1024]{2,1,0:T(8,128)(2,1)}, u32[]{:S(2)}, u32[]{:S(2)}) collective-permute-start(bf16[16,32,1024]{2,1,0:T(8,128)(2,1)} %constant_dynamic-update-slice_fusion.refs_5_), channel_id=1, source_target_pairs={{384,0},{0,128},{128,256},{256,384},{385,1},{1,129},{129,257},{257... | collective-permute-start | bytes 3145736 | tf_op jit(solution)/shard_map/gather_key_proj/ppermute | solution.py:30
  66.7 51.7 %collective-permute-start.2 = (bf16[640,1024]{1,0:T(8,128)(2,1)}, bf16[640,1024]{1,0:T(8,128)(2,1)S(1)}, u32[]{:S(2)}, u32[]{:S(2)}) collective-permute-start(bf16[640,1024]{1,0:T(8,128)(2,1)} %bitcast.34), channel_id=1, source_target_pairs={{3,0},{0,1},{1,2},{2,3},{7,4},{4,5},{5,6},{6,7},{11,8},{8,9},{9,10... | collective-permute-start | bytes 3932168 | tf_op jit(solution)/shard_map/gather_enc_out/ppermute | solution.py:30
  69.2 0.8 copy-start.24
  69.2 0.8 copy-start.22
  72.1 23.8 %all-to-all-start.1 = ((bf16[16,2,448]{2,1,0:T(2,128)(2,1)}), bf16[16,2,448]{2,1,0:T(2,128)(2,1)S(1)}, u32[]{:S(2)}, u32[]{:S(2)}) async-start(bf16[16,2,448]{2,1,0:T(2,128)(2,1)} %reshape.206), calls=%async_computation.1 | async-start | bytes 65536 | tf_op jit(solution)/shard_map/gather_queries/all_to_all | solution.py:35
  80.6 15.1 %copy-start.23 = (s32[4,20]{1,0:T(4,128)S(1)}, s32[4,20]{1,0:T(4,128)}, u32[]{:S(2)}) copy-start(s32[4,20]{1,0:T(4,128)} %param.13) | copy-start | bytes 964
  85.5 24.7 %collective-permute-start.9 = (bf16[8,32,1024]{2,1,0:T(8,128)(2,1)}, bf16[8,32,1024]{2,1,0:T(8,128)(2,1)}, u32[]{:S(2)}, u32[]{:S(2)}) collective-permute-start(bf16[8,32,1024]{2,1,0:T(8,128)(2,1)} %slice.34), channel_id=1, source_target_pairs={{128,0},{256,128},{384,256},{0,384},{129,1},{257,129},{385,257},{1... | collective-permute-start | bytes 1572872 | tf_op jit(solution)/shard_map/gather_key_proj/ppermute | solution.py:30
  93.0 19.7 %collective-permute-start.11 = (bf16[8,32,1024]{2,1,0:T(8,128)(2,1)}, bf16[8,32,1024]{2,1,0:T(8,128)(2,1)}, u32[]{:S(2)}, u32[]{:S(2)}) collective-permute-start(bf16[8,32,1024]{2,1,0:T(8,128)(2,1)} %slice.35), channel_id=1, source_target_pairs={{384,0},{0,128},{128,256},{256,384},{385,1},{1,129},{129,257},{257... | collective-permute-start | bytes 1572872 | tf_op jit(solution)/shard_map/gather_key_proj/ppermute | solution.py:30
  97.0 37.9 %all-to-all-start.2 = ((bf16[32,16,896]{2,1,0:T(8,128)(2,1)}), bf16[32,16,896]{2,1,0:T(8,128)(2,1)S(1)}, u32[]{:S(2)}, u32[]{:S(2)}) async-start(bf16[32,16,896]{2,1,0:T(8,128)(2,1)} %broadcast_in_dim.17), calls=%async_computation.2 | async-start | bytes 1835008 | tf_op jit(solution)/shard_map/gather_queries/all_to_all | solution.py:35
  105.5 24.5 %collective-permute-start.1 = (bf16[320,1024]{1,0:T(8,128)(2,1)}, bf16[320,1024]{1,0:T(8,128)(2,1)}, u32[]{:S(2)}, u32[]{:S(2)}) collective-permute-start(bf16[320,1024]{1,0:T(8,128)(2,1)} %slice.32), channel_id=1, source_target_pairs={{1,0},{2,1},{3,2},{0,3},{5,4},{6,5},{7,6},{4,7},{9,8},{10,9},{11,1... | collective-permute-start | bytes 1966088 | tf_op jit(solution)/shard_map/gather_enc_out/ppermute | solution.py:30
  108.3 54.8 %collective-permute-start.13 = (bf16[16,32,1024]{2,1,0:T(8,128)(2,1)}, bf16[16,32,1024]{2,1,0:T(8,128)(2,1)}, u32[]{:S(2)}, u32[]{:S(2)}) collective-permute-start(bf16[16,32,1024]{2,1,0:T(8,128)(2,1)} %constant_dynamic-update-slice_fusion.refs_5_), channel_id=1, source_target_pairs={{4,0},{0,4},{5,1},{1,5},{6,2},{2,6},{7,3},{3,7},{12,8},{8,12},{13,... | collective-permute-start | bytes 3145736 | tf_op jit(solution)/shard_map/gather_key_proj/ppermute | solution.py:30
  110.3 52.9 %collective-permute-start.14 = (bf16[16,32,1024]{2,1,0:T(8,128)(2,1)}, bf16[16,32,1024]{2,1,0:T(8,128)(2,1)}, u32[]{:S(2)}, u32[]{:S(2)}) collective-permute-start(bf16[16,32,1024]{2,1,0:T(8,128)(2,1)} %collective-permute-done.8.refs_7_), channel_id=1, source_target_pairs={{4,0},{0,4},{5,1},{1,5},{6,2},{2,6},{7,3},{3,7},{12,8},{8,12},{13,... | collective-permute-start | bytes 3145736 | tf_op jit(solution)/shard_map/gather_key_proj/ppermute | solution.py:30
  112.7 50.4 %collective-permute-start.15 = (bf16[16,32,1024]{2,1,0:T(8,128)(2,1)}, bf16[16,32,1024]{2,1,0:T(8,128)(2,1)}, u32[]{:S(2)}, u32[]{:S(2)}) collective-permute-start(bf16[16,32,1024]{2,1,0:T(8,128)(2,1)} %collective-permute-done.10.refs_9_), channel_id=1, source_target_pairs={{4,0},{0,4},{5,1},{1,5},{6,2},{2,6},{7,3},{3,7},{12,8},{8,12},{13,... | collective-permute-start | bytes 3145736 | tf_op jit(solution)/shard_map/gather_key_proj/ppermute | solution.py:30
  118.4 60.2 %collective-permute-start.12 = (bf16[16,32,1024]{2,1,0:T(8,128)(2,1)}, bf16[16,32,1024]{2,1,0:T(8,128)(2,1)}, u32[]{:S(2)}, u32[]{:S(2)}) collective-permute-start(bf16[16,32,1024]{2,1,0:T(8,128)(2,1)} %constant_dynamic-update-slice_fusion.5.refs_5_), channel_id=1, source_target_pairs={{4,0},{0,4},{5,1},{1,5},{6,2},{2,6},{7,3},{3,7},{12,8},{8,12},{13,... | collective-permute-start | bytes 3145736 | tf_op jit(solution)/shard_map/gather_key_proj/ppermute | solution.py:30
  130.0 33.1 %collective-permute-start.3 = (bf16[320,1024]{1,0:T(8,128)(2,1)}, bf16[320,1024]{1,0:T(8,128)(2,1)}, u32[]{:S(2)}, u32[]{:S(2)}) collective-permute-start(bf16[320,1024]{1,0:T(8,128)(2,1)} %slice.33), channel_id=1, source_target_pairs={{3,0},{0,1},{1,2},{2,3},{7,4},{4,5},{5,6},{6,7},{11,8},{8,9},{9,10... | collective-permute-start | bytes 1966088 | tf_op jit(solution)/shard_map/gather_enc_out/ppermute | solution.py:30
  134.9 1.3 copy-start.4
  136.2 1.4 copy-start.19
  137.6 1.3 copy-start.20
  143.9 0.9 copy-start.5
  144.8 0.8 copy-start.8
  145.6 0.8 copy-start.10
  146.4 0.7 copy-start.14
  147.1 0.6 copy-start.16
  147.7 0.6 copy-start.18
  148.3 30.3 %copy-start.7 = (bf16[4,16,1024]{2,1,0:T(8,128)(2,1)S(1)}, bf16[4,16,1024]{2,1,0:T(8,128)(2,1)}, u32[]{:S(2)}) copy-start(bf16[4,16,1024]{2,1,0:T(8,128)(2,1)} %fusion.1.refs_8_) | copy-start | bytes 393220
  148.3 29.6 %all-to-all-start.3 = ((f32[128,1,128]{2,1,0:T(1,128)}), f32[128,1,128]{2,1,0:T(1,128)S(1)}, u32[]{:S(2)}, u32[]{:S(2)}) async-start(f32[128,1,128]{2,1,0:T(1,128)} %bitcast.39), calls=%async_computation.3 | async-start | bytes 131072 | tf_op jit(solution)/shard_map/reduce_scores/all_to_all | solution.py:416
  163.1 1.3 copy-start.2
  172.9 1.5 copy-start
  178.0 0.6 copy-start.12
  178.6 1.7 copy-start.1
  180.3 1.3 copy-start.3
  181.7 0.8 copy-start.13
  182.5 43.9 %copy-start.6 = (bf16[768,512]{1,0:T(8,128)(2,1)S(1)}, bf16[768,512]{1,0:T(8,128)(2,1)}, u32[]{:S(2)}) copy-start(bf16[768,512]{1,0:T(8,128)(2,1)} %copy-done.5) | copy-start | bytes 2359300
  226.4 1.0 copy-start.9
  227.4 1.0 copy-start.11
  228.5 0.9 copy-start.15
  229.4 0.8 copy-start.17
  236.9 3.6 %collective-permute-start.16 = (f32[384,192]{1,0:T(8,128)S(1)}, f32[384,192]{1,0:T(8,128)S(1)}, u32[]{:S(2)}, u32[]{:S(2)}) collective-permute-start(f32[384,192]{1,0:T(8,128)S(1)} %get-tuple-element.28), channel_id=1, source_target_pairs={{4,0},{0,4},{5,1},{1,5},{6,2},{2,6},{7,3},{3,7},{12,8},{8,12},{13,... | collective-permute-start | bytes 884744 | tf_op jit(solution)/shard_map/reduce_gradient/ppermute | solution.py:30
  252.3 17.7 %all-to-all-start.7 = ((f32[16,6,192]{2,1,0:T(8,128)}), f32[16,6,192]{2,1,0:T(8,128)S(1)}, u32[]{:S(2)}, u32[]{:S(2)}) async-start(f32[16,6,192]{2,1,0:T(8,128)} %reshape.201), calls=%async_computation.7 | async-start | bytes 262144 | tf_op jit(solution)/shard_map/reduce_gradient/all_to_all | solution.py:468
  270.6 8.7 %all-to-all-start.8 = ((f32[4,6,192]{2,1,0:T(8,128)}), f32[4,6,192]{2,1,0:T(8,128)S(1)}, u32[]{:S(2)}, u32[]{:S(2)}) async-start(f32[4,6,192]{2,1,0:T(8,128)} %broadcast_in_dim.18), calls=%async_computation.8 | async-start | bytes 65536 | tf_op jit(solution)/shard_map/reduce_gradient/all_to_all | solution.py:35

commit v7 on v6

--- a/solution.py
+++ b/solution.py
@@ -21,6 +21,7 @@
 SLOT = 32
 TILE = 256
 N_OWNERS = 128
+GRANT = 56 << 20
 EARLY = (0, 1, 3)
 LATE = 2
 
@@ -42,6 +43,17 @@
 
 def dot32(a, b):
     return jnp.dot(a, b, preferred_element_type=jnp.float32)
+
+
+def load(far, near, sems):
+    copies = [pltpu.make_async_copy(a, b, sems.at[i]) for i, (a, b) in enumerate(zip(far, near))]
+    for copy in copies:
+        copy.start()
+    return copies
+
+
+def like(*arrays):
+    return [pltpu.VMEM(x.shape, x.dtype) for x in arrays]
 
 
 def token_copies(r, chunk, tokens, target, sems):
@@ -74,7 +86,7 @@
 
 
 def early_keys_kernel(place, *refs):
-    tokens, rows, (keys, token_v, weight_v, sems) = refs[:5], refs[5:11], refs[11:]
+    tokens, rows, (keys_out, keys, token_v, weight_v, sems) = refs[:5], refs[5:11], refs[11:]
     y, r = place[0], place[3]
     copies = []
     for slot, ahead in enumerate(EARLY):
@@ -95,6 +107,10 @@
                 keys[:, cols] = term
             else:
                 keys[:, cols] += term
+
+    copy = pltpu.make_async_copy(keys, keys_out, sems.at[0, 0])
+    copy.start()
+    copy.wait()
 
 
 def attend(keys, offset, dec, gain, live, column_v):
@@ -128,13 +144,18 @@
 
 def late_heads_kernel(place, *refs):
     tokens, (own, other), refs = refs[:5], refs[5:7], refs[7:]
-    early, dec, gain, live, states, out, own_scores, token_v, weight_v, column_v, sems = refs
+    far, (out, own_scores), near, refs = refs[:5], refs[5:7], refs[7:12], refs[12:]
+    token_v, weight_v, column_v, load_sems, sems = refs
     y, r = place[0], place[3]
+    loads = load(far, near, load_sems)
+    early, dec, gain, live, states = near
     copies = row_copies(place, own, other, weight_v, sems.at[0, 0])
     copies += token_copies(r, (y + LATE) % 4, tokens, token_v, sems.at[1])
     column_v[...] = jnp.zeros_like(column_v)
 
     lane = lax.broadcasted_iota(jnp.int32, (1, LANES), 1)
+    for copy in loads:
+        copy.wait()
     found = states[...]
     fetched = jnp.where(lane < 20, jnp.sum(found, axis=0, keepdims=True), 0.0)
     expo = jnp.where(lane < 20, jnp.exp(fetched), 0.0)
@@ -184,14 +205,15 @@
         early_keys_kernel,
         out_shape=jax.ShapeDtypeStruct((token_rows, width), jnp.float32),
         in_specs=[smem] + [anywhere] * 11,
-        out_specs=vmem,
+        out_specs=anywhere,
         scratch_shapes=[
+            pltpu.VMEM((token_rows, width), jnp.float32),
             pltpu.VMEM((3, token_rows, width), jnp.bfloat16),
             pltpu.VMEM((3, *block), jnp.bfloat16),
             pltpu.SemaphoreType.DMA((6, 2)),
         ],
-        compiler_params=pltpu.CompilerParams(vmem_limit_bytes=24 << 20),
-        cost_estimate=cost(3, 13),
+        compiler_params=pltpu.CompilerParams(vmem_limit_bytes=GRANT),
+        cost_estimate=cost(12, 13),
         name="early_keys",
     )(place, *tokens, *[part for ahead in EARLY for part in rows[ahead]])
     return pl.pallas_call(
@@ -200,25 +222,34 @@
             jax.ShapeDtypeStruct((32, 2 * LANES), jnp.float32),
             jax.ShapeDtypeStruct((8, LANES), jnp.float32),
         ),
-        in_specs=[smem] + [anywhere] * 7 + [vmem] * 5,
+        in_specs=[smem] + [anywhere] * 12,
         out_specs=(vmem, vmem),
         scratch_shapes=[
+            *like(early, dec, gain, live, states),
             pltpu.VMEM((token_rows, width), jnp.bfloat16),
             pltpu.VMEM(block, jnp.bfloat16),
             pltpu.VMEM((8, live.shape[1]), jnp.float32),
+            pltpu.SemaphoreType.DMA((5,)),
             pltpu.SemaphoreType.DMA((2, 2)),
         ],
-        compiler_params=pltpu.CompilerParams(vmem_limit_bytes=24 << 20),
+        compiler_params=pltpu.CompilerParams(vmem_limit_bytes=GRANT),
         cost_estimate=cost(1, 6),
         name="late_heads",
     )(place, *tokens, *rows[LATE], early, dec, gain, live, states)
 
 
-def scores_kernel(place, packed, proj, emb, chosen, state, slots, rows, unit, scale, ordered, unit_v, ids_v):
+def scores_kernel(place, *refs):
+    far, (state, *outs), near, refs = refs[:4], refs[4:10], refs[10:14], refs[14:]
+    near_outs, (unit_v, ids_v, sems) = refs[:5], refs[5:]
+    copies = load(far, near, sems)
+    packed, proj, emb, chosen = near
+    slots, rows, unit, scale, ordered = near_outs
     shard, r = place[0], place[1]
     n_rows, width = emb.shape
     per_x = state.shape[0]
     cols = rows.shape[1]
+    for copy in copies:
+        copy.wait()
     feats = packed[:, :, :width].reshape(4 * per_x, width)
     ordered[...] = lax.dot_general(
         chosen[...], feats, (((1,), (1,)), ((), ())), preferred_element_type=jnp.float32
@@ -250,6 +281,7 @@
             rows[...] = row_unit[:, x * cols : (x + 1) * cols]
             unit[...] = unit_all[:, x * cols : (x + 1) * cols]
 
+    copies = load(near_outs, outs, sems)
     share = unit_v[pl.ds(pl.multiple_of(r * per_x, per_x), per_x), :]
     found = (
         lax.dot_general(
@@ -268,6 +300,8 @@
         picked = jnp.where(places[:, k : k + 1] == row, found, 0.0)
         total = jnp.where(lane == k, jnp.sum(picked, axis=1, keepdims=True), total)
     state[...] = total
+    for copy in copies:
+        copy.wait()
 
 
 def coef_kernel(packets, out):
@@ -291,12 +325,11 @@
     out[...] = jnp.broadcast_to(packed[None], out.shape)
 
 
-def gradient_kernel(coef, slot, *refs):
-    far, (keep, send, matrix_v), near, sems = refs[:4], refs[4:7], refs[7:11], refs[11]
-    copies = [pltpu.make_async_copy(a, b, sems.at[i]) for i, (a, b) in enumerate(zip(far, near))]
-    for copy in copies:
-        copy.start()
-    rows, unit, scale, ordered = near
+def gradient_kernel(coef, *refs):
+    far, (keep, send, matrix_v), near, sems = refs[:5], refs[5:8], refs[8:13], refs[13]
+    copies = load(far, near, sems)
+    slot, rows, unit, scale, ordered = near
+    copies[0].wait()
     n_rows = matrix_v.shape[1]
     blocks = coef.shape[0]
 
@@ -312,7 +345,7 @@
                 total += jnp.where(places[:, k : k + 1] == row, values[:, k : k + 1], 0.0)
             matrix_v[pl.ds(pl.multiple_of(x * blocks + b * 8, 8), 8), :] = total
 
-    for copy in copies:
+    for copy in copies[1:]:
         copy.wait()
     along_all = jnp.concatenate([coef[pl.ds(p, 16, stride=8), :] for p in range(8)], axis=0)
     row_high, row_low = halves(rows[...])
@@ -389,28 +422,32 @@
     vmem = pl.BlockSpec(memory_space=pltpu.VMEM)
     with jax.named_scope("scores"):
         queries = n_index * nx
+        operands = (packed, query_proj, index_emb, chosen)
+        results = (
+            jax.ShapeDtypeStruct((n_index, LANES), jnp.int32),
+            jax.ShapeDtypeStruct((shard_rows, cols), jnp.float32),
+            jax.ShapeDtypeStruct((queries, cols), jnp.float32),
+            jax.ShapeDtypeStruct((queries, 1), jnp.float32),
+            jax.ShapeDtypeStruct((width, queries), jnp.bfloat16),
+        )
+        anywhere = pl.BlockSpec(memory_space=pl.ANY)
         state, slots, my_rows, my_unit, query_scale, ordered = pl.pallas_call(
             scores_kernel,
-            out_shape=(
-                jax.ShapeDtypeStruct((n_index, LANES), jnp.float32),
-                jax.ShapeDtypeStruct((n_index, LANES), jnp.int32),
-                jax.ShapeDtypeStruct((shard_rows, cols), jnp.float32),
-                jax.ShapeDtypeStruct((queries, cols), jnp.float32),
-                jax.ShapeDtypeStruct((queries, 1), jnp.float32),
-                jax.ShapeDtypeStruct((width, queries), jnp.bfloat16),
-            ),
-            in_specs=[pl.BlockSpec(memory_space=pltpu.SMEM)] + [vmem] * 4,
-            out_specs=(vmem,) * 6,
+            out_shape=(jax.ShapeDtypeStruct((n_index, LANES), jnp.float32), *results),
+            in_specs=[pl.BlockSpec(memory_space=pltpu.SMEM)] + [anywhere] * 4,
+            out_specs=(vmem,) + (anywhere,) * 5,
             scratch_shapes=[
+                *like(*operands, *results),
                 pltpu.VMEM((queries, width), jnp.float32),
                 pltpu.VMEM((nx, n_index, LANES), jnp.int32),
+                pltpu.SemaphoreType.DMA((5,)),
             ],
-            compiler_params=pltpu.CompilerParams(vmem_limit_bytes=28 << 20),
+            compiler_params=pltpu.CompilerParams(vmem_limit_bytes=GRANT),
             cost_estimate=pl.CostEstimate(
-                flops=4 << 30, bytes_accessed=8 << 20, transcendentals=0
+                flops=64 << 30, bytes_accessed=8 << 20, transcendentals=0
             ),
             name="scores",
-        )(jnp.stack([my_shard, r]).astype(jnp.int32), packed, query_proj, index_emb, chosen)
+        )(jnp.stack([my_shard, r]).astype(jnp.int32), *operands)
 
     with jax.named_scope("reduce_scores"):
         states = lax.all_to_all(state, ("y", "core", *Z), 0, 0, tiled=True)
@@ -450,14 +487,14 @@
         keep, send = pl.pallas_call(
             gradient_kernel,
             out_shape=(part, part),
-            in_specs=[vmem] * 2 + [pl.BlockSpec(memory_space=pl.ANY)] * 4,
+            in_specs=[vmem] + [anywhere] * 5,
             out_specs=(vmem, vmem),
             scratch_shapes=[
                 pltpu.VMEM((queries, shard_rows), jnp.float32),
-                *[pltpu.VMEM(x.shape, x.dtype) for x in (my_rows, my_unit, query_scale, ordered)],
-                pltpu.SemaphoreType.DMA((4,)),
+                *like(slots, my_rows, my_unit, query_scale, ordered),
+                pltpu.SemaphoreType.DMA((5,)),
             ],
-            compiler_params=pltpu.CompilerParams(vmem_limit_bytes=16 << 20),
+            compiler_params=pltpu.CompilerParams(vmem_limit_bytes=GRANT),
             name="gradient",
         )(coef, slots, my_rows, my_unit, query_scale, ordered)
 

time: 283 us -> 268 us (0.947)
  local copies, waits for them, and re-layouts: 40.2 us -> 22.4 us
  Pallas kernels: 29.4 us -> 39 us
  waiting for transfers between devices: 53.1 us -> 44.3 us
  starting transfers between devices: 105 us -> 100 us
  blocking collectives: 45 us -> 48.5 us
  other arithmetic: 6.05 us -> 9.27 us
    unnamed x59 -> x29, local copies, waits for them, and re-layouts: 25.7 us -> 6.31 us
    ppermute x17, waiting for transfers between devices: 18.9 us -> 7.51 us  [shift(): return lax.ppermute(x, axis, [((i + step) % size, i) for i in range(size)])]
    all_to_all x1, starting transfers between devices: 14.7 us -> 7.21 us  [body(): states = lax.all_to_all(state, ('y', 'core', *Z), 0, 0, tiled=True)]
    all_to_all x4, waiting for transfers between devices: 17.9 us -> 24.7 us  [send_all(): lax.all_to_all(jnp.broadcast_to(x[None], (size, *x.shape)), axis, 0, 0, t...]
    all_to_all x1, waiting for transfers between devices: 3.55 us -> 0.04 us  [body(): states = lax.all_to_all(state, ('y', 'core', *Z), 0, 0, tiled=True)]
    pallas_call x1, Pallas kernels: 5.06 us -> 8.24 us  [body(): pl.pallas_call(scores_kernel, out_shape=(jax.ShapeDtypeStruct((n_index, L...]
    ppermute x17, starting transfers between devices: 50.3 us -> 53.2 us  [shift(): return lax.ppermute(x, axis, [((i + step) % size, i) for i in range(size)])]
  transfers between devices with their start and end apart: 23 -> 23, of which waited for: 9 -> 7; matrix products, arithmetic and copies ran while one was open for 8% -> 9% of each run, Pallas kernels for 5% -> 7%
where the time goes in v7:
time: 268 us; the launch traced here: 265 us
  starting transfers between devices  100 us (37%)
  blocking collectives  48.5 us (18%)
  waiting for transfers between devices  44.3 us (17%)
  Pallas kernels  39 us (15%)
  local copies, waits for them, and re-layouts  22.4 us (8%)
  other arithmetic  9.27 us (3%)
    ppermute x17, starting transfers between devices, shift(): return lax.ppermute(x, axis, [((i + step) % size, i) for i in range(size)])  53.2 us
    all_to_all x4, starting transfers between devices, send_all(): lax.all_to_all(jnp.broadcast_to(x[None], (size, *x.shape)), axis, 0, 0, t...  36.1 us
    all_to_all x1, blocking collectives, body(): coef = lax.all_to_all(coef, Z, 0, 0, tiled=True).reshape(n_index, LANES)  24.7 us
    all_to_all x4, waiting for transfers between devices, send_all(): lax.all_to_all(jnp.broadcast_to(x[None], (size, *x.shape)), axis, 0, 0, t...  24.7 us
    all_to_all x1, blocking collectives, body(): lax.all_to_all(packet, NEAR, 0, 0, tiled=True)  12.7 us
    all_to_all x1, waiting for transfers between devices, body(): term = jnp.sum(lax.all_to_all(term, Z, 0, 0, tiled=True), axis=0)  12.1 us
    all_to_all x1, blocking collectives, body(): term = jnp.sum(lax.all_to_all(term, 'y', 0, 0, tiled=True), axis=0)  11 us
    pallas_call x1, Pallas kernels, attention_packet(): pl.pallas_call(early_keys_kernel, out_shape=jax.ShapeDtypeStruct((token_r...  10.4 us
  transfers between devices with their start and end apart: 23, of which 7 were waited for; matrix products, arithmetic and copies ran while one was open for 9% of the time, Pallas kernels for 7%

profile of v7, /device:TPU:6, one launch (start us, length us, event | category | flops | bytes accessed | tf_op | source)
XLA Modules:
  0.0 264.7 jit_solution(18300363858650519044)
XLA Ops:
  0.6 1.6 broadcast_in_dim.14
  2.2 15.1 %all-to-all-start = ((bf16[4,32,1024]{2,1,0:T(8,128)(2,1)}), bf16[4,32,1024]{2,1,0:T(8,128)(2,1)S(1)}, u32[]{:S(2)}, u32[]{:S(2)}) async-start(bf16[4,32,1024]{2,1,0:T(8,128)(2,1)} %broadcast_in_dim.14), calls=%async_computation | async-start | bytes 524288 | tf_op jit(solution)/shard_map/gather_key_proj/all_to_all | solution.py:36
  17.3 2.7 %collective-permute-start = (bf16[640,1024]{1,0:T(8,128)(2,1)}, bf16[640,1024]{1,0:T(8,128)(2,1)S(1)}, u32[]{:S(2)}, u32[]{:S(2)}) collective-permute-start(bf16[640,1024]{1,0:T(8,128)(2,1)} %bitcast.34), channel_id=1, source_target_pairs={{1,0},{2,1},{3,2},{0,3},{5,4},{6,5},{7,6},{4,7},{9,8},{10,9},{11,1... | collective-permute-start | bytes 3932168 | tf_op jit(solution)/shard_map/gather_enc_out/ppermute | solution.py:31
  20.0 4.3 %collective-permute-start.2 = (bf16[640,1024]{1,0:T(8,128)(2,1)}, bf16[640,1024]{1,0:T(8,128)(2,1)S(1)}, u32[]{:S(2)}, u32[]{:S(2)}) collective-permute-start(bf16[640,1024]{1,0:T(8,128)(2,1)} %bitcast.35), channel_id=1, source_target_pairs={{3,0},{0,1},{1,2},{2,3},{7,4},{4,5},{5,6},{6,7},{11,8},{8,9},{9,10... | collective-permute-start | bytes 3932168 | tf_op jit(solution)/shard_map/gather_enc_out/ppermute | solution.py:31
  25.3 10.5 %all-to-all-done = bf16[4,32,1024]{2,1,0:T(8,128)(2,1)S(1)} async-done(((bf16[4,32,1024]{2,1,0:T(8,128)(2,1)}), bf16[4,32,1024]{2,1,0:T(8,128)(2,1)S(1)}, u32[]{:S(2)}, u32[]{:S(2)}) %all-to-all-start) | async-done | bytes 262176 | tf_op jit(solution)/shard_map/gather_key_proj/all_to_all | solution.py:36
  35.9 4.9 %collective-permute-start.4 = (bf16[4,32,1024]{2,1,0:T(8,128)(2,1)S(1)}, bf16[4,32,1024]{2,1,0:T(8,128)(2,1)S(1)}, u32[]{:S(2)}, u32[]{:S(2)}) collective-permute-start(bf16[4,32,1024]{2,1,0:T(8,128)(2,1)S(1)} %all-to-all-done), channel_id=1, source_target_pairs={{8,0},{16,8},{24,16},{32,24},{40,32},{48,40},{56,48},{64,56},{72,6... | collective-permute-start | bytes 786440 | tf_op jit(solution)/shard_map/gather_key_proj/ppermute | solution.py:31
  40.8 1.9 collective-permute-start.5
  43.4 3.9 %collective-permute-start.7 = (bf16[4,32,1024]{2,1,0:T(8,128)(2,1)S(1)}, bf16[4,32,1024]{2,1,0:T(8,128)(2,1)S(1)}, u32[]{:S(2)}, u32[]{:S(2)}) collective-permute-start(bf16[4,32,1024]{2,1,0:T(8,128)(2,1)S(1)} %all-to-all-done), channel_id=1, source_target_pairs={{120,0},{0,8},{8,16},{16,24},{24,32},{32,40},{40,48},{48,56},{56,6... | collective-permute-start | bytes 786440 | tf_op jit(solution)/shard_map/gather_key_proj/ppermute | solution.py:31
  47.3 1.3 collective-permute-done.4
  48.6 4.7 %collective-permute-start.6 = (bf16[2,32,1024]{2,1,0:T(8,128)(2,1)S(1)}, bf16[2,32,1024]{2,1,0:T(8,128)(2,1)S(1)}, u32[]{:S(2)}, u32[]{:S(2)}) collective-permute-start(bf16[2,32,1024]{2,1,0:T(8,128)(2,1)S(1)} %get-tuple-element.30), channel_id=1, source_target_pairs={{112,0},{120,8},{0,16},{8,24},{16,32},{24,40},{32,48},{40,56},{48,... | collective-permute-start | bytes 393224 | tf_op jit(solution)/shard_map/gather_key_proj/ppermute | solution.py:31
  54.7 4.3 %collective-permute-done.6 = bf16[2,32,1024]{2,1,0:T(8,128)(2,1)S(1)} collective-permute-done((bf16[2,32,1024]{2,1,0:T(8,128)(2,1)S(1)}, bf16[2,32,1024]{2,1,0:T(8,128)(2,1)S(1)}, u32[]{:S(2)}, u32[]{:S(2)}) %collective-permute-start.6) | collective-permute-done | bytes 131104 | tf_op jit(solution)/shard_map/gather_key_proj/ppermute | solution.py:31
  60.4 4.9 %collective-permute-start.8 = (bf16[16,32,1024]{2,1,0:T(8,128)(2,1)}, bf16[16,32,1024]{2,1,0:T(8,128)(2,1)}, u32[]{:S(2)}, u32[]{:S(2)}) collective-permute-start(bf16[16,32,1024]{2,1,0:T(8,128)(2,1)} %constant_dynamic-update-slice_fusion.refs_5_), channel_id=1, source_target_pairs={{128,0},{256,128},{384,256},{0,384},{129,1},{257,129},{385,257},{1... | collective-permute-start | bytes 3145736 | tf_op jit(solution)/shard_map/gather_key_proj/ppermute | solution.py:31
  65.3 1.9 collective-permute-start.10
  70.4 8.0 %all-to-all-start.1 = ((bf16[16,2,448]{2,1,0:T(2,128)(2,1)}), bf16[16,2,448]{2,1,0:T(2,128)(2,1)S(1)}, u32[]{:S(2)}, u32[]{:S(2)}) async-start(bf16[16,2,448]{2,1,0:T(2,128)(2,1)} %reshape.206), calls=%async_computation.1 | async-start | bytes 65536 | tf_op jit(solution)/shard_map/gather_queries/all_to_all | solution.py:36
  78.4 12.6 %all-to-all-done.1 = bf16[16,2,448]{2,1,0:T(2,128)(2,1)S(1)} async-done(((bf16[16,2,448]{2,1,0:T(2,128)(2,1)}), bf16[16,2,448]{2,1,0:T(2,128)(2,1)S(1)}, u32[]{:S(2)}, u32[]{:S(2)}) %all-to-all-start.1) | async-done | bytes 28704 | tf_op jit(solution)/shard_map/gather_queries/all_to_all | solution.py:36
  91.2 1.0 broadcast_in_dim.17
  92.2 7.7 %all-to-all-start.2 = ((bf16[32,16,896]{2,1,0:T(8,128)(2,1)}), bf16[32,16,896]{2,1,0:T(8,128)(2,1)}, u32[]{:S(2)}, u32[]{:S(2)}) async-start(bf16[32,16,896]{2,1,0:T(8,128)(2,1)} %broadcast_in_dim.17), calls=%async_computation.2 | async-start | bytes 1835008 | tf_op jit(solution)/shard_map/gather_queries/all_to_all | solution.py:36
  100.5 1.9 slice.34
  102.4 4.7 %collective-permute-start.9 = (bf16[8,32,1024]{2,1,0:T(8,128)(2,1)}, bf16[8,32,1024]{2,1,0:T(8,128)(2,1)}, u32[]{:S(2)}, u32[]{:S(2)}) collective-permute-start(bf16[8,32,1024]{2,1,0:T(8,128)(2,1)} %slice.34), channel_id=1, source_target_pairs={{128,0},{256,128},{384,256},{0,384},{129,1},{257,129},{385,257},{1... | collective-permute-start | bytes 1572872 | tf_op jit(solution)/shard_map/gather_key_proj/ppermute | solution.py:31
  107.2 1.9 slice.35
  109.0 1.9 collective-permute-start.11
  113.2 1.3 fusion.refs_3_
  114.5 1.9 collective-permute-start.13
  117.4 2.7 %collective-permute-start.1 = (bf16[320,1024]{1,0:T(8,128)(2,1)}, bf16[320,1024]{1,0:T(8,128)(2,1)S(1)}, u32[]{:S(2)}, u32[]{:S(2)}) collective-permute-start(bf16[320,1024]{1,0:T(8,128)(2,1)} %slice.32), channel_id=1, source_target_pairs={{1,0},{2,1},{3,2},{0,3},{5,4},{6,5},{7,6},{4,7},{9,8},{10,9},{11,1... | collective-permute-start | bytes 1966088 | tf_op jit(solution)/shard_map/gather_enc_out/ppermute | solution.py:31
  121.1 4.3 %collective-permute-start.3 = (bf16[320,1024]{1,0:T(8,128)(2,1)}, bf16[320,1024]{1,0:T(8,128)(2,1)}, u32[]{:S(2)}, u32[]{:S(2)}) collective-permute-start(bf16[320,1024]{1,0:T(8,128)(2,1)} %slice.33), channel_id=1, source_target_pairs={{3,0},{0,1},{1,2},{2,3},{7,4},{4,5},{5,6},{6,7},{11,8},{8,9},{9,10... | collective-permute-start | bytes 1966088 | tf_op jit(solution)/shard_map/gather_enc_out/ppermute | solution.py:31
  125.4 1.9 collective-permute-start.14
  127.3 2.4 collective-permute-start.15
  129.8 8.2 %scores.1 = (f32[128,128]{1,0:T(8,128)}, s32[128,128]{1,0:T(8,128)}, f32[512,192]{1,0:T(8,128)}, f32[512,192]{1,0:T(8,128)}, f32[512,1]{1,0:T(8,128)}, /*index=5*/bf16[768,512]{1,0:T(8,128)(2,1)}) custom-call(s32[2]{0:T(128)} %pad_add_fusion.1.place, bf16[32,16,896]{2,1,0:T(8,128)(2,1)} %all-to-all-done.2.refs_0_, bf16[768,768]{1,0:T(8,128)(2,1)} %refs_1_.1, ...), custom_call_target="tpu_custom_call" | custom-call | flops 68719476736 | bytes 8388608 | tf_op jit(solution)/shard_map/scores/scores/pallas_call | solution.py:434
  138.0 7.2 %all-to-all-start.3 = ((f32[128,1,128]{2,1,0:T(1,128)}), f32[128,1,128]{2,1,0:T(1,128)S(1)}, u32[]{:S(2)}, u32[]{:S(2)}) async-start(f32[128,1,128]{2,1,0:T(1,128)} %bitcast.44), calls=%async_computation.3 | async-start | bytes 131072 | tf_op jit(solution)/shard_map/reduce_scores/all_to_all | solution.py:453
  145.3 1.1 constant_dynamic-update-slice_fusion.6
  146.3 1.1 constant_dynamic-update-slice_fusion.5.refs_5_
  147.4 2.1 collective-permute-start.12
  149.6 10.4 %early_keys.1.refs_7_ = f32[640,1024]{1,0:T(8,128)} custom-call(s32[4]{0:T(128)} %pad_add_fusion.place, bf16[640,1024]{1,0:T(8,128)(2,1)} %bitcast.36, bf16[640,1024]{1,0:T(8,128)(2,1)} %copy-done, bf16[320,1024]{1,0:T(8,128)(2,1)} %copy-done.4, bf16[320,1024]{1,0:T(8,128)(2,1)} %collective-permute-done.3.refs_3_, bf16[640,1024]{1,0:T(8,128)(2,1)} %copy-done.1, ...), custom_call_target="tpu_custom_call" | custom-call | flops 16106127360 | bytes 13631488 | tf_op jit(solution)/shard_map/attention/early_keys/pallas_call | solution.py:204
  161.1 9.7 %late_heads.1 = (f32[32,256]{1,0:T(8,128)}, f32[8,128]{1,0:T(8,128)}) custom-call(s32[4]{0:T(128)} %pad_add_fusion.place, bf16[640,1024]{1,0:T(8,128)(2,1)} %bitcast.37, bf16[640,1024]{1,0:T(8,128)(2,1)} %copy-done, bf16[320,1024]{1,0:T(8,128)(2,1)} %copy-done.4, bf16[320,1024]{1,0:T(8,128)(2,1)} %collective-permute-done.3.refs_3_, ...), custom_call_target="tpu_custom_call" | custom-call | flops 1342177280 | bytes 6291456 | tf_op jit(solution)/shard_map/attention/late_heads/pallas_call | solution.py:219
  171.6 12.7 %all_to_all.56 = f32[32,1,256]{2,1,0:T(1,128)S(1)} all-to-all(f32[32,1,256]{2,1,0:T(1,128)S(1)} %copy.16), channel_id=1, replica_groups=mesh['y'=4,'zq'=4,'zr'=4,'core'=2,'reader'=4] {'reader','y','core'}, dimensions={0} | all-to-all | bytes 65536 | tf_op jit(solution)/shard_map/targets/all_to_all | solution.py:475
  184.9 1.6 coef.1
  186.5 24.7 %all_to_all.57 = f32[16,8,128]{2,1,0:T(8,128)} all-to-all(f32[16,8,128]{2,1,0:T(8,128)} %coef.1), channel_id=1, replica_groups=mesh['y'=4,'zq'=4,'zr'=4,'core'=2,'reader'=4] {'zq','zr'}, dimensions={0} | all-to-all | bytes 131072 | tf_op jit(solution)/shard_map/targets/all_to_all | solution.py:483
  211.2 9.1 %gradient.1 = (f32[384,192]{1,0:T(8,128)}, f32[384,192]{1,0:T(8,128)}) custom-call(f32[128,128]{1,0:T(8,128)} %bitcast.39, s32[128,128]{1,0:T(8,128)} %get-tuple-element.22.refs_0_, f32[512,192]{1,0:T(8,128)} %get-tuple-element.23.refs_1_, f32[512,192]{1,0:T(8,128)} %get-tuple-element.24.refs_2_, f32[512,1]{1,0:T(8,128)} %get-tuple-element.25.refs_3_, ...), custom_call_target="tpu_custom_call" | custom-call | tf_op jit(solution)/shard_map/gradient/gradient/pallas_call | solution.py:487
  220.3 1.9 collective-permute-start.16
  222.2 1.9 collective-permute-done.16
  224.1 1.0 add.150
  225.2 11.0 %all_to_all.58 = f32[4,96,192]{2,1,0:T(8,128)S(1)} all-to-all(f32[4,96,192]{2,1,0:T(8,128)S(1)} %bitcast.33), channel_id=1, replica_groups=mesh['y'=4,'zq'=4,'zr'=4,'core'=2,'reader'=4] {'y'}, dimensions={0} | all-to-all | bytes 589824 | tf_op jit(solution)/shard_map/reduce_gradient/all_to_all | solution.py:503
  236.9 3.5 %all-to-all-start.7 = ((f32[16,6,192]{2,1,0:T(8,128)}), f32[16,6,192]{2,1,0:T(8,128)S(1)}, u32[]{:S(2)}, u32[]{:S(2)}) async-start(f32[16,6,192]{2,1,0:T(8,128)} %reshape.201), calls=%async_computation.7 | async-start | bytes 262144 | tf_op jit(solution)/shard_map/reduce_gradient/all_to_all | solution.py:505
  240.5 1.3 slice.30
  242.5 12.1 %all-to-all-done.7 = f32[16,6,192]{2,1,0:T(8,128)S(1)} async-done(((f32[16,6,192]{2,1,0:T(8,128)}), f32[16,6,192]{2,1,0:T(8,128)S(1)}, u32[]{:S(2)}, u32[]{:S(2)}) %all-to-all-start.7) | async-done | bytes 73760 | tf_op jit(solution)/shard_map/reduce_gradient/all_to_all | solution.py:505
  255.3 5.3 %all-to-all-start.8 = ((f32[4,6,192]{2,1,0:T(8,128)}), f32[4,6,192]{2,1,0:T(8,128)S(1)}, u32[]{:S(2)}, u32[]{:S(2)}) async-start(f32[4,6,192]{2,1,0:T(8,128)} %broadcast_in_dim.18), calls=%async_computation.8 | async-start | bytes 65536 | tf_op jit(solution)/shard_map/reduce_gradient/all_to_all | solution.py:36
  260.6 1.9 log_bitcast_fusion
  262.5 1.5 all-to-all-done.8
  (77 shorter events, 17.8 us)
Async XLA Ops:
  2.2 33.6 %all-to-all-start = ((bf16[4,32,1024]{2,1,0:T(8,128)(2,1)}), bf16[4,32,1024]{2,1,0:T(8,128)(2,1)S(1)}, u32[]{:S(2)}, u32[]{:S(2)}) async-start(bf16[4,32,1024]{2,1,0:T(8,128)(2,1)} %broadcast_in_dim.14), calls=%async_computation | async-start | bytes 524288 | tf_op jit(solution)/shard_map/gather_key_proj/all_to_all | solution.py:36
  17.3 99.1 %collective-permute-start = (bf16[640,1024]{1,0:T(8,128)(2,1)}, bf16[640,1024]{1,0:T(8,128)(2,1)S(1)}, u32[]{:S(2)}, u32[]{:S(2)}) collective-permute-start(bf16[640,1024]{1,0:T(8,128)(2,1)} %bitcast.34), channel_id=1, source_target_pairs={{1,0},{2,1},{3,2},{0,3},{5,4},{6,5},{7,6},{4,7},{9,8},{10,9},{11,1... | collective-permute-start | bytes 3932168 | tf_op jit(solution)/shard_map/gather_enc_out/ppermute | solution.py:31
  20.0 100.1 %collective-permute-start.2 = (bf16[640,1024]{1,0:T(8,128)(2,1)}, bf16[640,1024]{1,0:T(8,128)(2,1)S(1)}, u32[]{:S(2)}, u32[]{:S(2)}) collective-permute-start(bf16[640,1024]{1,0:T(8,128)(2,1)} %bitcast.35), channel_id=1, source_target_pairs={{3,0},{0,1},{1,2},{2,3},{7,4},{4,5},{5,6},{6,7},{11,8},{8,9},{9,10... | collective-permute-start | bytes 3932168 | tf_op jit(solution)/shard_map/gather_enc_out/ppermute | solution.py:31
  25.3 41.9 %copy-start.5 = (bf16[4,16,1024]{2,1,0:T(8,128)(2,1)S(1)}, bf16[4,16,1024]{2,1,0:T(8,128)(2,1)}, u32[]{:S(2)}) copy-start(bf16[4,16,1024]{2,1,0:T(8,128)(2,1)} %param.17) | copy-start | bytes 393220
  35.9 12.7 %collective-permute-start.4 = (bf16[4,32,1024]{2,1,0:T(8,128)(2,1)S(1)}, bf16[4,32,1024]{2,1,0:T(8,128)(2,1)S(1)}, u32[]{:S(2)}, u32[]{:S(2)}) collective-permute-start(bf16[4,32,1024]{2,1,0:T(8,128)(2,1)S(1)} %all-to-all-done), channel_id=1, source_target_pairs={{8,0},{16,8},{24,16},{32,24},{40,32},{48,40},{56,48},{64,56},{72,6... | collective-permute-start | bytes 786440 | tf_op jit(solution)/shard_map/gather_key_proj/ppermute | solution.py:31
  40.8 13.2 %collective-permute-start.5 = (bf16[2,32,1024]{2,1,0:T(8,128)(2,1)S(1)}, bf16[2,32,1024]{2,1,0:T(8,128)(2,1)S(1)}, u32[]{:S(2)}, u32[]{:S(2)}) collective-permute-start(bf16[2,32,1024]{2,1,0:T(8,128)(2,1)S(1)} %get-tuple-element.31), channel_id=1, source_target_pairs={{16,0},{24,8},{32,16},{40,24},{48,32},{56,40},{64,48},{72,56},{80,... | collective-permute-start | bytes 393224 | tf_op jit(solution)/shard_map/gather_key_proj/ppermute | solution.py:31
  43.4 16.2 %collective-permute-start.7 = (bf16[4,32,1024]{2,1,0:T(8,128)(2,1)S(1)}, bf16[4,32,1024]{2,1,0:T(8,128)(2,1)S(1)}, u32[]{:S(2)}, u32[]{:S(2)}) collective-permute-start(bf16[4,32,1024]{2,1,0:T(8,128)(2,1)S(1)} %all-to-all-done), channel_id=1, source_target_pairs={{120,0},{0,8},{8,16},{16,24},{24,32},{32,40},{40,48},{48,56},{56,6... | collective-permute-start | bytes 786440 | tf_op jit(solution)/shard_map/gather_key_proj/ppermute | solution.py:31
  48.6 10.4 %collective-permute-start.6 = (bf16[2,32,1024]{2,1,0:T(8,128)(2,1)S(1)}, bf16[2,32,1024]{2,1,0:T(8,128)(2,1)S(1)}, u32[]{:S(2)}, u32[]{:S(2)}) collective-permute-start(bf16[2,32,1024]{2,1,0:T(8,128)(2,1)S(1)} %get-tuple-element.30), channel_id=1, source_target_pairs={{112,0},{120,8},{0,16},{8,24},{16,32},{24,40},{32,48},{40,56},{48,... | collective-permute-start | bytes 393224 | tf_op jit(solution)/shard_map/gather_key_proj/ppermute | solution.py:31
  54.7 13.5 %copy-start.9 = (s32[1,20]{1,0:T(1,128)S(1)}, s32[1,20]{1,0:T(1,128)}, u32[]{:S(2)}) copy-start(s32[1,20]{1,0:T(1,128)} %param.12) | copy-start | bytes 244
  54.7 13.6 %copy-start.7 = (bf16[1,768]{1,0:T(2,128)(2,1)S(1)}, bf16[1,768]{1,0:T(2,128)(2,1)}, u32[]{:S(2)}) copy-start(bf16[1,768]{1,0:T(2,128)(2,1)} %param.10) | copy-start | bytes 4612
  60.4 40.2 %collective-permute-start.8 = (bf16[16,32,1024]{2,1,0:T(8,128)(2,1)}, bf16[16,32,1024]{2,1,0:T(8,128)(2,1)}, u32[]{:S(2)}, u32[]{:S(2)}) collective-permute-start(bf16[16,32,1024]{2,1,0:T(8,128)(2,1)} %constant_dynamic-update-slice_fusion.refs_5_), channel_id=1, source_target_pairs={{128,0},{256,128},{384,256},{0,384},{129,1},{257,129},{385,257},{1... | collective-permute-start | bytes 3145736 | tf_op jit(solution)/shard_map/gather_key_proj/ppermute | solution.py:31
  65.3 41.9 %collective-permute-start.10 = (bf16[16,32,1024]{2,1,0:T(8,128)(2,1)}, bf16[16,32,1024]{2,1,0:T(8,128)(2,1)}, u32[]{:S(2)}, u32[]{:S(2)}) collective-permute-start(bf16[16,32,1024]{2,1,0:T(8,128)(2,1)} %constant_dynamic-update-slice_fusion.refs_5_), channel_id=1, source_target_pairs={{384,0},{0,128},{128,256},{256,384},{385,1},{1,129},{129,257},{257... | collective-permute-start | bytes 3145736 | tf_op jit(solution)/shard_map/gather_key_proj/ppermute | solution.py:31
  70.4 20.6 %all-to-all-start.1 = ((bf16[16,2,448]{2,1,0:T(2,128)(2,1)}), bf16[16,2,448]{2,1,0:T(2,128)(2,1)S(1)}, u32[]{:S(2)}, u32[]{:S(2)}) async-start(bf16[16,2,448]{2,1,0:T(2,128)(2,1)} %reshape.206), calls=%async_computation.1 | async-start | bytes 65536 | tf_op jit(solution)/shard_map/gather_queries/all_to_all | solution.py:36
  92.2 37.6 %all-to-all-start.2 = ((bf16[32,16,896]{2,1,0:T(8,128)(2,1)}), bf16[32,16,896]{2,1,0:T(8,128)(2,1)}, u32[]{:S(2)}, u32[]{:S(2)}) async-start(bf16[32,16,896]{2,1,0:T(8,128)(2,1)} %broadcast_in_dim.17), calls=%async_computation.2 | async-start | bytes 1835008 | tf_op jit(solution)/shard_map/gather_queries/all_to_all | solution.py:36
  102.4 9.5 %copy-start.8 = (bf16[1024]{0:T(1024)(128)(2,1)S(1)}, bf16[1024]{0:T(1024)(128)(2,1)}, u32[]{:S(2)}) copy-start(bf16[1024]{0:T(1024)(128)(2,1)} %param.16) | copy-start | bytes 6148
  102.4 23.0 %collective-permute-start.9 = (bf16[8,32,1024]{2,1,0:T(8,128)(2,1)}, bf16[8,32,1024]{2,1,0:T(8,128)(2,1)}, u32[]{:S(2)}, u32[]{:S(2)}) collective-permute-start(bf16[8,32,1024]{2,1,0:T(8,128)(2,1)} %slice.34), channel_id=1, source_target_pairs={{128,0},{256,128},{384,256},{0,384},{129,1},{257,129},{385,257},{1... | collective-permute-start | bytes 1572872 | tf_op jit(solution)/shard_map/gather_key_proj/ppermute | solution.py:31
  109.0 18.3 %collective-permute-start.11 = (bf16[8,32,1024]{2,1,0:T(8,128)(2,1)}, bf16[8,32,1024]{2,1,0:T(8,128)(2,1)}, u32[]{:S(2)}, u32[]{:S(2)}) collective-permute-start(bf16[8,32,1024]{2,1,0:T(8,128)(2,1)} %slice.35), channel_id=1, source_target_pairs={{384,0},{0,128},{128,256},{256,384},{385,1},{1,129},{129,257},{257... | collective-permute-start | bytes 1572872 | tf_op jit(solution)/shard_map/gather_key_proj/ppermute | solution.py:31
  114.5 35.1 %collective-permute-start.13 = (bf16[16,32,1024]{2,1,0:T(8,128)(2,1)}, bf16[16,32,1024]{2,1,0:T(8,128)(2,1)}, u32[]{:S(2)}, u32[]{:S(2)}) collective-permute-start(bf16[16,32,1024]{2,1,0:T(8,128)(2,1)} %constant_dynamic-update-slice_fusion.refs_5_), channel_id=1, source_target_pairs={{4,0},{0,4},{5,1},{1,5},{6,2},{2,6},{7,3},{3,7},{12,8},{8,12},{13,... | collective-permute-start | bytes 3145736 | tf_op jit(solution)/shard_map/gather_key_proj/ppermute | solution.py:31
  116.4 21.6 %copy-start = (bf16[640,1024]{1,0:T(8,128)(2,1)}, bf16[640,1024]{1,0:T(8,128)(2,1)S(1)}, u32[]{:S(2)}) copy-start(bf16[640,1024]{1,0:T(8,128)(2,1)S(1)} %collective-permute-done.refs_1_) | copy-start | bytes 3932164
  117.4 30.0 %collective-permute-start.1 = (bf16[320,1024]{1,0:T(8,128)(2,1)}, bf16[320,1024]{1,0:T(8,128)(2,1)S(1)}, u32[]{:S(2)}, u32[]{:S(2)}) collective-permute-start(bf16[320,1024]{1,0:T(8,128)(2,1)} %slice.32), channel_id=1, source_target_pairs={{1,0},{2,1},{3,2},{0,3},{5,4},{6,5},{7,6},{4,7},{9,8},{10,9},{11,1... | collective-permute-start | bytes 1966088 | tf_op jit(solution)/shard_map/gather_enc_out/ppermute | solution.py:31
  120.1 17.9 %copy-start.1 = (bf16[640,1024]{1,0:T(8,128)(2,1)}, bf16[640,1024]{1,0:T(8,128)(2,1)S(1)}, u32[]{:S(2)}) copy-start(bf16[640,1024]{1,0:T(8,128)(2,1)S(1)} %collective-permute-done.2.refs_4_) | copy-start | bytes 3932164
  121.1 28.5 %collective-permute-start.3 = (bf16[320,1024]{1,0:T(8,128)(2,1)}, bf16[320,1024]{1,0:T(8,128)(2,1)}, u32[]{:S(2)}, u32[]{:S(2)}) collective-permute-start(bf16[320,1024]{1,0:T(8,128)(2,1)} %slice.33), channel_id=1, source_target_pairs={{3,0},{0,1},{1,2},{2,3},{7,4},{4,5},{5,6},{6,7},{11,8},{8,9},{9,10... | collective-permute-start | bytes 1966088 | tf_op jit(solution)/shard_map/gather_enc_out/ppermute | solution.py:31
  125.4 24.2 %collective-permute-start.14 = (bf16[16,32,1024]{2,1,0:T(8,128)(2,1)}, bf16[16,32,1024]{2,1,0:T(8,128)(2,1)}, u32[]{:S(2)}, u32[]{:S(2)}) collective-permute-start(bf16[16,32,1024]{2,1,0:T(8,128)(2,1)} %collective-permute-done.8.refs_7_), channel_id=1, source_target_pairs={{4,0},{0,4},{5,1},{1,5},{6,2},{2,6},{7,3},{3,7},{12,8},{8,12},{13,... | collective-permute-start | bytes 3145736 | tf_op jit(solution)/shard_map/gather_key_proj/ppermute | solution.py:31
  127.3 22.2 %collective-permute-start.15 = (bf16[16,32,1024]{2,1,0:T(8,128)(2,1)}, bf16[16,32,1024]{2,1,0:T(8,128)(2,1)}, u32[]{:S(2)}, u32[]{:S(2)}) collective-permute-start(bf16[16,32,1024]{2,1,0:T(8,128)(2,1)} %collective-permute-done.10.refs_9_), channel_id=1, source_target_pairs={{4,0},{0,4},{5,1},{1,5},{6,2},{2,6},{7,3},{3,7},{12,8},{8,12},{13,... | collective-permute-start | bytes 3145736 | tf_op jit(solution)/shard_map/gather_key_proj/ppermute | solution.py:31
  138.0 22.0 %all-to-all-start.3 = ((f32[128,1,128]{2,1,0:T(1,128)}), f32[128,1,128]{2,1,0:T(1,128)S(1)}, u32[]{:S(2)}, u32[]{:S(2)}) async-start(f32[128,1,128]{2,1,0:T(1,128)} %bitcast.44), calls=%async_computation.3 | async-start | bytes 131072 | tf_op jit(solution)/shard_map/reduce_scores/all_to_all | solution.py:453
  147.4 12.6 %copy-start.2 = (bf16[16,32,1024]{2,1,0:T(8,128)(2,1)}, bf16[16,32,1024]{2,1,0:T(8,128)(2,1)S(1)}, u32[]{:S(2)}) copy-start(bf16[16,32,1024]{2,1,0:T(8,128)(2,1)S(1)} %constant_dynamic-update-slice_fusion.5.refs_5_) | copy-start | bytes 3145732
  147.4 2.2 copy-start.4
  147.4 12.6 %collective-permute-start.12 = (bf16[16,32,1024]{2,1,0:T(8,128)(2,1)S(1)}, bf16[16,32,1024]{2,1,0:T(8,128)(2,1)S(1)}, u32[]{:S(2)}, u32[]{:S(2)}) collective-permute-start(bf16[16,32,1024]{2,1,0:T(8,128)(2,1)S(1)} %constant_dynamic-update-slice_fusion.5.refs_5_), channel_id=1, source_target_pairs={{4,0},{0,4},{5,1},{1,5},{6,2},{2,6},{7,3},{3,7},{12,8},{8,12},{13,... | collective-permute-start | bytes 3145736 | tf_op jit(solution)/shard_map/gather_key_proj/ppermute | solution.py:31
  160.1 0.6 copy-start.6
  160.1 1.0 copy-start.3
  220.3 3.8 %collective-permute-start.16 = (f32[384,192]{1,0:T(8,128)}, f32[384,192]{1,0:T(8,128)S(1)}, u32[]{:S(2)}, u32[]{:S(2)}) collective-permute-start(f32[384,192]{1,0:T(8,128)} %get-tuple-element.28), channel_id=1, source_target_pairs={{4,0},{0,4},{5,1},{1,5},{6,2},{2,6},{7,3},{3,7},{12,8},{8,12},{13,... | collective-permute-start | bytes 884744 | tf_op jit(solution)/shard_map/reduce_gradient/ppermute | solution.py:31
  236.9 17.7 %all-to-all-start.7 = ((f32[16,6,192]{2,1,0:T(8,128)}), f32[16,6,192]{2,1,0:T(8,128)S(1)}, u32[]{:S(2)}, u32[]{:S(2)}) async-start(f32[16,6,192]{2,1,0:T(8,128)} %reshape.201), calls=%async_computation.7 | async-start | bytes 262144 | tf_op jit(solution)/shard_map/reduce_gradient/all_to_all | solution.py:505
  255.3 8.7 %all-to-all-start.8 = ((f32[4,6,192]{2,1,0:T(8,128)}), f32[4,6,192]{2,1,0:T(8,128)S(1)}, u32[]{:S(2)}, u32[]{:S(2)}) async-start(f32[4,6,192]{2,1,0:T(8,128)} %broadcast_in_dim.18), calls=%async_computation.8 | async-start | bytes 65536 | tf_op jit(solution)/shard_map/reduce_gradient/all_to_all | solution.py:36

commit v8 on v7

--- a/solution.py
+++ b/solution.py
@@ -16,6 +16,7 @@
 EXACT = lax.Precision.HIGHEST
 INDEX = ("y", "zq", "zr", "core")
 Z = ("zq", "zr")
+Z_BY_CLASS = ("zr", "zq")
 NEAR = ("reader", "y", "core")
 LANES = 128
 SLOT = 32
@@ -269,7 +270,10 @@
 
     vec = dot32(feats, proj[...])
     scale_all = lax.rsqrt(jnp.sum(vec * vec, axis=1, keepdims=True) + EPSILON)
-    scale[...] = scale_all
+    spread = jnp.zeros((per_x, LANES), jnp.float32)
+    for x in range(4):
+        spread = jnp.where(lane // SLOT == x, scale_all[x * per_x : (x + 1) * per_x], spread)
+    scale[...] = spread
     unit_all = vec * scale_all
     unit_v[...] = unit_all
     emb_all = emb[...]
@@ -328,8 +332,9 @@
 def gradient_kernel(coef, *refs):
     far, (keep, send, matrix_v), near, sems = refs[:5], refs[5:8], refs[8:13], refs[13]
     copies = load(far, near, sems)
-    slot, rows, unit, scale, ordered = near
+    slot, scale, rows, unit, ordered = near
     copies[0].wait()
+    copies[1].wait()
     n_rows = matrix_v.shape[1]
     blocks = coef.shape[0]
 
@@ -337,7 +342,7 @@
     def _(b):
         eight = pl.ds(pl.multiple_of(b * 8, 8), 8)
         row = lax.broadcasted_iota(jnp.int32, (8, n_rows), 1)
-        values = coef[pl.ds(b // 2 + b % 2 * 64, 8, stride=8), :]
+        values = coef[pl.ds(b // 2 + b % 2 * 64, 8, stride=8), :] * scale[eight, :]
         places = slot[eight, :]
         for x in range(4):
             total = jnp.zeros((8, n_rows), jnp.float32)
@@ -345,9 +350,10 @@
                 total += jnp.where(places[:, k : k + 1] == row, values[:, k : k + 1], 0.0)
             matrix_v[pl.ds(pl.multiple_of(x * blocks + b * 8, 8), 8), :] = total
 
-    for copy in copies[1:]:
+    for copy in copies[2:]:
         copy.wait()
     along_all = jnp.concatenate([coef[pl.ds(p, 16, stride=8), :] for p in range(8)], axis=0)
+    along_all = along_all * scale[...]
     row_high, row_low = halves(rows[...])
     parts_high, parts_low = [], []
     for x in range(4):
@@ -355,7 +361,7 @@
         high, low = halves(matrix_v[mine, :])
         part = dot32(high, row_high) + (dot32(high, row_low) + dot32(low, row_high))
         along = along_all[:, SLOT * x + 20 : SLOT * x + 21]
-        part = (part - unit[mine, :] * along) * scale[mine, :]
+        part = part - unit[mine, :] * along
         high, low = halves(part)
         parts_high.append(high)
         parts_low.append(low)
@@ -394,22 +400,26 @@
         far_low, far_high = shift(after[:mid], "reader", 1), shift(before[mid:], "reader", -1)
         tokens = (own, after, far_low, far_high, before)
 
+    width_here = key_proj.shape[1]
+    ids_high = (passage_id // 256).astype(jnp.bfloat16)
+    ids_low = (passage_id % 256).astype(jnp.bfloat16)
+    gap = ((0, 0), (0, LANES // 2 - topk))
+    coded = jnp.concatenate([query_feat, jnp.pad(ids_high, gap), jnp.pad(ids_low, gap)], axis=1)
+    coded = jnp.pad(coded, ((0, 0), (0, width_here - coded.shape[1])))
     with jax.named_scope("gather_key_proj"):
-        own = send_all(key_proj, "zq")
-        own, query_feat, passage_id = lax.optimization_barrier((own, query_feat, passage_id))
+        own = send_all(jnp.concatenate([key_proj, coded]), "zq")
         after, before = shift(own, Z, 1), shift(own, Z, -1)
         far = [shift(own[:2], Z, 2), shift(own[2:], Z, -2)]
-        own = jnp.concatenate([own, after, *far, before])
+        classes = (own, after, *far, before)
+        own = jnp.concatenate([block[:, :-1] for block in classes])
         after, before = shift(own, "y", 1), shift(own, "y", -1)
         far = jnp.concatenate([shift(after[:8], "y", 1), shift(before[8:], "y", -1)])
         key_rows = [(block, shift(block, "core", 1)) for block in (own, after, far, before)]
 
     with jax.named_scope("gather_queries"):
-        ids_high = (passage_id // 256).astype(jnp.bfloat16)
-        ids_low = (passage_id % 256).astype(jnp.bfloat16)
-        gap = ((0, 0), (0, LANES // 2 - topk))
-        coded = [query_feat, jnp.pad(ids_high, gap), jnp.pad(ids_low, gap)]
-        packed = send_all(send_all(jnp.concatenate(coded, axis=1)[0], Z), NEAR)
+        coded = jnp.concatenate([block[:, -1] for block in classes])
+        coded = jnp.roll(coded.reshape(4, 4, width_here), zr, axis=0).reshape(nz, width_here)
+        packed = send_all(coded[:, : width + LANES], NEAR)
 
     cols = width // nx
     six = width // n_index
@@ -427,7 +437,7 @@
             jax.ShapeDtypeStruct((n_index, LANES), jnp.int32),
             jax.ShapeDtypeStruct((shard_rows, cols), jnp.float32),
             jax.ShapeDtypeStruct((queries, cols), jnp.float32),
-            jax.ShapeDtypeStruct((queries, 1), jnp.float32),
+            jax.ShapeDtypeStruct((n_index, LANES), jnp.float32),
             jax.ShapeDtypeStruct((width, queries), jnp.bfloat16),
         )
         anywhere = pl.BlockSpec(memory_space=pl.ANY)
@@ -450,7 +460,7 @@
         )(jnp.stack([my_shard, r]).astype(jnp.int32), *operands)
 
     with jax.named_scope("reduce_scores"):
-        states = lax.all_to_all(state, ("y", "core", *Z), 0, 0, tiled=True)
+        states = lax.all_to_all(state, ("y", "core", *Z_BY_CLASS), 0, 0, tiled=True)
 
     with jax.named_scope("attention"):
         answer = dec_query.shape[1]
@@ -480,7 +490,7 @@
             out_specs=vmem,
             name="coef",
         )(packets)
-        coef = lax.all_to_all(coef, Z, 0, 0, tiled=True).reshape(n_index, LANES)
+        coef = lax.all_to_all(coef, Z_BY_CLASS, 0, 0, tiled=True).reshape(n_index, LANES)
 
     with jax.named_scope("gradient"):
         part = jax.ShapeDtypeStruct((width // ncore, cols), jnp.float32)
@@ -491,12 +501,12 @@
             out_specs=(vmem, vmem),
             scratch_shapes=[
                 pltpu.VMEM((queries, shard_rows), jnp.float32),
-                *like(slots, my_rows, my_unit, query_scale, ordered),
+                *like(slots, query_scale, my_rows, my_unit, ordered),
                 pltpu.SemaphoreType.DMA((5,)),
             ],
             compiler_params=pltpu.CompilerParams(vmem_limit_bytes=GRANT),
             name="gradient",
-        )(coef, slots, my_rows, my_unit, query_scale, ordered)
+        )(coef, slots, query_scale, my_rows, my_unit, ordered)
 
     with jax.named_scope("reduce_gradient"):
         term = (keep + shift(send, "core", 1)).reshape(ny, nz * six, cols)

time: 268 us -> 268 us (level)
  blocking collectives: 48.5 us -> 83.1 us
  starting transfers between devices: 100 us -> 77.9 us
  waiting for transfers between devices: 44.3 us -> 28.5 us
    all_to_all x1 -> x2, blocking collectives: 24.7 us -> 59.2 us  [the longest x1 34.5 us: send_all(): lax.all_to_all(jnp.broadcast_to(x[None], (size, *x.shape)), axis, 0, 0, t...]
    all_to_all x4 -> x2, starting transfers between devices: 36.1 us -> 12.7 us  [send_all(): lax.all_to_all(jnp.broadcast_to(x[None], (size, *x.shape)), axis, 0, 0, t...]
    all_to_all x4 -> x2, waiting for transfers between devices: 24.7 us -> 1.51 us  [send_all(): lax.all_to_all(jnp.broadcast_to(x[None], (size, *x.shape)), axis, 0, 0, t...]
    ppermute x17, waiting for transfers between devices: 7.51 us -> 14.9 us  [shift(): return lax.ppermute(x, axis, [((i + step) % size, i) for i in range(size)])]
    slice x0 -> x6, local copies, waits for them, and re-layouts: none -> 3.25 us  [the longest x5 3.25 us: body(): coded = jnp.concatenate([block[:, -1] for block in classes])]
    unnamed x29 -> x39, local copies, waits for them, and re-layouts: 6.31 us -> 5.64 us
  transfers between devices with their start and end apart: 23 -> 21, of which waited for: 7 -> 9; matrix products, arithmetic and copies ran while one was open for 9% -> 10% of each run, Pallas kernels for 7% -> 7%
where the time goes in v8:
time: 268 us; the launch traced here: 265 us
  blocking collectives  83.1 us (31%)
  starting transfers between devices  77.9 us (29%)
  Pallas kernels  39.1 us (15%)
  waiting for transfers between devices  28.5 us (11%)
  local copies, waits for them, and re-layouts  23.3 us (9%)
  other arithmetic  11.5 us (4%)
    ppermute x17, starting transfers between devices, shift(): return lax.ppermute(x, axis, [((i + step) % size, i) for i in range(size)])  53.9 us
    all_to_all x1, blocking collectives, send_all(): lax.all_to_all(jnp.broadcast_to(x[None], (size, *x.shape)), axis, 0, 0, t...  34.5 us
    all_to_all x1, blocking collectives, body(): lax.all_to_all(coef, Z_BY_CLASS, 0, 0, tiled=True).reshape(n_index, LANES)  24.8 us
    ppermute x17, waiting for transfers between devices, shift(): return lax.ppermute(x, axis, [((i + step) % size, i) for i in range(size)])  14.9 us
    all_to_all x1, blocking collectives, body(): lax.all_to_all(packet, NEAR, 0, 0, tiled=True)  12.8 us
    all_to_all x2, starting transfers between devices, send_all(): lax.all_to_all(jnp.broadcast_to(x[None], (size, *x.shape)), axis, 0, 0, t...  12.7 us
    all_to_all x1, waiting for transfers between devices, body(): term = jnp.sum(lax.all_to_all(term, Z, 0, 0, tiled=True), axis=0)  12.1 us
    all_to_all x1, blocking collectives, body(): term = jnp.sum(lax.all_to_all(term, 'y', 0, 0, tiled=True), axis=0)  11 us
  transfers between devices with their start and end apart: 21, of which 9 were waited for; matrix products, arithmetic and copies ran while one was open for 10% of the time, Pallas kernels for 7%

profile of v8, /device:TPU:6, one launch (start us, length us, event | category | flops | bytes accessed | tf_op | source)
XLA Modules:
  0.0 264.6 jit_solution(17060513252764759469)
XLA Ops:
  2.9 34.5 %all_to_all.50 = bf16[4,33,1024]{2,1,0:T(8,128)(2,1)S(1)} all-to-all(bf16[4,33,1024]{2,1,0:T(8,128)(2,1)S(1)} %broadcast_in_dim.10), channel_id=1, replica_groups=mesh['y'=4,'zq'=4,'zr'=4,'core'=2,'reader'=4] {'zq'}, dimensions={0} | all-to-all | bytes 540672 | tf_op jit(solution)/shard_map/gather_key_proj/all_to_all | solution.py:37
  37.4 6.8 %collective-permute-start.4 = (bf16[4,33,1024]{2,1,0:T(8,128)(2,1)S(1)}, bf16[4,33,1024]{2,1,0:T(8,128)(2,1)S(1)}, u32[]{:S(2)}, u32[]{:S(2)}) collective-permute-start(bf16[4,33,1024]{2,1,0:T(8,128)(2,1)S(1)} %all_to_all.50), channel_id=1, source_target_pairs={{8,0},{16,8},{24,16},{32,24},{40,32},{48,40},{56,48},{64,56},{72,6... | collective-permute-start | bytes 811016 | tf_op jit(solution)/shard_map/gather_key_proj/ppermute | solution.py:32
  44.2 1.9 collective-permute-start.5
  46.2 4.8 %collective-permute-start.6 = (bf16[2,33,1024]{2,1,0:T(8,128)(2,1)S(1)}, bf16[2,33,1024]{2,1,0:T(8,128)(2,1)S(1)}, u32[]{:S(2)}, u32[]{:S(2)}) collective-permute-start(bf16[2,33,1024]{2,1,0:T(8,128)(2,1)S(1)} %get-tuple-element.24), channel_id=1, source_target_pairs={{112,0},{120,8},{0,16},{8,24},{16,32},{24,40},{32,48},{40,56},{48,... | collective-permute-start | bytes 405512 | tf_op jit(solution)/shard_map/gather_key_proj/ppermute | solution.py:32
  51.0 3.0 %collective-permute-start.7 = (bf16[4,33,1024]{2,1,0:T(8,128)(2,1)S(1)}, bf16[4,33,1024]{2,1,0:T(8,128)(2,1)S(1)}, u32[]{:S(2)}, u32[]{:S(2)}) collective-permute-start(bf16[4,33,1024]{2,1,0:T(8,128)(2,1)S(1)} %all_to_all.50), channel_id=1, source_target_pairs={{120,0},{0,8},{8,16},{16,24},{24,32},{32,40},{40,48},{48,56},{56,6... | collective-permute-start | bytes 811016 | tf_op jit(solution)/shard_map/gather_key_proj/ppermute | solution.py:32
  56.2 2.1 collective-permute-done.5
  60.0 6.4 %collective-permute-done.7 = bf16[4,33,1024]{2,1,0:T(8,128)(2,1)S(1)} collective-permute-done((bf16[4,33,1024]{2,1,0:T(8,128)(2,1)S(1)}, bf16[4,33,1024]{2,1,0:T(8,128)(2,1)S(1)}, u32[]{:S(2)}, u32[]{:S(2)}) %collective-permute-start.7) | collective-permute-done | bytes 270368 | tf_op jit(solution)/shard_map/gather_key_proj/ppermute | solution.py:32
  67.2 4.9 %collective-permute-start.8 = (bf16[16,32,1024]{2,1,0:T(8,128)(2,1)}, bf16[16,32,1024]{2,1,0:T(8,128)(2,1)}, u32[]{:S(2)}, u32[]{:S(2)}) collective-permute-start(bf16[16,32,1024]{2,1,0:T(8,128)(2,1)} %slice_dynamic-update-slice_fusion.refs_5_), channel_id=1, source_target_pairs={{128,0},{256,128},{384,256},{0,384},{129,1},{257,129},{385,257},{1... | collective-permute-start | bytes 3145736 | tf_op jit(solution)/shard_map/gather_key_proj/ppermute | solution.py:32
  72.1 1.9 collective-permute-start.10
  74.0 2.7 %collective-permute-start = (bf16[640,1024]{1,0:T(8,128)(2,1)}, bf16[640,1024]{1,0:T(8,128)(2,1)S(1)}, u32[]{:S(2)}, u32[]{:S(2)}) collective-permute-start(bf16[640,1024]{1,0:T(8,128)(2,1)} %bitcast.4.refs_0_), channel_id=1, source_target_pairs={{1,0},{2,1},{3,2},{0,3},{5,4},{6,5},{7,6},{4,7},{9,8},{10,9},{11,1... | collective-permute-start | bytes 3932168 | tf_op jit(solution)/shard_map/gather_enc_out/ppermute | solution.py:32
  76.8 4.3 %collective-permute-start.2 = (bf16[640,1024]{1,0:T(8,128)(2,1)}, bf16[640,1024]{1,0:T(8,128)(2,1)S(1)}, u32[]{:S(2)}, u32[]{:S(2)}) collective-permute-start(bf16[640,1024]{1,0:T(8,128)(2,1)} %bitcast.4.refs_0_), channel_id=1, source_target_pairs={{3,0},{0,1},{1,2},{2,3},{7,4},{4,5},{5,6},{6,7},{11,8},{8,9},{9,10... | collective-permute-start | bytes 3932168 | tf_op jit(solution)/shard_map/gather_enc_out/ppermute | solution.py:32
  81.9 1.1 mul.67
  87.6 1.0 broadcast_in_dim.11
  88.6 7.4 %all-to-all-start.1 = ((bf16[32,16,896]{2,1,0:T(8,128)(2,1)}), bf16[32,16,896]{2,1,0:T(8,128)(2,1)}, u32[]{:S(2)}, u32[]{:S(2)}) async-start(bf16[32,16,896]{2,1,0:T(8,128)(2,1)} %broadcast_in_dim.11), calls=%async_computation.1 | async-start | bytes 1835008 | tf_op jit(solution)/shard_map/gather_queries/all_to_all | solution.py:37
  96.7 1.9 slice.85
  98.6 4.7 %collective-permute-start.9 = (bf16[8,32,1024]{2,1,0:T(8,128)(2,1)}, bf16[8,32,1024]{2,1,0:T(8,128)(2,1)}, u32[]{:S(2)}, u32[]{:S(2)}) collective-permute-start(bf16[8,32,1024]{2,1,0:T(8,128)(2,1)} %slice.85), channel_id=1, source_target_pairs={{128,0},{256,128},{384,256},{0,384},{129,1},{257,129},{385,257},{1... | collective-permute-start | bytes 1572872 | tf_op jit(solution)/shard_map/gather_key_proj/ppermute | solution.py:32
  103.3 1.9 slice.86
  105.2 1.9 collective-permute-start.11
  109.4 1.3 fusion.refs_3_
  110.7 1.9 collective-permute-start.13
  112.6 0.9 slice.76
  113.6 2.7 %collective-permute-start.1 = (bf16[320,1024]{1,0:T(8,128)(2,1)}, bf16[320,1024]{1,0:T(8,128)(2,1)S(1)}, u32[]{:S(2)}, u32[]{:S(2)}) collective-permute-start(bf16[320,1024]{1,0:T(8,128)(2,1)} %slice.76), channel_id=1, source_target_pairs={{1,0},{2,1},{3,2},{0,3},{5,4},{6,5},{7,6},{4,7},{9,8},{10,9},{11,1... | collective-permute-start | bytes 1966088 | tf_op jit(solution)/shard_map/gather_enc_out/ppermute | solution.py:32
  116.3 0.9 slice.77
  117.2 4.3 %collective-permute-start.3 = (bf16[320,1024]{1,0:T(8,128)(2,1)}, bf16[320,1024]{1,0:T(8,128)(2,1)}, u32[]{:S(2)}, u32[]{:S(2)}) collective-permute-start(bf16[320,1024]{1,0:T(8,128)(2,1)} %slice.77), channel_id=1, source_target_pairs={{3,0},{0,1},{1,2},{2,3},{7,4},{4,5},{5,6},{6,7},{11,8},{8,9},{9,10... | collective-permute-start | bytes 1966088 | tf_op jit(solution)/shard_map/gather_enc_out/ppermute | solution.py:32
  121.9 1.9 collective-permute-start.14
  123.8 3.2 %collective-permute-done.11 = bf16[8,32,1024]{2,1,0:T(8,128)(2,1)} collective-permute-done((bf16[8,32,1024]{2,1,0:T(8,128)(2,1)}, bf16[8,32,1024]{2,1,0:T(8,128)(2,1)}, u32[]{:S(2)}, u32[]{:S(2)}) %collective-permute-start.11) | collective-permute-done | bytes 524320 | tf_op jit(solution)/shard_map/gather_key_proj/ppermute | solution.py:32
  127.0 1.9 collective-permute-start.15
  128.9 8.2 %scores.1 = (f32[128,128]{1,0:T(8,128)}, s32[128,128]{1,0:T(8,128)}, f32[512,192]{1,0:T(8,128)}, f32[512,192]{1,0:T(8,128)}, f32[128,128]{1,0:T(8,128)}, /*index=5*/bf16[768,512]{1,0:T(8,128)(2,1)}) custom-call(s32[2]{0:T(128)} %pad_add_fusion.1.place, bf16[32,16,896]{2,1,0:T(8,128)(2,1)} %all-to-all-done.1.refs_0_, bf16[768,768]{1,0:T(8,128)(2,1)} %refs_1_.1, ...), custom_call_target="tpu_custom_call" | custom-call | flops 68719476736 | bytes 8388608 | tf_op jit(solution)/shard_map/scores/scores/pallas_call | solution.py:444
  137.2 7.8 %all-to-all-start.2 = ((f32[128,1,128]{2,1,0:T(1,128)}), f32[128,1,128]{2,1,0:T(1,128)S(1)}, u32[]{:S(2)}, u32[]{:S(2)}) async-start(f32[128,1,128]{2,1,0:T(1,128)} %bitcast.51), calls=%async_computation.2 | async-start | bytes 131072 | tf_op jit(solution)/shard_map/reduce_scores/all_to_all | solution.py:463
  145.0 1.1 constant_dynamic-update-slice_fusion.1
  146.0 1.1 constant_dynamic-update-slice_fusion.refs_5_
  147.2 2.1 collective-permute-start.12
  149.3 10.4 %early_keys.1.refs_7_ = f32[640,1024]{1,0:T(8,128)} custom-call(s32[4]{0:T(128)} %pad_add_fusion.place, bf16[640,1024]{1,0:T(8,128)(2,1)} %bitcast.4.refs_0_, bf16[640,1024]{1,0:T(8,128)(2,1)} %copy-done, bf16[320,1024]{1,0:T(8,128)(2,1)} %copy-done.4, bf16[320,1024]{1,0:T(8,128)(2,1)} %collective-permute-done.3.refs_3_, bf16[640,1024]{1,0:T(8,128)(2,1)} %copy-done.1, ...), custom_call_target="tpu_custom_call" | custom-call | flops 16106127360 | bytes 13631488 | tf_op jit(solution)/shard_map/attention/early_keys/pallas_call | solution.py:205
  160.8 9.7 %late_heads.1 = (f32[32,256]{1,0:T(8,128)}, f32[8,128]{1,0:T(8,128)}) custom-call(s32[4]{0:T(128)} %pad_add_fusion.place, bf16[640,1024]{1,0:T(8,128)(2,1)} %bitcast.4.refs_0_, bf16[640,1024]{1,0:T(8,128)(2,1)} %copy-done, bf16[320,1024]{1,0:T(8,128)(2,1)} %copy-done.4, bf16[320,1024]{1,0:T(8,128)(2,1)} %collective-permute-done.3.refs_3_, ...), custom_call_target="tpu_custom_call" | custom-call | flops 1342177280 | bytes 6291456 | tf_op jit(solution)/shard_map/attention/late_heads/pallas_call | solution.py:220
  171.3 12.8 %all_to_all.51 = f32[32,1,256]{2,1,0:T(1,128)S(1)} all-to-all(f32[32,1,256]{2,1,0:T(1,128)S(1)} %copy.27), channel_id=1, replica_groups=mesh['y'=4,'zq'=4,'zr'=4,'core'=2,'reader'=4] {'reader','y','core'}, dimensions={0} | all-to-all | bytes 65536 | tf_op jit(solution)/shard_map/targets/all_to_all | solution.py:485
  184.8 1.6 coef.1
  186.4 24.8 %all_to_all.52 = f32[16,8,128]{2,1,0:T(8,128)} all-to-all(f32[16,8,128]{2,1,0:T(8,128)} %coef.1), channel_id=1, replica_groups=mesh['y'=4,'zq'=4,'zr'=4,'core'=2,'reader'=4] {'zr','zq'}, dimensions={0} | all-to-all | bytes 131072 | tf_op jit(solution)/shard_map/targets/all_to_all | solution.py:493
  211.1 9.1 %gradient.1 = (f32[384,192]{1,0:T(8,128)}, f32[384,192]{1,0:T(8,128)}) custom-call(f32[128,128]{1,0:T(8,128)} %bitcast.47, s32[128,128]{1,0:T(8,128)} %get-tuple-element.16.refs_0_, f32[128,128]{1,0:T(8,128)} %get-tuple-element.17.refs_1_, f32[512,192]{1,0:T(8,128)} %get-tuple-element.18.refs_2_, f32[512,192]{1,0:T(8,128)} %get-tuple-element.19.refs_3_, ...), custom_call_target="tpu_custom_call" | custom-call | tf_op jit(solution)/shard_map/gradient/gradient/pallas_call | solution.py:497
  220.2 1.9 collective-permute-start.16
  222.2 1.9 collective-permute-done.16
  224.1 1.0 add.164
  225.1 11.0 %all_to_all.53 = f32[4,96,192]{2,1,0:T(8,128)S(1)} all-to-all(f32[4,96,192]{2,1,0:T(8,128)S(1)} %bitcast.45), channel_id=1, replica_groups=mesh['y'=4,'zq'=4,'zr'=4,'core'=2,'reader'=4] {'y'}, dimensions={0} | all-to-all | bytes 589824 | tf_op jit(solution)/shard_map/reduce_gradient/all_to_all | solution.py:513
  236.9 3.5 %all-to-all-start.6 = ((f32[16,6,192]{2,1,0:T(8,128)}), f32[16,6,192]{2,1,0:T(8,128)S(1)}, u32[]{:S(2)}, u32[]{:S(2)}) async-start(f32[16,6,192]{2,1,0:T(8,128)} %reshape.202), calls=%async_computation.6 | async-start | bytes 262144 | tf_op jit(solution)/shard_map/reduce_gradient/all_to_all | solution.py:515
  240.4 1.3 slice.74
  242.4 12.1 %all-to-all-done.6 = f32[16,6,192]{2,1,0:T(8,128)S(1)} async-done(((f32[16,6,192]{2,1,0:T(8,128)}), f32[16,6,192]{2,1,0:T(8,128)S(1)}, u32[]{:S(2)}, u32[]{:S(2)}) %all-to-all-start.6) | async-done | bytes 73760 | tf_op jit(solution)/shard_map/reduce_gradient/all_to_all | solution.py:515
  255.2 5.3 %all-to-all-start.7 = ((f32[4,6,192]{2,1,0:T(8,128)}), f32[4,6,192]{2,1,0:T(8,128)S(1)}, u32[]{:S(2)}, u32[]{:S(2)}) async-start(f32[4,6,192]{2,1,0:T(8,128)} %broadcast_in_dim.12), calls=%async_computation.7 | async-start | bytes 65536 | tf_op jit(solution)/shard_map/reduce_gradient/all_to_all | solution.py:37
  260.5 1.9 log_bitcast_fusion
  262.4 1.5 all-to-all-done.7
  (92 shorter events, 20.5 us)
Async XLA Ops:
  37.4 43.7 %copy-start.5 = (bf16[4,16,1024]{2,1,0:T(8,128)(2,1)S(1)}, bf16[4,16,1024]{2,1,0:T(8,128)(2,1)}, u32[]{:S(2)}) copy-start(bf16[4,16,1024]{2,1,0:T(8,128)(2,1)} %param.17) | copy-start | bytes 393220
  37.4 18.1 %collective-permute-start.4 = (bf16[4,33,1024]{2,1,0:T(8,128)(2,1)S(1)}, bf16[4,33,1024]{2,1,0:T(8,128)(2,1)S(1)}, u32[]{:S(2)}, u32[]{:S(2)}) collective-permute-start(bf16[4,33,1024]{2,1,0:T(8,128)(2,1)S(1)} %all_to_all.50), channel_id=1, source_target_pairs={{8,0},{16,8},{24,16},{32,24},{40,32},{48,40},{56,48},{64,56},{72,6... | collective-permute-start | bytes 811016 | tf_op jit(solution)/shard_map/gather_key_proj/ppermute | solution.py:32
  44.2 14.1 %collective-permute-start.5 = (bf16[2,33,1024]{2,1,0:T(8,128)(2,1)S(1)}, bf16[2,33,1024]{2,1,0:T(8,128)(2,1)S(1)}, u32[]{:S(2)}, u32[]{:S(2)}) collective-permute-start(bf16[2,33,1024]{2,1,0:T(8,128)(2,1)S(1)} %get-tuple-element.25), channel_id=1, source_target_pairs={{16,0},{24,8},{32,16},{40,24},{48,32},{56,40},{64,48},{72,56},{80,... | collective-permute-start | bytes 405512 | tf_op jit(solution)/shard_map/gather_key_proj/ppermute | solution.py:32
  46.2 13.1 %collective-permute-start.6 = (bf16[2,33,1024]{2,1,0:T(8,128)(2,1)S(1)}, bf16[2,33,1024]{2,1,0:T(8,128)(2,1)S(1)}, u32[]{:S(2)}, u32[]{:S(2)}) collective-permute-start(bf16[2,33,1024]{2,1,0:T(8,128)(2,1)S(1)} %get-tuple-element.24), channel_id=1, source_target_pairs={{112,0},{120,8},{0,16},{8,24},{16,32},{24,40},{32,48},{40,56},{48,... | collective-permute-start | bytes 405512 | tf_op jit(solution)/shard_map/gather_key_proj/ppermute | solution.py:32
  51.0 15.4 %collective-permute-start.7 = (bf16[4,33,1024]{2,1,0:T(8,128)(2,1)S(1)}, bf16[4,33,1024]{2,1,0:T(8,128)(2,1)S(1)}, u32[]{:S(2)}, u32[]{:S(2)}) collective-permute-start(bf16[4,33,1024]{2,1,0:T(8,128)(2,1)S(1)} %all_to_all.50), channel_id=1, source_target_pairs={{120,0},{0,8},{8,16},{16,24},{24,32},{32,40},{40,48},{48,56},{56,6... | collective-permute-start | bytes 811016 | tf_op jit(solution)/shard_map/gather_key_proj/ppermute | solution.py:32
  54.8 28.3 %copy-start.12 = (s32[4,20]{1,0:T(4,128)S(1)}, s32[4,20]{1,0:T(4,128)}, u32[]{:S(2)}) copy-start(s32[4,20]{1,0:T(4,128)} %param.13) | copy-start | bytes 964
  55.5 18.5 %copy-start.8 = (bf16[4,33,1024]{2,1,0:T(8,128)(2,1)}, bf16[4,33,1024]{2,1,0:T(8,128)(2,1)S(1)}, u32[]{:S(2)}) copy-start(bf16[4,33,1024]{2,1,0:T(8,128)(2,1)S(1)} %collective-permute-done.4) | copy-start | bytes 811012
  58.4 22.7 %copy-start.10 = (bf16[2,33,1024]{2,1,0:T(8,128)(2,1)}, bf16[2,33,1024]{2,1,0:T(8,128)(2,1)S(1)}, u32[]{:S(2)}) copy-start(bf16[2,33,1024]{2,1,0:T(8,128)(2,1)S(1)} %collective-permute-done.5) | copy-start | bytes 405508
  59.2 21.9 %copy-start.11 = (bf16[2,33,1024]{2,1,0:T(8,128)(2,1)}, bf16[2,33,1024]{2,1,0:T(8,128)(2,1)S(1)}, u32[]{:S(2)}) copy-start(bf16[2,33,1024]{2,1,0:T(8,128)(2,1)S(1)} %collective-permute-done.6) | copy-start | bytes 405508
  66.4 10.4 %copy-start.9 = (bf16[4,33,1024]{2,1,0:T(8,128)(2,1)}, bf16[4,33,1024]{2,1,0:T(8,128)(2,1)S(1)}, u32[]{:S(2)}) copy-start(bf16[4,33,1024]{2,1,0:T(8,128)(2,1)S(1)} %collective-permute-done.7) | copy-start | bytes 811012
  67.2 29.5 %collective-permute-start.8 = (bf16[16,32,1024]{2,1,0:T(8,128)(2,1)}, bf16[16,32,1024]{2,1,0:T(8,128)(2,1)}, u32[]{:S(2)}, u32[]{:S(2)}) collective-permute-start(bf16[16,32,1024]{2,1,0:T(8,128)(2,1)} %slice_dynamic-update-slice_fusion.refs_5_), channel_id=1, source_target_pairs={{128,0},{256,128},{384,256},{0,384},{129,1},{257,129},{385,257},{1... | collective-permute-start | bytes 3145736 | tf_op jit(solution)/shard_map/gather_key_proj/ppermute | solution.py:32
  72.1 31.2 %collective-permute-start.10 = (bf16[16,32,1024]{2,1,0:T(8,128)(2,1)}, bf16[16,32,1024]{2,1,0:T(8,128)(2,1)}, u32[]{:S(2)}, u32[]{:S(2)}) collective-permute-start(bf16[16,32,1024]{2,1,0:T(8,128)(2,1)} %slice_dynamic-update-slice_fusion.refs_5_), channel_id=1, source_target_pairs={{384,0},{0,128},{128,256},{256,384},{385,1},{1,129},{129,257},{257... | collective-permute-start | bytes 3145736 | tf_op jit(solution)/shard_map/gather_key_proj/ppermute | solution.py:32
  74.0 38.6 %collective-permute-start = (bf16[640,1024]{1,0:T(8,128)(2,1)}, bf16[640,1024]{1,0:T(8,128)(2,1)S(1)}, u32[]{:S(2)}, u32[]{:S(2)}) collective-permute-start(bf16[640,1024]{1,0:T(8,128)(2,1)} %bitcast.4.refs_0_), channel_id=1, source_target_pairs={{1,0},{2,1},{3,2},{0,3},{5,4},{6,5},{7,6},{4,7},{9,8},{10,9},{11,1... | collective-permute-start | bytes 3932168 | tf_op jit(solution)/shard_map/gather_enc_out/ppermute | solution.py:32
  76.8 39.5 %collective-permute-start.2 = (bf16[640,1024]{1,0:T(8,128)(2,1)}, bf16[640,1024]{1,0:T(8,128)(2,1)S(1)}, u32[]{:S(2)}, u32[]{:S(2)}) collective-permute-start(bf16[640,1024]{1,0:T(8,128)(2,1)} %bitcast.4.refs_0_), channel_id=1, source_target_pairs={{3,0},{0,1},{1,2},{2,3},{7,4},{4,5},{5,6},{6,7},{11,8},{8,9},{9,10... | collective-permute-start | bytes 3932168 | tf_op jit(solution)/shard_map/gather_enc_out/ppermute | solution.py:32
  88.6 40.3 %all-to-all-start.1 = ((bf16[32,16,896]{2,1,0:T(8,128)(2,1)}), bf16[32,16,896]{2,1,0:T(8,128)(2,1)}, u32[]{:S(2)}, u32[]{:S(2)}) async-start(bf16[32,16,896]{2,1,0:T(8,128)(2,1)} %broadcast_in_dim.11), calls=%async_computation.1 | async-start | bytes 1835008 | tf_op jit(solution)/shard_map/gather_queries/all_to_all | solution.py:37
  98.6 9.5 %copy-start.13 = (bf16[1024]{0:T(1024)(128)(2,1)S(1)}, bf16[1024]{0:T(1024)(128)(2,1)}, u32[]{:S(2)}) copy-start(bf16[1024]{0:T(1024)(128)(2,1)} %param.16) | copy-start | bytes 6148
  98.6 10.1 %copy-start.6 = (bf16[4,16,1024]{2,1,0:T(8,128)(2,1)S(1)}, bf16[4,16,1024]{2,1,0:T(8,128)(2,1)}, u32[]{:S(2)}) copy-start(bf16[4,16,1024]{2,1,0:T(8,128)(2,1)} %param.17) | copy-start | bytes 393220
  98.6 23.3 %collective-permute-start.9 = (bf16[8,32,1024]{2,1,0:T(8,128)(2,1)}, bf16[8,32,1024]{2,1,0:T(8,128)(2,1)}, u32[]{:S(2)}, u32[]{:S(2)}) collective-permute-start(bf16[8,32,1024]{2,1,0:T(8,128)(2,1)} %slice.85), channel_id=1, source_target_pairs={{128,0},{256,128},{384,256},{0,384},{129,1},{257,129},{385,257},{1... | collective-permute-start | bytes 1572872 | tf_op jit(solution)/shard_map/gather_key_proj/ppermute | solution.py:32
  105.2 21.8 %collective-permute-start.11 = (bf16[8,32,1024]{2,1,0:T(8,128)(2,1)}, bf16[8,32,1024]{2,1,0:T(8,128)(2,1)}, u32[]{:S(2)}, u32[]{:S(2)}) collective-permute-start(bf16[8,32,1024]{2,1,0:T(8,128)(2,1)} %slice.86), channel_id=1, source_target_pairs={{384,0},{0,128},{128,256},{256,384},{385,1},{1,129},{129,257},{257... | collective-permute-start | bytes 1572872 | tf_op jit(solution)/shard_map/gather_key_proj/ppermute | solution.py:32
  110.7 38.6 %collective-permute-start.13 = (bf16[16,32,1024]{2,1,0:T(8,128)(2,1)}, bf16[16,32,1024]{2,1,0:T(8,128)(2,1)}, u32[]{:S(2)}, u32[]{:S(2)}) collective-permute-start(bf16[16,32,1024]{2,1,0:T(8,128)(2,1)} %slice_dynamic-update-slice_fusion.refs_5_), channel_id=1, source_target_pairs={{4,0},{0,4},{5,1},{1,5},{6,2},{2,6},{7,3},{3,7},{12,8},{8,12},{13,... | collective-permute-start | bytes 3145736 | tf_op jit(solution)/shard_map/gather_key_proj/ppermute | solution.py:32
  112.6 4.6 %copy-start = (bf16[640,1024]{1,0:T(8,128)(2,1)}, bf16[640,1024]{1,0:T(8,128)(2,1)S(1)}, u32[]{:S(2)}) copy-start(bf16[640,1024]{1,0:T(8,128)(2,1)S(1)} %collective-permute-done.refs_1_) | copy-start | bytes 3932164
  113.6 33.6 %collective-permute-start.1 = (bf16[320,1024]{1,0:T(8,128)(2,1)}, bf16[320,1024]{1,0:T(8,128)(2,1)S(1)}, u32[]{:S(2)}, u32[]{:S(2)}) collective-permute-start(bf16[320,1024]{1,0:T(8,128)(2,1)} %slice.76), channel_id=1, source_target_pairs={{1,0},{2,1},{3,2},{0,3},{5,4},{6,5},{7,6},{4,7},{9,8},{10,9},{11,1... | collective-permute-start | bytes 1966088 | tf_op jit(solution)/shard_map/gather_enc_out/ppermute | solution.py:32
  116.3 20.9 %copy-start.1 = (bf16[640,1024]{1,0:T(8,128)(2,1)}, bf16[640,1024]{1,0:T(8,128)(2,1)S(1)}, u32[]{:S(2)}) copy-start(bf16[640,1024]{1,0:T(8,128)(2,1)S(1)} %collective-permute-done.2.refs_4_) | copy-start | bytes 3932164
  117.2 32.1 %collective-permute-start.3 = (bf16[320,1024]{1,0:T(8,128)(2,1)}, bf16[320,1024]{1,0:T(8,128)(2,1)}, u32[]{:S(2)}, u32[]{:S(2)}) collective-permute-start(bf16[320,1024]{1,0:T(8,128)(2,1)} %slice.77), channel_id=1, source_target_pairs={{3,0},{0,1},{1,2},{2,3},{7,4},{4,5},{5,6},{6,7},{11,8},{8,9},{9,10... | collective-permute-start | bytes 1966088 | tf_op jit(solution)/shard_map/gather_enc_out/ppermute | solution.py:32
  121.9 27.4 %collective-permute-start.14 = (bf16[16,32,1024]{2,1,0:T(8,128)(2,1)}, bf16[16,32,1024]{2,1,0:T(8,128)(2,1)}, u32[]{:S(2)}, u32[]{:S(2)}) collective-permute-start(bf16[16,32,1024]{2,1,0:T(8,128)(2,1)} %collective-permute-done.8.refs_7_), channel_id=1, source_target_pairs={{4,0},{0,4},{5,1},{1,5},{6,2},{2,6},{7,3},{3,7},{12,8},{8,12},{13,... | collective-permute-start | bytes 3145736 | tf_op jit(solution)/shard_map/gather_key_proj/ppermute | solution.py:32
  127.0 22.3 %collective-permute-start.15 = (bf16[16,32,1024]{2,1,0:T(8,128)(2,1)}, bf16[16,32,1024]{2,1,0:T(8,128)(2,1)}, u32[]{:S(2)}, u32[]{:S(2)}) collective-permute-start(bf16[16,32,1024]{2,1,0:T(8,128)(2,1)} %collective-permute-done.10.refs_9_), channel_id=1, source_target_pairs={{4,0},{0,4},{5,1},{1,5},{6,2},{2,6},{7,3},{3,7},{12,8},{8,12},{13,... | collective-permute-start | bytes 3145736 | tf_op jit(solution)/shard_map/gather_key_proj/ppermute | solution.py:32
  137.2 22.6 %all-to-all-start.2 = ((f32[128,1,128]{2,1,0:T(1,128)}), f32[128,1,128]{2,1,0:T(1,128)S(1)}, u32[]{:S(2)}, u32[]{:S(2)}) async-start(f32[128,1,128]{2,1,0:T(1,128)} %bitcast.51), calls=%async_computation.2 | async-start | bytes 131072 | tf_op jit(solution)/shard_map/reduce_scores/all_to_all | solution.py:463
  147.1 12.6 %copy-start.2 = (bf16[16,32,1024]{2,1,0:T(8,128)(2,1)}, bf16[16,32,1024]{2,1,0:T(8,128)(2,1)S(1)}, u32[]{:S(2)}) copy-start(bf16[16,32,1024]{2,1,0:T(8,128)(2,1)S(1)} %constant_dynamic-update-slice_fusion.refs_5_) | copy-start | bytes 3145732
  147.2 2.2 copy-start.4
  147.2 12.6 %collective-permute-start.12 = (bf16[16,32,1024]{2,1,0:T(8,128)(2,1)S(1)}, bf16[16,32,1024]{2,1,0:T(8,128)(2,1)S(1)}, u32[]{:S(2)}, u32[]{:S(2)}) collective-permute-start(bf16[16,32,1024]{2,1,0:T(8,128)(2,1)S(1)} %constant_dynamic-update-slice_fusion.refs_5_), channel_id=1, source_target_pairs={{4,0},{0,4},{5,1},{1,5},{6,2},{2,6},{7,3},{3,7},{12,8},{8,12},{13,... | collective-permute-start | bytes 3145736 | tf_op jit(solution)/shard_map/gather_key_proj/ppermute | solution.py:32
  159.8 0.6 copy-start.7
  159.8 1.0 copy-start.3
  220.2 3.8 %collective-permute-start.16 = (f32[384,192]{1,0:T(8,128)}, f32[384,192]{1,0:T(8,128)S(1)}, u32[]{:S(2)}, u32[]{:S(2)}) collective-permute-start(f32[384,192]{1,0:T(8,128)} %get-tuple-element.22), channel_id=1, source_target_pairs={{4,0},{0,4},{5,1},{1,5},{6,2},{2,6},{7,3},{3,7},{12,8},{8,12},{13,... | collective-permute-start | bytes 884744 | tf_op jit(solution)/shard_map/reduce_gradient/ppermute | solution.py:32
  236.9 17.7 %all-to-all-start.6 = ((f32[16,6,192]{2,1,0:T(8,128)}), f32[16,6,192]{2,1,0:T(8,128)S(1)}, u32[]{:S(2)}, u32[]{:S(2)}) async-start(f32[16,6,192]{2,1,0:T(8,128)} %reshape.202), calls=%async_computation.6 | async-start | bytes 262144 | tf_op jit(solution)/shard_map/reduce_gradient/all_to_all | solution.py:515
  255.2 8.7 %all-to-all-start.7 = ((f32[4,6,192]{2,1,0:T(8,128)}), f32[4,6,192]{2,1,0:T(8,128)S(1)}, u32[]{:S(2)}, u32[]{:S(2)}) async-start(f32[4,6,192]{2,1,0:T(8,128)} %broadcast_in_dim.12), calls=%async_computation.7 | async-start | bytes 65536 | tf_op jit(solution)/shard_map/reduce_gradient/all_to_all | solution.py:37

commit v9 on v8

--- a/solution.py
+++ b/solution.py
@@ -22,7 +22,7 @@
 SLOT = 32
 TILE = 256
 N_OWNERS = 128
-GRANT = 56 << 20
+GRANT = 48 << 20
 EARLY = (0, 1, 3)
 LATE = 2
 
@@ -57,23 +57,14 @@
     return [pltpu.VMEM(x.shape, x.dtype) for x in arrays]
 
 
-def token_copies(r, chunk, tokens, target, sems):
-    own, after, far_low, far_high, before = tokens
-    half = target.shape[0] // 2
-    low, high = target.at[pl.ds(0, half)], target.at[pl.ds(half, half)]
-    for j, block in enumerate((own, after, None, before)):
+def token_copies(r, chunk, tokens, target, sem):
+    for j, block in enumerate(tokens):
 
         @pl.when((r + j) % 4 == chunk)
         def _():
-            first = far_low if block is None else block.at[pl.ds(0, half)]
-            second = far_high if block is None else block.at[pl.ds(half, half)]
-            pltpu.make_async_copy(first, low, sems.at[0]).start()
-            pltpu.make_async_copy(second, high, sems.at[1]).start()
-
-    return [
-        pltpu.make_async_copy(low, low, sems.at[0]),
-        pltpu.make_async_copy(high, high, sems.at[1]),
-    ]
+            pltpu.make_async_copy(block, target, sem).start()
+
+    return [pltpu.make_async_copy(target, target, sem)]
 
 
 def row_copies(place, own, other, target, sem):
@@ -87,31 +78,33 @@
 
 
 def early_keys_kernel(place, *refs):
-    tokens, rows, (keys_out, keys, token_v, weight_v, sems) = refs[:5], refs[5:11], refs[11:]
+    tokens, rows, (keys_out, keys, token_v, weight_v, sems) = refs[:4], refs[4:10], refs[10:]
     y, r = place[0], place[3]
     copies = []
     for slot, ahead in enumerate(EARLY):
         own, other = rows[2 * slot], rows[2 * slot + 1]
-        waits = row_copies(place, own, other, weight_v.at[slot], sems.at[slot, 0])
-        target = token_v.at[slot]
-        waits += token_copies(r, (y + ahead) % 4, tokens, target, sems.at[3 + slot])
-        copies.append(waits)
-    for slot in range(len(EARLY)):
-        for copy in copies[slot]:
-            copy.wait()
-
-        @pl.loop(0, keys.shape[1] // TILE)
-        def _(t):
-            cols = pl.ds(pl.multiple_of(t * TILE, TILE), TILE)
-            term = dot32(token_v[slot], weight_v[slot, :, :, :, :, cols].reshape(-1, TILE))
-            if slot == 0:
-                keys[:, cols] = term
-            else:
-                keys[:, cols] += term
-
-    copy = pltpu.make_async_copy(keys, keys_out, sems.at[0, 0])
-    copy.start()
-    copy.wait()
+        copies += row_copies(place, own, other, weight_v.at[slot], sems.at[0, slot])
+        copies += token_copies(r, (y + ahead) % 4, tokens, token_v.at[slot], sems.at[1, slot])
+    for copy in copies:
+        copy.wait()
+    tiles = keys.shape[0]
+
+    def leave(t):
+        cols = pl.ds(pl.multiple_of(t * TILE, TILE), TILE)
+        return pltpu.make_async_copy(keys.at[t], keys_out.at[:, cols], sems.at[2, t])
+
+    @pl.loop(0, tiles)
+    def _(t):
+        cols = pl.ds(pl.multiple_of(t * TILE, TILE), TILE)
+        total = dot32(token_v[0], weight_v[0, :, :, :, :, cols].reshape(-1, TILE))
+        for slot in range(1, len(EARLY)):
+            total += dot32(token_v[slot], weight_v[slot, :, :, :, :, cols].reshape(-1, TILE))
+        keys[t] = total
+        leave(t).start()
+
+    @pl.loop(0, tiles)
+    def _(t):
+        leave(t).wait()
 
 
 def attend(keys, offset, dec, gain, live, column_v):
@@ -144,13 +137,13 @@
 
 
 def late_heads_kernel(place, *refs):
-    tokens, (own, other), refs = refs[:5], refs[5:7], refs[7:]
+    tokens, (own, other), refs = refs[:4], refs[4:6], refs[6:]
     far, (out, own_scores), near, refs = refs[:5], refs[5:7], refs[7:12], refs[12:]
     token_v, weight_v, column_v, load_sems, sems = refs
     y, r = place[0], place[3]
     loads = load(far, near, load_sems)
     early, dec, gain, live, states = near
-    copies = row_copies(place, own, other, weight_v, sems.at[0, 0])
+    copies = row_copies(place, own, other, weight_v, sems.at[0])
     copies += token_copies(r, (y + LATE) % 4, tokens, token_v, sems.at[1])
     column_v[...] = jnp.zeros_like(column_v)
 
@@ -205,13 +198,13 @@
     early = pl.pallas_call(
         early_keys_kernel,
         out_shape=jax.ShapeDtypeStruct((token_rows, width), jnp.float32),
-        in_specs=[smem] + [anywhere] * 11,
+        in_specs=[smem] + [anywhere] * 10,
         out_specs=anywhere,
         scratch_shapes=[
-            pltpu.VMEM((token_rows, width), jnp.float32),
+            pltpu.VMEM((width // TILE, token_rows, TILE), jnp.float32),
             pltpu.VMEM((3, token_rows, width), jnp.bfloat16),
             pltpu.VMEM((3, *block), jnp.bfloat16),
-            pltpu.SemaphoreType.DMA((6, 2)),
+            pltpu.SemaphoreType.DMA((3, 4)),
         ],
         compiler_params=pltpu.CompilerParams(vmem_limit_bytes=GRANT),
         cost_estimate=cost(12, 13),
@@ -223,7 +216,7 @@
             jax.ShapeDtypeStruct((32, 2 * LANES), jnp.float32),
             jax.ShapeDtypeStruct((8, LANES), jnp.float32),
         ),
-        in_specs=[smem] + [anywhere] * 12,
+        in_specs=[smem] + [anywhere] * 11,
         out_specs=(vmem, vmem),
         scratch_shapes=[
             *like(early, dec, gain, live, states),
@@ -231,7 +224,7 @@
             pltpu.VMEM(block, jnp.bfloat16),
             pltpu.VMEM((8, live.shape[1]), jnp.float32),
             pltpu.SemaphoreType.DMA((5,)),
-            pltpu.SemaphoreType.DMA((2, 2)),
+            pltpu.SemaphoreType.DMA((2,)),
         ],
         compiler_params=pltpu.CompilerParams(vmem_limit_bytes=GRANT),
         cost_estimate=cost(1, 6),
@@ -394,11 +387,8 @@
     group, _, plen, feats_here = enc_out.shape
     token_rows = group * topk * plen
     with jax.named_scope("gather_enc_out"):
-        own = enc_out.reshape(token_rows, feats_here)
-        after, before = shift(own, "reader", 1), shift(own, "reader", -1)
-        mid = token_rows // 2
-        far_low, far_high = shift(after[:mid], "reader", 1), shift(before[mid:], "reader", -1)
-        tokens = (own, after, far_low, far_high, before)
+        token_own = enc_out.reshape(token_rows, feats_here)
+        token_after, token_before = shift(token_own, "reader", 1), shift(token_own, "reader", -1)
 
     width_here = key_proj.shape[1]
     ids_high = (passage_id // 256).astype(jnp.bfloat16)
@@ -409,12 +399,11 @@
     with jax.named_scope("gather_key_proj"):
         own = send_all(jnp.concatenate([key_proj, coded]), "zq")
         after, before = shift(own, Z, 1), shift(own, Z, -1)
-        far = [shift(own[:2], Z, 2), shift(own[2:], Z, -2)]
-        classes = (own, after, *far, before)
+        classes = (own, after, shift(own, Z, 2), before)
         own = jnp.concatenate([block[:, :-1] for block in classes])
+        own, token_after, token_before = lax.optimization_barrier((own, token_after, token_before))
         after, before = shift(own, "y", 1), shift(own, "y", -1)
-        far = jnp.concatenate([shift(after[:8], "y", 1), shift(before[8:], "y", -1)])
-        key_rows = [(block, shift(block, "core", 1)) for block in (own, after, far, before)]
+    token_far = shift(token_after, "reader", 1)
 
     with jax.named_scope("gather_queries"):
         coded = jnp.concatenate([block[:, -1] for block in classes])
@@ -459,6 +448,14 @@
             name="scores",
         )(jnp.stack([my_shard, r]).astype(jnp.int32), *operands)
 
+    with jax.named_scope("gather_key_proj"):
+        after, before, state, token_far = lax.optimization_barrier(
+            (after, before, state, token_far)
+        )
+        far = jnp.concatenate([shift(after[:8], "y", 1), shift(before[8:], "y", -1)])
+        key_rows = [(block, shift(block, "core", 1)) for block in (own, after, far, before)]
+    tokens = (token_own, token_after, token_far, token_before)
+
     with jax.named_scope("reduce_scores"):
         states = lax.all_to_all(state, ("y", "core", *Z_BY_CLASS), 0, 0, tiled=True)
 
@@ -504,7 +501,7 @@
                 *like(slots, query_scale, my_rows, my_unit, ordered),
                 pltpu.SemaphoreType.DMA((5,)),
             ],
-            compiler_params=pltpu.CompilerParams(vmem_limit_bytes=GRANT),
+            compiler_params=pltpu.CompilerParams(vmem_limit_bytes=40 << 20),
             name="gradient",
         )(coef, slots, query_scale, my_rows, my_unit, ordered)
 

time: 268 us -> 278 us (1.037)
  waiting for transfers between devices: 28.5 us -> 59.5 us
  other arithmetic: 11.5 us -> 6.87 us
  starting transfers between devices: 77.9 us -> 73.6 us
  Pallas kernels: 39.1 us -> 35 us
  local copies, waits for them, and re-layouts: 23.3 us -> 19.7 us
  blocking collectives: 83.1 us -> 79.6 us
    ppermute x17 -> x15, waiting for transfers between devices: 14.9 us -> 44.5 us  [shift(): return lax.ppermute(x, axis, [((i + step) % size, i) for i in range(size)])]
    ppermute x17 -> x15, starting transfers between devices: 53.9 us -> 46.1 us  [shift(): return lax.ppermute(x, axis, [((i + step) % size, i) for i in range(size)])]
    unnamed x39 -> x50, local copies, waits for them, and re-layouts: 5.64 us -> 11.9 us
    all_to_all x1, starting transfers between devices: 7.76 us -> 11 us  [body(): states = lax.all_to_all(state, ('y', 'core', *Z_BY_CLASS), 0, 0, tiled=True)]
    slice x5 -> x4, local copies, waits for them, and re-layouts: 3.25 us -> 0.05 us  [body(): coded = jnp.concatenate([block[:, -1] for block in classes])]
  transfers between devices with their start and end apart: 21 -> 19, of which waited for: 9 -> 11; matrix products, arithmetic and copies ran while one was open for 10% -> 4% of each run, Pallas kernels for 7% -> 7%
where the time goes in v9:
time: 278 us; the launch traced here: 276 us
  blocking collectives  79.6 us (29%)
  starting transfers between devices  73.6 us (26%)
  waiting for transfers between devices  59.5 us (21%)
  Pallas kernels  35 us (13%)
  local copies, waits for them, and re-layouts  19.7 us (7%)
  other arithmetic  6.87 us (2%)
    ppermute x15, starting transfers between devices, shift(): return lax.ppermute(x, axis, [((i + step) % size, i) for i in range(size)])  46.1 us
    ppermute x15, waiting for transfers between devices, shift(): return lax.ppermute(x, axis, [((i + step) % size, i) for i in range(size)])  44.5 us
    all_to_all x1, blocking collectives, send_all(): lax.all_to_all(jnp.broadcast_to(x[None], (size, *x.shape)), axis, 0, 0, t...  34.5 us
    all_to_all x1, blocking collectives, body(): lax.all_to_all(coef, Z_BY_CLASS, 0, 0, tiled=True).reshape(n_index, LANES)  23.9 us
    all_to_all x2, starting transfers between devices, send_all(): lax.all_to_all(jnp.broadcast_to(x[None], (size, *x.shape)), axis, 0, 0, t...  12.9 us
    all_to_all x1, waiting for transfers between devices, body(): term = jnp.sum(lax.all_to_all(term, Z, 0, 0, tiled=True), axis=0)  12.8 us
    unnamed x50, local copies, waits for them, and re-layouts  11.9 us
    all_to_all x1, blocking collectives, body(): term = jnp.sum(lax.all_to_all(term, 'y', 0, 0, tiled=True), axis=0)  11 us
  transfers between devices with their start and end apart: 19, of which 11 were waited for; matrix products, arithmetic and copies ran while one was open for 4% of the time, Pallas kernels for 7%

profile of v9, /device:TPU:6, one launch (start us, length us, event | category | flops | bytes accessed | tf_op | source)
XLA Modules:
  0.0 275.5 jit_solution(13714637419262745425)
XLA Ops:
  2.9 34.5 %all_to_all.50 = bf16[4,33,1024]{2,1,0:T(8,128)(2,1)S(1)} all-to-all(bf16[4,33,1024]{2,1,0:T(8,128)(2,1)S(1)} %broadcast_in_dim.10), channel_id=1, replica_groups=mesh['y'=4,'zq'=4,'zr'=4,'core'=2,'reader'=4] {'zq'}, dimensions={0} | all-to-all | bytes 540672 | tf_op jit(solution)/shard_map/gather_key_proj/all_to_all | solution.py:37
  37.4 7.8 %collective-permute-start.2 = (bf16[4,33,1024]{2,1,0:T(8,128)(2,1)S(1)}, bf16[4,33,1024]{2,1,0:T(8,128)(2,1)S(1)}, u32[]{:S(2)}, u32[]{:S(2)}) collective-permute-start(bf16[4,33,1024]{2,1,0:T(8,128)(2,1)S(1)} %all_to_all.50), channel_id=1, source_target_pairs={{120,0},{0,8},{8,16},{16,24},{24,32},{32,40},{40,48},{48,56},{56,6... | collective-permute-start | bytes 811016 | tf_op jit(solution)/shard_map/gather_key_proj/ppermute | solution.py:32
  45.2 2.3 collective-permute-start.1
  47.5 2.4 collective-permute-start
  49.9 2.7 collective-permute-start.3
  52.6 4.3 %collective-permute-start.4 = (bf16[640,1024]{1,0:T(8,128)(2,1)}, bf16[640,1024]{1,0:T(8,128)(2,1)}, u32[]{:S(2)}, u32[]{:S(2)}) collective-permute-start(bf16[640,1024]{1,0:T(8,128)(2,1)} %bitcast.43), channel_id=1, source_target_pairs={{3,0},{0,1},{1,2},{2,3},{7,4},{4,5},{5,6},{6,7},{11,8},{8,9},{9,10... | collective-permute-start | bytes 3932168 | tf_op jit(solution)/shard_map/gather_enc_out/ppermute | solution.py:32
  57.1 4.9 %collective-permute-done.1 = bf16[4,33,1024]{2,1,0:T(8,128)(2,1)S(1)} collective-permute-done((bf16[4,33,1024]{2,1,0:T(8,128)(2,1)S(1)}, bf16[4,33,1024]{2,1,0:T(8,128)(2,1)S(1)}, u32[]{:S(2)}, u32[]{:S(2)}) %collective-permute-start.1) | collective-permute-done | bytes 270368 | tf_op jit(solution)/shard_map/gather_key_proj/ppermute | solution.py:32
  61.9 6.7 %collective-permute-done = bf16[4,33,1024]{2,1,0:T(8,128)(2,1)S(1)} collective-permute-done((bf16[4,33,1024]{2,1,0:T(8,128)(2,1)S(1)}, bf16[4,33,1024]{2,1,0:T(8,128)(2,1)S(1)}, u32[]{:S(2)}, u32[]{:S(2)}) %collective-permute-start) | collective-permute-done | bytes 270368 | tf_op jit(solution)/shard_map/gather_key_proj/ppermute | solution.py:32
  69.8 7.6 %all-to-all-start.1 = ((bf16[32,16,896]{2,1,0:T(8,128)(2,1)}), bf16[32,16,896]{2,1,0:T(8,128)(2,1)S(1)}, u32[]{:S(2)}, u32[]{:S(2)}) async-start(bf16[32,16,896]{2,1,0:T(8,128)(2,1)} %broadcast_in_dim.11), calls=%async_computation.1 | async-start | bytes 1835008 | tf_op jit(solution)/shard_map/gather_queries/all_to_all | solution.py:37
  79.2 1.0 slice.52
  80.3 1.1 pad_maximum_fusion.refs_4_
  81.4 5.9 %collective-permute-done.3.refs_1_ = bf16[640,1024]{1,0:T(8,128)(2,1)S(1)} collective-permute-done((bf16[640,1024]{1,0:T(8,128)(2,1)}, bf16[640,1024]{1,0:T(8,128)(2,1)S(1)}, u32[]{:S(2)}, u32[]{:S(2)}) %collective-permute-start.3) | collective-permute-done | bytes 1310752 | tf_op jit(solution)/shard_map/gather_enc_out/ppermute | solution.py:32
  87.4 1.4 collective-permute-done.4.refs_3_
  88.8 5.5 %collective-permute-start.5 = (bf16[16,32,1024]{2,1,0:T(8,128)(2,1)}, bf16[16,32,1024]{2,1,0:T(8,128)(2,1)}, u32[]{:S(2)}, u32[]{:S(2)}) collective-permute-start(bf16[16,32,1024]{2,1,0:T(8,128)(2,1)} %pad_maximum_fusion.refs_4_), channel_id=1, source_target_pairs={{128,0},{256,128},{384,256},{0,384},{129,1},{257,129},{385,257},{1... | collective-permute-start | bytes 3145736 | tf_op jit(solution)/shard_map/gather_key_proj/ppermute | solution.py:32
  94.3 1.9 collective-permute-start.6
  96.2 1.9 collective-permute-start.11
  98.2 1.9 collective-permute-start.7
  100.1 1.3 copy-done.13
  101.4 7.9 %scores.1 = (f32[128,128]{1,0:T(8,128)}, s32[128,128]{1,0:T(8,128)S(1)}, f32[512,192]{1,0:T(8,128)S(1)}, f32[512,192]{1,0:T(8,128)S(1)}, f32[128,128]{1,0:T(8,128)S(1)}, /*index=5*/bf16[768,512]{1,0:T(8,128)(2,1)S(1)}) custom-call(s32[2]{0:T(128)S(1)} %pad_add_fusion.1.place, bf16[32,16,896]{2,1,0:T(8,128)(2,1)S(1)} %all-to-all-done.1.refs_0_, ...), custom_call_target="tpu_custom_call" | custom-call | flops 68719476736 | bytes 8388608 | tf_op jit(solution)/shard_map/scores/scores/pallas_call | solution.py:433
  113.6 4.3 %collective-permute-done.6.refs_8_ = bf16[16,32,1024]{2,1,0:T(8,128)(2,1)} collective-permute-done((bf16[16,32,1024]{2,1,0:T(8,128)(2,1)}, bf16[16,32,1024]{2,1,0:T(8,128)(2,1)}, u32[]{:S(2)}, u32[]{:S(2)}) %collective-permute-start.6) | collective-permute-done | bytes 1048608 | tf_op jit(solution)/shard_map/gather_key_proj/ppermute | solution.py:32
  117.9 15.9 %collective-permute-done.7.refs_2_ = bf16[640,1024]{1,0:T(8,128)(2,1)} collective-permute-done((bf16[640,1024]{1,0:T(8,128)(2,1)S(1)}, bf16[640,1024]{1,0:T(8,128)(2,1)}, u32[]{:S(2)}, u32[]{:S(2)}) %collective-permute-start.7) | collective-permute-done | bytes 1310752 | tf_op jit(solution)/shard_map/ppermute | solution.py:32
  133.8 1.9 collective-permute-start.12
  135.7 2.4 collective-permute-start.13
  138.2 1.1 slice.48
  139.3 1.1 slice.49
  140.3 5.1 %collective-permute-start.8 = (bf16[8,32,1024]{2,1,0:T(8,128)(2,1)S(1)}, bf16[8,32,1024]{2,1,0:T(8,128)(2,1)S(1)}, u32[]{:S(2)}, u32[]{:S(2)}) collective-permute-start(bf16[8,32,1024]{2,1,0:T(8,128)(2,1)S(1)} %slice.48), channel_id=1, source_target_pairs={{128,0},{256,128},{384,256},{0,384},{129,1},{257,129},{385,257},{1... | collective-permute-start | bytes 1572872 | tf_op jit(solution)/shard_map/gather_key_proj/ppermute | solution.py:32
  145.5 1.9 collective-permute-start.9
  147.9 11.0 %all-to-all-start.2 = ((f32[128,1,128]{2,1,0:T(1,128)}), f32[128,1,128]{2,1,0:T(1,128)}, u32[]{:S(2)}, u32[]{:S(2)}) async-start(f32[128,1,128]{2,1,0:T(1,128)} %bitcast.8), calls=%async_computation.2 | async-start | bytes 131072 | tf_op jit(solution)/shard_map/reduce_scores/all_to_all | solution.py:460
  159.0 3.1 %collective-permute-done.9 = bf16[8,32,1024]{2,1,0:T(8,128)(2,1)S(1)} collective-permute-done((bf16[8,32,1024]{2,1,0:T(8,128)(2,1)S(1)}, bf16[8,32,1024]{2,1,0:T(8,128)(2,1)S(1)}, u32[]{:S(2)}, u32[]{:S(2)}) %collective-permute-start.9) | collective-permute-done | bytes 524320 | tf_op jit(solution)/shard_map/gather_key_proj/ppermute | solution.py:32
  162.2 2.1 collective-permute-start.10
  164.3 10.3 %early_keys.1.refs_6_ = f32[640,1024]{1,0:T(8,128)} custom-call(s32[4]{0:T(128)S(1)} %pad_add_fusion.place, bf16[640,1024]{1,0:T(8,128)(2,1)} %bitcast.44, bf16[640,1024]{1,0:T(8,128)(2,1)} %copy-done.1, bf16[640,1024]{1,0:T(8,128)(2,1)} %collective-permute-done.7.refs_2_, bf16[640,1024]{1,0:T(8,128)(2,1)} %collective-permute-done.4.refs_3_, ...), custom_call_target="tpu_custom_call" | custom-call | flops 16106127360 | bytes 13631488 | tf_op jit(solution)/shard_map/attention/early_keys/pallas_call | solution.py:198
  174.7 1.3 copy-done.2
  176.0 8.4 %late_heads.1 = (f32[32,256]{1,0:T(8,128)S(1)}, f32[8,128]{1,0:T(8,128)S(1)}) custom-call(s32[4]{0:T(128)S(1)} %pad_add_fusion.place, bf16[640,1024]{1,0:T(8,128)(2,1)S(1)} %bitcast.45, bf16[640,1024]{1,0:T(8,128)(2,1)S(1)} %copy-done.2, bf16[640,1024]{1,0:T(8,128)(2,1)} %collective-permute-done.7.refs_2_, bf16[640,1024]{1,0:T(8,128)(2,1)} %collective-permute-done.4.refs_3_, ...), custom_call_target="tpu_custom_call" | custom-call | flops 1342177280 | bytes 6291456 | tf_op jit(solution)/shard_map/attention/late_heads/pallas_call | solution.py:213
  184.4 10.1 %all_to_all.51 = f32[32,1,256]{2,1,0:T(1,128)S(1)} all-to-all(f32[32,1,256]{2,1,0:T(1,128)S(1)} %copy.26), channel_id=1, replica_groups=mesh['y'=4,'zq'=4,'zr'=4,'core'=2,'reader'=4] {'reader','y','core'}, dimensions={0} | all-to-all | bytes 65536 | tf_op jit(solution)/shard_map/targets/all_to_all | solution.py:482
  195.2 1.6 coef.1
  196.8 23.9 %all_to_all.52 = f32[16,8,128]{2,1,0:T(8,128)S(1)} all-to-all(f32[16,8,128]{2,1,0:T(8,128)} %coef.1), channel_id=1, replica_groups=mesh['y'=4,'zq'=4,'zr'=4,'core'=2,'reader'=4] {'zr','zq'}, dimensions={0} | all-to-all | bytes 131072 | tf_op jit(solution)/shard_map/targets/all_to_all | solution.py:490
  220.7 1.1 copy-done.4
  221.9 1.0 copy-done.6
  222.9 1.0 copy-done.8
  225.6 6.8 %gradient.1 = (f32[384,192]{1,0:T(8,128)S(1)}, f32[384,192]{1,0:T(8,128)S(1)}) custom-call(f32[128,128]{1,0:T(8,128)S(1)} %bitcast.46, s32[128,128]{1,0:T(8,128)S(1)} %copy-done.10, f32[128,128]{1,0:T(8,128)S(1)} %copy-done.12, f32[512,192]{1,0:T(8,128)S(1)} %copy-done.6, f32[512,192]{1,0:T(8,128)S(1)} %copy-done.8, bf16[768,512]{1,0:T(8,128)(2,1)S(1)} %copy-done.4), custom_call_target="tpu_custom_call" | custom-call | tf_op jit(solution)/shard_map/gradient/gradient/pallas_call | solution.py:494
  232.4 1.9 collective-permute-start.14
  234.3 1.7 collective-permute-done.14
  236.1 11.0 %all_to_all.53 = f32[4,96,192]{2,1,0:T(8,128)S(1)} all-to-all(f32[4,96,192]{2,1,0:T(8,128)S(1)} %bitcast.49), channel_id=1, replica_groups=mesh['y'=4,'zq'=4,'zr'=4,'core'=2,'reader'=4] {'y'}, dimensions={0} | all-to-all | bytes 589824 | tf_op jit(solution)/shard_map/reduce_gradient/all_to_all | solution.py:510
  247.8 3.5 %all-to-all-start.6 = ((f32[16,6,192]{2,1,0:T(8,128)}), f32[16,6,192]{2,1,0:T(8,128)S(1)}, u32[]{:S(2)}, u32[]{:S(2)}) async-start(f32[16,6,192]{2,1,0:T(8,128)} %reshape.202), calls=%async_computation.6 | async-start | bytes 262144 | tf_op jit(solution)/shard_map/reduce_gradient/all_to_all | solution.py:512
  252.7 12.8 %all-to-all-done.6 = f32[16,6,192]{2,1,0:T(8,128)S(1)} async-done(((f32[16,6,192]{2,1,0:T(8,128)}), f32[16,6,192]{2,1,0:T(8,128)S(1)}, u32[]{:S(2)}, u32[]{:S(2)}) %all-to-all-start.6) | async-done | bytes 73760 | tf_op jit(solution)/shard_map/reduce_gradient/all_to_all | solution.py:512
  266.1 5.3 %all-to-all-start.7 = ((f32[4,6,192]{2,1,0:T(8,128)}), f32[4,6,192]{2,1,0:T(8,128)S(1)}, u32[]{:S(2)}, u32[]{:S(2)}) async-start(f32[4,6,192]{2,1,0:T(8,128)} %broadcast_in_dim.12), calls=%async_computation.7 | async-start | bytes 65536 | tf_op jit(solution)/shard_map/reduce_gradient/all_to_all | solution.py:37
  271.4 1.2 log_bitcast_fusion
  272.6 2.2 all-to-all-done.7
  (102 shorter events, 15.9 us)
Async XLA Ops:
  37.4 32.4 %copy-start.14 = (bf16[4,33,1024]{2,1,0:T(8,128)(2,1)}, bf16[4,33,1024]{2,1,0:T(8,128)(2,1)S(1)}, u32[]{:S(2)}) copy-start(bf16[4,33,1024]{2,1,0:T(8,128)(2,1)S(1)} %all_to_all.50) | copy-start | bytes 811012
  37.4 19.6 %collective-permute-start.2 = (bf16[4,33,1024]{2,1,0:T(8,128)(2,1)S(1)}, bf16[4,33,1024]{2,1,0:T(8,128)(2,1)S(1)}, u32[]{:S(2)}, u32[]{:S(2)}) collective-permute-start(bf16[4,33,1024]{2,1,0:T(8,128)(2,1)S(1)} %all_to_all.50), channel_id=1, source_target_pairs={{120,0},{0,8},{8,16},{16,24},{24,32},{32,40},{40,48},{48,56},{56,6... | collective-permute-start | bytes 811016 | tf_op jit(solution)/shard_map/gather_key_proj/ppermute | solution.py:32
  45.2 16.7 %collective-permute-start.1 = (bf16[4,33,1024]{2,1,0:T(8,128)(2,1)S(1)}, bf16[4,33,1024]{2,1,0:T(8,128)(2,1)S(1)}, u32[]{:S(2)}, u32[]{:S(2)}) collective-permute-start(bf16[4,33,1024]{2,1,0:T(8,128)(2,1)S(1)} %all_to_all.50), channel_id=1, source_target_pairs={{16,0},{24,8},{32,16},{40,24},{48,32},{56,40},{64,48},{72,56},{80,... | collective-permute-start | bytes 811016 | tf_op jit(solution)/shard_map/gather_key_proj/ppermute | solution.py:32
  47.5 21.2 %collective-permute-start = (bf16[4,33,1024]{2,1,0:T(8,128)(2,1)S(1)}, bf16[4,33,1024]{2,1,0:T(8,128)(2,1)S(1)}, u32[]{:S(2)}, u32[]{:S(2)}) collective-permute-start(bf16[4,33,1024]{2,1,0:T(8,128)(2,1)S(1)} %all_to_all.50), channel_id=1, source_target_pairs={{8,0},{16,8},{24,16},{32,24},{40,32},{48,40},{56,48},{64,56},{72,6... | collective-permute-start | bytes 811016 | tf_op jit(solution)/shard_map/gather_key_proj/ppermute | solution.py:32
  49.9 37.5 %collective-permute-start.3 = (bf16[640,1024]{1,0:T(8,128)(2,1)}, bf16[640,1024]{1,0:T(8,128)(2,1)S(1)}, u32[]{:S(2)}, u32[]{:S(2)}) collective-permute-start(bf16[640,1024]{1,0:T(8,128)(2,1)} %bitcast.42), channel_id=1, source_target_pairs={{1,0},{2,1},{3,2},{0,3},{5,4},{6,5},{7,6},{4,7},{9,8},{10,9},{11,1... | collective-permute-start | bytes 3932168 | tf_op jit(solution)/shard_map/gather_enc_out/ppermute | solution.py:32
  52.6 36.1 %collective-permute-start.4 = (bf16[640,1024]{1,0:T(8,128)(2,1)}, bf16[640,1024]{1,0:T(8,128)(2,1)}, u32[]{:S(2)}, u32[]{:S(2)}) collective-permute-start(bf16[640,1024]{1,0:T(8,128)(2,1)} %bitcast.43), channel_id=1, source_target_pairs={{3,0},{0,1},{1,2},{2,3},{7,4},{4,5},{5,6},{6,7},{11,8},{8,9},{9,10... | collective-permute-start | bytes 3932168 | tf_op jit(solution)/shard_map/gather_enc_out/ppermute | solution.py:32
  57.0 12.8 %copy-start.17 = (bf16[4,33,1024]{2,1,0:T(8,128)(2,1)}, bf16[4,33,1024]{2,1,0:T(8,128)(2,1)S(1)}, u32[]{:S(2)}) copy-start(bf16[4,33,1024]{2,1,0:T(8,128)(2,1)S(1)} %collective-permute-done.2) | copy-start | bytes 811012
  61.9 7.9 %copy-start.16 = (bf16[4,33,1024]{2,1,0:T(8,128)(2,1)}, bf16[4,33,1024]{2,1,0:T(8,128)(2,1)S(1)}, u32[]{:S(2)}) copy-start(bf16[4,33,1024]{2,1,0:T(8,128)(2,1)S(1)} %collective-permute-done.1) | copy-start | bytes 811012
  68.6 1.2 copy-start.15
  68.8 8.7 %copy-start.18 = (bf16[4,16,1024]{2,1,0:T(8,128)(2,1)S(1)}, bf16[4,16,1024]{2,1,0:T(8,128)(2,1)}, u32[]{:S(2)}) copy-start(bf16[4,16,1024]{2,1,0:T(8,128)(2,1)} %param.17) | copy-start | bytes 393220
  69.8 7.8 %copy-start.20 = (s32[4,20]{1,0:T(4,128)S(1)}, s32[4,20]{1,0:T(4,128)}, u32[]{:S(2)}) copy-start(s32[4,20]{1,0:T(4,128)} %param.13) | copy-start | bytes 964
  69.8 30.3 %all-to-all-start.1 = ((bf16[32,16,896]{2,1,0:T(8,128)(2,1)}), bf16[32,16,896]{2,1,0:T(8,128)(2,1)S(1)}, u32[]{:S(2)}, u32[]{:S(2)}) async-start(bf16[32,16,896]{2,1,0:T(8,128)(2,1)} %broadcast_in_dim.11), calls=%async_computation.1 | async-start | bytes 1835008 | tf_op jit(solution)/shard_map/gather_queries/all_to_all | solution.py:37
  79.1 1.1 slice-start
  79.1 1.1 slice-start.1
  79.1 1.2 slice-start.2
  87.4 21.9 %copy-start.1 = (bf16[640,1024]{1,0:T(8,128)(2,1)}, bf16[640,1024]{1,0:T(8,128)(2,1)S(1)}, u32[]{:S(2)}) copy-start(bf16[640,1024]{1,0:T(8,128)(2,1)S(1)} %collective-permute-done.3.refs_1_) | copy-start | bytes 3932164
  88.8 24.9 %collective-permute-start.5 = (bf16[16,32,1024]{2,1,0:T(8,128)(2,1)}, bf16[16,32,1024]{2,1,0:T(8,128)(2,1)}, u32[]{:S(2)}, u32[]{:S(2)}) collective-permute-start(bf16[16,32,1024]{2,1,0:T(8,128)(2,1)} %pad_maximum_fusion.refs_4_), channel_id=1, source_target_pairs={{128,0},{256,128},{384,256},{0,384},{129,1},{257,129},{385,257},{1... | collective-permute-start | bytes 3145736 | tf_op jit(solution)/shard_map/gather_key_proj/ppermute | solution.py:32
  94.3 23.6 %collective-permute-start.6 = (bf16[16,32,1024]{2,1,0:T(8,128)(2,1)}, bf16[16,32,1024]{2,1,0:T(8,128)(2,1)}, u32[]{:S(2)}, u32[]{:S(2)}) collective-permute-start(bf16[16,32,1024]{2,1,0:T(8,128)(2,1)} %pad_maximum_fusion.refs_4_), channel_id=1, source_target_pairs={{384,0},{0,128},{128,256},{256,384},{385,1},{1,129},{129,257},{257... | collective-permute-start | bytes 3145736 | tf_op jit(solution)/shard_map/gather_key_proj/ppermute | solution.py:32
  96.2 68.0 %collective-permute-start.11 = (bf16[16,32,1024]{2,1,0:T(8,128)(2,1)}, bf16[16,32,1024]{2,1,0:T(8,128)(2,1)}, u32[]{:S(2)}, u32[]{:S(2)}) collective-permute-start(bf16[16,32,1024]{2,1,0:T(8,128)(2,1)} %pad_maximum_fusion.refs_4_), channel_id=1, source_target_pairs={{4,0},{0,4},{5,1},{1,5},{6,2},{2,6},{7,3},{3,7},{12,8},{8,12},{13,... | collective-permute-start | bytes 3145736 | tf_op jit(solution)/shard_map/gather_key_proj/ppermute | solution.py:32
  98.2 35.6 %collective-permute-start.7 = (bf16[640,1024]{1,0:T(8,128)(2,1)S(1)}, bf16[640,1024]{1,0:T(8,128)(2,1)}, u32[]{:S(2)}, u32[]{:S(2)}) collective-permute-start(bf16[640,1024]{1,0:T(8,128)(2,1)S(1)} %collective-permute-done.3.refs_1_), channel_id=1, source_target_pairs={{1,0},{2,1},{3,2},{0,3},{5,4},{6,5},{7,6},{4,7},{9,8},{10,9},{11,1... | collective-permute-start | bytes 3932168 | tf_op jit(solution)/shard_map/ppermute | solution.py:32
  100.1 1.3 copy-start.13
  101.4 36.8 %copy-start.19 = (f32[4,16,16]{2,1,0:T(8,128)S(1)}, f32[4,16,16]{2,1,0:T(8,128)}, u32[]{:S(2)}) copy-start(f32[4,16,16]{2,1,0:T(8,128)} %reduce_sum.45) | copy-start | bytes 12292
  109.3 0.9 copy-start.3
  110.2 0.8 copy-start.5
  110.9 0.8 copy-start.7
  111.7 0.6 copy-start.9
  112.4 0.6 copy-start.11
  133.8 30.5 %collective-permute-start.12 = (bf16[16,32,1024]{2,1,0:T(8,128)(2,1)}, bf16[16,32,1024]{2,1,0:T(8,128)(2,1)}, u32[]{:S(2)}, u32[]{:S(2)}) collective-permute-start(bf16[16,32,1024]{2,1,0:T(8,128)(2,1)} %collective-permute-done.5.refs_6_), channel_id=1, source_target_pairs={{4,0},{0,4},{5,1},{1,5},{6,2},{2,6},{7,3},{3,7},{12,8},{8,12},{13,... | collective-permute-start | bytes 3145736 | tf_op jit(solution)/shard_map/gather_key_proj/ppermute | solution.py:32
  135.7 28.6 %collective-permute-start.13 = (bf16[16,32,1024]{2,1,0:T(8,128)(2,1)}, bf16[16,32,1024]{2,1,0:T(8,128)(2,1)}, u32[]{:S(2)}, u32[]{:S(2)}) collective-permute-start(bf16[16,32,1024]{2,1,0:T(8,128)(2,1)} %collective-permute-done.6.refs_8_), channel_id=1, source_target_pairs={{4,0},{0,4},{5,1},{1,5},{6,2},{2,6},{7,3},{3,7},{12,8},{8,12},{13,... | collective-permute-start | bytes 3145736 | tf_op jit(solution)/shard_map/gather_key_proj/ppermute | solution.py:32
  139.2 8.6 %copy-start.21 = (bf16[1024]{0:T(1024)(128)(2,1)S(1)}, bf16[1024]{0:T(1024)(128)(2,1)}, u32[]{:S(2)}) copy-start(bf16[1024]{0:T(1024)(128)(2,1)} %param.16) | copy-start | bytes 6148
  140.3 18.7 %collective-permute-start.8 = (bf16[8,32,1024]{2,1,0:T(8,128)(2,1)S(1)}, bf16[8,32,1024]{2,1,0:T(8,128)(2,1)S(1)}, u32[]{:S(2)}, u32[]{:S(2)}) collective-permute-start(bf16[8,32,1024]{2,1,0:T(8,128)(2,1)S(1)} %slice.48), channel_id=1, source_target_pairs={{128,0},{256,128},{384,256},{0,384},{129,1},{257,129},{385,257},{1... | collective-permute-start | bytes 1572872 | tf_op jit(solution)/shard_map/gather_key_proj/ppermute | solution.py:32
  145.5 16.7 %collective-permute-start.9 = (bf16[8,32,1024]{2,1,0:T(8,128)(2,1)S(1)}, bf16[8,32,1024]{2,1,0:T(8,128)(2,1)S(1)}, u32[]{:S(2)}, u32[]{:S(2)}) collective-permute-start(bf16[8,32,1024]{2,1,0:T(8,128)(2,1)S(1)} %slice.49), channel_id=1, source_target_pairs={{384,0},{0,128},{128,256},{256,384},{385,1},{1,129},{129,257},{257... | collective-permute-start | bytes 1572872 | tf_op jit(solution)/shard_map/gather_key_proj/ppermute | solution.py:32
  147.9 26.7 %all-to-all-start.2 = ((f32[128,1,128]{2,1,0:T(1,128)}), f32[128,1,128]{2,1,0:T(1,128)}, u32[]{:S(2)}, u32[]{:S(2)}) async-start(f32[128,1,128]{2,1,0:T(1,128)} %bitcast.8), calls=%async_computation.2 | async-start | bytes 131072 | tf_op jit(solution)/shard_map/reduce_scores/all_to_all | solution.py:460
  162.2 12.4 %copy-start = (bf16[4,20,8,1024]{3,2,1,0:T(8,128)(2,1)S(1)}, bf16[4,20,8,1024]{3,2,1,0:T(8,128)(2,1)}, u32[]{:S(2)}) copy-start(bf16[4,20,8,1024]{3,2,1,0:T(8,128)(2,1)} %param.14) | copy-start | bytes 3932164
  162.2 12.4 %collective-permute-start.10 = (bf16[16,32,1024]{2,1,0:T(8,128)(2,1)S(1)}, bf16[16,32,1024]{2,1,0:T(8,128)(2,1)S(1)}, u32[]{:S(2)}, u32[]{:S(2)}) collective-permute-start(bf16[16,32,1024]{2,1,0:T(8,128)(2,1)S(1)} %constant_dynamic-update-slice_fusion.refs_4_), channel_id=1, source_target_pairs={{4,0},{0,4},{5,1},{1,5},{6,2},{2,6},{7,3},{3,7},{12,8},{8,12},{13,... | collective-permute-start | bytes 3145736 | tf_op jit(solution)/shard_map/gather_key_proj/ppermute | solution.py:32
  174.6 1.3 copy-start.2
  220.7 1.1 copy-start.4
  221.9 1.0 copy-start.6
  222.9 1.0 copy-start.8
  223.9 0.8 copy-start.10
  224.8 0.8 copy-start.12
  232.4 3.6 %collective-permute-start.14 = (f32[384,192]{1,0:T(8,128)S(1)}, f32[384,192]{1,0:T(8,128)S(1)}, u32[]{:S(2)}, u32[]{:S(2)}) collective-permute-start(f32[384,192]{1,0:T(8,128)S(1)} %get-tuple-element.36), channel_id=1, source_target_pairs={{4,0},{0,4},{5,1},{1,5},{6,2},{2,6},{7,3},{3,7},{12,8},{8,12},{13,... | collective-permute-start | bytes 884744 | tf_op jit(solution)/shard_map/reduce_gradient/ppermute | solution.py:32
  247.8 17.7 %all-to-all-start.6 = ((f32[16,6,192]{2,1,0:T(8,128)}), f32[16,6,192]{2,1,0:T(8,128)S(1)}, u32[]{:S(2)}, u32[]{:S(2)}) async-start(f32[16,6,192]{2,1,0:T(8,128)} %reshape.202), calls=%async_computation.6 | async-start | bytes 262144 | tf_op jit(solution)/shard_map/reduce_gradient/all_to_all | solution.py:512
  266.1 8.7 %all-to-all-start.7 = ((f32[4,6,192]{2,1,0:T(8,128)}), f32[4,6,192]{2,1,0:T(8,128)S(1)}, u32[]{:S(2)}, u32[]{:S(2)}) async-start(f32[4,6,192]{2,1,0:T(8,128)} %broadcast_in_dim.12), calls=%async_computation.7 | async-start | bytes 65536 | tf_op jit(solution)/shard_map/reduce_gradient/all_to_all | solution.py:37

commit v10 on v9

--- a/solution.py
+++ b/solution.py
@@ -47,24 +47,18 @@
 
 
 def load(far, near, sems):
-    copies = [pltpu.make_async_copy(a, b, sems.at[i]) for i, (a, b) in enumerate(zip(far, near))]
+    copies = [pltpu.make_async_copy(a, b, sem) for a, b, sem in zip(far, near, sems)]
     for copy in copies:
         copy.start()
     return copies
 
 
+def each(sems, arrays):
+    return [sems.at[i] for i in range(len(arrays))]
+
+
 def like(*arrays):
     return [pltpu.VMEM(x.shape, x.dtype) for x in arrays]
-
-
-def token_copies(r, chunk, tokens, target, sem):
-    for j, block in enumerate(tokens):
-
-        @pl.when((r + j) % 4 == chunk)
-        def _():
-            pltpu.make_async_copy(block, target, sem).start()
-
-    return [pltpu.make_async_copy(target, target, sem)]
 
 
 def row_copies(place, own, other, target, sem):
@@ -78,13 +72,13 @@
 
 
 def early_keys_kernel(place, *refs):
-    tokens, rows, (keys_out, keys, token_v, weight_v, sems) = refs[:4], refs[4:10], refs[10:]
-    y, r = place[0], place[3]
+    tokens, rows, (keys_out, keys, token_v, weight_v, sems) = refs[0], refs[1:7], refs[7:]
+    y = place[0]
     copies = []
     for slot, ahead in enumerate(EARLY):
         own, other = rows[2 * slot], rows[2 * slot + 1]
         copies += row_copies(place, own, other, weight_v.at[slot], sems.at[0, slot])
-        copies += token_copies(r, (y + ahead) % 4, tokens, token_v.at[slot], sems.at[1, slot])
+        copies += load([tokens.at[(y + ahead) % 4]], [token_v.at[slot]], [sems.at[1, slot]])
     for copy in copies:
         copy.wait()
     tiles = keys.shape[0]
@@ -137,14 +131,14 @@
 
 
 def late_heads_kernel(place, *refs):
-    tokens, (own, other), refs = refs[:4], refs[4:6], refs[6:]
+    tokens, (own, other), refs = refs[0], refs[1:3], refs[3:]
     far, (out, own_scores), near, refs = refs[:5], refs[5:7], refs[7:12], refs[12:]
     token_v, weight_v, column_v, load_sems, sems = refs
-    y, r = place[0], place[3]
-    loads = load(far, near, load_sems)
+    y = place[0]
+    loads = load(far, near, each(load_sems, far))
     early, dec, gain, live, states = near
     copies = row_copies(place, own, other, weight_v, sems.at[0])
-    copies += token_copies(r, (y + LATE) % 4, tokens, token_v, sems.at[1])
+    copies += load([tokens.at[(y + LATE) % 4]], [token_v], [sems.at[1]])
     column_v[...] = jnp.zeros_like(column_v)
 
     lane = lax.broadcasted_iota(jnp.int32, (1, LANES), 1)
@@ -185,7 +179,7 @@
     vmem = pl.BlockSpec(memory_space=pltpu.VMEM)
     anywhere = pl.BlockSpec(memory_space=pl.ANY)
     smem = pl.BlockSpec(memory_space=pltpu.SMEM)
-    token_rows, width = tokens[0].shape
+    _, token_rows, width = tokens.shape
     block = (4, 4, 2, *rows[0][0].shape[1:])
 
     def cost(count, size):
@@ -198,7 +192,7 @@
     early = pl.pallas_call(
         early_keys_kernel,
         out_shape=jax.ShapeDtypeStruct((token_rows, width), jnp.float32),
-        in_specs=[smem] + [anywhere] * 10,
+        in_specs=[smem] + [anywhere] * 7,
         out_specs=anywhere,
         scratch_shapes=[
             pltpu.VMEM((width // TILE, token_rows, TILE), jnp.float32),
@@ -207,16 +201,16 @@
             pltpu.SemaphoreType.DMA((3, 4)),
         ],
         compiler_params=pltpu.CompilerParams(vmem_limit_bytes=GRANT),
-        cost_estimate=cost(12, 13),
+        cost_estimate=cost(5, 13),
         name="early_keys",
-    )(place, *tokens, *[part for ahead in EARLY for part in rows[ahead]])
+    )(place, tokens, *[part for ahead in EARLY for part in rows[ahead]])
     return pl.pallas_call(
         late_heads_kernel,
         out_shape=(
             jax.ShapeDtypeStruct((32, 2 * LANES), jnp.float32),
             jax.ShapeDtypeStruct((8, LANES), jnp.float32),
         ),
-        in_specs=[smem] + [anywhere] * 11,
+        in_specs=[smem] + [anywhere] * 8,
         out_specs=(vmem, vmem),
         scratch_shapes=[
             *like(early, dec, gain, live, states),
@@ -229,13 +223,13 @@
         compiler_params=pltpu.CompilerParams(vmem_limit_bytes=GRANT),
         cost_estimate=cost(1, 6),
         name="late_heads",
-    )(place, *tokens, *rows[LATE], early, dec, gain, live, states)
+    )(place, tokens, *rows[LATE], early, dec, gain, live, states)
 
 
 def scores_kernel(place, *refs):
     far, (state, *outs), near, refs = refs[:4], refs[4:10], refs[10:14], refs[14:]
     near_outs, (unit_v, ids_v, sems) = refs[:5], refs[5:]
-    copies = load(far, near, sems)
+    copies = load(far, near, each(sems, far))
     packed, proj, emb, chosen = near
     slots, rows, unit, scale, ordered = near_outs
     shard, r = place[0], place[1]
@@ -278,7 +272,7 @@
             rows[...] = row_unit[:, x * cols : (x + 1) * cols]
             unit[...] = unit_all[:, x * cols : (x + 1) * cols]
 
-    copies = load(near_outs, outs, sems)
+    copies = load(near_outs, outs, each(sems, outs))
     share = unit_v[pl.ds(pl.multiple_of(r * per_x, per_x), per_x), :]
     found = (
         lax.dot_general(
@@ -324,7 +318,7 @@
 
 def gradient_kernel(coef, *refs):
     far, (keep, send, matrix_v), near, sems = refs[:5], refs[5:8], refs[8:13], refs[13]
-    copies = load(far, near, sems)
+    copies = load(far, near, each(sems, far))
     slot, scale, rows, unit, ordered = near
     copies[0].wait()
     copies[1].wait()
@@ -387,8 +381,7 @@
     group, _, plen, feats_here = enc_out.shape
     token_rows = group * topk * plen
     with jax.named_scope("gather_enc_out"):
-        token_own = enc_out.reshape(token_rows, feats_here)
-        token_after, token_before = shift(token_own, "reader", 1), shift(token_own, "reader", -1)
+        tokens = lax.all_gather(enc_out.reshape(token_rows, feats_here), "reader")
 
     width_here = key_proj.shape[1]
     ids_high = (passage_id // 256).astype(jnp.bfloat16)
@@ -401,9 +394,7 @@
         after, before = shift(own, Z, 1), shift(own, Z, -1)
         classes = (own, after, shift(own, Z, 2), before)
         own = jnp.concatenate([block[:, :-1] for block in classes])
-        own, token_after, token_before = lax.optimization_barrier((own, token_after, token_before))
         after, before = shift(own, "y", 1), shift(own, "y", -1)
-    token_far = shift(token_after, "reader", 1)
 
     with jax.named_scope("gather_queries"):
         coded = jnp.concatenate([block[:, -1] for block in classes])
@@ -443,21 +434,19 @@
             ],
             compiler_params=pltpu.CompilerParams(vmem_limit_bytes=GRANT),
             cost_estimate=pl.CostEstimate(
-                flops=64 << 30, bytes_accessed=8 << 20, transcendentals=0
+                flops=10 << 30, bytes_accessed=8 << 20, transcendentals=0
             ),
             name="scores",
         )(jnp.stack([my_shard, r]).astype(jnp.int32), *operands)
 
     with jax.named_scope("gather_key_proj"):
-        after, before, state, token_far = lax.optimization_barrier(
-            (after, before, state, token_far)
-        )
+        after, before, state = lax.optimization_barrier((after, before, state))
         far = jnp.concatenate([shift(after[:8], "y", 1), shift(before[8:], "y", -1)])
         key_rows = [(block, shift(block, "core", 1)) for block in (own, after, far, before)]
-    tokens = (token_own, token_after, token_far, token_before)
 
     with jax.named_scope("reduce_scores"):
         states = lax.all_to_all(state, ("y", "core", *Z_BY_CLASS), 0, 0, tiled=True)
+        key_rows[0], states = lax.optimization_barrier((key_rows[0], states))
 
     with jax.named_scope("attention"):
         answer = dec_query.shape[1]
@@ -469,7 +458,7 @@
         positions = lax.broadcasted_iota(jnp.int32, (group, topk, plen), 2)
         live = (positions < passage_len[:, :, None]).reshape(group, topk * plen)
         packet, own_scores = attention_packet(
-            jnp.stack([y, zr, core, r]).astype(jnp.int32),
+            jnp.stack([y, zr, core]).astype(jnp.int32),
             tokens,
             key_rows,
             dec_unit.reshape(group, answer, feats_here),

time: 278 us -> 279 us (level)
  starting transfers between devices: 73.6 us -> 58.4 us
  between operations: 1.3 us -> 14.5 us
  waiting for transfers between devices: 59.5 us -> 69.8 us
  blocking collectives: 79.6 us -> 72.9 us
    ppermute x15 -> x12, starting transfers between devices: 46.1 us -> 34.9 us  [shift(): return lax.ppermute(x, axis, [((i + step) % size, i) for i in range(size)])]
    all_to_all x1, waiting for transfers between devices: 0.01 us -> 10.6 us  [body(): states = lax.all_to_all(state, ('y', 'core', *Z_BY_CLASS), 0, 0, tiled=True)]
    all_to_all x1, blocking collectives: 23.9 us -> 16.5 us  [body(): lax.all_to_all(coef, Z_BY_CLASS, 0, 0, tiled=True).reshape(n_index, LANES)]
    ppermute x15 -> x12, waiting for transfers between devices: 44.5 us -> 37.4 us  [shift(): return lax.ppermute(x, axis, [((i + step) % size, i) for i in range(size)])]
    all_to_all x2, waiting for transfers between devices: 2.19 us -> 8.29 us  [send_all(): lax.all_to_all(jnp.broadcast_to(x[None], (size, *x.shape)), axis, 0, 0, t...]
    all_to_all x1, starting transfers between devices: 11 us -> 6.98 us  [body(): states = lax.all_to_all(state, ('y', 'core', *Z_BY_CLASS), 0, 0, tiled=True)]
    unnamed x50 -> x32, local copies, waits for them, and re-layouts: 11.9 us -> 8.92 us
  transfers between devices with their start and end apart: 19 -> 17, of which waited for: 11 -> 12; matrix products, arithmetic and copies ran while one was open for 4% -> 5% of each run, Pallas kernels for 7% -> 6%
where the time goes in v10:
time: 279 us; the launch traced here: 276 us
  blocking collectives  72.9 us (26%)
  waiting for transfers between devices  69.8 us (25%)
  starting transfers between devices  58.4 us (21%)
  Pallas kernels  34.4 us (12%)
  local copies, waits for them, and re-layouts  19.8 us (7%)
  between operations  14.5 us (5%)
  other arithmetic  6.27 us (2%)
    ppermute x12, waiting for transfers between devices, shift(): return lax.ppermute(x, axis, [((i + step) % size, i) for i in range(size)])  37.4 us
    ppermute x12, starting transfers between devices, shift(): return lax.ppermute(x, axis, [((i + step) % size, i) for i in range(size)])  34.9 us
    all_to_all x1, blocking collectives, send_all(): lax.all_to_all(jnp.broadcast_to(x[None], (size, *x.shape)), axis, 0, 0, t...  34.5 us
    all_to_all x1, blocking collectives, body(): lax.all_to_all(coef, Z_BY_CLASS, 0, 0, tiled=True).reshape(n_index, LANES)  16.5 us
    all_to_all x2, starting transfers between devices, send_all(): lax.all_to_all(jnp.broadcast_to(x[None], (size, *x.shape)), axis, 0, 0, t...  12.9 us
    all_to_all x1, waiting for transfers between devices, body(): term = jnp.sum(lax.all_to_all(term, Z, 0, 0, tiled=True), axis=0)  12.8 us
    all_to_all x1, blocking collectives, body(): term = jnp.sum(lax.all_to_all(term, 'y', 0, 0, tiled=True), axis=0)  11 us
    all_to_all x1, blocking collectives, body(): lax.all_to_all(packet, NEAR, 0, 0, tiled=True)  10.9 us
  transfers between devices with their start and end apart: 17, of which 12 were waited for; matrix products, arithmetic and copies ran while one was open for 5% of the time, Pallas kernels for 6%

profile of v10, /device:TPU:6, one launch (start us, length us, event | category | flops | bytes accessed | tf_op | source)
XLA Modules:
  0.0 276.1 jit_solution(15083101864819500818)
XLA Ops:
  10.2 34.5 %all_to_all.51 = bf16[4,33,1024]{2,1,0:T(8,128)(2,1)S(1)} all-to-all(bf16[4,33,1024]{2,1,0:T(8,128)(2,1)S(1)} %broadcast_in_dim.10), channel_id=1, replica_groups=mesh['y'=4,'zq'=4,'zr'=4,'core'=2,'reader'=4] {'zq'}, dimensions={0} | all-to-all | bytes 540672 | tf_op jit(solution)/shard_map/gather_key_proj/all_to_all | solution.py:37
  44.7 7.8 %collective-permute-start.2 = (bf16[4,33,1024]{2,1,0:T(8,128)(2,1)S(1)}, bf16[4,33,1024]{2,1,0:T(8,128)(2,1)S(1)}, u32[]{:S(2)}, u32[]{:S(2)}) collective-permute-start(bf16[4,33,1024]{2,1,0:T(8,128)(2,1)S(1)} %all_to_all.51), channel_id=1, source_target_pairs={{120,0},{0,8},{8,16},{16,24},{24,32},{32,40},{40,48},{48,56},{56,6... | collective-permute-start | bytes 811016 | tf_op jit(solution)/shard_map/gather_key_proj/ppermute | solution.py:32
  52.4 2.3 collective-permute-start.1
  54.7 2.4 collective-permute-start
  57.2 1.2 collective-permute-done.2
  58.4 10.8 %collective-permute-done.1 = bf16[4,33,1024]{2,1,0:T(8,128)(2,1)S(1)} collective-permute-done((bf16[4,33,1024]{2,1,0:T(8,128)(2,1)S(1)}, bf16[4,33,1024]{2,1,0:T(8,128)(2,1)S(1)}, u32[]{:S(2)}, u32[]{:S(2)}) %collective-permute-start.1) | collective-permute-done | bytes 270368 | tf_op jit(solution)/shard_map/gather_key_proj/ppermute | solution.py:32
  69.2 6.7 %collective-permute-done = bf16[4,33,1024]{2,1,0:T(8,128)(2,1)S(1)} collective-permute-done((bf16[4,33,1024]{2,1,0:T(8,128)(2,1)S(1)}, bf16[4,33,1024]{2,1,0:T(8,128)(2,1)S(1)}, u32[]{:S(2)}, u32[]{:S(2)}) %collective-permute-start) | collective-permute-done | bytes 270368 | tf_op jit(solution)/shard_map/gather_key_proj/ppermute | solution.py:32
  76.1 1.0 broadcast_in_dim.11
  77.1 7.6 %all-to-all-start.1 = ((bf16[32,16,896]{2,1,0:T(8,128)(2,1)}), bf16[32,16,896]{2,1,0:T(8,128)(2,1)S(1)}, u32[]{:S(2)}, u32[]{:S(2)}) async-start(bf16[32,16,896]{2,1,0:T(8,128)(2,1)} %broadcast_in_dim.11), calls=%async_computation.1 | async-start | bytes 1835008 | tf_op jit(solution)/shard_map/gather_queries/all_to_all | solution.py:37
  85.9 4.6 %collective-permute-start.3 = (bf16[16,32,1024]{2,1,0:T(8,128)(2,1)S(1)}, bf16[16,32,1024]{2,1,0:T(8,128)(2,1)}, u32[]{:S(2)}, u32[]{:S(2)}) collective-permute-start(bf16[16,32,1024]{2,1,0:T(8,128)(2,1)S(1)} %pad_maximum_fusion.refs_1_), channel_id=1, source_target_pairs={{128,0},{256,128},{384,256},{0,384},{129,1},{257,129},{385,257},{1... | collective-permute-start | bytes 3145736 | tf_op jit(solution)/shard_map/gather_key_proj/ppermute | solution.py:32
  90.5 1.9 collective-permute-start.4
  92.5 6.1 %all-to-all-done.1.refs_0_ = bf16[32,16,896]{2,1,0:T(8,128)(2,1)S(1)} async-done(((bf16[32,16,896]{2,1,0:T(8,128)(2,1)}), bf16[32,16,896]{2,1,0:T(8,128)(2,1)S(1)}, u32[]{:S(2)}, u32[]{:S(2)}) %all-to-all-start.1) | async-done | bytes 917536 | tf_op jit(solution)/shard_map/gather_queries/all_to_all | solution.py:37
  98.7 1.3 copy-done.7
  99.9 7.9 %scores.1 = (f32[128,128]{1,0:T(8,128)}, s32[128,128]{1,0:T(8,128)S(1)}, f32[512,192]{1,0:T(8,128)S(1)}, f32[512,192]{1,0:T(8,128)S(1)}, f32[128,128]{1,0:T(8,128)S(1)}, /*index=5*/bf16[768,512]{1,0:T(8,128)(2,1)S(1)}) custom-call(s32[2]{0:T(128)S(1)} %pad_add_fusion.1.place, bf16[32,16,896]{2,1,0:T(8,128)(2,1)S(1)} %all-to-all-done.1.refs_0_, ...), custom_call_target="tpu_custom_call" | custom-call | flops 10737418240 | bytes 8388608 | tf_op jit(solution)/shard_map/scores/scores/pallas_call | solution.py:424
  110.3 9.3 %collective-permute-done.3.refs_3_ = bf16[16,32,1024]{2,1,0:T(8,128)(2,1)} collective-permute-done((bf16[16,32,1024]{2,1,0:T(8,128)(2,1)S(1)}, bf16[16,32,1024]{2,1,0:T(8,128)(2,1)}, u32[]{:S(2)}, u32[]{:S(2)}) %collective-permute-start.3) | collective-permute-done | bytes 1048608 | tf_op jit(solution)/shard_map/gather_key_proj/ppermute | solution.py:32
  119.7 1.2 collective-permute-done.4.refs_5_
  120.9 1.9 slice.48
  122.8 2.7 collective-permute-start.5
  125.6 1.9 slice.49
  127.4 3.1 %collective-permute-start.6 = (bf16[8,32,1024]{2,1,0:T(8,128)(2,1)}, bf16[8,32,1024]{2,1,0:T(8,128)(2,1)S(1)}, u32[]{:S(2)}, u32[]{:S(2)}) collective-permute-start(bf16[8,32,1024]{2,1,0:T(8,128)(2,1)} %slice.49), channel_id=1, source_target_pairs={{384,0},{0,128},{128,256},{256,384},{385,1},{1,129},{129,257},{257... | collective-permute-start | bytes 1572872 | tf_op jit(solution)/shard_map/gather_key_proj/ppermute | solution.py:32
  131.2 1.9 collective-permute-start.8
  133.1 2.4 collective-permute-start.10
  135.5 1.9 collective-permute-start.9
  137.5 1.2 collective-permute-done.5
  138.8 5.3 %collective-permute-done.6 = bf16[8,32,1024]{2,1,0:T(8,128)(2,1)S(1)} collective-permute-done((bf16[8,32,1024]{2,1,0:T(8,128)(2,1)}, bf16[8,32,1024]{2,1,0:T(8,128)(2,1)S(1)}, u32[]{:S(2)}, u32[]{:S(2)}) %collective-permute-start.6) | collective-permute-done | bytes 524320 | tf_op jit(solution)/shard_map/gather_key_proj/ppermute | solution.py:32
  144.1 1.9 collective-permute-start.7
  146.0 7.0 %all-to-all-start.2 = ((f32[128,1,128]{2,1,0:T(1,128)}), f32[128,1,128]{2,1,0:T(1,128)S(1)}, u32[]{:S(2)}, u32[]{:S(2)}) async-start(f32[128,1,128]{2,1,0:T(1,128)} %bitcast.7), calls=%async_computation.2 | async-start | bytes 131072 | tf_op jit(solution)/shard_map/reduce_scores/all_to_all | solution.py:448
  153.1 1.0 mul.76
  154.1 1.9 mul.77
  156.0 1.0 fusion.1.refs_4_
  157.0 10.6 %all-to-all-done.2 = f32[128,1,128]{2,1,0:T(1,128)S(1)} async-done(((f32[128,1,128]{2,1,0:T(1,128)}), f32[128,1,128]{2,1,0:T(1,128)S(1)}, u32[]{:S(2)}, u32[]{:S(2)}) %all-to-all-start.2) | async-done | bytes 65568 | tf_op jit(solution)/shard_map/reduce_scores/all_to_all | solution.py:448
  167.6 10.0 %early_keys.1.refs_3_ = f32[640,1024]{1,0:T(8,128)} custom-call(s32[3]{0:T(128)S(1)} %pad_add_fusion.place, bf16[4,640,1024]{2,1,0:T(8,128)(2,1)} %all-gather.2.cloned.1.call-done.refs_0_, bf16[16,32,1024]{2,1,0:T(8,128)(2,1)S(1)} %pad_maximum_fusion.refs_1_, bf16[16,32,1024]{2,1,0:T(8,128)(2,1)} %collective-permute-done.8.refs_2_, ...), custom_call_target="tpu_custom_call" | custom-call | flops 6710886400 | bytes 13631488 | tf_op jit(solution)/shard_map/attention/early_keys/pallas_call | solution.py:192
  177.7 1.7 copy-done
  179.4 8.1 %late_heads.1 = (f32[32,256]{1,0:T(8,128)S(1)}, f32[8,128]{1,0:T(8,128)S(1)}) custom-call(s32[3]{0:T(128)S(1)} %pad_add_fusion.place, bf16[4,640,1024]{2,1,0:T(8,128)(2,1)} %all-gather.2.cloned.1.call-done.refs_0_, bf16[16,32,1024]{2,1,0:T(8,128)(2,1)S(1)} %constant_dynamic-update-slice_fusion.refs_1_, ...), custom_call_target="tpu_custom_call" | custom-call | flops 1342177280 | bytes 6291456 | tf_op jit(solution)/shard_map/attention/late_heads/pallas_call | solution.py:207
  187.6 10.9 %all_to_all.52 = f32[32,1,256]{2,1,0:T(1,128)S(1)} all-to-all(f32[32,1,256]{2,1,0:T(1,128)S(1)} %copy.26), channel_id=1, replica_groups=mesh['y'=4,'zq'=4,'zr'=4,'core'=2,'reader'=4] {'reader','y','core'}, dimensions={0} | all-to-all | bytes 65536 | tf_op jit(solution)/shard_map/targets/all_to_all | solution.py:471
  199.1 1.6 coef.1
  200.7 16.5 %all_to_all.53 = f32[16,8,128]{2,1,0:T(8,128)S(1)} all-to-all(f32[16,8,128]{2,1,0:T(8,128)} %coef.1), channel_id=1, replica_groups=mesh['y'=4,'zq'=4,'zr'=4,'core'=2,'reader'=4] {'zr','zq'}, dimensions={0} | all-to-all | bytes 131072 | tf_op jit(solution)/shard_map/targets/all_to_all | solution.py:479
  217.2 1.0 copy-done.4
  218.2 1.0 copy-done.6
  219.3 6.8 %gradient.1 = (f32[384,192]{1,0:T(8,128)S(1)}, f32[384,192]{1,0:T(8,128)S(1)}) custom-call(f32[128,128]{1,0:T(8,128)S(1)} %bitcast.43, s32[128,128]{1,0:T(8,128)S(1)} %get-tuple-element.28.refs_0_, f32[128,128]{1,0:T(8,128)S(1)} %get-tuple-element.29.refs_1_, f32[512,192]{1,0:T(8,128)S(1)} %copy-done.4, f32[512,192]{1,0:T(8,128)S(1)} %copy-done.6, ...), custom_call_target="tpu_custom_call" | custom-call | tf_op jit(solution)/shard_map/gradient/gradient/pallas_call | solution.py:483
  226.1 1.9 collective-permute-start.11
  228.0 1.7 collective-permute-done.11
  229.7 11.0 %all_to_all.54 = f32[4,96,192]{2,1,0:T(8,128)S(1)} all-to-all(f32[4,96,192]{2,1,0:T(8,128)S(1)} %bitcast.46), channel_id=1, replica_groups=mesh['y'=4,'zq'=4,'zr'=4,'core'=2,'reader'=4] {'y'}, dimensions={0} | all-to-all | bytes 589824 | tf_op jit(solution)/shard_map/reduce_gradient/all_to_all | solution.py:499
  241.5 3.5 %all-to-all-start.6 = ((f32[16,6,192]{2,1,0:T(8,128)}), f32[16,6,192]{2,1,0:T(8,128)S(1)}, u32[]{:S(2)}, u32[]{:S(2)}) async-start(f32[16,6,192]{2,1,0:T(8,128)} %reshape.202), calls=%async_computation.6 | async-start | bytes 262144 | tf_op jit(solution)/shard_map/reduce_gradient/all_to_all | solution.py:501
  246.4 12.8 %all-to-all-done.6 = f32[16,6,192]{2,1,0:T(8,128)S(1)} async-done(((f32[16,6,192]{2,1,0:T(8,128)}), f32[16,6,192]{2,1,0:T(8,128)S(1)}, u32[]{:S(2)}, u32[]{:S(2)}) %all-to-all-start.6) | async-done | bytes 73760 | tf_op jit(solution)/shard_map/reduce_gradient/all_to_all | solution.py:501
  259.8 5.3 %all-to-all-start.7 = ((f32[4,6,192]{2,1,0:T(8,128)}), f32[4,6,192]{2,1,0:T(8,128)S(1)}, u32[]{:S(2)}, u32[]{:S(2)}) async-start(f32[4,6,192]{2,1,0:T(8,128)} %broadcast_in_dim.12), calls=%async_computation.7 | async-start | bytes 65536 | tf_op jit(solution)/shard_map/reduce_gradient/all_to_all | solution.py:37
  265.1 1.2 log_bitcast_fusion
  266.3 2.2 all-to-all-done.7
  (78 shorter events, 11.9 us)
Async XLA Ops:
  7.2 160.5 %all-gather.2.cloned.1.call-start = ((), (), s32[]{:S(2)}) async-start(), calls=%async_computation.8 | async-start | bytes 6553600 | tf_op jit(solution)/shard_map/gather_enc_out/all_gather | solution.py:384
  44.7 13.7 %collective-permute-start.2 = (bf16[4,33,1024]{2,1,0:T(8,128)(2,1)S(1)}, bf16[4,33,1024]{2,1,0:T(8,128)(2,1)S(1)}, u32[]{:S(2)}, u32[]{:S(2)}) collective-permute-start(bf16[4,33,1024]{2,1,0:T(8,128)(2,1)S(1)} %all_to_all.51), channel_id=1, source_target_pairs={{120,0},{0,8},{8,16},{16,24},{24,32},{32,40},{40,48},{48,56},{56,6... | collective-permute-start | bytes 811016 | tf_op jit(solution)/shard_map/gather_key_proj/ppermute | solution.py:32
  52.4 16.7 %collective-permute-start.1 = (bf16[4,33,1024]{2,1,0:T(8,128)(2,1)S(1)}, bf16[4,33,1024]{2,1,0:T(8,128)(2,1)S(1)}, u32[]{:S(2)}, u32[]{:S(2)}) collective-permute-start(bf16[4,33,1024]{2,1,0:T(8,128)(2,1)S(1)} %all_to_all.51), channel_id=1, source_target_pairs={{16,0},{24,8},{32,16},{40,24},{48,32},{56,40},{64,48},{72,56},{80,... | collective-permute-start | bytes 811016 | tf_op jit(solution)/shard_map/gather_key_proj/ppermute | solution.py:32
  54.7 21.2 %collective-permute-start = (bf16[4,33,1024]{2,1,0:T(8,128)(2,1)S(1)}, bf16[4,33,1024]{2,1,0:T(8,128)(2,1)S(1)}, u32[]{:S(2)}, u32[]{:S(2)}) collective-permute-start(bf16[4,33,1024]{2,1,0:T(8,128)(2,1)S(1)} %all_to_all.51), channel_id=1, source_target_pairs={{8,0},{16,8},{24,16},{32,24},{40,32},{48,40},{56,48},{64,56},{72,6... | collective-permute-start | bytes 811016 | tf_op jit(solution)/shard_map/gather_key_proj/ppermute | solution.py:32
  75.9 1.2 copy-start.9
  77.1 21.6 %all-to-all-start.1 = ((bf16[32,16,896]{2,1,0:T(8,128)(2,1)}), bf16[32,16,896]{2,1,0:T(8,128)(2,1)S(1)}, u32[]{:S(2)}, u32[]{:S(2)}) async-start(bf16[32,16,896]{2,1,0:T(8,128)(2,1)} %broadcast_in_dim.11), calls=%async_computation.1 | async-start | bytes 1835008 | tf_op jit(solution)/shard_map/gather_queries/all_to_all | solution.py:37
  84.7 1.0 copy-start.10
  85.9 33.8 %collective-permute-start.3 = (bf16[16,32,1024]{2,1,0:T(8,128)(2,1)S(1)}, bf16[16,32,1024]{2,1,0:T(8,128)(2,1)}, u32[]{:S(2)}, u32[]{:S(2)}) collective-permute-start(bf16[16,32,1024]{2,1,0:T(8,128)(2,1)S(1)} %pad_maximum_fusion.refs_1_), channel_id=1, source_target_pairs={{128,0},{256,128},{384,256},{0,384},{129,1},{257,129},{385,257},{1... | collective-permute-start | bytes 3145736 | tf_op jit(solution)/shard_map/gather_key_proj/ppermute | solution.py:32
  90.5 30.4 %collective-permute-start.4 = (bf16[16,32,1024]{2,1,0:T(8,128)(2,1)S(1)}, bf16[16,32,1024]{2,1,0:T(8,128)(2,1)}, u32[]{:S(2)}, u32[]{:S(2)}) collective-permute-start(bf16[16,32,1024]{2,1,0:T(8,128)(2,1)S(1)} %pad_maximum_fusion.refs_1_), channel_id=1, source_target_pairs={{384,0},{0,128},{128,256},{256,384},{385,1},{1,129},{129,257},{257... | collective-permute-start | bytes 3145736 | tf_op jit(solution)/shard_map/gather_key_proj/ppermute | solution.py:32
  98.6 1.3 copy-start.7
  107.8 0.9 copy-start.1
  108.7 0.8 copy-start.3
  109.5 0.8 copy-start.5
  110.3 20.2 %copy-start.8 = (bf16[4,16,1024]{2,1,0:T(8,128)(2,1)S(1)}, bf16[4,16,1024]{2,1,0:T(8,128)(2,1)}, u32[]{:S(2)}) copy-start(bf16[4,16,1024]{2,1,0:T(8,128)(2,1)} %param.17) | copy-start | bytes 393220
  120.9 9.8 %copy-start.11 = (s32[4,20]{1,0:T(4,128)S(1)}, s32[4,20]{1,0:T(4,128)}, u32[]{:S(2)}) copy-start(s32[4,20]{1,0:T(4,128)} %param.13) | copy-start | bytes 964
  122.8 15.9 %collective-permute-start.5 = (bf16[8,32,1024]{2,1,0:T(8,128)(2,1)}, bf16[8,32,1024]{2,1,0:T(8,128)(2,1)S(1)}, u32[]{:S(2)}, u32[]{:S(2)}) collective-permute-start(bf16[8,32,1024]{2,1,0:T(8,128)(2,1)} %slice.48), channel_id=1, source_target_pairs={{128,0},{256,128},{384,256},{0,384},{129,1},{257,129},{385,257},{1... | collective-permute-start | bytes 1572872 | tf_op jit(solution)/shard_map/gather_key_proj/ppermute | solution.py:32
  127.4 16.6 %collective-permute-start.6 = (bf16[8,32,1024]{2,1,0:T(8,128)(2,1)}, bf16[8,32,1024]{2,1,0:T(8,128)(2,1)S(1)}, u32[]{:S(2)}, u32[]{:S(2)}) collective-permute-start(bf16[8,32,1024]{2,1,0:T(8,128)(2,1)} %slice.49), channel_id=1, source_target_pairs={{384,0},{0,128},{128,256},{256,384},{385,1},{1,129},{129,257},{257... | collective-permute-start | bytes 1572872 | tf_op jit(solution)/shard_map/gather_key_proj/ppermute | solution.py:32
  131.2 25.8 %collective-permute-start.8 = (bf16[16,32,1024]{2,1,0:T(8,128)(2,1)S(1)}, bf16[16,32,1024]{2,1,0:T(8,128)(2,1)}, u32[]{:S(2)}, u32[]{:S(2)}) collective-permute-start(bf16[16,32,1024]{2,1,0:T(8,128)(2,1)S(1)} %pad_maximum_fusion.refs_1_), channel_id=1, source_target_pairs={{4,0},{0,4},{5,1},{1,5},{6,2},{2,6},{7,3},{3,7},{12,8},{8,12},{13,... | collective-permute-start | bytes 3145736 | tf_op jit(solution)/shard_map/gather_key_proj/ppermute | solution.py:32
  133.1 34.5 %collective-permute-start.10 = (bf16[16,32,1024]{2,1,0:T(8,128)(2,1)}, bf16[16,32,1024]{2,1,0:T(8,128)(2,1)}, u32[]{:S(2)}, u32[]{:S(2)}) collective-permute-start(bf16[16,32,1024]{2,1,0:T(8,128)(2,1)} %collective-permute-done.4.refs_5_), channel_id=1, source_target_pairs={{4,0},{0,4},{5,1},{1,5},{6,2},{2,6},{7,3},{3,7},{12,8},{8,12},{13,... | collective-permute-start | bytes 3145736 | tf_op jit(solution)/shard_map/gather_key_proj/ppermute | solution.py:32
  135.5 32.1 %collective-permute-start.9 = (bf16[16,32,1024]{2,1,0:T(8,128)(2,1)}, bf16[16,32,1024]{2,1,0:T(8,128)(2,1)}, u32[]{:S(2)}, u32[]{:S(2)}) collective-permute-start(bf16[16,32,1024]{2,1,0:T(8,128)(2,1)} %collective-permute-done.3.refs_3_), channel_id=1, source_target_pairs={{4,0},{0,4},{5,1},{1,5},{6,2},{2,6},{7,3},{3,7},{12,8},{8,12},{13,... | collective-permute-start | bytes 3145736 | tf_op jit(solution)/shard_map/gather_key_proj/ppermute | solution.py:32
  137.5 18.5 %copy-start.12 = (bf16[1024]{0:T(1024)(128)(2,1)S(1)}, bf16[1024]{0:T(1024)(128)(2,1)}, u32[]{:S(2)}) copy-start(bf16[1024]{0:T(1024)(128)(2,1)} %param.16) | copy-start | bytes 6148
  144.1 33.6 %collective-permute-start.7 = (bf16[16,32,1024]{2,1,0:T(8,128)(2,1)S(1)}, bf16[16,32,1024]{2,1,0:T(8,128)(2,1)S(1)}, u32[]{:S(2)}, u32[]{:S(2)}) collective-permute-start(bf16[16,32,1024]{2,1,0:T(8,128)(2,1)S(1)} %constant_dynamic-update-slice_fusion.refs_1_), channel_id=1, source_target_pairs={{4,0},{0,4},{5,1},{1,5},{6,2},{2,6},{7,3},{3,7},{12,8},{8,12},{13,... | collective-permute-start | bytes 3145736 | tf_op jit(solution)/shard_map/gather_key_proj/ppermute | solution.py:32
  146.0 21.6 %all-to-all-start.2 = ((f32[128,1,128]{2,1,0:T(1,128)}), f32[128,1,128]{2,1,0:T(1,128)S(1)}, u32[]{:S(2)}, u32[]{:S(2)}) async-start(f32[128,1,128]{2,1,0:T(1,128)} %bitcast.7), calls=%async_computation.2 | async-start | bytes 131072 | tf_op jit(solution)/shard_map/reduce_scores/all_to_all | solution.py:448
  177.7 1.7 copy-start
  179.4 37.8 %copy-start.2 = (bf16[768,512]{1,0:T(8,128)(2,1)S(1)}, bf16[768,512]{1,0:T(8,128)(2,1)}, u32[]{:S(2)}) copy-start(bf16[768,512]{1,0:T(8,128)(2,1)} %copy-done.1) | copy-start | bytes 2359300
  217.2 1.0 copy-start.4
  218.2 1.0 copy-start.6
  226.1 3.6 %collective-permute-start.11 = (f32[384,192]{1,0:T(8,128)S(1)}, f32[384,192]{1,0:T(8,128)S(1)}, u32[]{:S(2)}, u32[]{:S(2)}) collective-permute-start(f32[384,192]{1,0:T(8,128)S(1)} %get-tuple-element.34), channel_id=1, source_target_pairs={{4,0},{0,4},{5,1},{1,5},{6,2},{2,6},{7,3},{3,7},{12,8},{8,12},{13,... | collective-permute-start | bytes 884744 | tf_op jit(solution)/shard_map/reduce_gradient/ppermute | solution.py:32
  241.5 17.7 %all-to-all-start.6 = ((f32[16,6,192]{2,1,0:T(8,128)}), f32[16,6,192]{2,1,0:T(8,128)S(1)}, u32[]{:S(2)}, u32[]{:S(2)}) async-start(f32[16,6,192]{2,1,0:T(8,128)} %reshape.202), calls=%async_computation.6 | async-start | bytes 262144 | tf_op jit(solution)/shard_map/reduce_gradient/all_to_all | solution.py:501
  259.8 8.7 %all-to-all-start.7 = ((f32[4,6,192]{2,1,0:T(8,128)}), f32[4,6,192]{2,1,0:T(8,128)S(1)}, u32[]{:S(2)}, u32[]{:S(2)}) async-start(f32[4,6,192]{2,1,0:T(8,128)} %broadcast_in_dim.12), calls=%async_computation.7 | async-start | bytes 65536 | tf_op jit(solution)/shard_map/reduce_gradient/all_to_all | solution.py:37
Sparse Core Ops, SparseCore 0:
  10.1 67.4 all-gather.1

commit v11 on v10

--- a/solution.py
+++ b/solution.py
@@ -200,7 +200,7 @@
             pltpu.VMEM((3, *block), jnp.bfloat16),
             pltpu.SemaphoreType.DMA((3, 4)),
         ],
-        compiler_params=pltpu.CompilerParams(vmem_limit_bytes=GRANT),
+        compiler_params=pltpu.CompilerParams(vmem_limit_bytes=56 << 20),
         cost_estimate=cost(5, 13),
         name="early_keys",
     )(place, tokens, *[part for ahead in EARLY for part in rows[ahead]])
@@ -432,9 +432,9 @@
                 pltpu.VMEM((nx, n_index, LANES), jnp.int32),
                 pltpu.SemaphoreType.DMA((5,)),
             ],
-            compiler_params=pltpu.CompilerParams(vmem_limit_bytes=GRANT),
+            compiler_params=pltpu.CompilerParams(vmem_limit_bytes=56 << 20),
             cost_estimate=pl.CostEstimate(
-                flops=10 << 30, bytes_accessed=8 << 20, transcendentals=0
+                flops=1 << 30, bytes_accessed=4 << 20, transcendentals=0
             ),
             name="scores",
         )(jnp.stack([my_shard, r]).astype(jnp.int32), *operands)
@@ -446,7 +446,6 @@
 
     with jax.named_scope("reduce_scores"):
         states = lax.all_to_all(state, ("y", "core", *Z_BY_CLASS), 0, 0, tiled=True)
-        key_rows[0], states = lax.optimization_barrier((key_rows[0], states))
 
     with jax.named_scope("attention"):
         answer = dec_query.shape[1]

time: 279 us -> 279 us (level)
  waiting for transfers between devices: 69.8 us -> 62.2 us
  blocking collectives: 72.9 us -> 78.3 us
  local copies, waits for them, and re-layouts: 19.8 us -> 15.1 us
  starting transfers between devices: 58.4 us -> 62.4 us
    ppermute x12, waiting for transfers between devices: 37.4 us -> 20.4 us  [shift(): return lax.ppermute(x, axis, [((i + step) % size, i) for i in range(size)])]
    all_to_all x2, waiting for transfers between devices: 8.29 us -> 24.2 us  [send_all(): lax.all_to_all(jnp.broadcast_to(x[None], (size, *x.shape)), axis, 0, 0, t...]
    all_to_all x1, waiting for transfers between devices: 10.6 us -> 4.12 us  [body(): states = lax.all_to_all(state, ('y', 'core', *Z_BY_CLASS), 0, 0, tiled=True)]
    all_to_all x1, blocking collectives: 16.5 us -> 22.4 us  [body(): lax.all_to_all(coef, Z_BY_CLASS, 0, 0, tiled=True).reshape(n_index, LANES)]
    all_to_all x1, starting transfers between devices: 6.98 us -> 10.7 us  [body(): states = lax.all_to_all(state, ('y', 'core', *Z_BY_CLASS), 0, 0, tiled=True)]
  transfers between devices with their start and end apart: 17 -> 17, of which waited for: 12 -> 9; matrix products, arithmetic and copies ran while one was open for 5% -> 5% of each run, Pallas kernels for 6% -> 7%
where the time goes in v11:
time: 279 us; the launch traced here: 276 us
  blocking collectives  78.3 us (28%)
  starting transfers between devices  62.4 us (22%)
  waiting for transfers between devices  62.2 us (22%)
  Pallas kernels  35.1 us (13%)
  local copies, waits for them, and re-layouts  15.1 us (5%)
  between operations  14.6 us (5%)
  other arithmetic  8.45 us (3%)
    ppermute x12, starting transfers between devices, shift(): return lax.ppermute(x, axis, [((i + step) % size, i) for i in range(size)])  35.2 us
    all_to_all x1, blocking collectives, send_all(): lax.all_to_all(jnp.broadcast_to(x[None], (size, *x.shape)), axis, 0, 0, t...  34.5 us
    all_to_all x2, waiting for transfers between devices, send_all(): lax.all_to_all(jnp.broadcast_to(x[None], (size, *x.shape)), axis, 0, 0, t...  24.2 us
    all_to_all x1, blocking collectives, body(): lax.all_to_all(coef, Z_BY_CLASS, 0, 0, tiled=True).reshape(n_index, LANES)  22.4 us
    ppermute x12, waiting for transfers between devices, shift(): return lax.ppermute(x, axis, [((i + step) % size, i) for i in range(size)])  20.4 us
    all_to_all x2, starting transfers between devices, send_all(): lax.all_to_all(jnp.broadcast_to(x[None], (size, *x.shape)), axis, 0, 0, t...  13 us
    all_to_all x1, waiting for transfers between devices, body(): term = jnp.sum(lax.all_to_all(term, Z, 0, 0, tiled=True), axis=0)  12.8 us
    all_to_all x1, blocking collectives, body(): term = jnp.sum(lax.all_to_all(term, 'y', 0, 0, tiled=True), axis=0)  11 us
  transfers between devices with their start and end apart: 17, of which 9 were waited for; matrix products, arithmetic and copies ran while one was open for 5% of the time, Pallas kernels for 7%

profile of v11, /device:TPU:6, one launch (start us, length us, event | category | flops | bytes accessed | tf_op | source)
XLA Modules:
  0.0 276.2 jit_solution(15078919329516408024)
XLA Ops:
  8.6 0.8 fusion.27
  9.3 0.8 fusion.3
  10.2 34.5 %all_to_all.50 = bf16[4,33,1024]{2,1,0:T(8,128)(2,1)S(1)} all-to-all(bf16[4,33,1024]{2,1,0:T(8,128)(2,1)S(1)} %broadcast_in_dim.10), channel_id=1, replica_groups=mesh['y'=4,'zq'=4,'zr'=4,'core'=2,'reader'=4] {'zq'}, dimensions={0} | all-to-all | bytes 540672 | tf_op jit(solution)/shard_map/gather_key_proj/all_to_all | solution.py:37
  44.7 6.7 %collective-permute-start = (bf16[4,33,1024]{2,1,0:T(8,128)(2,1)S(1)}, bf16[4,33,1024]{2,1,0:T(8,128)(2,1)S(1)}, u32[]{:S(2)}, u32[]{:S(2)}) collective-permute-start(bf16[4,33,1024]{2,1,0:T(8,128)(2,1)S(1)} %all_to_all.50), channel_id=1, source_target_pairs={{8,0},{16,8},{24,16},{32,24},{40,32},{48,40},{56,48},{64,56},{72,6... | collective-permute-start | bytes 811016 | tf_op jit(solution)/shard_map/gather_key_proj/ppermute | solution.py:32
  51.3 1.9 collective-permute-start.1
  53.3 3.9 %collective-permute-start.2 = (bf16[4,33,1024]{2,1,0:T(8,128)(2,1)S(1)}, bf16[4,33,1024]{2,1,0:T(8,128)(2,1)S(1)}, u32[]{:S(2)}, u32[]{:S(2)}) collective-permute-start(bf16[4,33,1024]{2,1,0:T(8,128)(2,1)S(1)} %all_to_all.50), channel_id=1, source_target_pairs={{120,0},{0,8},{8,16},{16,24},{24,32},{32,40},{40,48},{48,56},{56,6... | collective-permute-start | bytes 811016 | tf_op jit(solution)/shard_map/gather_key_proj/ppermute | solution.py:32
  57.2 5.9 %collective-permute-done = bf16[4,33,1024]{2,1,0:T(8,128)(2,1)S(1)} collective-permute-done((bf16[4,33,1024]{2,1,0:T(8,128)(2,1)S(1)}, bf16[4,33,1024]{2,1,0:T(8,128)(2,1)S(1)}, u32[]{:S(2)}, u32[]{:S(2)}) %collective-permute-start) | collective-permute-done | bytes 270368 | tf_op jit(solution)/shard_map/gather_key_proj/ppermute | solution.py:32
  63.1 8.2 %collective-permute-done.1 = bf16[4,33,1024]{2,1,0:T(8,128)(2,1)S(1)} collective-permute-done((bf16[4,33,1024]{2,1,0:T(8,128)(2,1)S(1)}, bf16[4,33,1024]{2,1,0:T(8,128)(2,1)S(1)}, u32[]{:S(2)}, u32[]{:S(2)}) %collective-permute-start.1) | collective-permute-done | bytes 270368 | tf_op jit(solution)/shard_map/gather_key_proj/ppermute | solution.py:32
  71.4 1.2 pad_maximum_fusion.refs_1_
  72.6 4.9 %collective-permute-start.3 = (bf16[16,32,1024]{2,1,0:T(8,128)(2,1)}, bf16[16,32,1024]{2,1,0:T(8,128)(2,1)}, u32[]{:S(2)}, u32[]{:S(2)}) collective-permute-start(bf16[16,32,1024]{2,1,0:T(8,128)(2,1)} %pad_maximum_fusion.refs_1_), channel_id=1, source_target_pairs={{128,0},{256,128},{384,256},{0,384},{129,1},{257,129},{385,257},{1... | collective-permute-start | bytes 3145736 | tf_op jit(solution)/shard_map/gather_key_proj/ppermute | solution.py:32
  77.5 1.9 collective-permute-start.4
  79.7 1.0 broadcast_in_dim.11
  80.7 7.6 %all-to-all-start.1 = ((bf16[32,16,896]{2,1,0:T(8,128)(2,1)}), bf16[32,16,896]{2,1,0:T(8,128)(2,1)S(1)}, u32[]{:S(2)}, u32[]{:S(2)}) async-start(bf16[32,16,896]{2,1,0:T(8,128)(2,1)} %broadcast_in_dim.11), calls=%async_computation.1 | async-start | bytes 1835008 | tf_op jit(solution)/shard_map/gather_queries/all_to_all | solution.py:37
  89.0 1.3 fusion.refs_3_
  90.3 22.0 %all-to-all-done.1.refs_0_ = bf16[32,16,896]{2,1,0:T(8,128)(2,1)S(1)} async-done(((bf16[32,16,896]{2,1,0:T(8,128)(2,1)}), bf16[32,16,896]{2,1,0:T(8,128)(2,1)S(1)}, u32[]{:S(2)}, u32[]{:S(2)}) %all-to-all-start.1) | async-done | bytes 917536 | tf_op jit(solution)/shard_map/gather_queries/all_to_all | solution.py:37
  112.3 0.9 copy-done.9
  113.2 8.2 %scores.1 = (f32[128,128]{1,0:T(8,128)}, s32[128,128]{1,0:T(8,128)}, f32[512,192]{1,0:T(8,128)}, f32[512,192]{1,0:T(8,128)}, f32[128,128]{1,0:T(8,128)}, /*index=5*/bf16[768,512]{1,0:T(8,128)(2,1)}) custom-call(s32[2]{0:T(128)} %pad_add_fusion.1.place, bf16[32,16,896]{2,1,0:T(8,128)(2,1)} %copy-done.9, bf16[768,768]{1,0:T(8,128)(2,1)} %refs_1_.1, ...), custom_call_target="tpu_custom_call" | custom-call | flops 1073741824 | bytes 4194304 | tf_op jit(solution)/shard_map/scores/scores/pallas_call | solution.py:424
  121.5 1.9 slice.48
  123.4 1.9 collective-permute-start.5
  125.3 1.1 slice.49
  126.4 3.9 %collective-permute-start.6 = (bf16[8,32,1024]{2,1,0:T(8,128)(2,1)S(1)}, bf16[8,32,1024]{2,1,0:T(8,128)(2,1)S(1)}, u32[]{:S(2)}, u32[]{:S(2)}) collective-permute-start(bf16[8,32,1024]{2,1,0:T(8,128)(2,1)S(1)} %slice.49), channel_id=1, source_target_pairs={{384,0},{0,128},{128,256},{256,384},{385,1},{1,129},{129,257},{257... | collective-permute-start | bytes 1572872 | tf_op jit(solution)/shard_map/gather_key_proj/ppermute | solution.py:32
  130.8 1.9 collective-permute-start.8
  132.7 2.4 collective-permute-start.10
  135.1 1.9 collective-permute-start.9
  139.0 4.0 %collective-permute-done.6 = bf16[8,32,1024]{2,1,0:T(8,128)(2,1)S(1)} collective-permute-done((bf16[8,32,1024]{2,1,0:T(8,128)(2,1)S(1)}, bf16[8,32,1024]{2,1,0:T(8,128)(2,1)S(1)}, u32[]{:S(2)}, u32[]{:S(2)}) %collective-permute-start.6) | collective-permute-done | bytes 524320 | tf_op jit(solution)/shard_map/gather_key_proj/ppermute | solution.py:32
  143.0 1.9 collective-permute-start.7
  145.0 10.7 %all-to-all-start.2 = ((f32[128,1,128]{2,1,0:T(1,128)}), f32[128,1,128]{2,1,0:T(1,128)S(1)}, u32[]{:S(2)}, u32[]{:S(2)}) async-start(f32[128,1,128]{2,1,0:T(1,128)} %bitcast.8), calls=%async_computation.2 | async-start | bytes 131072 | tf_op jit(solution)/shard_map/reduce_scores/all_to_all | solution.py:448
  155.8 10.4 %early_keys.1.refs_3_ = f32[640,1024]{1,0:T(8,128)} custom-call(s32[3]{0:T(128)} %pad_add_fusion.place, bf16[4,640,1024]{2,1,0:T(8,128)(2,1)} %all-gather.2.cloned.1.call-done.refs_0_, bf16[16,32,1024]{2,1,0:T(8,128)(2,1)} %pad_maximum_fusion.refs_1_, bf16[16,32,1024]{2,1,0:T(8,128)(2,1)} %collective-permute-done.8.refs_2_, ...), custom_call_target="tpu_custom_call" | custom-call | flops 6710886400 | bytes 13631488 | tf_op jit(solution)/shard_map/attention/early_keys/pallas_call | solution.py:192
  166.2 4.1 %all-to-all-done.2 = f32[128,1,128]{2,1,0:T(1,128)S(1)} async-done(((f32[128,1,128]{2,1,0:T(1,128)}), f32[128,1,128]{2,1,0:T(1,128)S(1)}, u32[]{:S(2)}, u32[]{:S(2)}) %all-to-all-start.2) | async-done | bytes 65568 | tf_op jit(solution)/shard_map/reduce_scores/all_to_all | solution.py:448
  171.0 1.7 copy-done
  172.7 0.8 copy-done.5
  173.6 8.1 %late_heads.1 = (f32[32,256]{1,0:T(8,128)S(1)}, f32[8,128]{1,0:T(8,128)S(1)}) custom-call(s32[3]{0:T(128)S(1)} %copy-done.8, bf16[4,640,1024]{2,1,0:T(8,128)(2,1)} %all-gather.2.cloned.1.call-done.refs_0_, bf16[16,32,1024]{2,1,0:T(8,128)(2,1)S(1)} %constant_dynamic-update-slice_fusion.refs_1_, bf16[16,32,1024]{2,1,0:T(8,128)(2,1)S(1)} %collective-permute-done.7.refs_2_, ...), custom_call_target="tpu_custom_call" | custom-call | flops 1342177280 | bytes 6291456 | tf_op jit(solution)/shard_map/attention/late_heads/pallas_call | solution.py:207
  181.7 10.4 %all_to_all.51 = f32[32,1,256]{2,1,0:T(1,128)S(1)} all-to-all(f32[32,1,256]{2,1,0:T(1,128)S(1)} %copy.26), channel_id=1, replica_groups=mesh['y'=4,'zq'=4,'zr'=4,'core'=2,'reader'=4] {'reader','y','core'}, dimensions={0} | all-to-all | bytes 65536 | tf_op jit(solution)/shard_map/targets/all_to_all | solution.py:470
  192.7 1.6 coef.1
  194.3 22.4 %all_to_all.52 = f32[16,8,128]{2,1,0:T(8,128)S(1)} all-to-all(f32[16,8,128]{2,1,0:T(8,128)} %coef.1), channel_id=1, replica_groups=mesh['y'=4,'zq'=4,'zr'=4,'core'=2,'reader'=4] {'zr','zq'}, dimensions={0} | all-to-all | bytes 131072 | tf_op jit(solution)/shard_map/targets/all_to_all | solution.py:478
  216.8 1.0 copy-done.3
  217.8 0.8 copy-done.6
  218.6 0.8 copy-done.7
  219.5 6.8 %gradient.1 = (f32[384,192]{1,0:T(8,128)S(1)}, f32[384,192]{1,0:T(8,128)S(1)}) custom-call(f32[128,128]{1,0:T(8,128)S(1)} %bitcast.43, s32[128,128]{1,0:T(8,128)S(1)} %copy-done.6, f32[128,128]{1,0:T(8,128)S(1)} %copy-done.7, f32[512,192]{1,0:T(8,128)S(1)} %copy-done.2, f32[512,192]{1,0:T(8,128)S(1)} %copy-done.3, bf16[768,512]{1,0:T(8,128)(2,1)S(1)} %copy-done.1), custom_call_target="tpu_custom_call" | custom-call | tf_op jit(solution)/shard_map/gradient/gradient/pallas_call | solution.py:482
  226.2 1.9 collective-permute-start.11
  228.2 1.7 collective-permute-done.11
  229.9 11.0 %all_to_all.53 = f32[4,96,192]{2,1,0:T(8,128)S(1)} all-to-all(f32[4,96,192]{2,1,0:T(8,128)S(1)} %bitcast.46), channel_id=1, replica_groups=mesh['y'=4,'zq'=4,'zr'=4,'core'=2,'reader'=4] {'y'}, dimensions={0} | all-to-all | bytes 589824 | tf_op jit(solution)/shard_map/reduce_gradient/all_to_all | solution.py:498
  241.7 3.5 %all-to-all-start.6 = ((f32[16,6,192]{2,1,0:T(8,128)}), f32[16,6,192]{2,1,0:T(8,128)S(1)}, u32[]{:S(2)}, u32[]{:S(2)}) async-start(f32[16,6,192]{2,1,0:T(8,128)} %reshape.202), calls=%async_computation.6 | async-start | bytes 262144 | tf_op jit(solution)/shard_map/reduce_gradient/all_to_all | solution.py:500
  245.8 0.8 dynamic-slice_reduce_fusion
  246.5 12.8 %all-to-all-done.6 = f32[16,6,192]{2,1,0:T(8,128)S(1)} async-done(((f32[16,6,192]{2,1,0:T(8,128)}), f32[16,6,192]{2,1,0:T(8,128)S(1)}, u32[]{:S(2)}, u32[]{:S(2)}) %all-to-all-start.6) | async-done | bytes 73760 | tf_op jit(solution)/shard_map/reduce_gradient/all_to_all | solution.py:500
  260.0 5.3 %all-to-all-start.7 = ((f32[4,6,192]{2,1,0:T(8,128)}), f32[4,6,192]{2,1,0:T(8,128)S(1)}, u32[]{:S(2)}, u32[]{:S(2)}) async-start(f32[4,6,192]{2,1,0:T(8,128)} %broadcast_in_dim.12), calls=%async_computation.7 | async-start | bytes 65536 | tf_op jit(solution)/shard_map/reduce_gradient/all_to_all | solution.py:37
  265.3 1.2 log_bitcast_fusion
  266.5 2.2 all-to-all-done.7
  (78 shorter events, 8.7 us)
Async XLA Ops:
  7.2 148.6 %all-gather.2.cloned.1.call-start = ((), (), s32[]{:S(2)}) async-start(), calls=%async_computation.8 | async-start | bytes 6553600 | tf_op jit(solution)/shard_map/gather_enc_out/all_gather | solution.py:384
  44.7 18.4 %collective-permute-start = (bf16[4,33,1024]{2,1,0:T(8,128)(2,1)S(1)}, bf16[4,33,1024]{2,1,0:T(8,128)(2,1)S(1)}, u32[]{:S(2)}, u32[]{:S(2)}) collective-permute-start(bf16[4,33,1024]{2,1,0:T(8,128)(2,1)S(1)} %all_to_all.50), channel_id=1, source_target_pairs={{8,0},{16,8},{24,16},{32,24},{40,32},{48,40},{56,48},{64,56},{72,6... | collective-permute-start | bytes 811016 | tf_op jit(solution)/shard_map/gather_key_proj/ppermute | solution.py:32
  51.3 20.0 %collective-permute-start.1 = (bf16[4,33,1024]{2,1,0:T(8,128)(2,1)S(1)}, bf16[4,33,1024]{2,1,0:T(8,128)(2,1)S(1)}, u32[]{:S(2)}, u32[]{:S(2)}) collective-permute-start(bf16[4,33,1024]{2,1,0:T(8,128)(2,1)S(1)} %all_to_all.50), channel_id=1, source_target_pairs={{16,0},{24,8},{32,16},{40,24},{48,32},{56,40},{64,48},{72,56},{80,... | collective-permute-start | bytes 811016 | tf_op jit(solution)/shard_map/gather_key_proj/ppermute | solution.py:32
  53.3 18.1 %collective-permute-start.2 = (bf16[4,33,1024]{2,1,0:T(8,128)(2,1)S(1)}, bf16[4,33,1024]{2,1,0:T(8,128)(2,1)S(1)}, u32[]{:S(2)}, u32[]{:S(2)}) collective-permute-start(bf16[4,33,1024]{2,1,0:T(8,128)(2,1)S(1)} %all_to_all.50), channel_id=1, source_target_pairs={{120,0},{0,8},{8,16},{16,24},{24,32},{32,40},{40,48},{48,56},{56,6... | collective-permute-start | bytes 811016 | tf_op jit(solution)/shard_map/gather_key_proj/ppermute | solution.py:32
  72.6 48.9 %collective-permute-start.3 = (bf16[16,32,1024]{2,1,0:T(8,128)(2,1)}, bf16[16,32,1024]{2,1,0:T(8,128)(2,1)}, u32[]{:S(2)}, u32[]{:S(2)}) collective-permute-start(bf16[16,32,1024]{2,1,0:T(8,128)(2,1)} %pad_maximum_fusion.refs_1_), channel_id=1, source_target_pairs={{128,0},{256,128},{384,256},{0,384},{129,1},{257,129},{385,257},{1... | collective-permute-start | bytes 3145736 | tf_op jit(solution)/shard_map/gather_key_proj/ppermute | solution.py:32
  77.5 44.0 %collective-permute-start.4 = (bf16[16,32,1024]{2,1,0:T(8,128)(2,1)}, bf16[16,32,1024]{2,1,0:T(8,128)(2,1)}, u32[]{:S(2)}, u32[]{:S(2)}) collective-permute-start(bf16[16,32,1024]{2,1,0:T(8,128)(2,1)} %pad_maximum_fusion.refs_1_), channel_id=1, source_target_pairs={{384,0},{0,128},{128,256},{256,384},{385,1},{1,129},{129,257},{257... | collective-permute-start | bytes 3145736 | tf_op jit(solution)/shard_map/gather_key_proj/ppermute | solution.py:32
  80.7 31.6 %all-to-all-start.1 = ((bf16[32,16,896]{2,1,0:T(8,128)(2,1)}), bf16[32,16,896]{2,1,0:T(8,128)(2,1)S(1)}, u32[]{:S(2)}, u32[]{:S(2)}) async-start(bf16[32,16,896]{2,1,0:T(8,128)(2,1)} %broadcast_in_dim.11), calls=%async_computation.1 | async-start | bytes 1835008 | tf_op jit(solution)/shard_map/gather_queries/all_to_all | solution.py:37
  112.3 0.9 copy-start.9
  121.5 8.9 %copy-start.10 = (bf16[4,16,1024]{2,1,0:T(8,128)(2,1)S(1)}, bf16[4,16,1024]{2,1,0:T(8,128)(2,1)}, u32[]{:S(2)}) copy-start(bf16[4,16,1024]{2,1,0:T(8,128)(2,1)} %param.17) | copy-start | bytes 393220
  123.4 15.5 %collective-permute-start.5 = (bf16[8,32,1024]{2,1,0:T(8,128)(2,1)}, bf16[8,32,1024]{2,1,0:T(8,128)(2,1)S(1)}, u32[]{:S(2)}, u32[]{:S(2)}) collective-permute-start(bf16[8,32,1024]{2,1,0:T(8,128)(2,1)} %slice.48), channel_id=1, source_target_pairs={{128,0},{256,128},{384,256},{0,384},{129,1},{257,129},{385,257},{1... | collective-permute-start | bytes 1572872 | tf_op jit(solution)/shard_map/gather_key_proj/ppermute | solution.py:32
  126.4 11.0 %copy-start.11 = (s32[4,20]{1,0:T(4,128)S(1)}, s32[4,20]{1,0:T(4,128)}, u32[]{:S(2)}) copy-start(s32[4,20]{1,0:T(4,128)} %param.13) | copy-start | bytes 964
  126.4 11.3 %copy-start.12 = (bf16[1024]{0:T(1024)(128)(2,1)S(1)}, bf16[1024]{0:T(1024)(128)(2,1)}, u32[]{:S(2)}) copy-start(bf16[1024]{0:T(1024)(128)(2,1)} %param.16) | copy-start | bytes 6148
  126.4 16.5 %collective-permute-start.6 = (bf16[8,32,1024]{2,1,0:T(8,128)(2,1)S(1)}, bf16[8,32,1024]{2,1,0:T(8,128)(2,1)S(1)}, u32[]{:S(2)}, u32[]{:S(2)}) collective-permute-start(bf16[8,32,1024]{2,1,0:T(8,128)(2,1)S(1)} %slice.49), channel_id=1, source_target_pairs={{384,0},{0,128},{128,256},{256,384},{385,1},{1,129},{129,257},{257... | collective-permute-start | bytes 1572872 | tf_op jit(solution)/shard_map/gather_key_proj/ppermute | solution.py:32
  130.8 24.9 %collective-permute-start.8 = (bf16[16,32,1024]{2,1,0:T(8,128)(2,1)}, bf16[16,32,1024]{2,1,0:T(8,128)(2,1)}, u32[]{:S(2)}, u32[]{:S(2)}) collective-permute-start(bf16[16,32,1024]{2,1,0:T(8,128)(2,1)} %pad_maximum_fusion.refs_1_), channel_id=1, source_target_pairs={{4,0},{0,4},{5,1},{1,5},{6,2},{2,6},{7,3},{3,7},{12,8},{8,12},{13,... | collective-permute-start | bytes 3145736 | tf_op jit(solution)/shard_map/gather_key_proj/ppermute | solution.py:32
  132.7 23.0 %collective-permute-start.10 = (bf16[16,32,1024]{2,1,0:T(8,128)(2,1)}, bf16[16,32,1024]{2,1,0:T(8,128)(2,1)}, u32[]{:S(2)}, u32[]{:S(2)}) collective-permute-start(bf16[16,32,1024]{2,1,0:T(8,128)(2,1)} %collective-permute-done.4.refs_5_), channel_id=1, source_target_pairs={{4,0},{0,4},{5,1},{1,5},{6,2},{2,6},{7,3},{3,7},{12,8},{8,12},{13,... | collective-permute-start | bytes 3145736 | tf_op jit(solution)/shard_map/gather_key_proj/ppermute | solution.py:32
  135.1 20.6 %collective-permute-start.9 = (bf16[16,32,1024]{2,1,0:T(8,128)(2,1)}, bf16[16,32,1024]{2,1,0:T(8,128)(2,1)}, u32[]{:S(2)}, u32[]{:S(2)}) collective-permute-start(bf16[16,32,1024]{2,1,0:T(8,128)(2,1)} %collective-permute-done.3.refs_3_), channel_id=1, source_target_pairs={{4,0},{0,4},{5,1},{1,5},{6,2},{2,6},{7,3},{3,7},{12,8},{8,12},{13,... | collective-permute-start | bytes 3145736 | tf_op jit(solution)/shard_map/gather_key_proj/ppermute | solution.py:32
  143.0 28.0 %collective-permute-start.7 = (bf16[16,32,1024]{2,1,0:T(8,128)(2,1)S(1)}, bf16[16,32,1024]{2,1,0:T(8,128)(2,1)S(1)}, u32[]{:S(2)}, u32[]{:S(2)}) collective-permute-start(bf16[16,32,1024]{2,1,0:T(8,128)(2,1)S(1)} %constant_dynamic-update-slice_fusion.refs_1_), channel_id=1, source_target_pairs={{4,0},{0,4},{5,1},{1,5},{6,2},{2,6},{7,3},{3,7},{12,8},{8,12},{13,... | collective-permute-start | bytes 3145736 | tf_op jit(solution)/shard_map/gather_key_proj/ppermute | solution.py:32
  145.0 25.3 %all-to-all-start.2 = ((f32[128,1,128]{2,1,0:T(1,128)}), f32[128,1,128]{2,1,0:T(1,128)S(1)}, u32[]{:S(2)}, u32[]{:S(2)}) async-start(f32[128,1,128]{2,1,0:T(1,128)} %bitcast.8), calls=%async_computation.2 | async-start | bytes 131072 | tf_op jit(solution)/shard_map/reduce_scores/all_to_all | solution.py:448
  155.7 15.3 %copy-start.8 = (s32[3]{0:T(128)S(1)}, s32[3]{0:T(128)}, u32[]{:S(2)}) copy-start(s32[3]{0:T(128)} %pad_add_fusion.place) | copy-start | bytes 40
  170.3 0.6 copy-start.4
  171.0 1.7 copy-start
  172.7 0.8 copy-start.5
  173.6 43.2 %copy-start.1 = (bf16[768,512]{1,0:T(8,128)(2,1)S(1)}, bf16[768,512]{1,0:T(8,128)(2,1)}, u32[]{:S(2)}) copy-start(bf16[768,512]{1,0:T(8,128)(2,1)} %get-tuple-element.26.refs_4_) | copy-start | bytes 2359300
  173.6 43.2 %copy-start.2 = (f32[512,192]{1,0:T(8,128)S(1)}, f32[512,192]{1,0:T(8,128)}, u32[]{:S(2)}) copy-start(f32[512,192]{1,0:T(8,128)} %get-tuple-element.24.refs_2_) | copy-start | bytes 1179652
  216.7 1.0 copy-start.3
  217.8 0.8 copy-start.6
  218.6 0.8 copy-start.7
  226.2 3.6 %collective-permute-start.11 = (f32[384,192]{1,0:T(8,128)S(1)}, f32[384,192]{1,0:T(8,128)S(1)}, u32[]{:S(2)}, u32[]{:S(2)}) collective-permute-start(f32[384,192]{1,0:T(8,128)S(1)} %get-tuple-element.28), channel_id=1, source_target_pairs={{4,0},{0,4},{5,1},{1,5},{6,2},{2,6},{7,3},{3,7},{12,8},{8,12},{13,... | collective-permute-start | bytes 884744 | tf_op jit(solution)/shard_map/reduce_gradient/ppermute | solution.py:32
  241.7 17.7 %all-to-all-start.6 = ((f32[16,6,192]{2,1,0:T(8,128)}), f32[16,6,192]{2,1,0:T(8,128)S(1)}, u32[]{:S(2)}, u32[]{:S(2)}) async-start(f32[16,6,192]{2,1,0:T(8,128)} %reshape.202), calls=%async_computation.6 | async-start | bytes 262144 | tf_op jit(solution)/shard_map/reduce_gradient/all_to_all | solution.py:500
  260.0 8.7 %all-to-all-start.7 = ((f32[4,6,192]{2,1,0:T(8,128)}), f32[4,6,192]{2,1,0:T(8,128)S(1)}, u32[]{:S(2)}, u32[]{:S(2)}) async-start(f32[4,6,192]{2,1,0:T(8,128)} %broadcast_in_dim.12), calls=%async_computation.7 | async-start | bytes 65536 | tf_op jit(solution)/shard_map/reduce_gradient/all_to_all | solution.py:37
Sparse Core Ops, SparseCore 0:
  10.1 67.4 all-gather.1

commit v12 on v9

--- a/solution.py
+++ b/solution.py
@@ -206,7 +206,7 @@
             pltpu.VMEM((3, *block), jnp.bfloat16),
             pltpu.SemaphoreType.DMA((3, 4)),
         ],
-        compiler_params=pltpu.CompilerParams(vmem_limit_bytes=GRANT),
+        compiler_params=pltpu.CompilerParams(vmem_limit_bytes=56 << 20),
         cost_estimate=cost(12, 13),
         name="early_keys",
     )(place, *tokens, *[part for ahead in EARLY for part in rows[ahead]])
@@ -401,9 +401,11 @@
         after, before = shift(own, Z, 1), shift(own, Z, -1)
         classes = (own, after, shift(own, Z, 2), before)
         own = jnp.concatenate([block[:, :-1] for block in classes])
-        own, token_after, token_before = lax.optimization_barrier((own, token_after, token_before))
         after, before = shift(own, "y", 1), shift(own, "y", -1)
+        far = jnp.concatenate([shift(after[:8], "y", 1), shift(before[8:], "y", -1)])
+        key_rows = [(block, shift(block, "core", 1)) for block in (own, after, far, before)]
     token_far = shift(token_after, "reader", 1)
+    tokens = (token_own, token_after, token_far, token_before)
 
     with jax.named_scope("gather_queries"):
         coded = jnp.concatenate([block[:, -1] for block in classes])
@@ -441,20 +443,12 @@
                 pltpu.VMEM((nx, n_index, LANES), jnp.int32),
                 pltpu.SemaphoreType.DMA((5,)),
             ],
-            compiler_params=pltpu.CompilerParams(vmem_limit_bytes=GRANT),
+            compiler_params=pltpu.CompilerParams(vmem_limit_bytes=56 << 20),
             cost_estimate=pl.CostEstimate(
                 flops=64 << 30, bytes_accessed=8 << 20, transcendentals=0
             ),
             name="scores",
         )(jnp.stack([my_shard, r]).astype(jnp.int32), *operands)
-
-    with jax.named_scope("gather_key_proj"):
-        after, before, state, token_far = lax.optimization_barrier(
-            (after, before, state, token_far)
-        )
-        far = jnp.concatenate([shift(after[:8], "y", 1), shift(before[8:], "y", -1)])
-        key_rows = [(block, shift(block, "core", 1)) for block in (own, after, far, before)]
-    tokens = (token_own, token_after, token_far, token_before)
 
     with jax.named_scope("reduce_scores"):
         states = lax.all_to_all(state, ("y", "core", *Z_BY_CLASS), 0, 0, tiled=True)

time: 278 us -> 262 us (0.942)
  waiting for transfers between devices: 59.5 us -> 43.8 us
  local copies, waits for them, and re-layouts: 19.7 us -> 14.7 us
    ppermute x15, waiting for transfers between devices: 44.5 us -> 28.9 us  [shift(): return lax.ppermute(x, axis, [((i + step) % size, i) for i in range(size)])]
    unnamed x50 -> x26, local copies, waits for them, and re-layouts: 11.9 us -> 6.5 us
  transfers between devices with their start and end apart: 19 -> 19, of which waited for: 11 -> 7; matrix products, arithmetic and copies ran while one was open for 4% -> 5% of each run, Pallas kernels for 7% -> 7%
where the time goes in v12:
time: 262 us; the launch traced here: 259 us
  blocking collectives  79.8 us (30%)
  starting transfers between devices  75.4 us (29%)
  waiting for transfers between devices  43.8 us (17%)
  Pallas kernels  35.4 us (14%)
  local copies, waits for them, and re-layouts  14.7 us (6%)
  other arithmetic  8.33 us (3%)
    ppermute x15, starting transfers between devices, shift(): return lax.ppermute(x, axis, [((i + step) % size, i) for i in range(size)])  46.8 us
    all_to_all x1, blocking collectives, send_all(): lax.all_to_all(jnp.broadcast_to(x[None], (size, *x.shape)), axis, 0, 0, t...  34.5 us
    ppermute x15, waiting for transfers between devices, shift(): return lax.ppermute(x, axis, [((i + step) % size, i) for i in range(size)])  28.9 us
    all_to_all x1, blocking collectives, body(): lax.all_to_all(coef, Z_BY_CLASS, 0, 0, tiled=True).reshape(n_index, LANES)  21.6 us
    all_to_all x2, starting transfers between devices, send_all(): lax.all_to_all(jnp.broadcast_to(x[None], (size, *x.shape)), axis, 0, 0, t...  13 us
    all_to_all x1, waiting for transfers between devices, body(): term = jnp.sum(lax.all_to_all(term, Z, 0, 0, tiled=True), axis=0)  12.8 us
    all_to_all x1, blocking collectives, body(): lax.all_to_all(packet, NEAR, 0, 0, tiled=True)  12.7 us
    all_to_all x1, starting transfers between devices, body(): states = lax.all_to_all(state, ('y', 'core', *Z_BY_CLASS), 0, 0, tiled=True)  12 us
  transfers between devices with their start and end apart: 19, of which 7 were waited for; matrix products, arithmetic and copies ran while one was open for 5% of the time, Pallas kernels for 7%

profile of v12, /device:TPU:6, one launch (start us, length us, event | category | flops | bytes accessed | tf_op | source)
XLA Modules:
  0.0 258.8 jit_solution(15311822155860289683)
XLA Ops:
  2.1 0.8 fusion.3
  2.9 34.5 %all_to_all.50 = bf16[4,33,1024]{2,1,0:T(8,128)(2,1)S(1)} all-to-all(bf16[4,33,1024]{2,1,0:T(8,128)(2,1)S(1)} %broadcast_in_dim.10), channel_id=1, replica_groups=mesh['y'=4,'zq'=4,'zr'=4,'core'=2,'reader'=4] {'zq'}, dimensions={0} | all-to-all | bytes 540672 | tf_op jit(solution)/shard_map/gather_key_proj/all_to_all | solution.py:37
  37.4 6.7 %collective-permute-start.3 = (bf16[4,33,1024]{2,1,0:T(8,128)(2,1)S(1)}, bf16[4,33,1024]{2,1,0:T(8,128)(2,1)S(1)}, u32[]{:S(2)}, u32[]{:S(2)}) collective-permute-start(bf16[4,33,1024]{2,1,0:T(8,128)(2,1)S(1)} %all_to_all.50), channel_id=1, source_target_pairs={{8,0},{16,8},{24,16},{32,24},{40,32},{48,40},{56,48},{64,56},{72,6... | collective-permute-start | bytes 811016 | tf_op jit(solution)/shard_map/gather_key_proj/ppermute | solution.py:32
  44.1 1.9 collective-permute-start.4
  46.0 3.9 %collective-permute-start.5 = (bf16[4,33,1024]{2,1,0:T(8,128)(2,1)S(1)}, bf16[4,33,1024]{2,1,0:T(8,128)(2,1)S(1)}, u32[]{:S(2)}, u32[]{:S(2)}) collective-permute-start(bf16[4,33,1024]{2,1,0:T(8,128)(2,1)S(1)} %all_to_all.50), channel_id=1, source_target_pairs={{120,0},{0,8},{8,16},{16,24},{24,32},{32,40},{40,48},{48,56},{56,6... | collective-permute-start | bytes 811016 | tf_op jit(solution)/shard_map/gather_key_proj/ppermute | solution.py:32
  49.9 2.7 %collective-permute-start = (bf16[640,1024]{1,0:T(8,128)(2,1)}, bf16[640,1024]{1,0:T(8,128)(2,1)}, u32[]{:S(2)}, u32[]{:S(2)}) collective-permute-start(bf16[640,1024]{1,0:T(8,128)(2,1)} %bitcast.42), channel_id=1, source_target_pairs={{1,0},{2,1},{3,2},{0,3},{5,4},{6,5},{7,6},{4,7},{9,8},{10,9},{11,1... | collective-permute-start | bytes 3932168 | tf_op jit(solution)/shard_map/gather_enc_out/ppermute | solution.py:32
  52.6 4.3 %collective-permute-start.2 = (bf16[640,1024]{1,0:T(8,128)(2,1)}, bf16[640,1024]{1,0:T(8,128)(2,1)}, u32[]{:S(2)}, u32[]{:S(2)}) collective-permute-start(bf16[640,1024]{1,0:T(8,128)(2,1)} %bitcast.43), channel_id=1, source_target_pairs={{3,0},{0,1},{1,2},{2,3},{7,4},{4,5},{5,6},{6,7},{11,8},{8,9},{9,10... | collective-permute-start | bytes 3932168 | tf_op jit(solution)/shard_map/gather_enc_out/ppermute | solution.py:32
  58.0 6.1 %collective-permute-done.4 = bf16[4,33,1024]{2,1,0:T(8,128)(2,1)S(1)} collective-permute-done((bf16[4,33,1024]{2,1,0:T(8,128)(2,1)S(1)}, bf16[4,33,1024]{2,1,0:T(8,128)(2,1)S(1)}, u32[]{:S(2)}, u32[]{:S(2)}) %collective-permute-start.4) | collective-permute-done | bytes 270368 | tf_op jit(solution)/shard_map/gather_key_proj/ppermute | solution.py:32
  64.1 1.1 pad_maximum_fusion.refs_4_
  65.2 4.9 %collective-permute-start.6 = (bf16[16,32,1024]{2,1,0:T(8,128)(2,1)}, bf16[16,32,1024]{2,1,0:T(8,128)(2,1)}, u32[]{:S(2)}, u32[]{:S(2)}) collective-permute-start(bf16[16,32,1024]{2,1,0:T(8,128)(2,1)} %pad_maximum_fusion.refs_4_), channel_id=1, source_target_pairs={{128,0},{256,128},{384,256},{0,384},{129,1},{257,129},{385,257},{1... | collective-permute-start | bytes 3145736 | tf_op jit(solution)/shard_map/gather_key_proj/ppermute | solution.py:32
  70.2 1.9 collective-permute-start.8
  72.9 1.0 broadcast_in_dim.11
  73.9 7.6 %all-to-all-start.1 = ((bf16[32,16,896]{2,1,0:T(8,128)(2,1)}), bf16[32,16,896]{2,1,0:T(8,128)(2,1)S(1)}, u32[]{:S(2)}, u32[]{:S(2)}) async-start(bf16[32,16,896]{2,1,0:T(8,128)(2,1)} %broadcast_in_dim.11), calls=%async_computation.1 | async-start | bytes 1835008 | tf_op jit(solution)/shard_map/gather_queries/all_to_all | solution.py:37
  82.2 17.0 %collective-permute-done.6.refs_6_ = bf16[16,32,1024]{2,1,0:T(8,128)(2,1)} collective-permute-done((bf16[16,32,1024]{2,1,0:T(8,128)(2,1)}, bf16[16,32,1024]{2,1,0:T(8,128)(2,1)}, u32[]{:S(2)}, u32[]{:S(2)}) %collective-permute-start.6) | collective-permute-done | bytes 1048608 | tf_op jit(solution)/shard_map/gather_key_proj/ppermute | solution.py:32
  99.2 1.1 slice.56
  100.3 5.6 %collective-permute-start.7 = (bf16[8,32,1024]{2,1,0:T(8,128)(2,1)S(1)}, bf16[8,32,1024]{2,1,0:T(8,128)(2,1)S(1)}, u32[]{:S(2)}, u32[]{:S(2)}) collective-permute-start(bf16[8,32,1024]{2,1,0:T(8,128)(2,1)S(1)} %slice.56), channel_id=1, source_target_pairs={{128,0},{256,128},{384,256},{0,384},{129,1},{257,129},{385,257},{1... | collective-permute-start | bytes 1572872 | tf_op jit(solution)/shard_map/gather_key_proj/ppermute | solution.py:32
  105.9 1.9 slice.57
  107.7 1.9 collective-permute-start.9
  110.6 1.3 fusion.refs_3_
  111.9 1.9 collective-permute-start.11
  113.8 3.1 %collective-permute-start.1 = (bf16[640,1024]{1,0:T(8,128)(2,1)}, bf16[640,1024]{1,0:T(8,128)(2,1)}, u32[]{:S(2)}, u32[]{:S(2)}) collective-permute-start(bf16[640,1024]{1,0:T(8,128)(2,1)} %collective-permute-done.refs_1_), channel_id=1, source_target_pairs={{1,0},{2,1},{3,2},{0,3},{5,4},{6,5},{7,6},{4,7},{9,8},{10,9},{11,1... | collective-permute-start | bytes 3932168 | tf_op jit(solution)/shard_map/ppermute | solution.py:32
  117.0 2.1 collective-permute-start.12
  119.1 1.1 collective-permute-done.9
  120.2 1.9 collective-permute-start.13
  122.1 0.9 copy-done.7
  123.1 8.2 %scores.1 = (f32[128,128]{1,0:T(8,128)}, s32[128,128]{1,0:T(8,128)}, f32[512,192]{1,0:T(8,128)}, f32[512,192]{1,0:T(8,128)}, f32[128,128]{1,0:T(8,128)}, /*index=5*/bf16[768,512]{1,0:T(8,128)(2,1)}) custom-call(s32[2]{0:T(128)} %pad_add_fusion.1.place, bf16[32,16,896]{2,1,0:T(8,128)(2,1)} %copy-done.7, bf16[768,768]{1,0:T(8,128)(2,1)} %refs_1_.1, ...), custom_call_target="tpu_custom_call" | custom-call | flops 68719476736 | bytes 8388608 | tf_op jit(solution)/shard_map/scores/scores/pallas_call | solution.py:435
  131.3 12.0 %all-to-all-start.2 = ((f32[128,1,128]{2,1,0:T(1,128)}), f32[128,1,128]{2,1,0:T(1,128)}, u32[]{:S(2)}, u32[]{:S(2)}) async-start(f32[128,1,128]{2,1,0:T(1,128)} %bitcast.53), calls=%async_computation.2 | async-start | bytes 131072 | tf_op jit(solution)/shard_map/reduce_scores/all_to_all | solution.py:454
  143.4 2.1 collective-permute-start.10
  145.5 2.9 %collective-permute-done.1.refs_2_ = bf16[640,1024]{1,0:T(8,128)(2,1)} collective-permute-done((bf16[640,1024]{1,0:T(8,128)(2,1)}, bf16[640,1024]{1,0:T(8,128)(2,1)}, u32[]{:S(2)}, u32[]{:S(2)}) %collective-permute-start.1) | collective-permute-done | bytes 1310752 | tf_op jit(solution)/shard_map/ppermute | solution.py:32
  148.5 10.4 %early_keys.1.refs_6_ = f32[640,1024]{1,0:T(8,128)} custom-call(s32[4]{0:T(128)} %pad_add_fusion.place, bf16[640,1024]{1,0:T(8,128)(2,1)} %bitcast.44, bf16[640,1024]{1,0:T(8,128)(2,1)} %collective-permute-done.refs_1_, bf16[640,1024]{1,0:T(8,128)(2,1)} %collective-permute-done.1.refs_2_, bf16[640,1024]{1,0:T(8,128)(2,1)} %collective-permute-done.2.refs_3_, ...), custom_call_target="tpu_custom_call" | custom-call | flops 16106127360 | bytes 13631488 | tf_op jit(solution)/shard_map/attention/early_keys/pallas_call | solution.py:198
  158.9 8.4 %late_heads.1 = (f32[32,256]{1,0:T(8,128)S(1)}, f32[8,128]{1,0:T(8,128)S(1)}) custom-call(s32[4]{0:T(128)S(1)} %copy-done.6, bf16[640,1024]{1,0:T(8,128)(2,1)S(1)} %bitcast.45, bf16[640,1024]{1,0:T(8,128)(2,1)} %collective-permute-done.refs_1_, bf16[640,1024]{1,0:T(8,128)(2,1)} %collective-permute-done.1.refs_2_, ...), custom_call_target="tpu_custom_call" | custom-call | flops 1342177280 | bytes 6291456 | tf_op jit(solution)/shard_map/attention/late_heads/pallas_call | solution.py:213
  167.4 12.7 %all_to_all.51 = f32[32,1,256]{2,1,0:T(1,128)S(1)} all-to-all(f32[32,1,256]{2,1,0:T(1,128)S(1)} %copy.26), channel_id=1, replica_groups=mesh['y'=4,'zq'=4,'zr'=4,'core'=2,'reader'=4] {'reader','y','core'}, dimensions={0} | all-to-all | bytes 65536 | tf_op jit(solution)/shard_map/targets/all_to_all | solution.py:476
  180.7 1.6 coef.1
  182.3 21.6 %all_to_all.52 = f32[16,8,128]{2,1,0:T(8,128)S(1)} all-to-all(f32[16,8,128]{2,1,0:T(8,128)} %coef.1), channel_id=1, replica_groups=mesh['y'=4,'zq'=4,'zr'=4,'core'=2,'reader'=4] {'zr','zq'}, dimensions={0} | all-to-all | bytes 131072 | tf_op jit(solution)/shard_map/targets/all_to_all | solution.py:484
  203.9 1.1 copy-done.1
  205.1 1.0 copy-done.2
  206.1 1.0 copy-done.3
  207.2 0.8 copy-done.4
  208.0 0.8 copy-done.5
  208.8 6.8 %gradient.1 = (f32[384,192]{1,0:T(8,128)S(1)}, f32[384,192]{1,0:T(8,128)S(1)}) custom-call(f32[128,128]{1,0:T(8,128)S(1)} %bitcast.46, s32[128,128]{1,0:T(8,128)S(1)} %copy-done.4, f32[128,128]{1,0:T(8,128)S(1)} %copy-done.5, f32[512,192]{1,0:T(8,128)S(1)} %copy-done.2, f32[512,192]{1,0:T(8,128)S(1)} %copy-done.3, bf16[768,512]{1,0:T(8,128)(2,1)S(1)} %copy-done.1), custom_call_target="tpu_custom_call" | custom-call | tf_op jit(solution)/shard_map/gradient/gradient/pallas_call | solution.py:488
  215.6 1.9 collective-permute-start.14
  217.5 1.7 collective-permute-done.14
  219.3 11.0 %all_to_all.53 = f32[4,96,192]{2,1,0:T(8,128)S(1)} all-to-all(f32[4,96,192]{2,1,0:T(8,128)S(1)} %bitcast.49), channel_id=1, replica_groups=mesh['y'=4,'zq'=4,'zr'=4,'core'=2,'reader'=4] {'y'}, dimensions={0} | all-to-all | bytes 589824 | tf_op jit(solution)/shard_map/reduce_gradient/all_to_all | solution.py:504
  231.0 3.5 %all-to-all-start.6 = ((f32[16,6,192]{2,1,0:T(8,128)}), f32[16,6,192]{2,1,0:T(8,128)S(1)}, u32[]{:S(2)}, u32[]{:S(2)}) async-start(f32[16,6,192]{2,1,0:T(8,128)} %reshape.202), calls=%async_computation.6 | async-start | bytes 262144 | tf_op jit(solution)/shard_map/reduce_gradient/all_to_all | solution.py:506
  235.9 12.8 %all-to-all-done.6 = f32[16,6,192]{2,1,0:T(8,128)S(1)} async-done(((f32[16,6,192]{2,1,0:T(8,128)}), f32[16,6,192]{2,1,0:T(8,128)S(1)}, u32[]{:S(2)}, u32[]{:S(2)}) %all-to-all-start.6) | async-done | bytes 73760 | tf_op jit(solution)/shard_map/reduce_gradient/all_to_all | solution.py:506
  249.3 5.3 %all-to-all-start.7 = ((f32[4,6,192]{2,1,0:T(8,128)}), f32[4,6,192]{2,1,0:T(8,128)S(1)}, u32[]{:S(2)}, u32[]{:S(2)}) async-start(f32[4,6,192]{2,1,0:T(8,128)} %broadcast_in_dim.12), calls=%async_computation.7 | async-start | bytes 65536 | tf_op jit(solution)/shard_map/reduce_gradient/all_to_all | solution.py:37
  254.7 1.2 log_bitcast_fusion
  255.9 2.2 all-to-all-done.7
  (75 shorter events, 8.9 us)
Async XLA Ops:
  37.4 20.5 %collective-permute-start.3 = (bf16[4,33,1024]{2,1,0:T(8,128)(2,1)S(1)}, bf16[4,33,1024]{2,1,0:T(8,128)(2,1)S(1)}, u32[]{:S(2)}, u32[]{:S(2)}) collective-permute-start(bf16[4,33,1024]{2,1,0:T(8,128)(2,1)S(1)} %all_to_all.50), channel_id=1, source_target_pairs={{8,0},{16,8},{24,16},{32,24},{40,32},{48,40},{56,48},{64,56},{72,6... | collective-permute-start | bytes 811016 | tf_op jit(solution)/shard_map/gather_key_proj/ppermute | solution.py:32
  44.1 20.0 %collective-permute-start.4 = (bf16[4,33,1024]{2,1,0:T(8,128)(2,1)S(1)}, bf16[4,33,1024]{2,1,0:T(8,128)(2,1)S(1)}, u32[]{:S(2)}, u32[]{:S(2)}) collective-permute-start(bf16[4,33,1024]{2,1,0:T(8,128)(2,1)S(1)} %all_to_all.50), channel_id=1, source_target_pairs={{16,0},{24,8},{32,16},{40,24},{48,32},{56,40},{64,48},{72,56},{80,... | collective-permute-start | bytes 811016 | tf_op jit(solution)/shard_map/gather_key_proj/ppermute | solution.py:32
  46.0 18.1 %collective-permute-start.5 = (bf16[4,33,1024]{2,1,0:T(8,128)(2,1)S(1)}, bf16[4,33,1024]{2,1,0:T(8,128)(2,1)S(1)}, u32[]{:S(2)}, u32[]{:S(2)}) collective-permute-start(bf16[4,33,1024]{2,1,0:T(8,128)(2,1)S(1)} %all_to_all.50), channel_id=1, source_target_pairs={{120,0},{0,8},{8,16},{16,24},{24,32},{32,40},{40,48},{48,56},{56,6... | collective-permute-start | bytes 811016 | tf_op jit(solution)/shard_map/gather_key_proj/ppermute | solution.py:32
  49.9 64.0 %collective-permute-start = (bf16[640,1024]{1,0:T(8,128)(2,1)}, bf16[640,1024]{1,0:T(8,128)(2,1)}, u32[]{:S(2)}, u32[]{:S(2)}) collective-permute-start(bf16[640,1024]{1,0:T(8,128)(2,1)} %bitcast.42), channel_id=1, source_target_pairs={{1,0},{2,1},{3,2},{0,3},{5,4},{6,5},{7,6},{4,7},{9,8},{10,9},{11,1... | collective-permute-start | bytes 3932168 | tf_op jit(solution)/shard_map/gather_enc_out/ppermute | solution.py:32
  52.6 90.8 %collective-permute-start.2 = (bf16[640,1024]{1,0:T(8,128)(2,1)}, bf16[640,1024]{1,0:T(8,128)(2,1)}, u32[]{:S(2)}, u32[]{:S(2)}) collective-permute-start(bf16[640,1024]{1,0:T(8,128)(2,1)} %bitcast.43), channel_id=1, source_target_pairs={{3,0},{0,1},{1,2},{2,3},{7,4},{4,5},{5,6},{6,7},{11,8},{8,9},{9,10... | collective-permute-start | bytes 3932168 | tf_op jit(solution)/shard_map/gather_enc_out/ppermute | solution.py:32
  64.1 8.0 %copy-start.8 = (bf16[4,16,1024]{2,1,0:T(8,128)(2,1)S(1)}, bf16[4,16,1024]{2,1,0:T(8,128)(2,1)}, u32[]{:S(2)}) copy-start(bf16[4,16,1024]{2,1,0:T(8,128)(2,1)} %param.17) | copy-start | bytes 393220
  65.2 33.9 %collective-permute-start.6 = (bf16[16,32,1024]{2,1,0:T(8,128)(2,1)}, bf16[16,32,1024]{2,1,0:T(8,128)(2,1)}, u32[]{:S(2)}, u32[]{:S(2)}) collective-permute-start(bf16[16,32,1024]{2,1,0:T(8,128)(2,1)} %pad_maximum_fusion.refs_4_), channel_id=1, source_target_pairs={{128,0},{256,128},{384,256},{0,384},{129,1},{257,129},{385,257},{1... | collective-permute-start | bytes 3145736 | tf_op jit(solution)/shard_map/gather_key_proj/ppermute | solution.py:32
  70.2 35.7 %collective-permute-start.8 = (bf16[16,32,1024]{2,1,0:T(8,128)(2,1)}, bf16[16,32,1024]{2,1,0:T(8,128)(2,1)}, u32[]{:S(2)}, u32[]{:S(2)}) collective-permute-start(bf16[16,32,1024]{2,1,0:T(8,128)(2,1)} %pad_maximum_fusion.refs_4_), channel_id=1, source_target_pairs={{384,0},{0,128},{128,256},{256,384},{385,1},{1,129},{129,257},{257... | collective-permute-start | bytes 3145736 | tf_op jit(solution)/shard_map/gather_key_proj/ppermute | solution.py:32
  73.9 48.3 %all-to-all-start.1 = ((bf16[32,16,896]{2,1,0:T(8,128)(2,1)}), bf16[32,16,896]{2,1,0:T(8,128)(2,1)S(1)}, u32[]{:S(2)}, u32[]{:S(2)}) async-start(bf16[32,16,896]{2,1,0:T(8,128)(2,1)} %broadcast_in_dim.11), calls=%async_computation.1 | async-start | bytes 1835008 | tf_op jit(solution)/shard_map/gather_queries/all_to_all | solution.py:37
  100.3 10.3 %copy-start.9 = (bf16[1024]{0:T(1024)(128)(2,1)S(1)}, bf16[1024]{0:T(1024)(128)(2,1)}, u32[]{:S(2)}) copy-start(bf16[1024]{0:T(1024)(128)(2,1)} %param.16) | copy-start | bytes 6148
  100.3 16.7 %collective-permute-start.7 = (bf16[8,32,1024]{2,1,0:T(8,128)(2,1)S(1)}, bf16[8,32,1024]{2,1,0:T(8,128)(2,1)S(1)}, u32[]{:S(2)}, u32[]{:S(2)}) collective-permute-start(bf16[8,32,1024]{2,1,0:T(8,128)(2,1)S(1)} %slice.56), channel_id=1, source_target_pairs={{128,0},{256,128},{384,256},{0,384},{129,1},{257,129},{385,257},{1... | collective-permute-start | bytes 1572872 | tf_op jit(solution)/shard_map/gather_key_proj/ppermute | solution.py:32
  107.7 12.5 %collective-permute-start.9 = (bf16[8,32,1024]{2,1,0:T(8,128)(2,1)}, bf16[8,32,1024]{2,1,0:T(8,128)(2,1)S(1)}, u32[]{:S(2)}, u32[]{:S(2)}) collective-permute-start(bf16[8,32,1024]{2,1,0:T(8,128)(2,1)} %slice.57), channel_id=1, source_target_pairs={{384,0},{0,128},{128,256},{256,384},{385,1},{1,129},{129,257},{257... | collective-permute-start | bytes 1572872 | tf_op jit(solution)/shard_map/gather_key_proj/ppermute | solution.py:32
  111.9 33.6 %collective-permute-start.11 = (bf16[16,32,1024]{2,1,0:T(8,128)(2,1)}, bf16[16,32,1024]{2,1,0:T(8,128)(2,1)}, u32[]{:S(2)}, u32[]{:S(2)}) collective-permute-start(bf16[16,32,1024]{2,1,0:T(8,128)(2,1)} %pad_maximum_fusion.refs_4_), channel_id=1, source_target_pairs={{4,0},{0,4},{5,1},{1,5},{6,2},{2,6},{7,3},{3,7},{12,8},{8,12},{13,... | collective-permute-start | bytes 3145736 | tf_op jit(solution)/shard_map/gather_key_proj/ppermute | solution.py:32
  113.8 34.6 %collective-permute-start.1 = (bf16[640,1024]{1,0:T(8,128)(2,1)}, bf16[640,1024]{1,0:T(8,128)(2,1)}, u32[]{:S(2)}, u32[]{:S(2)}) collective-permute-start(bf16[640,1024]{1,0:T(8,128)(2,1)} %collective-permute-done.refs_1_), channel_id=1, source_target_pairs={{1,0},{2,1},{3,2},{0,3},{5,4},{6,5},{7,6},{4,7},{9,8},{10,9},{11,1... | collective-permute-start | bytes 3932168 | tf_op jit(solution)/shard_map/ppermute | solution.py:32
  117.0 31.5 %collective-permute-start.12 = (bf16[16,32,1024]{2,1,0:T(8,128)(2,1)}, bf16[16,32,1024]{2,1,0:T(8,128)(2,1)}, u32[]{:S(2)}, u32[]{:S(2)}) collective-permute-start(bf16[16,32,1024]{2,1,0:T(8,128)(2,1)} %collective-permute-done.6.refs_6_), channel_id=1, source_target_pairs={{4,0},{0,4},{5,1},{1,5},{6,2},{2,6},{7,3},{3,7},{12,8},{8,12},{13,... | collective-permute-start | bytes 3145736 | tf_op jit(solution)/shard_map/gather_key_proj/ppermute | solution.py:32
  120.2 28.3 %collective-permute-start.13 = (bf16[16,32,1024]{2,1,0:T(8,128)(2,1)}, bf16[16,32,1024]{2,1,0:T(8,128)(2,1)}, u32[]{:S(2)}, u32[]{:S(2)}) collective-permute-start(bf16[16,32,1024]{2,1,0:T(8,128)(2,1)} %collective-permute-done.8.refs_8_), channel_id=1, source_target_pairs={{4,0},{0,4},{5,1},{1,5},{6,2},{2,6},{7,3},{3,7},{12,8},{8,12},{13,... | collective-permute-start | bytes 3145736 | tf_op jit(solution)/shard_map/gather_key_proj/ppermute | solution.py:32
  122.1 0.9 copy-start.7
  131.3 27.6 %all-to-all-start.2 = ((f32[128,1,128]{2,1,0:T(1,128)}), f32[128,1,128]{2,1,0:T(1,128)}, u32[]{:S(2)}, u32[]{:S(2)}) async-start(f32[128,1,128]{2,1,0:T(1,128)} %bitcast.53), calls=%async_computation.2 | async-start | bytes 131072 | tf_op jit(solution)/shard_map/reduce_scores/all_to_all | solution.py:454
  143.4 15.5 %copy-start = (bf16[4,20,8,1024]{3,2,1,0:T(8,128)(2,1)S(1)}, bf16[4,20,8,1024]{3,2,1,0:T(8,128)(2,1)}, u32[]{:S(2)}) copy-start(bf16[4,20,8,1024]{3,2,1,0:T(8,128)(2,1)} %param.14) | copy-start | bytes 3932164
  143.4 15.5 %copy-start.6 = (s32[4]{0:T(128)S(1)}, s32[4]{0:T(128)}, u32[]{:S(2)}) copy-start(s32[4]{0:T(128)} %pad_add_fusion.place) | copy-start | bytes 52
  143.4 15.4 %collective-permute-start.10 = (bf16[16,32,1024]{2,1,0:T(8,128)(2,1)S(1)}, bf16[16,32,1024]{2,1,0:T(8,128)(2,1)S(1)}, u32[]{:S(2)}, u32[]{:S(2)}) collective-permute-start(bf16[16,32,1024]{2,1,0:T(8,128)(2,1)S(1)} %constant_dynamic-update-slice_fusion.refs_4_), channel_id=1, source_target_pairs={{4,0},{0,4},{5,1},{1,5},{6,2},{2,6},{7,3},{3,7},{12,8},{8,12},{13,... | collective-permute-start | bytes 3145736 | tf_op jit(solution)/shard_map/gather_key_proj/ppermute | solution.py:32
  203.9 1.1 copy-start.1
  205.1 1.0 copy-start.2
  206.1 1.0 copy-start.3
  207.2 0.8 copy-start.4
  208.0 0.8 copy-start.5
  215.6 3.6 %collective-permute-start.14 = (f32[384,192]{1,0:T(8,128)S(1)}, f32[384,192]{1,0:T(8,128)S(1)}, u32[]{:S(2)}, u32[]{:S(2)}) collective-permute-start(f32[384,192]{1,0:T(8,128)S(1)} %get-tuple-element.22), channel_id=1, source_target_pairs={{4,0},{0,4},{5,1},{1,5},{6,2},{2,6},{7,3},{3,7},{12,8},{8,12},{13,... | collective-permute-start | bytes 884744 | tf_op jit(solution)/shard_map/reduce_gradient/ppermute | solution.py:32
  231.0 17.7 %all-to-all-start.6 = ((f32[16,6,192]{2,1,0:T(8,128)}), f32[16,6,192]{2,1,0:T(8,128)S(1)}, u32[]{:S(2)}, u32[]{:S(2)}) async-start(f32[16,6,192]{2,1,0:T(8,128)} %reshape.202), calls=%async_computation.6 | async-start | bytes 262144 | tf_op jit(solution)/shard_map/reduce_gradient/all_to_all | solution.py:506
  249.3 8.7 %all-to-all-start.7 = ((f32[4,6,192]{2,1,0:T(8,128)}), f32[4,6,192]{2,1,0:T(8,128)S(1)}, u32[]{:S(2)}, u32[]{:S(2)}) async-start(f32[4,6,192]{2,1,0:T(8,128)} %broadcast_in_dim.12), calls=%async_computation.7 | async-start | bytes 65536 | tf_op jit(solution)/shard_map/reduce_gradient/all_to_all | solution.py:37

commit v13 on v12

--- a/solution.py
+++ b/solution.py
@@ -87,24 +87,12 @@
         copies += token_copies(r, (y + ahead) % 4, tokens, token_v.at[slot], sems.at[1, slot])
     for copy in copies:
         copy.wait()
-    tiles = keys.shape[0]
-
-    def leave(t):
-        cols = pl.ds(pl.multiple_of(t * TILE, TILE), TILE)
-        return pltpu.make_async_copy(keys.at[t], keys_out.at[:, cols], sems.at[2, t])
-
-    @pl.loop(0, tiles)
-    def _(t):
-        cols = pl.ds(pl.multiple_of(t * TILE, TILE), TILE)
-        total = dot32(token_v[0], weight_v[0, :, :, :, :, cols].reshape(-1, TILE))
-        for slot in range(1, len(EARLY)):
-            total += dot32(token_v[slot], weight_v[slot, :, :, :, :, cols].reshape(-1, TILE))
-        keys[t] = total
-        leave(t).start()
-
-    @pl.loop(0, tiles)
-    def _(t):
-        leave(t).wait()
+    keys[...] = dot32(token_v[0], weight_v[0].reshape(-1, keys.shape[1]))
+    for slot in range(1, len(EARLY)):
+        keys[...] += dot32(token_v[slot], weight_v[slot].reshape(-1, keys.shape[1]))
+    copy = pltpu.make_async_copy(keys, keys_out, sems.at[2, 0])
+    copy.start()
+    copy.wait()
 
 
 def attend(keys, offset, dec, gain, live, column_v):
@@ -163,11 +151,12 @@
     for copy in copies:
         copy.wait()
 
+    early[...] += dot32(token_v[...], weight_v[...].reshape(-1, early.shape[1]))
+
     @pl.loop(0, early.shape[1] // TILE)
     def _(t):
         cols = pl.ds(pl.multiple_of(t * TILE, TILE), TILE)
-        keys = early[:, cols] + dot32(token_v[...], weight_v[:, :, :, :, cols].reshape(-1, TILE))
-        attend(keys, t * TILE, dec, gain, live, column_v)
+        attend(early[:, cols], t * TILE, dec, gain, live, column_v)
 
     n = live.shape[1]
     mass = jnp.zeros((8, LANES), jnp.float32)
@@ -201,7 +190,7 @@
         in_specs=[smem] + [anywhere] * 10,
         out_specs=anywhere,
         scratch_shapes=[
-            pltpu.VMEM((width // TILE, token_rows, TILE), jnp.float32),
+            pltpu.VMEM((token_rows, width), jnp.float32),
             pltpu.VMEM((3, token_rows, width), jnp.bfloat16),
             pltpu.VMEM((3, *block), jnp.bfloat16),
             pltpu.SemaphoreType.DMA((3, 4)),
@@ -432,11 +421,12 @@
             jax.ShapeDtypeStruct((width, queries), jnp.bfloat16),
         )
         anywhere = pl.BlockSpec(memory_space=pl.ANY)
+        in_hbm = pl.BlockSpec(memory_space=pltpu.HBM)
         state, slots, my_rows, my_unit, query_scale, ordered = pl.pallas_call(
             scores_kernel,
             out_shape=(jax.ShapeDtypeStruct((n_index, LANES), jnp.float32), *results),
             in_specs=[pl.BlockSpec(memory_space=pltpu.SMEM)] + [anywhere] * 4,
-            out_specs=(vmem,) + (anywhere,) * 5,
+            out_specs=(vmem,) + (in_hbm,) * 5,
             scratch_shapes=[
                 *like(*operands, *results),
                 pltpu.VMEM((queries, width), jnp.float32),
@@ -488,7 +478,7 @@
         keep, send = pl.pallas_call(
             gradient_kernel,
             out_shape=(part, part),
-            in_specs=[vmem] + [anywhere] * 5,
+            in_specs=[vmem] + [in_hbm] * 5,
             out_specs=(vmem, vmem),
             scratch_shapes=[
                 pltpu.VMEM((queries, shard_rows), jnp.float32),

time: 262 us -> 261 us (level)
  no operation moved by 1% of the time
where the time goes in v13:
time: 261 us; the launch traced here: 258 us
  blocking collectives  80 us (31%)
  starting transfers between devices  75.5 us (29%)
  waiting for transfers between devices  43.7 us (17%)
  Pallas kernels  34.4 us (13%)
  local copies, waits for them, and re-layouts  14.7 us (6%)
  other arithmetic  8.33 us (3%)
    ppermute x15, starting transfers between devices, shift(): return lax.ppermute(x, axis, [((i + step) % size, i) for i in range(size)])  47 us
    all_to_all x1, blocking collectives, send_all(): lax.all_to_all(jnp.broadcast_to(x[None], (size, *x.shape)), axis, 0, 0, t...  34.5 us
    ppermute x15, waiting for transfers between devices, shift(): return lax.ppermute(x, axis, [((i + step) % size, i) for i in range(size)])  28.7 us
    all_to_all x1, blocking collectives, body(): lax.all_to_all(coef, Z_BY_CLASS, 0, 0, tiled=True).reshape(n_index, LANES)  21.8 us
    all_to_all x2, starting transfers between devices, send_all(): lax.all_to_all(jnp.broadcast_to(x[None], (size, *x.shape)), axis, 0, 0, t...  13 us
    all_to_all x1, waiting for transfers between devices, body(): term = jnp.sum(lax.all_to_all(term, Z, 0, 0, tiled=True), axis=0)  12.8 us
    all_to_all x1, blocking collectives, body(): lax.all_to_all(packet, NEAR, 0, 0, tiled=True)  12.7 us
    all_to_all x1, starting transfers between devices, body(): states = lax.all_to_all(state, ('y', 'core', *Z_BY_CLASS), 0, 0, tiled=True)  12 us
  transfers between devices with their start and end apart: 19, of which 7 were waited for; matrix products, arithmetic and copies ran while one was open for 5% of the time, Pallas kernels for 7%

profile of v13, /device:TPU:6, one launch (start us, length us, event | category | flops | bytes accessed | tf_op | source)
XLA Modules:
  0.0 257.9 jit_solution(16651556424691555402)
XLA Ops:
  2.1 0.8 fusion.3
  2.9 34.5 %all_to_all.50 = bf16[4,33,1024]{2,1,0:T(8,128)(2,1)S(1)} all-to-all(bf16[4,33,1024]{2,1,0:T(8,128)(2,1)S(1)} %broadcast_in_dim.10), channel_id=1, replica_groups=mesh['y'=4,'zq'=4,'zr'=4,'core'=2,'reader'=4] {'zq'}, dimensions={0} | all-to-all | bytes 540672 | tf_op jit(solution)/shard_map/gather_key_proj/all_to_all | solution.py:37
  37.4 6.7 %collective-permute-start.3 = (bf16[4,33,1024]{2,1,0:T(8,128)(2,1)S(1)}, bf16[4,33,1024]{2,1,0:T(8,128)(2,1)S(1)}, u32[]{:S(2)}, u32[]{:S(2)}) collective-permute-start(bf16[4,33,1024]{2,1,0:T(8,128)(2,1)S(1)} %all_to_all.50), channel_id=1, source_target_pairs={{8,0},{16,8},{24,16},{32,24},{40,32},{48,40},{56,48},{64,56},{72,6... | collective-permute-start | bytes 811016 | tf_op jit(solution)/shard_map/gather_key_proj/ppermute | solution.py:32
  44.1 1.9 collective-permute-start.4
  46.0 3.9 %collective-permute-start.5 = (bf16[4,33,1024]{2,1,0:T(8,128)(2,1)S(1)}, bf16[4,33,1024]{2,1,0:T(8,128)(2,1)S(1)}, u32[]{:S(2)}, u32[]{:S(2)}) collective-permute-start(bf16[4,33,1024]{2,1,0:T(8,128)(2,1)S(1)} %all_to_all.50), channel_id=1, source_target_pairs={{120,0},{0,8},{8,16},{16,24},{24,32},{32,40},{40,48},{48,56},{56,6... | collective-permute-start | bytes 811016 | tf_op jit(solution)/shard_map/gather_key_proj/ppermute | solution.py:32
  49.9 2.7 %collective-permute-start = (bf16[640,1024]{1,0:T(8,128)(2,1)}, bf16[640,1024]{1,0:T(8,128)(2,1)}, u32[]{:S(2)}, u32[]{:S(2)}) collective-permute-start(bf16[640,1024]{1,0:T(8,128)(2,1)} %bitcast.42), channel_id=1, source_target_pairs={{1,0},{2,1},{3,2},{0,3},{5,4},{6,5},{7,6},{4,7},{9,8},{10,9},{11,1... | collective-permute-start | bytes 3932168 | tf_op jit(solution)/shard_map/gather_enc_out/ppermute | solution.py:32
  52.6 4.3 %collective-permute-start.2 = (bf16[640,1024]{1,0:T(8,128)(2,1)}, bf16[640,1024]{1,0:T(8,128)(2,1)}, u32[]{:S(2)}, u32[]{:S(2)}) collective-permute-start(bf16[640,1024]{1,0:T(8,128)(2,1)} %bitcast.43), channel_id=1, source_target_pairs={{3,0},{0,1},{1,2},{2,3},{7,4},{4,5},{5,6},{6,7},{11,8},{8,9},{9,10... | collective-permute-start | bytes 3932168 | tf_op jit(solution)/shard_map/gather_enc_out/ppermute | solution.py:32
  58.0 6.1 %collective-permute-done.4 = bf16[4,33,1024]{2,1,0:T(8,128)(2,1)S(1)} collective-permute-done((bf16[4,33,1024]{2,1,0:T(8,128)(2,1)S(1)}, bf16[4,33,1024]{2,1,0:T(8,128)(2,1)S(1)}, u32[]{:S(2)}, u32[]{:S(2)}) %collective-permute-start.4) | collective-permute-done | bytes 270368 | tf_op jit(solution)/shard_map/gather_key_proj/ppermute | solution.py:32
  64.1 1.1 pad_maximum_fusion.refs_4_
  65.2 4.9 %collective-permute-start.6 = (bf16[16,32,1024]{2,1,0:T(8,128)(2,1)}, bf16[16,32,1024]{2,1,0:T(8,128)(2,1)}, u32[]{:S(2)}, u32[]{:S(2)}) collective-permute-start(bf16[16,32,1024]{2,1,0:T(8,128)(2,1)} %pad_maximum_fusion.refs_4_), channel_id=1, source_target_pairs={{128,0},{256,128},{384,256},{0,384},{129,1},{257,129},{385,257},{1... | collective-permute-start | bytes 3145736 | tf_op jit(solution)/shard_map/gather_key_proj/ppermute | solution.py:32
  70.2 1.9 collective-permute-start.8
  72.9 1.0 broadcast_in_dim.11
  73.9 7.6 %all-to-all-start.1 = ((bf16[32,16,896]{2,1,0:T(8,128)(2,1)}), bf16[32,16,896]{2,1,0:T(8,128)(2,1)S(1)}, u32[]{:S(2)}, u32[]{:S(2)}) async-start(bf16[32,16,896]{2,1,0:T(8,128)(2,1)} %broadcast_in_dim.11), calls=%async_computation.1 | async-start | bytes 1835008 | tf_op jit(solution)/shard_map/gather_queries/all_to_all | solution.py:37
  82.2 17.0 %collective-permute-done.6.refs_6_ = bf16[16,32,1024]{2,1,0:T(8,128)(2,1)} collective-permute-done((bf16[16,32,1024]{2,1,0:T(8,128)(2,1)}, bf16[16,32,1024]{2,1,0:T(8,128)(2,1)}, u32[]{:S(2)}, u32[]{:S(2)}) %collective-permute-start.6) | collective-permute-done | bytes 1048608 | tf_op jit(solution)/shard_map/gather_key_proj/ppermute | solution.py:32
  99.2 1.1 slice.56
  100.3 5.6 %collective-permute-start.7 = (bf16[8,32,1024]{2,1,0:T(8,128)(2,1)S(1)}, bf16[8,32,1024]{2,1,0:T(8,128)(2,1)S(1)}, u32[]{:S(2)}, u32[]{:S(2)}) collective-permute-start(bf16[8,32,1024]{2,1,0:T(8,128)(2,1)S(1)} %slice.56), channel_id=1, source_target_pairs={{128,0},{256,128},{384,256},{0,384},{129,1},{257,129},{385,257},{1... | collective-permute-start | bytes 1572872 | tf_op jit(solution)/shard_map/gather_key_proj/ppermute | solution.py:32
  105.9 1.9 slice.57
  107.7 1.9 collective-permute-start.9
  110.6 1.3 fusion.refs_3_
  111.9 1.9 collective-permute-start.11
  113.8 3.1 %collective-permute-start.1 = (bf16[640,1024]{1,0:T(8,128)(2,1)}, bf16[640,1024]{1,0:T(8,128)(2,1)}, u32[]{:S(2)}, u32[]{:S(2)}) collective-permute-start(bf16[640,1024]{1,0:T(8,128)(2,1)} %collective-permute-done.refs_1_), channel_id=1, source_target_pairs={{1,0},{2,1},{3,2},{0,3},{5,4},{6,5},{7,6},{4,7},{9,8},{10,9},{11,1... | collective-permute-start | bytes 3932168 | tf_op jit(solution)/shard_map/ppermute | solution.py:32
  117.0 2.1 collective-permute-start.12
  119.1 1.1 collective-permute-done.9
  120.2 1.9 collective-permute-start.13
  122.1 0.9 copy-done.7
  123.1 8.2 %scores.1 = (f32[128,128]{1,0:T(8,128)}, s32[128,128]{1,0:T(8,128)}, f32[512,192]{1,0:T(8,128)}, f32[512,192]{1,0:T(8,128)}, f32[128,128]{1,0:T(8,128)}, /*index=5*/bf16[768,512]{1,0:T(8,128)(2,1)}) custom-call(s32[2]{0:T(128)} %pad_add_fusion.1.place, bf16[32,16,896]{2,1,0:T(8,128)(2,1)} %copy-done.7, bf16[768,768]{1,0:T(8,128)(2,1)} %refs_1_.1, ...), custom_call_target="tpu_custom_call" | custom-call | flops 68719476736 | bytes 8388608 | tf_op jit(solution)/shard_map/scores/scores/pallas_call | solution.py:425
  131.3 12.0 %all-to-all-start.2 = ((f32[128,1,128]{2,1,0:T(1,128)}), f32[128,1,128]{2,1,0:T(1,128)}, u32[]{:S(2)}, u32[]{:S(2)}) async-start(f32[128,1,128]{2,1,0:T(1,128)} %bitcast.53), calls=%async_computation.2 | async-start | bytes 131072 | tf_op jit(solution)/shard_map/reduce_scores/all_to_all | solution.py:444
  143.4 2.2 collective-permute-start.10
  145.7 2.7 %collective-permute-done.1.refs_2_ = bf16[640,1024]{1,0:T(8,128)(2,1)} collective-permute-done((bf16[640,1024]{1,0:T(8,128)(2,1)}, bf16[640,1024]{1,0:T(8,128)(2,1)}, u32[]{:S(2)}, u32[]{:S(2)}) %collective-permute-start.1) | collective-permute-done | bytes 1310752 | tf_op jit(solution)/shard_map/ppermute | solution.py:32
  148.5 10.5 %early_keys.1.refs_6_ = f32[640,1024]{1,0:T(8,128)} custom-call(s32[4]{0:T(128)} %pad_add_fusion.place, bf16[640,1024]{1,0:T(8,128)(2,1)} %bitcast.44, bf16[640,1024]{1,0:T(8,128)(2,1)} %collective-permute-done.refs_1_, bf16[640,1024]{1,0:T(8,128)(2,1)} %collective-permute-done.1.refs_2_, bf16[640,1024]{1,0:T(8,128)(2,1)} %collective-permute-done.2.refs_3_, ...), custom_call_target="tpu_custom_call" | custom-call | flops 16106127360 | bytes 13631488 | tf_op jit(solution)/shard_map/attention/early_keys/pallas_call | solution.py:187
  159.0 7.3 %late_heads.1 = (f32[32,256]{1,0:T(8,128)S(1)}, f32[8,128]{1,0:T(8,128)S(1)}) custom-call(s32[4]{0:T(128)S(1)} %copy-done.6, bf16[640,1024]{1,0:T(8,128)(2,1)S(1)} %bitcast.45, bf16[640,1024]{1,0:T(8,128)(2,1)} %collective-permute-done.refs_1_, bf16[640,1024]{1,0:T(8,128)(2,1)} %collective-permute-done.1.refs_2_, ...), custom_call_target="tpu_custom_call" | custom-call | flops 1342177280 | bytes 6291456 | tf_op jit(solution)/shard_map/attention/late_heads/pallas_call | solution.py:202
  166.4 12.7 %all_to_all.51 = f32[32,1,256]{2,1,0:T(1,128)S(1)} all-to-all(f32[32,1,256]{2,1,0:T(1,128)S(1)} %copy.26), channel_id=1, replica_groups=mesh['y'=4,'zq'=4,'zr'=4,'core'=2,'reader'=4] {'reader','y','core'}, dimensions={0} | all-to-all | bytes 65536 | tf_op jit(solution)/shard_map/targets/all_to_all | solution.py:466
  179.7 1.6 coef.1
  181.3 21.8 %all_to_all.52 = f32[16,8,128]{2,1,0:T(8,128)S(1)} all-to-all(f32[16,8,128]{2,1,0:T(8,128)} %coef.1), channel_id=1, replica_groups=mesh['y'=4,'zq'=4,'zr'=4,'core'=2,'reader'=4] {'zr','zq'}, dimensions={0} | all-to-all | bytes 131072 | tf_op jit(solution)/shard_map/targets/all_to_all | solution.py:474
  203.1 1.1 copy-done.1
  204.2 1.0 copy-done.2
  205.3 1.0 copy-done.3
  206.3 0.8 copy-done.4
  207.2 0.8 copy-done.5
  208.0 6.8 %gradient.1 = (f32[384,192]{1,0:T(8,128)S(1)}, f32[384,192]{1,0:T(8,128)S(1)}) custom-call(f32[128,128]{1,0:T(8,128)S(1)} %bitcast.46, s32[128,128]{1,0:T(8,128)S(1)} %copy-done.4, f32[128,128]{1,0:T(8,128)S(1)} %copy-done.5, f32[512,192]{1,0:T(8,128)S(1)} %copy-done.2, f32[512,192]{1,0:T(8,128)S(1)} %copy-done.3, bf16[768,512]{1,0:T(8,128)(2,1)S(1)} %copy-done.1), custom_call_target="tpu_custom_call" | custom-call | tf_op jit(solution)/shard_map/gradient/gradient/pallas_call | solution.py:478
  214.8 1.9 collective-permute-start.14
  216.7 1.7 collective-permute-done.14
  218.4 11.0 %all_to_all.53 = f32[4,96,192]{2,1,0:T(8,128)S(1)} all-to-all(f32[4,96,192]{2,1,0:T(8,128)S(1)} %bitcast.49), channel_id=1, replica_groups=mesh['y'=4,'zq'=4,'zr'=4,'core'=2,'reader'=4] {'y'}, dimensions={0} | all-to-all | bytes 589824 | tf_op jit(solution)/shard_map/reduce_gradient/all_to_all | solution.py:494
  230.2 3.5 %all-to-all-start.6 = ((f32[16,6,192]{2,1,0:T(8,128)}), f32[16,6,192]{2,1,0:T(8,128)S(1)}, u32[]{:S(2)}, u32[]{:S(2)}) async-start(f32[16,6,192]{2,1,0:T(8,128)} %reshape.202), calls=%async_computation.6 | async-start | bytes 262144 | tf_op jit(solution)/shard_map/reduce_gradient/all_to_all | solution.py:496
  235.1 12.8 %all-to-all-done.6 = f32[16,6,192]{2,1,0:T(8,128)S(1)} async-done(((f32[16,6,192]{2,1,0:T(8,128)}), f32[16,6,192]{2,1,0:T(8,128)S(1)}, u32[]{:S(2)}, u32[]{:S(2)}) %all-to-all-start.6) | async-done | bytes 73760 | tf_op jit(solution)/shard_map/reduce_gradient/all_to_all | solution.py:496
  248.5 5.3 %all-to-all-start.7 = ((f32[4,6,192]{2,1,0:T(8,128)}), f32[4,6,192]{2,1,0:T(8,128)S(1)}, u32[]{:S(2)}, u32[]{:S(2)}) async-start(f32[4,6,192]{2,1,0:T(8,128)} %broadcast_in_dim.12), calls=%async_computation.7 | async-start | bytes 65536 | tf_op jit(solution)/shard_map/reduce_gradient/all_to_all | solution.py:37
  253.8 1.2 log_bitcast_fusion
  255.0 2.2 all-to-all-done.7
  (75 shorter events, 8.9 us)
Async XLA Ops:
  37.4 20.5 %collective-permute-start.3 = (bf16[4,33,1024]{2,1,0:T(8,128)(2,1)S(1)}, bf16[4,33,1024]{2,1,0:T(8,128)(2,1)S(1)}, u32[]{:S(2)}, u32[]{:S(2)}) collective-permute-start(bf16[4,33,1024]{2,1,0:T(8,128)(2,1)S(1)} %all_to_all.50), channel_id=1, source_target_pairs={{8,0},{16,8},{24,16},{32,24},{40,32},{48,40},{56,48},{64,56},{72,6... | collective-permute-start | bytes 811016 | tf_op jit(solution)/shard_map/gather_key_proj/ppermute | solution.py:32
  44.1 20.0 %collective-permute-start.4 = (bf16[4,33,1024]{2,1,0:T(8,128)(2,1)S(1)}, bf16[4,33,1024]{2,1,0:T(8,128)(2,1)S(1)}, u32[]{:S(2)}, u32[]{:S(2)}) collective-permute-start(bf16[4,33,1024]{2,1,0:T(8,128)(2,1)S(1)} %all_to_all.50), channel_id=1, source_target_pairs={{16,0},{24,8},{32,16},{40,24},{48,32},{56,40},{64,48},{72,56},{80,... | collective-permute-start | bytes 811016 | tf_op jit(solution)/shard_map/gather_key_proj/ppermute | solution.py:32
  46.0 18.1 %collective-permute-start.5 = (bf16[4,33,1024]{2,1,0:T(8,128)(2,1)S(1)}, bf16[4,33,1024]{2,1,0:T(8,128)(2,1)S(1)}, u32[]{:S(2)}, u32[]{:S(2)}) collective-permute-start(bf16[4,33,1024]{2,1,0:T(8,128)(2,1)S(1)} %all_to_all.50), channel_id=1, source_target_pairs={{120,0},{0,8},{8,16},{16,24},{24,32},{32,40},{40,48},{48,56},{56,6... | collective-permute-start | bytes 811016 | tf_op jit(solution)/shard_map/gather_key_proj/ppermute | solution.py:32
  49.9 64.0 %collective-permute-start = (bf16[640,1024]{1,0:T(8,128)(2,1)}, bf16[640,1024]{1,0:T(8,128)(2,1)}, u32[]{:S(2)}, u32[]{:S(2)}) collective-permute-start(bf16[640,1024]{1,0:T(8,128)(2,1)} %bitcast.42), channel_id=1, source_target_pairs={{1,0},{2,1},{3,2},{0,3},{5,4},{6,5},{7,6},{4,7},{9,8},{10,9},{11,1... | collective-permute-start | bytes 3932168 | tf_op jit(solution)/shard_map/gather_enc_out/ppermute | solution.py:32
  52.6 90.8 %collective-permute-start.2 = (bf16[640,1024]{1,0:T(8,128)(2,1)}, bf16[640,1024]{1,0:T(8,128)(2,1)}, u32[]{:S(2)}, u32[]{:S(2)}) collective-permute-start(bf16[640,1024]{1,0:T(8,128)(2,1)} %bitcast.43), channel_id=1, source_target_pairs={{3,0},{0,1},{1,2},{2,3},{7,4},{4,5},{5,6},{6,7},{11,8},{8,9},{9,10... | collective-permute-start | bytes 3932168 | tf_op jit(solution)/shard_map/gather_enc_out/ppermute | solution.py:32
  64.1 8.0 %copy-start.8 = (bf16[4,16,1024]{2,1,0:T(8,128)(2,1)S(1)}, bf16[4,16,1024]{2,1,0:T(8,128)(2,1)}, u32[]{:S(2)}) copy-start(bf16[4,16,1024]{2,1,0:T(8,128)(2,1)} %param.17) | copy-start | bytes 393220
  65.2 33.9 %collective-permute-start.6 = (bf16[16,32,1024]{2,1,0:T(8,128)(2,1)}, bf16[16,32,1024]{2,1,0:T(8,128)(2,1)}, u32[]{:S(2)}, u32[]{:S(2)}) collective-permute-start(bf16[16,32,1024]{2,1,0:T(8,128)(2,1)} %pad_maximum_fusion.refs_4_), channel_id=1, source_target_pairs={{128,0},{256,128},{384,256},{0,384},{129,1},{257,129},{385,257},{1... | collective-permute-start | bytes 3145736 | tf_op jit(solution)/shard_map/gather_key_proj/ppermute | solution.py:32
  70.2 35.7 %collective-permute-start.8 = (bf16[16,32,1024]{2,1,0:T(8,128)(2,1)}, bf16[16,32,1024]{2,1,0:T(8,128)(2,1)}, u32[]{:S(2)}, u32[]{:S(2)}) collective-permute-start(bf16[16,32,1024]{2,1,0:T(8,128)(2,1)} %pad_maximum_fusion.refs_4_), channel_id=1, source_target_pairs={{384,0},{0,128},{128,256},{256,384},{385,1},{1,129},{129,257},{257... | collective-permute-start | bytes 3145736 | tf_op jit(solution)/shard_map/gather_key_proj/ppermute | solution.py:32
  73.9 48.3 %all-to-all-start.1 = ((bf16[32,16,896]{2,1,0:T(8,128)(2,1)}), bf16[32,16,896]{2,1,0:T(8,128)(2,1)S(1)}, u32[]{:S(2)}, u32[]{:S(2)}) async-start(bf16[32,16,896]{2,1,0:T(8,128)(2,1)} %broadcast_in_dim.11), calls=%async_computation.1 | async-start | bytes 1835008 | tf_op jit(solution)/shard_map/gather_queries/all_to_all | solution.py:37
  100.3 10.3 %copy-start.9 = (bf16[1024]{0:T(1024)(128)(2,1)S(1)}, bf16[1024]{0:T(1024)(128)(2,1)}, u32[]{:S(2)}) copy-start(bf16[1024]{0:T(1024)(128)(2,1)} %param.16) | copy-start | bytes 6148
  100.3 16.7 %collective-permute-start.7 = (bf16[8,32,1024]{2,1,0:T(8,128)(2,1)S(1)}, bf16[8,32,1024]{2,1,0:T(8,128)(2,1)S(1)}, u32[]{:S(2)}, u32[]{:S(2)}) collective-permute-start(bf16[8,32,1024]{2,1,0:T(8,128)(2,1)S(1)} %slice.56), channel_id=1, source_target_pairs={{128,0},{256,128},{384,256},{0,384},{129,1},{257,129},{385,257},{1... | collective-permute-start | bytes 1572872 | tf_op jit(solution)/shard_map/gather_key_proj/ppermute | solution.py:32
  107.7 12.5 %collective-permute-start.9 = (bf16[8,32,1024]{2,1,0:T(8,128)(2,1)}, bf16[8,32,1024]{2,1,0:T(8,128)(2,1)S(1)}, u32[]{:S(2)}, u32[]{:S(2)}) collective-permute-start(bf16[8,32,1024]{2,1,0:T(8,128)(2,1)} %slice.57), channel_id=1, source_target_pairs={{384,0},{0,128},{128,256},{256,384},{385,1},{1,129},{129,257},{257... | collective-permute-start | bytes 1572872 | tf_op jit(solution)/shard_map/gather_key_proj/ppermute | solution.py:32
  111.9 33.8 %collective-permute-start.11 = (bf16[16,32,1024]{2,1,0:T(8,128)(2,1)}, bf16[16,32,1024]{2,1,0:T(8,128)(2,1)}, u32[]{:S(2)}, u32[]{:S(2)}) collective-permute-start(bf16[16,32,1024]{2,1,0:T(8,128)(2,1)} %pad_maximum_fusion.refs_4_), channel_id=1, source_target_pairs={{4,0},{0,4},{5,1},{1,5},{6,2},{2,6},{7,3},{3,7},{12,8},{8,12},{13,... | collective-permute-start | bytes 3145736 | tf_op jit(solution)/shard_map/gather_key_proj/ppermute | solution.py:32
  113.8 34.6 %collective-permute-start.1 = (bf16[640,1024]{1,0:T(8,128)(2,1)}, bf16[640,1024]{1,0:T(8,128)(2,1)}, u32[]{:S(2)}, u32[]{:S(2)}) collective-permute-start(bf16[640,1024]{1,0:T(8,128)(2,1)} %collective-permute-done.refs_1_), channel_id=1, source_target_pairs={{1,0},{2,1},{3,2},{0,3},{5,4},{6,5},{7,6},{4,7},{9,8},{10,9},{11,1... | collective-permute-start | bytes 3932168 | tf_op jit(solution)/shard_map/ppermute | solution.py:32
  117.0 31.5 %collective-permute-start.12 = (bf16[16,32,1024]{2,1,0:T(8,128)(2,1)}, bf16[16,32,1024]{2,1,0:T(8,128)(2,1)}, u32[]{:S(2)}, u32[]{:S(2)}) collective-permute-start(bf16[16,32,1024]{2,1,0:T(8,128)(2,1)} %collective-permute-done.6.refs_6_), channel_id=1, source_target_pairs={{4,0},{0,4},{5,1},{1,5},{6,2},{2,6},{7,3},{3,7},{12,8},{8,12},{13,... | collective-permute-start | bytes 3145736 | tf_op jit(solution)/shard_map/gather_key_proj/ppermute | solution.py:32
  120.2 28.3 %collective-permute-start.13 = (bf16[16,32,1024]{2,1,0:T(8,128)(2,1)}, bf16[16,32,1024]{2,1,0:T(8,128)(2,1)}, u32[]{:S(2)}, u32[]{:S(2)}) collective-permute-start(bf16[16,32,1024]{2,1,0:T(8,128)(2,1)} %collective-permute-done.8.refs_8_), channel_id=1, source_target_pairs={{4,0},{0,4},{5,1},{1,5},{6,2},{2,6},{7,3},{3,7},{12,8},{8,12},{13,... | collective-permute-start | bytes 3145736 | tf_op jit(solution)/shard_map/gather_key_proj/ppermute | solution.py:32
  122.1 0.9 copy-start.7
  131.3 27.6 %all-to-all-start.2 = ((f32[128,1,128]{2,1,0:T(1,128)}), f32[128,1,128]{2,1,0:T(1,128)}, u32[]{:S(2)}, u32[]{:S(2)}) async-start(f32[128,1,128]{2,1,0:T(1,128)} %bitcast.53), calls=%async_computation.2 | async-start | bytes 131072 | tf_op jit(solution)/shard_map/reduce_scores/all_to_all | solution.py:444
  143.4 15.5 %copy-start = (bf16[4,20,8,1024]{3,2,1,0:T(8,128)(2,1)S(1)}, bf16[4,20,8,1024]{3,2,1,0:T(8,128)(2,1)}, u32[]{:S(2)}) copy-start(bf16[4,20,8,1024]{3,2,1,0:T(8,128)(2,1)} %param.14) | copy-start | bytes 3932164
  143.4 15.5 %copy-start.6 = (s32[4]{0:T(128)S(1)}, s32[4]{0:T(128)}, u32[]{:S(2)}) copy-start(s32[4]{0:T(128)} %pad_add_fusion.place) | copy-start | bytes 52
  143.4 15.5 %collective-permute-start.10 = (bf16[16,32,1024]{2,1,0:T(8,128)(2,1)S(1)}, bf16[16,32,1024]{2,1,0:T(8,128)(2,1)S(1)}, u32[]{:S(2)}, u32[]{:S(2)}) collective-permute-start(bf16[16,32,1024]{2,1,0:T(8,128)(2,1)S(1)} %constant_dynamic-update-slice_fusion.refs_4_), channel_id=1, source_target_pairs={{4,0},{0,4},{5,1},{1,5},{6,2},{2,6},{7,3},{3,7},{12,8},{8,12},{13,... | collective-permute-start | bytes 3145736 | tf_op jit(solution)/shard_map/gather_key_proj/ppermute | solution.py:32
  203.1 1.1 copy-start.1
  204.2 1.0 copy-start.2
  205.3 1.0 copy-start.3
  206.3 0.8 copy-start.4
  207.1 0.8 copy-start.5
  214.8 3.6 %collective-permute-start.14 = (f32[384,192]{1,0:T(8,128)S(1)}, f32[384,192]{1,0:T(8,128)S(1)}, u32[]{:S(2)}, u32[]{:S(2)}) collective-permute-start(f32[384,192]{1,0:T(8,128)S(1)} %get-tuple-element.22), channel_id=1, source_target_pairs={{4,0},{0,4},{5,1},{1,5},{6,2},{2,6},{7,3},{3,7},{12,8},{8,12},{13,... | collective-permute-start | bytes 884744 | tf_op jit(solution)/shard_map/reduce_gradient/ppermute | solution.py:32
  230.2 17.7 %all-to-all-start.6 = ((f32[16,6,192]{2,1,0:T(8,128)}), f32[16,6,192]{2,1,0:T(8,128)S(1)}, u32[]{:S(2)}, u32[]{:S(2)}) async-start(f32[16,6,192]{2,1,0:T(8,128)} %reshape.202), calls=%async_computation.6 | async-start | bytes 262144 | tf_op jit(solution)/shard_map/reduce_gradient/all_to_all | solution.py:496
  248.5 8.7 %all-to-all-start.7 = ((f32[4,6,192]{2,1,0:T(8,128)}), f32[4,6,192]{2,1,0:T(8,128)S(1)}, u32[]{:S(2)}, u32[]{:S(2)}) async-start(f32[4,6,192]{2,1,0:T(8,128)} %broadcast_in_dim.12), calls=%async_computation.7 | async-start | bytes 65536 | tf_op jit(solution)/shard_map/reduce_gradient/all_to_all | solution.py:37

commit v14 on v13

--- a/solution.py
+++ b/solution.py
@@ -222,15 +222,15 @@
 
 
 def scores_kernel(place, *refs):
-    far, (state, *outs), near, refs = refs[:4], refs[4:10], refs[10:14], refs[14:]
-    near_outs, (unit_v, ids_v, sems) = refs[:5], refs[5:]
+    far, (state, *outs), near, refs = refs[:4], refs[4:8], refs[8:12], refs[12:]
+    near_outs, (unit_v, ids_v, sems) = refs[:3], refs[3:]
     copies = load(far, near, sems)
     packed, proj, emb, chosen = near
-    slots, rows, unit, scale, ordered = near_outs
+    lanes, sides, ordered = near_outs
     shard, r = place[0], place[1]
     n_rows, width = emb.shape
     per_x = state.shape[0]
-    cols = rows.shape[1]
+    cols = sides.shape[1]
     for copy in copies:
         copy.wait()
     feats = packed[:, :, :width].reshape(4 * per_x, width)
@@ -248,14 +248,14 @@
         ids_v[x] = ids
         moved = ids if x == 0 else pltpu.roll(ids, SLOT * x, 1)
         spread = jnp.where((lane // SLOT == x) & (lane % SLOT < 20), moved, spread)
-    slots[...] = spread
+    lanes[:per_x, :] = spread.astype(jnp.float32)
 
     vec = dot32(feats, proj[...])
     scale_all = lax.rsqrt(jnp.sum(vec * vec, axis=1, keepdims=True) + EPSILON)
     spread = jnp.zeros((per_x, LANES), jnp.float32)
     for x in range(4):
         spread = jnp.where(lane // SLOT == x, scale_all[x * per_x : (x + 1) * per_x], spread)
-    scale[...] = spread
+    lanes[per_x:, :] = spread
     unit_all = vec * scale_all
     unit_v[...] = unit_all
     emb_all = emb[...]
@@ -264,8 +264,8 @@
 
         @pl.when(r == x)
         def _():
-            rows[...] = row_unit[:, x * cols : (x + 1) * cols]
-            unit[...] = unit_all[:, x * cols : (x + 1) * cols]
+            sides[:n_rows, :] = row_unit[:, x * cols : (x + 1) * cols]
+            sides[n_rows:, :] = unit_all[:, x * cols : (x + 1) * cols]
 
     copies = load(near_outs, outs, sems)
     share = unit_v[pl.ds(pl.multiple_of(r * per_x, per_x), per_x), :]
@@ -312,38 +312,38 @@
 
 
 def gradient_kernel(coef, *refs):
-    far, (keep, send, matrix_v), near, sems = refs[:5], refs[5:8], refs[8:13], refs[13]
+    far, (keep, send, matrix_v), near, sems = refs[:3], refs[3:6], refs[6:9], refs[9]
     copies = load(far, near, sems)
-    slot, scale, rows, unit, ordered = near
+    lanes, sides, ordered = near
     copies[0].wait()
-    copies[1].wait()
     n_rows = matrix_v.shape[1]
     blocks = coef.shape[0]
 
     @pl.loop(0, blocks // 8)
     def _(b):
         eight = pl.ds(pl.multiple_of(b * 8, 8), 8)
-        row = lax.broadcasted_iota(jnp.int32, (8, n_rows), 1)
-        values = coef[pl.ds(b // 2 + b % 2 * 64, 8, stride=8), :] * scale[eight, :]
-        places = slot[eight, :]
+        scaled = pl.ds(pl.multiple_of(blocks + b * 8, 8), 8)
+        row = lax.broadcasted_iota(jnp.int32, (8, n_rows), 1).astype(jnp.float32)
+        values = coef[pl.ds(b // 2 + b % 2 * 64, 8, stride=8), :] * lanes[scaled, :]
+        places = lanes[eight, :]
         for x in range(4):
             total = jnp.zeros((8, n_rows), jnp.float32)
             for k in range(SLOT * x, SLOT * x + 20):
                 total += jnp.where(places[:, k : k + 1] == row, values[:, k : k + 1], 0.0)
             matrix_v[pl.ds(pl.multiple_of(x * blocks + b * 8, 8), 8), :] = total
 
-    for copy in copies[2:]:
+    for copy in copies[1:]:
         copy.wait()
     along_all = jnp.concatenate([coef[pl.ds(p, 16, stride=8), :] for p in range(8)], axis=0)
-    along_all = along_all * scale[...]
-    row_high, row_low = halves(rows[...])
+    along_all = along_all * lanes[blocks:, :]
+    row_high, row_low = halves(sides[:n_rows, :])
     parts_high, parts_low = [], []
     for x in range(4):
         mine = slice(x * blocks, (x + 1) * blocks)
         high, low = halves(matrix_v[mine, :])
         part = dot32(high, row_high) + (dot32(high, row_low) + dot32(low, row_high))
         along = along_all[:, SLOT * x + 20 : SLOT * x + 21]
-        part = part - unit[mine, :] * along
+        part = part - sides[n_rows + x * blocks : n_rows + (x + 1) * blocks, :] * along
         high, low = halves(part)
         parts_high.append(high)
         parts_low.append(low)
@@ -391,7 +391,7 @@
         classes = (own, after, shift(own, Z, 2), before)
         own = jnp.concatenate([block[:, :-1] for block in classes])
         after, before = shift(own, "y", 1), shift(own, "y", -1)
-        far = jnp.concatenate([shift(after[:8], "y", 1), shift(before[8:], "y", -1)])
+        far = shift(after, "y", 1)
         key_rows = [(block, shift(block, "core", 1)) for block in (own, after, far, before)]
     token_far = shift(token_after, "reader", 1)
     tokens = (token_own, token_after, token_far, token_before)
@@ -414,19 +414,17 @@
         queries = n_index * nx
         operands = (packed, query_proj, index_emb, chosen)
         results = (
-            jax.ShapeDtypeStruct((n_index, LANES), jnp.int32),
-            jax.ShapeDtypeStruct((shard_rows, cols), jnp.float32),
-            jax.ShapeDtypeStruct((queries, cols), jnp.float32),
-            jax.ShapeDtypeStruct((n_index, LANES), jnp.float32),
+            jax.ShapeDtypeStruct((2 * n_index, LANES), jnp.float32),
+            jax.ShapeDtypeStruct((shard_rows + queries, cols), jnp.float32),
             jax.ShapeDtypeStruct((width, queries), jnp.bfloat16),
         )
         anywhere = pl.BlockSpec(memory_space=pl.ANY)
         in_hbm = pl.BlockSpec(memory_space=pltpu.HBM)
-        state, slots, my_rows, my_unit, query_scale, ordered = pl.pallas_call(
+        state, lanes, sides, ordered = pl.pallas_call(
             scores_kernel,
             out_shape=(jax.ShapeDtypeStruct((n_index, LANES), jnp.float32), *results),
             in_specs=[pl.BlockSpec(memory_space=pltpu.SMEM)] + [anywhere] * 4,
-            out_specs=(vmem,) + (in_hbm,) * 5,
+            out_specs=(vmem,) + (in_hbm,) * 3,
             scratch_shapes=[
                 *like(*operands, *results),
                 pltpu.VMEM((queries, width), jnp.float32),
@@ -478,16 +476,16 @@
         keep, send = pl.pallas_call(
             gradient_kernel,
             out_shape=(part, part),
-            in_specs=[vmem] + [in_hbm] * 5,
+            in_specs=[vmem] + [in_hbm] * 3,
             out_specs=(vmem, vmem),
             scratch_shapes=[
                 pltpu.VMEM((queries, shard_rows), jnp.float32),
-                *like(slots, query_scale, my_rows, my_unit, ordered),
+                *like(lanes, sides, ordered),
                 pltpu.SemaphoreType.DMA((5,)),
             ],
             compiler_params=pltpu.CompilerParams(vmem_limit_bytes=40 << 20),
             name="gradient",
-        )(coef, slots, query_scale, my_rows, my_unit, ordered)
+        )(coef, lanes, sides, ordered)
 
     with jax.named_scope("reduce_gradient"):
         term = (keep + shift(send, "core", 1)).reshape(ny, nz * six, cols)

time: 261 us -> 245 us (0.939)
  blocking collectives: 80 us -> 46.9 us
  starting transfers between devices: 75.5 us -> 89.1 us
  waiting for transfers between devices: 43.7 us -> 51.9 us
  local copies, waits for them, and re-layouts: 14.7 us -> 10.1 us
    all_to_all x1 -> x0, blocking collectives: 34.5 us -> none  [send_all(): lax.all_to_all(jnp.broadcast_to(x[None], (size, *x.shape)), axis, 0, 0, t...]
    all_to_all x2 -> x3, starting transfers between devices: 13 us -> 28 us  [send_all(): lax.all_to_all(jnp.broadcast_to(x[None], (size, *x.shape)), axis, 0, 0, t...]
    all_to_all x2 -> x3, waiting for transfers between devices: 2.19 us -> 13.8 us  [send_all(): lax.all_to_all(jnp.broadcast_to(x[None], (size, *x.shape)), axis, 0, 0, t...]
    ppermute x15 -> x14, waiting for transfers between devices: 28.7 us -> 23.9 us  [shift(): return lax.ppermute(x, axis, [((i + step) % size, i) for i in range(size)])]
    slice x2 -> x0, local copies, waits for them, and re-layouts: 2.94 us -> none  [the longest x1 1.86 us: body(): before[8:]]
    unnamed x26 -> x23, local copies, waits for them, and re-layouts: 6.5 us -> 4.83 us
    ppermute x15 -> x14, starting transfers between devices: 47 us -> 45.4 us  [shift(): return lax.ppermute(x, axis, [((i + step) % size, i) for i in range(size)])]
  transfers between devices with their start and end apart: 19 -> 19, of which waited for: 7 -> 8; matrix products, arithmetic and copies ran while one was open for 5% -> 4% of each run, Pallas kernels for 7% -> 8%
where the time goes in v14:
time: 245 us; the launch traced here: 242 us
  starting transfers between devices  89.1 us (36%)
  waiting for transfers between devices  51.9 us (21%)
  blocking collectives  46.9 us (19%)
  Pallas kernels  34.4 us (14%)
  local copies, waits for them, and re-layouts  10.1 us (4%)
  other arithmetic  8.48 us (3%)
    ppermute x14, starting transfers between devices, shift(): return lax.ppermute(x, axis, [((i + step) % size, i) for i in range(size)])  45.4 us
    all_to_all x3, starting transfers between devices, send_all(): lax.all_to_all(jnp.broadcast_to(x[None], (size, *x.shape)), axis, 0, 0, t...  28 us
    all_to_all x1, blocking collectives, body(): lax.all_to_all(coef, Z_BY_CLASS, 0, 0, tiled=True).reshape(n_index, LANES)  24.1 us
    ppermute x14, waiting for transfers between devices, shift(): return lax.ppermute(x, axis, [((i + step) % size, i) for i in range(size)])  23.9 us
    all_to_all x3, waiting for transfers between devices, send_all(): lax.all_to_all(jnp.broadcast_to(x[None], (size, *x.shape)), axis, 0, 0, t...  13.8 us
    all_to_all x1, waiting for transfers between devices, body(): term = jnp.sum(lax.all_to_all(term, Z, 0, 0, tiled=True), axis=0)  12.8 us
    all_to_all x1, starting transfers between devices, body(): states = lax.all_to_all(state, ('y', 'core', *Z_BY_CLASS), 0, 0, tiled=True)  12.2 us
    all_to_all x1, blocking collectives, body(): lax.all_to_all(packet, NEAR, 0, 0, tiled=True)  11.8 us
  transfers between devices with their start and end apart: 19, of which 8 were waited for; matrix products, arithmetic and copies ran while one was open for 4% of the time, Pallas kernels for 8%

profile of v14, /device:TPU:6, one launch (start us, length us, event | category | flops | bytes accessed | tf_op | source)
XLA Modules:
  0.0 242.1 jit_solution(4027667769826668320)
XLA Ops:
  0.6 0.7 fusion.31
  1.3 0.8 fusion.27
  2.1 0.8 fusion.3
  3.0 0.8 broadcast_in_dim.10
  3.7 15.1 %all-to-all-start = ((bf16[4,33,1024]{2,1,0:T(8,128)(2,1)}), bf16[4,33,1024]{2,1,0:T(8,128)(2,1)S(1)}, u32[]{:S(2)}, u32[]{:S(2)}) async-start(bf16[4,33,1024]{2,1,0:T(8,128)(2,1)} %broadcast_in_dim.10), calls=%async_computation | async-start | bytes 655360 | tf_op jit(solution)/shard_map/gather_key_proj/all_to_all | solution.py:37
  18.8 2.7 %collective-permute-start = (bf16[640,1024]{1,0:T(8,128)(2,1)}, bf16[640,1024]{1,0:T(8,128)(2,1)}, u32[]{:S(2)}, u32[]{:S(2)}) collective-permute-start(bf16[640,1024]{1,0:T(8,128)(2,1)} %bitcast.42), channel_id=1, source_target_pairs={{1,0},{2,1},{3,2},{0,3},{5,4},{6,5},{7,6},{4,7},{9,8},{10,9},{11,1... | collective-permute-start | bytes 3932168 | tf_op jit(solution)/shard_map/gather_enc_out/ppermute | solution.py:32
  21.5 4.3 %collective-permute-start.2 = (bf16[640,1024]{1,0:T(8,128)(2,1)}, bf16[640,1024]{1,0:T(8,128)(2,1)}, u32[]{:S(2)}, u32[]{:S(2)}) collective-permute-start(bf16[640,1024]{1,0:T(8,128)(2,1)} %bitcast.43), channel_id=1, source_target_pairs={{3,0},{0,1},{1,2},{2,3},{7,4},{4,5},{5,6},{6,7},{11,8},{8,9},{9,10... | collective-permute-start | bytes 3932168 | tf_op jit(solution)/shard_map/gather_enc_out/ppermute | solution.py:32
  26.3 11.6 %all-to-all-done = bf16[4,33,1024]{2,1,0:T(8,128)(2,1)S(1)} async-done(((bf16[4,33,1024]{2,1,0:T(8,128)(2,1)}), bf16[4,33,1024]{2,1,0:T(8,128)(2,1)S(1)}, u32[]{:S(2)}, u32[]{:S(2)}) %all-to-all-start) | async-done | bytes 270368 | tf_op jit(solution)/shard_map/gather_key_proj/all_to_all | solution.py:37
  37.9 7.2 %collective-permute-start.3 = (bf16[4,33,1024]{2,1,0:T(8,128)(2,1)S(1)}, bf16[4,33,1024]{2,1,0:T(8,128)(2,1)S(1)}, u32[]{:S(2)}, u32[]{:S(2)}) collective-permute-start(bf16[4,33,1024]{2,1,0:T(8,128)(2,1)S(1)} %all-to-all-done), channel_id=1, source_target_pairs={{8,0},{16,8},{24,16},{32,24},{40,32},{48,40},{56,48},{64,56},{72,6... | collective-permute-start | bytes 811016 | tf_op jit(solution)/shard_map/gather_key_proj/ppermute | solution.py:32
  45.0 1.9 collective-permute-start.4
  47.0 3.9 %collective-permute-start.5 = (bf16[4,33,1024]{2,1,0:T(8,128)(2,1)S(1)}, bf16[4,33,1024]{2,1,0:T(8,128)(2,1)S(1)}, u32[]{:S(2)}, u32[]{:S(2)}) collective-permute-start(bf16[4,33,1024]{2,1,0:T(8,128)(2,1)S(1)} %all-to-all-done), channel_id=1, source_target_pairs={{120,0},{0,8},{8,16},{16,24},{24,32},{32,40},{40,48},{48,56},{56,6... | collective-permute-start | bytes 811016 | tf_op jit(solution)/shard_map/gather_key_proj/ppermute | solution.py:32
  52.2 3.4 %collective-permute-done.3 = bf16[4,33,1024]{2,1,0:T(8,128)(2,1)S(1)} collective-permute-done((bf16[4,33,1024]{2,1,0:T(8,128)(2,1)S(1)}, bf16[4,33,1024]{2,1,0:T(8,128)(2,1)S(1)}, u32[]{:S(2)}, u32[]{:S(2)}) %collective-permute-start.3) | collective-permute-done | bytes 270368 | tf_op jit(solution)/shard_map/gather_key_proj/ppermute | solution.py:32
  55.7 8.2 %collective-permute-done.4 = bf16[4,33,1024]{2,1,0:T(8,128)(2,1)S(1)} collective-permute-done((bf16[4,33,1024]{2,1,0:T(8,128)(2,1)S(1)}, bf16[4,33,1024]{2,1,0:T(8,128)(2,1)S(1)}, u32[]{:S(2)}, u32[]{:S(2)}) %collective-permute-start.4) | collective-permute-done | bytes 270368 | tf_op jit(solution)/shard_map/gather_key_proj/ppermute | solution.py:32
  63.9 1.2 pad_maximum_fusion.refs_4_
  65.1 4.9 %collective-permute-start.6 = (bf16[16,32,1024]{2,1,0:T(8,128)(2,1)}, bf16[16,32,1024]{2,1,0:T(8,128)(2,1)}, u32[]{:S(2)}, u32[]{:S(2)}) collective-permute-start(bf16[16,32,1024]{2,1,0:T(8,128)(2,1)} %pad_maximum_fusion.refs_4_), channel_id=1, source_target_pairs={{128,0},{256,128},{384,256},{0,384},{129,1},{257,129},{385,257},{1... | collective-permute-start | bytes 3145736 | tf_op jit(solution)/shard_map/gather_key_proj/ppermute | solution.py:32
  70.1 1.9 collective-permute-start.11
  72.2 1.0 broadcast_in_dim.11
  73.2 7.6 %all-to-all-start.1 = ((bf16[32,16,896]{2,1,0:T(8,128)(2,1)}), bf16[32,16,896]{2,1,0:T(8,128)(2,1)S(1)}, u32[]{:S(2)}, u32[]{:S(2)}) async-start(bf16[32,16,896]{2,1,0:T(8,128)(2,1)} %broadcast_in_dim.11), calls=%async_computation.1 | async-start | bytes 1835008 | tf_op jit(solution)/shard_map/gather_queries/all_to_all | solution.py:37
  81.5 1.3 fusion.refs_3_
  82.8 2.0 collective-permute-start.9
  84.9 2.7 %collective-permute-start.1 = (bf16[640,1024]{1,0:T(8,128)(2,1)}, bf16[640,1024]{1,0:T(8,128)(2,1)}, u32[]{:S(2)}, u32[]{:S(2)}) collective-permute-start(bf16[640,1024]{1,0:T(8,128)(2,1)} %collective-permute-done.refs_1_), channel_id=1, source_target_pairs={{1,0},{2,1},{3,2},{0,3},{5,4},{6,5},{7,6},{4,7},{9,8},{10,9},{11,1... | collective-permute-start | bytes 3932168 | tf_op jit(solution)/shard_map/ppermute | solution.py:32
  87.6 10.6 %collective-permute-done.6.refs_6_ = bf16[16,32,1024]{2,1,0:T(8,128)(2,1)} collective-permute-done((bf16[16,32,1024]{2,1,0:T(8,128)(2,1)}, bf16[16,32,1024]{2,1,0:T(8,128)(2,1)}, u32[]{:S(2)}, u32[]{:S(2)}) %collective-permute-start.6) | collective-permute-done | bytes 1048608 | tf_op jit(solution)/shard_map/gather_key_proj/ppermute | solution.py:32
  98.2 1.9 collective-permute-start.10
  100.2 5.6 %collective-permute-start.7 = (bf16[16,32,1024]{2,1,0:T(8,128)(2,1)}, bf16[16,32,1024]{2,1,0:T(8,128)(2,1)S(1)}, u32[]{:S(2)}, u32[]{:S(2)}) collective-permute-start(bf16[16,32,1024]{2,1,0:T(8,128)(2,1)} %collective-permute-done.6.refs_6_), channel_id=1, source_target_pairs={{128,0},{256,128},{384,256},{0,384},{129,1},{257,129},{385,257},{1... | collective-permute-start | bytes 3145736 | tf_op jit(solution)/shard_map/gather_key_proj/ppermute | solution.py:32
  105.7 2.1 collective-permute-start.12
  107.9 0.9 copy-done.5
  108.8 8.2 %scores.1 = (f32[128,128]{1,0:T(8,128)}, f32[256,128]{1,0:T(8,128)}, f32[1024,192]{1,0:T(8,128)}, bf16[768,512]{1,0:T(8,128)(2,1)}) custom-call(s32[2]{0:T(128)} %pad_add_fusion.1.place, bf16[32,16,896]{2,1,0:T(8,128)(2,1)} %copy-done.5, bf16[768,768]{1,0:T(8,128)(2,1)} %refs_1_.1, f32[512,768]{1,0:T(8,128)} %refs_2_.1, bf16[768,768]{1,0:T(8,128)(2,1)} %fusion.refs_3_), custom_call_target="tpu_custom_call" | custom-call | flops 68719476736 | bytes 8388608 | tf_op jit(solution)/shard_map/scores/scores/pallas_call | solution.py:423
  117.1 12.2 %all-to-all-start.2 = ((f32[128,1,128]{2,1,0:T(1,128)}), f32[128,1,128]{2,1,0:T(1,128)}, u32[]{:S(2)}, u32[]{:S(2)}) async-start(f32[128,1,128]{2,1,0:T(1,128)} %bitcast.53), calls=%async_computation.2 | async-start | bytes 131072 | tf_op jit(solution)/shard_map/reduce_scores/all_to_all | solution.py:442
  129.3 2.2 collective-permute-start.8
  131.5 10.5 %early_keys.1.refs_6_ = f32[640,1024]{1,0:T(8,128)} custom-call(s32[4]{0:T(128)} %pad_add_fusion.place, bf16[640,1024]{1,0:T(8,128)(2,1)} %bitcast.44, bf16[640,1024]{1,0:T(8,128)(2,1)} %collective-permute-done.refs_1_, bf16[640,1024]{1,0:T(8,128)(2,1)} %collective-permute-done.1.refs_2_, bf16[640,1024]{1,0:T(8,128)(2,1)} %collective-permute-done.2.refs_3_, ...), custom_call_target="tpu_custom_call" | custom-call | flops 16106127360 | bytes 13631488 | tf_op jit(solution)/shard_map/attention/early_keys/pallas_call | solution.py:187
  142.0 1.4 all-to-all-done.2
  143.4 7.3 %late_heads.1 = (f32[32,256]{1,0:T(8,128)S(1)}, f32[8,128]{1,0:T(8,128)S(1)}) custom-call(s32[4]{0:T(128)S(1)} %copy-done.4, bf16[640,1024]{1,0:T(8,128)(2,1)S(1)} %bitcast.45, bf16[640,1024]{1,0:T(8,128)(2,1)} %collective-permute-done.refs_1_, bf16[640,1024]{1,0:T(8,128)(2,1)} %collective-permute-done.1.refs_2_, ...), custom_call_target="tpu_custom_call" | custom-call | flops 1342177280 | bytes 6291456 | tf_op jit(solution)/shard_map/attention/late_heads/pallas_call | solution.py:202
  150.8 11.8 %all_to_all.50 = f32[32,1,256]{2,1,0:T(1,128)S(1)} all-to-all(f32[32,1,256]{2,1,0:T(1,128)S(1)} %copy.26), channel_id=1, replica_groups=mesh['y'=4,'zq'=4,'zr'=4,'core'=2,'reader'=4] {'reader','y','core'}, dimensions={0} | all-to-all | bytes 65536 | tf_op jit(solution)/shard_map/targets/all_to_all | solution.py:464
  163.2 1.6 coef.1
  164.8 24.1 %all_to_all.51 = f32[16,8,128]{2,1,0:T(8,128)S(1)} all-to-all(f32[16,8,128]{2,1,0:T(8,128)} %coef.1), channel_id=1, replica_groups=mesh['y'=4,'zq'=4,'zr'=4,'core'=2,'reader'=4] {'zr','zq'}, dimensions={0} | all-to-all | bytes 131072 | tf_op jit(solution)/shard_map/targets/all_to_all | solution.py:472
  188.9 1.2 copy-done.1
  190.1 1.1 copy-done.2
  191.3 0.9 copy-done.3
  192.2 6.8 %gradient.1 = (f32[384,192]{1,0:T(8,128)S(1)}, f32[384,192]{1,0:T(8,128)S(1)}) custom-call(f32[128,128]{1,0:T(8,128)S(1)} %bitcast.46, f32[256,128]{1,0:T(8,128)S(1)} %copy-done.3, f32[1024,192]{1,0:T(8,128)S(1)} %copy-done.1, bf16[768,512]{1,0:T(8,128)(2,1)S(1)} %copy-done.2), custom_call_target="tpu_custom_call" | custom-call | tf_op jit(solution)/shard_map/gradient/gradient/pallas_call | solution.py:476
  198.9 1.9 collective-permute-start.13
  200.9 1.7 collective-permute-done.13
  202.6 11.0 %all_to_all.52 = f32[4,96,192]{2,1,0:T(8,128)S(1)} all-to-all(f32[4,96,192]{2,1,0:T(8,128)S(1)} %bitcast.49), channel_id=1, replica_groups=mesh['y'=4,'zq'=4,'zr'=4,'core'=2,'reader'=4] {'y'}, dimensions={0} | all-to-all | bytes 589824 | tf_op jit(solution)/shard_map/reduce_gradient/all_to_all | solution.py:492
  214.3 3.5 %all-to-all-start.6 = ((f32[16,6,192]{2,1,0:T(8,128)}), f32[16,6,192]{2,1,0:T(8,128)S(1)}, u32[]{:S(2)}, u32[]{:S(2)}) async-start(f32[16,6,192]{2,1,0:T(8,128)} %reshape.202), calls=%async_computation.6 | async-start | bytes 262144 | tf_op jit(solution)/shard_map/reduce_gradient/all_to_all | solution.py:494
  218.5 0.8 dynamic-slice_reduce_fusion
  219.2 12.8 %all-to-all-done.6 = f32[16,6,192]{2,1,0:T(8,128)S(1)} async-done(((f32[16,6,192]{2,1,0:T(8,128)}), f32[16,6,192]{2,1,0:T(8,128)S(1)}, u32[]{:S(2)}, u32[]{:S(2)}) %all-to-all-start.6) | async-done | bytes 73760 | tf_op jit(solution)/shard_map/reduce_gradient/all_to_all | solution.py:494
  232.7 5.3 %all-to-all-start.7 = ((f32[4,6,192]{2,1,0:T(8,128)}), f32[4,6,192]{2,1,0:T(8,128)S(1)}, u32[]{:S(2)}, u32[]{:S(2)}) async-start(f32[4,6,192]{2,1,0:T(8,128)} %broadcast_in_dim.12), calls=%async_computation.7 | async-start | bytes 65536 | tf_op jit(solution)/shard_map/reduce_gradient/all_to_all | solution.py:37
  238.0 1.2 log_bitcast_fusion
  239.2 2.2 all-to-all-done.7
  (68 shorter events, 5.9 us)
Async XLA Ops:
  0.6 25.2 %copy-start.6 = (bf16[4,16,1024]{2,1,0:T(8,128)(2,1)S(1)}, bf16[4,16,1024]{2,1,0:T(8,128)(2,1)}, u32[]{:S(2)}) copy-start(bf16[4,16,1024]{2,1,0:T(8,128)(2,1)} %param.17) | copy-start | bytes 393220
  3.7 34.2 %all-to-all-start = ((bf16[4,33,1024]{2,1,0:T(8,128)(2,1)}), bf16[4,33,1024]{2,1,0:T(8,128)(2,1)S(1)}, u32[]{:S(2)}, u32[]{:S(2)}) async-start(bf16[4,33,1024]{2,1,0:T(8,128)(2,1)} %broadcast_in_dim.10), calls=%async_computation | async-start | bytes 655360 | tf_op jit(solution)/shard_map/gather_key_proj/all_to_all | solution.py:37
  18.8 66.1 %collective-permute-start = (bf16[640,1024]{1,0:T(8,128)(2,1)}, bf16[640,1024]{1,0:T(8,128)(2,1)}, u32[]{:S(2)}, u32[]{:S(2)}) collective-permute-start(bf16[640,1024]{1,0:T(8,128)(2,1)} %bitcast.42), channel_id=1, source_target_pairs={{1,0},{2,1},{3,2},{0,3},{5,4},{6,5},{7,6},{4,7},{9,8},{10,9},{11,1... | collective-permute-start | bytes 3932168 | tf_op jit(solution)/shard_map/gather_enc_out/ppermute | solution.py:32
  21.5 78.6 %collective-permute-start.2 = (bf16[640,1024]{1,0:T(8,128)(2,1)}, bf16[640,1024]{1,0:T(8,128)(2,1)}, u32[]{:S(2)}, u32[]{:S(2)}) collective-permute-start(bf16[640,1024]{1,0:T(8,128)(2,1)} %bitcast.43), channel_id=1, source_target_pairs={{3,0},{0,1},{1,2},{2,3},{7,4},{4,5},{5,6},{6,7},{11,8},{8,9},{9,10... | collective-permute-start | bytes 3932168 | tf_op jit(solution)/shard_map/gather_enc_out/ppermute | solution.py:32
  25.9 26.0 %copy-start.7 = (s32[4,20]{1,0:T(4,128)S(1)}, s32[4,20]{1,0:T(4,128)}, u32[]{:S(2)}) copy-start(s32[4,20]{1,0:T(4,128)} %param.13) | copy-start | bytes 964
  25.9 26.2 %copy-start.8 = (bf16[1024]{0:T(1024)(128)(2,1)S(1)}, bf16[1024]{0:T(1024)(128)(2,1)}, u32[]{:S(2)}) copy-start(bf16[1024]{0:T(1024)(128)(2,1)} %param.16) | copy-start | bytes 6148
  37.9 17.8 %collective-permute-start.3 = (bf16[4,33,1024]{2,1,0:T(8,128)(2,1)S(1)}, bf16[4,33,1024]{2,1,0:T(8,128)(2,1)S(1)}, u32[]{:S(2)}, u32[]{:S(2)}) collective-permute-start(bf16[4,33,1024]{2,1,0:T(8,128)(2,1)S(1)} %all-to-all-done), channel_id=1, source_target_pairs={{8,0},{16,8},{24,16},{32,24},{40,32},{48,40},{56,48},{64,56},{72,6... | collective-permute-start | bytes 811016 | tf_op jit(solution)/shard_map/gather_key_proj/ppermute | solution.py:32
  45.0 18.8 %collective-permute-start.4 = (bf16[4,33,1024]{2,1,0:T(8,128)(2,1)S(1)}, bf16[4,33,1024]{2,1,0:T(8,128)(2,1)S(1)}, u32[]{:S(2)}, u32[]{:S(2)}) collective-permute-start(bf16[4,33,1024]{2,1,0:T(8,128)(2,1)S(1)} %all-to-all-done), channel_id=1, source_target_pairs={{16,0},{24,8},{32,16},{40,24},{48,32},{56,40},{64,48},{72,56},{80,... | collective-permute-start | bytes 811016 | tf_op jit(solution)/shard_map/gather_key_proj/ppermute | solution.py:32
  47.0 16.9 %collective-permute-start.5 = (bf16[4,33,1024]{2,1,0:T(8,128)(2,1)S(1)}, bf16[4,33,1024]{2,1,0:T(8,128)(2,1)S(1)}, u32[]{:S(2)}, u32[]{:S(2)}) collective-permute-start(bf16[4,33,1024]{2,1,0:T(8,128)(2,1)S(1)} %all-to-all-done), channel_id=1, source_target_pairs={{120,0},{0,8},{8,16},{16,24},{24,32},{32,40},{40,48},{48,56},{56,6... | collective-permute-start | bytes 811016 | tf_op jit(solution)/shard_map/gather_key_proj/ppermute | solution.py:32
  65.1 33.1 %collective-permute-start.6 = (bf16[16,32,1024]{2,1,0:T(8,128)(2,1)}, bf16[16,32,1024]{2,1,0:T(8,128)(2,1)}, u32[]{:S(2)}, u32[]{:S(2)}) collective-permute-start(bf16[16,32,1024]{2,1,0:T(8,128)(2,1)} %pad_maximum_fusion.refs_4_), channel_id=1, source_target_pairs={{128,0},{256,128},{384,256},{0,384},{129,1},{257,129},{385,257},{1... | collective-permute-start | bytes 3145736 | tf_op jit(solution)/shard_map/gather_key_proj/ppermute | solution.py:32
  70.1 35.7 %collective-permute-start.11 = (bf16[16,32,1024]{2,1,0:T(8,128)(2,1)}, bf16[16,32,1024]{2,1,0:T(8,128)(2,1)}, u32[]{:S(2)}, u32[]{:S(2)}) collective-permute-start(bf16[16,32,1024]{2,1,0:T(8,128)(2,1)} %pad_maximum_fusion.refs_4_), channel_id=1, source_target_pairs={{384,0},{0,128},{128,256},{256,384},{385,1},{1,129},{129,257},{257... | collective-permute-start | bytes 3145736 | tf_op jit(solution)/shard_map/gather_key_proj/ppermute | solution.py:32
  73.2 34.6 %all-to-all-start.1 = ((bf16[32,16,896]{2,1,0:T(8,128)(2,1)}), bf16[32,16,896]{2,1,0:T(8,128)(2,1)S(1)}, u32[]{:S(2)}, u32[]{:S(2)}) async-start(bf16[32,16,896]{2,1,0:T(8,128)(2,1)} %broadcast_in_dim.11), calls=%async_computation.1 | async-start | bytes 1835008 | tf_op jit(solution)/shard_map/gather_queries/all_to_all | solution.py:37
  82.8 48.7 %collective-permute-start.9 = (bf16[16,32,1024]{2,1,0:T(8,128)(2,1)}, bf16[16,32,1024]{2,1,0:T(8,128)(2,1)}, u32[]{:S(2)}, u32[]{:S(2)}) collective-permute-start(bf16[16,32,1024]{2,1,0:T(8,128)(2,1)} %pad_maximum_fusion.refs_4_), channel_id=1, source_target_pairs={{4,0},{0,4},{5,1},{1,5},{6,2},{2,6},{7,3},{3,7},{12,8},{8,12},{13,... | collective-permute-start | bytes 3145736 | tf_op jit(solution)/shard_map/gather_key_proj/ppermute | solution.py:32
  84.9 46.6 %collective-permute-start.1 = (bf16[640,1024]{1,0:T(8,128)(2,1)}, bf16[640,1024]{1,0:T(8,128)(2,1)}, u32[]{:S(2)}, u32[]{:S(2)}) collective-permute-start(bf16[640,1024]{1,0:T(8,128)(2,1)} %collective-permute-done.refs_1_), channel_id=1, source_target_pairs={{1,0},{2,1},{3,2},{0,3},{5,4},{6,5},{7,6},{4,7},{9,8},{10,9},{11,1... | collective-permute-start | bytes 3932168 | tf_op jit(solution)/shard_map/ppermute | solution.py:32
  98.2 33.3 %collective-permute-start.10 = (bf16[16,32,1024]{2,1,0:T(8,128)(2,1)}, bf16[16,32,1024]{2,1,0:T(8,128)(2,1)}, u32[]{:S(2)}, u32[]{:S(2)}) collective-permute-start(bf16[16,32,1024]{2,1,0:T(8,128)(2,1)} %collective-permute-done.6.refs_6_), channel_id=1, source_target_pairs={{4,0},{0,4},{5,1},{1,5},{6,2},{2,6},{7,3},{3,7},{12,8},{8,12},{13,... | collective-permute-start | bytes 3145736 | tf_op jit(solution)/shard_map/gather_key_proj/ppermute | solution.py:32
  100.2 29.1 %collective-permute-start.7 = (bf16[16,32,1024]{2,1,0:T(8,128)(2,1)}, bf16[16,32,1024]{2,1,0:T(8,128)(2,1)S(1)}, u32[]{:S(2)}, u32[]{:S(2)}) collective-permute-start(bf16[16,32,1024]{2,1,0:T(8,128)(2,1)} %collective-permute-done.6.refs_6_), channel_id=1, source_target_pairs={{128,0},{256,128},{384,256},{0,384},{129,1},{257,129},{385,257},{1... | collective-permute-start | bytes 3145736 | tf_op jit(solution)/shard_map/gather_key_proj/ppermute | solution.py:32
  105.7 25.8 %collective-permute-start.12 = (bf16[16,32,1024]{2,1,0:T(8,128)(2,1)}, bf16[16,32,1024]{2,1,0:T(8,128)(2,1)}, u32[]{:S(2)}, u32[]{:S(2)}) collective-permute-start(bf16[16,32,1024]{2,1,0:T(8,128)(2,1)} %collective-permute-done.11.refs_8_), channel_id=1, source_target_pairs={{4,0},{0,4},{5,1},{1,5},{6,2},{2,6},{7,3},{3,7},{12,8},{8,12},{13,... | collective-permute-start | bytes 3145736 | tf_op jit(solution)/shard_map/gather_key_proj/ppermute | solution.py:32
  107.9 0.9 copy-start.5
  117.1 26.3 %all-to-all-start.2 = ((f32[128,1,128]{2,1,0:T(1,128)}), f32[128,1,128]{2,1,0:T(1,128)}, u32[]{:S(2)}, u32[]{:S(2)}) async-start(f32[128,1,128]{2,1,0:T(1,128)} %bitcast.53), calls=%async_computation.2 | async-start | bytes 131072 | tf_op jit(solution)/shard_map/reduce_scores/all_to_all | solution.py:442
  129.2 14.2 %copy-start = (bf16[4,20,8,1024]{3,2,1,0:T(8,128)(2,1)S(1)}, bf16[4,20,8,1024]{3,2,1,0:T(8,128)(2,1)}, u32[]{:S(2)}) copy-start(bf16[4,20,8,1024]{3,2,1,0:T(8,128)(2,1)} %param.14) | copy-start | bytes 3932164
  129.2 14.2 %copy-start.4 = (s32[4]{0:T(128)S(1)}, s32[4]{0:T(128)}, u32[]{:S(2)}) copy-start(s32[4]{0:T(128)} %pad_add_fusion.place) | copy-start | bytes 52
  129.3 14.1 %collective-permute-start.8 = (bf16[16,32,1024]{2,1,0:T(8,128)(2,1)S(1)}, bf16[16,32,1024]{2,1,0:T(8,128)(2,1)S(1)}, u32[]{:S(2)}, u32[]{:S(2)}) collective-permute-start(bf16[16,32,1024]{2,1,0:T(8,128)(2,1)S(1)} %collective-permute-done.7.refs_4_), channel_id=1, source_target_pairs={{4,0},{0,4},{5,1},{1,5},{6,2},{2,6},{7,3},{3,7},{12,8},{8,12},{13,... | collective-permute-start | bytes 3145736 | tf_op jit(solution)/shard_map/gather_key_proj/ppermute | solution.py:32
  188.9 1.2 copy-start.1
  190.1 1.1 copy-start.2
  191.3 0.9 copy-start.3
  198.9 3.6 %collective-permute-start.13 = (f32[384,192]{1,0:T(8,128)S(1)}, f32[384,192]{1,0:T(8,128)S(1)}, u32[]{:S(2)}, u32[]{:S(2)}) collective-permute-start(f32[384,192]{1,0:T(8,128)S(1)} %get-tuple-element.18), channel_id=1, source_target_pairs={{4,0},{0,4},{5,1},{1,5},{6,2},{2,6},{7,3},{3,7},{12,8},{8,12},{13,... | collective-permute-start | bytes 884744 | tf_op jit(solution)/shard_map/reduce_gradient/ppermute | solution.py:32
  214.3 17.7 %all-to-all-start.6 = ((f32[16,6,192]{2,1,0:T(8,128)}), f32[16,6,192]{2,1,0:T(8,128)S(1)}, u32[]{:S(2)}, u32[]{:S(2)}) async-start(f32[16,6,192]{2,1,0:T(8,128)} %reshape.202), calls=%async_computation.6 | async-start | bytes 262144 | tf_op jit(solution)/shard_map/reduce_gradient/all_to_all | solution.py:494
  232.7 8.7 %all-to-all-start.7 = ((f32[4,6,192]{2,1,0:T(8,128)}), f32[4,6,192]{2,1,0:T(8,128)S(1)}, u32[]{:S(2)}, u32[]{:S(2)}) async-start(f32[4,6,192]{2,1,0:T(8,128)} %broadcast_in_dim.12), calls=%async_computation.7 | async-start | bytes 65536 | tf_op jit(solution)/shard_map/reduce_gradient/all_to_all | solution.py:37

commit v15 on v14

--- a/solution.py
+++ b/solution.py
@@ -467,6 +467,7 @@
             out_shape=jax.ShapeDtypeStruct((nz, n_pair, LANES), jnp.float32),
             in_specs=[vmem],
             out_specs=vmem,
+            compiler_params=pltpu.CompilerParams(vmem_limit_bytes=8 << 20),
             name="coef",
         )(packets)
         coef = lax.all_to_all(coef, Z_BY_CLASS, 0, 0, tiled=True).reshape(n_index, LANES)

time: 245 us -> 239 us (0.976)
  local copies, waits for them, and re-layouts: 10.1 us -> 6.27 us
    unnamed x23, local copies, waits for them, and re-layouts: 4.83 us -> 0.99 us
  transfers between devices with their start and end apart: 19 -> 19, of which waited for: 8 -> 8; matrix products, arithmetic and copies ran while one was open for 4% -> 3% of each run, Pallas kernels for 8% -> 8%
where the time goes in v15:
time: 239 us; the launch traced here: 237 us
  starting transfers between devices  89.1 us (37%)
  waiting for transfers between devices  52.6 us (22%)
  blocking collectives  46.7 us (20%)
  Pallas kernels  33.1 us (14%)
  other arithmetic  7.61 us (3%)
  local copies, waits for them, and re-layouts  6.27 us (3%)
    ppermute x14, starting transfers between devices, shift(): return lax.ppermute(x, axis, [((i + step) % size, i) for i in range(size)])  45.4 us
    all_to_all x3, starting transfers between devices, send_all(): lax.all_to_all(jnp.broadcast_to(x[None], (size, *x.shape)), axis, 0, 0, t...  28 us
    all_to_all x1, blocking collectives, body(): lax.all_to_all(coef, Z_BY_CLASS, 0, 0, tiled=True).reshape(n_index, LANES)  23.9 us
    ppermute x14, waiting for transfers between devices, shift(): return lax.ppermute(x, axis, [((i + step) % size, i) for i in range(size)])  23.9 us
    all_to_all x3, waiting for transfers between devices, send_all(): lax.all_to_all(jnp.broadcast_to(x[None], (size, *x.shape)), axis, 0, 0, t...  13.8 us
    all_to_all x1, waiting for transfers between devices, body(): term = jnp.sum(lax.all_to_all(term, Z, 0, 0, tiled=True), axis=0)  13.6 us
    all_to_all x1, starting transfers between devices, body(): states = lax.all_to_all(state, ('y', 'core', *Z_BY_CLASS), 0, 0, tiled=True)  12.2 us
    all_to_all x1, blocking collectives, body(): lax.all_to_all(packet, NEAR, 0, 0, tiled=True)  11.8 us
  transfers between devices with their start and end apart: 19, of which 8 were waited for; matrix products, arithmetic and copies ran while one was open for 3% of the time, Pallas kernels for 8%

profile of v15, /device:TPU:6, one launch (start us, length us, event | category | flops | bytes accessed | tf_op | source)
XLA Modules:
  0.0 236.6 jit_solution(18234331485654647075)
XLA Ops:
  0.6 0.7 fusion.31
  1.3 0.8 fusion.27
  2.1 0.8 fusion.3
  3.0 0.8 broadcast_in_dim.10
  3.7 15.1 %all-to-all-start = ((bf16[4,33,1024]{2,1,0:T(8,128)(2,1)}), bf16[4,33,1024]{2,1,0:T(8,128)(2,1)S(1)}, u32[]{:S(2)}, u32[]{:S(2)}) async-start(bf16[4,33,1024]{2,1,0:T(8,128)(2,1)} %broadcast_in_dim.10), calls=%async_computation | async-start | bytes 655360 | tf_op jit(solution)/shard_map/gather_key_proj/all_to_all | solution.py:37
  18.8 2.7 %collective-permute-start = (bf16[640,1024]{1,0:T(8,128)(2,1)}, bf16[640,1024]{1,0:T(8,128)(2,1)}, u32[]{:S(2)}, u32[]{:S(2)}) collective-permute-start(bf16[640,1024]{1,0:T(8,128)(2,1)} %bitcast.42), channel_id=1, source_target_pairs={{1,0},{2,1},{3,2},{0,3},{5,4},{6,5},{7,6},{4,7},{9,8},{10,9},{11,1... | collective-permute-start | bytes 3932168 | tf_op jit(solution)/shard_map/gather_enc_out/ppermute | solution.py:32
  21.5 4.3 %collective-permute-start.2 = (bf16[640,1024]{1,0:T(8,128)(2,1)}, bf16[640,1024]{1,0:T(8,128)(2,1)}, u32[]{:S(2)}, u32[]{:S(2)}) collective-permute-start(bf16[640,1024]{1,0:T(8,128)(2,1)} %bitcast.43), channel_id=1, source_target_pairs={{3,0},{0,1},{1,2},{2,3},{7,4},{4,5},{5,6},{6,7},{11,8},{8,9},{9,10... | collective-permute-start | bytes 3932168 | tf_op jit(solution)/shard_map/gather_enc_out/ppermute | solution.py:32
  26.3 11.6 %all-to-all-done = bf16[4,33,1024]{2,1,0:T(8,128)(2,1)S(1)} async-done(((bf16[4,33,1024]{2,1,0:T(8,128)(2,1)}), bf16[4,33,1024]{2,1,0:T(8,128)(2,1)S(1)}, u32[]{:S(2)}, u32[]{:S(2)}) %all-to-all-start) | async-done | bytes 270368 | tf_op jit(solution)/shard_map/gather_key_proj/all_to_all | solution.py:37
  37.9 7.2 %collective-permute-start.3 = (bf16[4,33,1024]{2,1,0:T(8,128)(2,1)S(1)}, bf16[4,33,1024]{2,1,0:T(8,128)(2,1)S(1)}, u32[]{:S(2)}, u32[]{:S(2)}) collective-permute-start(bf16[4,33,1024]{2,1,0:T(8,128)(2,1)S(1)} %all-to-all-done), channel_id=1, source_target_pairs={{8,0},{16,8},{24,16},{32,24},{40,32},{48,40},{56,48},{64,56},{72,6... | collective-permute-start | bytes 811016 | tf_op jit(solution)/shard_map/gather_key_proj/ppermute | solution.py:32
  45.0 1.9 collective-permute-start.4
  47.0 3.9 %collective-permute-start.5 = (bf16[4,33,1024]{2,1,0:T(8,128)(2,1)S(1)}, bf16[4,33,1024]{2,1,0:T(8,128)(2,1)S(1)}, u32[]{:S(2)}, u32[]{:S(2)}) collective-permute-start(bf16[4,33,1024]{2,1,0:T(8,128)(2,1)S(1)} %all-to-all-done), channel_id=1, source_target_pairs={{120,0},{0,8},{8,16},{16,24},{24,32},{32,40},{40,48},{48,56},{56,6... | collective-permute-start | bytes 811016 | tf_op jit(solution)/shard_map/gather_key_proj/ppermute | solution.py:32
  50.9 0.6 pad_add_fusion.1.place
  52.2 3.4 %collective-permute-done.3 = bf16[4,33,1024]{2,1,0:T(8,128)(2,1)S(1)} collective-permute-done((bf16[4,33,1024]{2,1,0:T(8,128)(2,1)S(1)}, bf16[4,33,1024]{2,1,0:T(8,128)(2,1)S(1)}, u32[]{:S(2)}, u32[]{:S(2)}) %collective-permute-start.3) | collective-permute-done | bytes 270368 | tf_op jit(solution)/shard_map/gather_key_proj/ppermute | solution.py:32
  55.7 8.2 %collective-permute-done.4 = bf16[4,33,1024]{2,1,0:T(8,128)(2,1)S(1)} collective-permute-done((bf16[4,33,1024]{2,1,0:T(8,128)(2,1)S(1)}, bf16[4,33,1024]{2,1,0:T(8,128)(2,1)S(1)}, u32[]{:S(2)}, u32[]{:S(2)}) %collective-permute-start.4) | collective-permute-done | bytes 270368 | tf_op jit(solution)/shard_map/gather_key_proj/ppermute | solution.py:32
  63.9 1.1 pad_maximum_fusion.refs_4_
  65.0 4.9 %collective-permute-start.6 = (bf16[16,32,1024]{2,1,0:T(8,128)(2,1)}, bf16[16,32,1024]{2,1,0:T(8,128)(2,1)}, u32[]{:S(2)}, u32[]{:S(2)}) collective-permute-start(bf16[16,32,1024]{2,1,0:T(8,128)(2,1)} %pad_maximum_fusion.refs_4_), channel_id=1, source_target_pairs={{128,0},{256,128},{384,256},{0,384},{129,1},{257,129},{385,257},{1... | collective-permute-start | bytes 3145736 | tf_op jit(solution)/shard_map/gather_key_proj/ppermute | solution.py:32
  69.9 1.9 collective-permute-start.11
  72.1 1.0 broadcast_in_dim.11
  73.2 7.6 %all-to-all-start.1 = ((bf16[32,16,896]{2,1,0:T(8,128)(2,1)}), bf16[32,16,896]{2,1,0:T(8,128)(2,1)S(1)}, u32[]{:S(2)}, u32[]{:S(2)}) async-start(bf16[32,16,896]{2,1,0:T(8,128)(2,1)} %broadcast_in_dim.11), calls=%async_computation.1 | async-start | bytes 1835008 | tf_op jit(solution)/shard_map/gather_queries/all_to_all | solution.py:37
  81.4 1.3 fusion.refs_3_
  82.7 2.0 collective-permute-start.9
  84.8 2.7 %collective-permute-start.1 = (bf16[640,1024]{1,0:T(8,128)(2,1)}, bf16[640,1024]{1,0:T(8,128)(2,1)}, u32[]{:S(2)}, u32[]{:S(2)}) collective-permute-start(bf16[640,1024]{1,0:T(8,128)(2,1)} %collective-permute-done.refs_1_), channel_id=1, source_target_pairs={{1,0},{2,1},{3,2},{0,3},{5,4},{6,5},{7,6},{4,7},{9,8},{10,9},{11,1... | collective-permute-start | bytes 3932168 | tf_op jit(solution)/shard_map/ppermute | solution.py:32
  87.5 10.6 %collective-permute-done.6.refs_6_ = bf16[16,32,1024]{2,1,0:T(8,128)(2,1)} collective-permute-done((bf16[16,32,1024]{2,1,0:T(8,128)(2,1)}, bf16[16,32,1024]{2,1,0:T(8,128)(2,1)}, u32[]{:S(2)}, u32[]{:S(2)}) %collective-permute-start.6) | collective-permute-done | bytes 1048608 | tf_op jit(solution)/shard_map/gather_key_proj/ppermute | solution.py:32
  98.1 1.9 collective-permute-start.10
  100.0 5.6 %collective-permute-start.7 = (bf16[16,32,1024]{2,1,0:T(8,128)(2,1)}, bf16[16,32,1024]{2,1,0:T(8,128)(2,1)S(1)}, u32[]{:S(2)}, u32[]{:S(2)}) collective-permute-start(bf16[16,32,1024]{2,1,0:T(8,128)(2,1)} %collective-permute-done.6.refs_6_), channel_id=1, source_target_pairs={{128,0},{256,128},{384,256},{0,384},{129,1},{257,129},{385,257},{1... | collective-permute-start | bytes 3145736 | tf_op jit(solution)/shard_map/gather_key_proj/ppermute | solution.py:32
  105.6 2.1 collective-permute-start.12
  107.8 0.9 copy-done.5
  108.7 8.2 %scores.1 = (f32[128,128]{1,0:T(8,128)}, f32[256,128]{1,0:T(8,128)}, f32[1024,192]{1,0:T(8,128)}, bf16[768,512]{1,0:T(8,128)(2,1)}) custom-call(s32[2]{0:T(128)} %pad_add_fusion.1.place, bf16[32,16,896]{2,1,0:T(8,128)(2,1)} %copy-done.5, bf16[768,768]{1,0:T(8,128)(2,1)} %refs_1_.1, f32[512,768]{1,0:T(8,128)} %refs_2_.1, bf16[768,768]{1,0:T(8,128)(2,1)} %fusion.refs_3_), custom_call_target="tpu_custom_call" | custom-call | flops 68719476736 | bytes 8388608 | tf_op jit(solution)/shard_map/scores/scores/pallas_call | solution.py:423
  116.9 12.2 %all-to-all-start.2 = ((f32[128,1,128]{2,1,0:T(1,128)}), f32[128,1,128]{2,1,0:T(1,128)}, u32[]{:S(2)}, u32[]{:S(2)}) async-start(f32[128,1,128]{2,1,0:T(1,128)} %bitcast.53), calls=%async_computation.2 | async-start | bytes 131072 | tf_op jit(solution)/shard_map/reduce_scores/all_to_all | solution.py:442
  129.1 2.2 collective-permute-start.8
  131.4 10.5 %early_keys.1.refs_6_ = f32[640,1024]{1,0:T(8,128)} custom-call(s32[4]{0:T(128)} %pad_add_fusion.place, bf16[640,1024]{1,0:T(8,128)(2,1)} %bitcast.44, bf16[640,1024]{1,0:T(8,128)(2,1)} %collective-permute-done.refs_1_, bf16[640,1024]{1,0:T(8,128)(2,1)} %collective-permute-done.1.refs_2_, bf16[640,1024]{1,0:T(8,128)(2,1)} %collective-permute-done.2.refs_3_, ...), custom_call_target="tpu_custom_call" | custom-call | flops 16106127360 | bytes 13631488 | tf_op jit(solution)/shard_map/attention/early_keys/pallas_call | solution.py:187
  141.9 1.4 all-to-all-done.2
  143.3 7.4 %late_heads.1 = (f32[32,256]{1,0:T(8,128)S(1)}, f32[8,128]{1,0:T(8,128)S(1)}) custom-call(s32[4]{0:T(128)S(1)} %copy-done.4, bf16[640,1024]{1,0:T(8,128)(2,1)S(1)} %bitcast.45, bf16[640,1024]{1,0:T(8,128)(2,1)} %collective-permute-done.refs_1_, bf16[640,1024]{1,0:T(8,128)(2,1)} %collective-permute-done.1.refs_2_, ...), custom_call_target="tpu_custom_call" | custom-call | flops 1342177280 | bytes 6291456 | tf_op jit(solution)/shard_map/attention/late_heads/pallas_call | solution.py:202
  150.7 11.8 %all_to_all.50 = f32[32,1,256]{2,1,0:T(1,128)S(1)} all-to-all(f32[32,1,256]{2,1,0:T(1,128)S(1)} %copy.26), channel_id=1, replica_groups=mesh['y'=4,'zq'=4,'zr'=4,'core'=2,'reader'=4] {'reader','y','core'}, dimensions={0} | all-to-all | bytes 65536 | tf_op jit(solution)/shard_map/targets/all_to_all | solution.py:464
  162.8 23.9 %all_to_all.51 = f32[16,8,128]{2,1,0:T(8,128)S(1)} all-to-all(f32[16,8,128]{2,1,0:T(8,128)S(1)} %coef.1), channel_id=1, replica_groups=mesh['y'=4,'zq'=4,'zr'=4,'core'=2,'reader'=4] {'zr','zq'}, dimensions={0} | all-to-all | bytes 131072 | tf_op jit(solution)/shard_map/targets/all_to_all | solution.py:473
  186.7 6.8 %gradient.1 = (f32[384,192]{1,0:T(8,128)S(1)}, f32[384,192]{1,0:T(8,128)S(1)}) custom-call(f32[128,128]{1,0:T(8,128)S(1)} %bitcast.46, f32[256,128]{1,0:T(8,128)S(1)} %copy-done.3, f32[1024,192]{1,0:T(8,128)S(1)} %copy-done.1, bf16[768,512]{1,0:T(8,128)(2,1)S(1)} %copy-done.2), custom_call_target="tpu_custom_call" | custom-call | tf_op jit(solution)/shard_map/gradient/gradient/pallas_call | solution.py:477
  193.5 1.9 collective-permute-start.13
  195.4 1.7 collective-permute-done.13
  197.1 11.0 %all_to_all.52 = f32[4,96,192]{2,1,0:T(8,128)S(1)} all-to-all(f32[4,96,192]{2,1,0:T(8,128)S(1)} %bitcast.51), channel_id=1, replica_groups=mesh['y'=4,'zq'=4,'zr'=4,'core'=2,'reader'=4] {'y'}, dimensions={0} | all-to-all | bytes 589824 | tf_op jit(solution)/shard_map/reduce_gradient/all_to_all | solution.py:493
  208.2 0.7 reshape.202
  208.9 3.5 %all-to-all-start.6 = ((f32[16,6,192]{2,1,0:T(8,128)}), f32[16,6,192]{2,1,0:T(8,128)S(1)}, u32[]{:S(2)}, u32[]{:S(2)}) async-start(f32[16,6,192]{2,1,0:T(8,128)} %reshape.202), calls=%async_computation.6 | async-start | bytes 262144 | tf_op jit(solution)/shard_map/reduce_gradient/all_to_all | solution.py:495
  212.4 0.6 slice.42
  213.0 13.6 %all-to-all-done.6 = f32[16,6,192]{2,1,0:T(8,128)S(1)} async-done(((f32[16,6,192]{2,1,0:T(8,128)}), f32[16,6,192]{2,1,0:T(8,128)S(1)}, u32[]{:S(2)}, u32[]{:S(2)}) %all-to-all-start.6) | async-done | bytes 73760 | tf_op jit(solution)/shard_map/reduce_gradient/all_to_all | solution.py:495
  226.6 0.6 broadcast_in_dim.12
  227.2 5.3 %all-to-all-start.7 = ((f32[4,6,192]{2,1,0:T(8,128)}), f32[4,6,192]{2,1,0:T(8,128)S(1)}, u32[]{:S(2)}, u32[]{:S(2)}) async-start(f32[4,6,192]{2,1,0:T(8,128)} %broadcast_in_dim.12), calls=%async_computation.7 | async-start | bytes 65536 | tf_op jit(solution)/shard_map/reduce_gradient/all_to_all | solution.py:37
  232.5 1.2 log_bitcast_fusion
  233.7 2.2 all-to-all-done.7
  235.9 0.7 reshape.203
  (68 shorter events, 2.4 us)
Async XLA Ops:
  0.6 25.2 %copy-start.6 = (bf16[4,16,1024]{2,1,0:T(8,128)(2,1)S(1)}, bf16[4,16,1024]{2,1,0:T(8,128)(2,1)}, u32[]{:S(2)}) copy-start(bf16[4,16,1024]{2,1,0:T(8,128)(2,1)} %param.17) | copy-start | bytes 393220
  3.7 34.2 %all-to-all-start = ((bf16[4,33,1024]{2,1,0:T(8,128)(2,1)}), bf16[4,33,1024]{2,1,0:T(8,128)(2,1)S(1)}, u32[]{:S(2)}, u32[]{:S(2)}) async-start(bf16[4,33,1024]{2,1,0:T(8,128)(2,1)} %broadcast_in_dim.10), calls=%async_computation | async-start | bytes 655360 | tf_op jit(solution)/shard_map/gather_key_proj/all_to_all | solution.py:37
  18.8 66.0 %collective-permute-start = (bf16[640,1024]{1,0:T(8,128)(2,1)}, bf16[640,1024]{1,0:T(8,128)(2,1)}, u32[]{:S(2)}, u32[]{:S(2)}) collective-permute-start(bf16[640,1024]{1,0:T(8,128)(2,1)} %bitcast.42), channel_id=1, source_target_pairs={{1,0},{2,1},{3,2},{0,3},{5,4},{6,5},{7,6},{4,7},{9,8},{10,9},{11,1... | collective-permute-start | bytes 3932168 | tf_op jit(solution)/shard_map/gather_enc_out/ppermute | solution.py:32
  21.5 78.5 %collective-permute-start.2 = (bf16[640,1024]{1,0:T(8,128)(2,1)}, bf16[640,1024]{1,0:T(8,128)(2,1)}, u32[]{:S(2)}, u32[]{:S(2)}) collective-permute-start(bf16[640,1024]{1,0:T(8,128)(2,1)} %bitcast.43), channel_id=1, source_target_pairs={{3,0},{0,1},{1,2},{2,3},{7,4},{4,5},{5,6},{6,7},{11,8},{8,9},{9,10... | collective-permute-start | bytes 3932168 | tf_op jit(solution)/shard_map/gather_enc_out/ppermute | solution.py:32
  25.9 26.0 %copy-start.7 = (s32[4,20]{1,0:T(4,128)S(1)}, s32[4,20]{1,0:T(4,128)}, u32[]{:S(2)}) copy-start(s32[4,20]{1,0:T(4,128)} %param.13) | copy-start | bytes 964
  25.9 26.2 %copy-start.8 = (bf16[1024]{0:T(1024)(128)(2,1)S(1)}, bf16[1024]{0:T(1024)(128)(2,1)}, u32[]{:S(2)}) copy-start(bf16[1024]{0:T(1024)(128)(2,1)} %param.16) | copy-start | bytes 6148
  37.9 17.8 %collective-permute-start.3 = (bf16[4,33,1024]{2,1,0:T(8,128)(2,1)S(1)}, bf16[4,33,1024]{2,1,0:T(8,128)(2,1)S(1)}, u32[]{:S(2)}, u32[]{:S(2)}) collective-permute-start(bf16[4,33,1024]{2,1,0:T(8,128)(2,1)S(1)} %all-to-all-done), channel_id=1, source_target_pairs={{8,0},{16,8},{24,16},{32,24},{40,32},{48,40},{56,48},{64,56},{72,6... | collective-permute-start | bytes 811016 | tf_op jit(solution)/shard_map/gather_key_proj/ppermute | solution.py:32
  45.0 18.8 %collective-permute-start.4 = (bf16[4,33,1024]{2,1,0:T(8,128)(2,1)S(1)}, bf16[4,33,1024]{2,1,0:T(8,128)(2,1)S(1)}, u32[]{:S(2)}, u32[]{:S(2)}) collective-permute-start(bf16[4,33,1024]{2,1,0:T(8,128)(2,1)S(1)} %all-to-all-done), channel_id=1, source_target_pairs={{16,0},{24,8},{32,16},{40,24},{48,32},{56,40},{64,48},{72,56},{80,... | collective-permute-start | bytes 811016 | tf_op jit(solution)/shard_map/gather_key_proj/ppermute | solution.py:32
  47.0 16.9 %collective-permute-start.5 = (bf16[4,33,1024]{2,1,0:T(8,128)(2,1)S(1)}, bf16[4,33,1024]{2,1,0:T(8,128)(2,1)S(1)}, u32[]{:S(2)}, u32[]{:S(2)}) collective-permute-start(bf16[4,33,1024]{2,1,0:T(8,128)(2,1)S(1)} %all-to-all-done), channel_id=1, source_target_pairs={{120,0},{0,8},{8,16},{16,24},{24,32},{32,40},{40,48},{48,56},{56,6... | collective-permute-start | bytes 811016 | tf_op jit(solution)/shard_map/gather_key_proj/ppermute | solution.py:32
  65.0 33.1 %collective-permute-start.6 = (bf16[16,32,1024]{2,1,0:T(8,128)(2,1)}, bf16[16,32,1024]{2,1,0:T(8,128)(2,1)}, u32[]{:S(2)}, u32[]{:S(2)}) collective-permute-start(bf16[16,32,1024]{2,1,0:T(8,128)(2,1)} %pad_maximum_fusion.refs_4_), channel_id=1, source_target_pairs={{128,0},{256,128},{384,256},{0,384},{129,1},{257,129},{385,257},{1... | collective-permute-start | bytes 3145736 | tf_op jit(solution)/shard_map/gather_key_proj/ppermute | solution.py:32
  69.9 35.7 %collective-permute-start.11 = (bf16[16,32,1024]{2,1,0:T(8,128)(2,1)}, bf16[16,32,1024]{2,1,0:T(8,128)(2,1)}, u32[]{:S(2)}, u32[]{:S(2)}) collective-permute-start(bf16[16,32,1024]{2,1,0:T(8,128)(2,1)} %pad_maximum_fusion.refs_4_), channel_id=1, source_target_pairs={{384,0},{0,128},{128,256},{256,384},{385,1},{1,129},{129,257},{257... | collective-permute-start | bytes 3145736 | tf_op jit(solution)/shard_map/gather_key_proj/ppermute | solution.py:32
  73.2 34.6 %all-to-all-start.1 = ((bf16[32,16,896]{2,1,0:T(8,128)(2,1)}), bf16[32,16,896]{2,1,0:T(8,128)(2,1)S(1)}, u32[]{:S(2)}, u32[]{:S(2)}) async-start(bf16[32,16,896]{2,1,0:T(8,128)(2,1)} %broadcast_in_dim.11), calls=%async_computation.1 | async-start | bytes 1835008 | tf_op jit(solution)/shard_map/gather_queries/all_to_all | solution.py:37
  82.7 48.7 %collective-permute-start.9 = (bf16[16,32,1024]{2,1,0:T(8,128)(2,1)}, bf16[16,32,1024]{2,1,0:T(8,128)(2,1)}, u32[]{:S(2)}, u32[]{:S(2)}) collective-permute-start(bf16[16,32,1024]{2,1,0:T(8,128)(2,1)} %pad_maximum_fusion.refs_4_), channel_id=1, source_target_pairs={{4,0},{0,4},{5,1},{1,5},{6,2},{2,6},{7,3},{3,7},{12,8},{8,12},{13,... | collective-permute-start | bytes 3145736 | tf_op jit(solution)/shard_map/gather_key_proj/ppermute | solution.py:32
  84.8 46.6 %collective-permute-start.1 = (bf16[640,1024]{1,0:T(8,128)(2,1)}, bf16[640,1024]{1,0:T(8,128)(2,1)}, u32[]{:S(2)}, u32[]{:S(2)}) collective-permute-start(bf16[640,1024]{1,0:T(8,128)(2,1)} %collective-permute-done.refs_1_), channel_id=1, source_target_pairs={{1,0},{2,1},{3,2},{0,3},{5,4},{6,5},{7,6},{4,7},{9,8},{10,9},{11,1... | collective-permute-start | bytes 3932168 | tf_op jit(solution)/shard_map/ppermute | solution.py:32
  98.1 33.3 %collective-permute-start.10 = (bf16[16,32,1024]{2,1,0:T(8,128)(2,1)}, bf16[16,32,1024]{2,1,0:T(8,128)(2,1)}, u32[]{:S(2)}, u32[]{:S(2)}) collective-permute-start(bf16[16,32,1024]{2,1,0:T(8,128)(2,1)} %collective-permute-done.6.refs_6_), channel_id=1, source_target_pairs={{4,0},{0,4},{5,1},{1,5},{6,2},{2,6},{7,3},{3,7},{12,8},{8,12},{13,... | collective-permute-start | bytes 3145736 | tf_op jit(solution)/shard_map/gather_key_proj/ppermute | solution.py:32
  100.0 29.1 %collective-permute-start.7 = (bf16[16,32,1024]{2,1,0:T(8,128)(2,1)}, bf16[16,32,1024]{2,1,0:T(8,128)(2,1)S(1)}, u32[]{:S(2)}, u32[]{:S(2)}) collective-permute-start(bf16[16,32,1024]{2,1,0:T(8,128)(2,1)} %collective-permute-done.6.refs_6_), channel_id=1, source_target_pairs={{128,0},{256,128},{384,256},{0,384},{129,1},{257,129},{385,257},{1... | collective-permute-start | bytes 3145736 | tf_op jit(solution)/shard_map/gather_key_proj/ppermute | solution.py:32
  105.6 25.8 %collective-permute-start.12 = (bf16[16,32,1024]{2,1,0:T(8,128)(2,1)}, bf16[16,32,1024]{2,1,0:T(8,128)(2,1)}, u32[]{:S(2)}, u32[]{:S(2)}) collective-permute-start(bf16[16,32,1024]{2,1,0:T(8,128)(2,1)} %collective-permute-done.11.refs_8_), channel_id=1, source_target_pairs={{4,0},{0,4},{5,1},{1,5},{6,2},{2,6},{7,3},{3,7},{12,8},{8,12},{13,... | collective-permute-start | bytes 3145736 | tf_op jit(solution)/shard_map/gather_key_proj/ppermute | solution.py:32
  107.8 0.9 copy-start.5
  116.9 26.3 %all-to-all-start.2 = ((f32[128,1,128]{2,1,0:T(1,128)}), f32[128,1,128]{2,1,0:T(1,128)}, u32[]{:S(2)}, u32[]{:S(2)}) async-start(f32[128,1,128]{2,1,0:T(1,128)} %bitcast.53), calls=%async_computation.2 | async-start | bytes 131072 | tf_op jit(solution)/shard_map/reduce_scores/all_to_all | solution.py:442
  129.1 14.2 %copy-start = (bf16[4,20,8,1024]{3,2,1,0:T(8,128)(2,1)S(1)}, bf16[4,20,8,1024]{3,2,1,0:T(8,128)(2,1)}, u32[]{:S(2)}) copy-start(bf16[4,20,8,1024]{3,2,1,0:T(8,128)(2,1)} %param.14) | copy-start | bytes 3932164
  129.1 14.2 %copy-start.4 = (s32[4]{0:T(128)S(1)}, s32[4]{0:T(128)}, u32[]{:S(2)}) copy-start(s32[4]{0:T(128)} %pad_add_fusion.place) | copy-start | bytes 52
  129.1 14.1 %collective-permute-start.8 = (bf16[16,32,1024]{2,1,0:T(8,128)(2,1)S(1)}, bf16[16,32,1024]{2,1,0:T(8,128)(2,1)S(1)}, u32[]{:S(2)}, u32[]{:S(2)}) collective-permute-start(bf16[16,32,1024]{2,1,0:T(8,128)(2,1)S(1)} %collective-permute-done.7.refs_4_), channel_id=1, source_target_pairs={{4,0},{0,4},{5,1},{1,5},{6,2},{2,6},{7,3},{3,7},{12,8},{8,12},{13,... | collective-permute-start | bytes 3145736 | tf_op jit(solution)/shard_map/gather_key_proj/ppermute | solution.py:32
  143.3 43.4 %copy-start.1 = (f32[1024,192]{1,0:T(8,128)S(1)}, f32[1024,192]{1,0:T(8,128)}, u32[]{:S(2)}) copy-start(f32[1024,192]{1,0:T(8,128)} %get-tuple-element.15.refs_1_) | copy-start | bytes 2359300
  143.3 43.4 %copy-start.2 = (bf16[768,512]{1,0:T(8,128)(2,1)S(1)}, bf16[768,512]{1,0:T(8,128)(2,1)}, u32[]{:S(2)}) copy-start(bf16[768,512]{1,0:T(8,128)(2,1)} %get-tuple-element.16.refs_2_) | copy-start | bytes 2359300
  143.3 43.4 %copy-start.3 = (f32[256,128]{1,0:T(8,128)S(1)}, f32[256,128]{1,0:T(8,128)}, u32[]{:S(2)}) copy-start(f32[256,128]{1,0:T(8,128)} %get-tuple-element.14.refs_0_) | copy-start | bytes 393220
  193.5 3.6 %collective-permute-start.13 = (f32[384,192]{1,0:T(8,128)S(1)}, f32[384,192]{1,0:T(8,128)S(1)}, u32[]{:S(2)}, u32[]{:S(2)}) collective-permute-start(f32[384,192]{1,0:T(8,128)S(1)} %get-tuple-element.18), channel_id=1, source_target_pairs={{4,0},{0,4},{5,1},{1,5},{6,2},{2,6},{7,3},{3,7},{12,8},{8,12},{13,... | collective-permute-start | bytes 884744 | tf_op jit(solution)/shard_map/reduce_gradient/ppermute | solution.py:32
  208.9 17.7 %all-to-all-start.6 = ((f32[16,6,192]{2,1,0:T(8,128)}), f32[16,6,192]{2,1,0:T(8,128)S(1)}, u32[]{:S(2)}, u32[]{:S(2)}) async-start(f32[16,6,192]{2,1,0:T(8,128)} %reshape.202), calls=%async_computation.6 | async-start | bytes 262144 | tf_op jit(solution)/shard_map/reduce_gradient/all_to_all | solution.py:495
  227.2 8.7 %all-to-all-start.7 = ((f32[4,6,192]{2,1,0:T(8,128)}), f32[4,6,192]{2,1,0:T(8,128)S(1)}, u32[]{:S(2)}, u32[]{:S(2)}) async-start(f32[4,6,192]{2,1,0:T(8,128)} %broadcast_in_dim.12), calls=%async_computation.7 | async-start | bytes 65536 | tf_op jit(solution)/shard_map/reduce_gradient/all_to_all | solution.py:37
